TPU v7x, 256 devices: a whole 4x4x8 slice. The times are simulated.
256 devices in a mesh: img: 32 (over x, y, core), txt: 8 (over z).
Axes of the slice: x: 4, y: 4, z: 8, core: 2. Of those that a mesh axis runs over, the one named last changes fastest.
Arguments:
- image_emb: bfloat16 [16384, 1280], P(('img', 'txt')), may hold values from -100 to 100, as said below
- text_emb: bfloat16 [16384, 1280], P(('img', 'txt')), may hold values from -100 to 100, as said below
- log_scale: float32 [1], replicated, may hold values from 3 to 6
Outputs:
- loss: float32 [1], replicated
- grad_image: bfloat16 [16384, 1280], P(('img', 'txt'))
- grad_text: bfloat16 [16384, 1280], P(('img', 'txt'))
Inputs may be any that keep to these rules, and one draw needn't show every extreme that they name: `image_emb`: each row is a direction times a row scale. `text_emb`: each row is a direction times a row scale.
All inputs are finite; a program needn't handle non-finite values.
Results may differ from a plain program's by a relative error of at most 0.011.
Values may be sent and summed in bfloat16 or wider, within the bound.
No kernel may reach another device: no remote copies, remote signals or barrier semaphores. Data moves between devices by JAX's collectives and lax.ppermute only.
A program may use at most 64 MiB of HBM per device.

v0:
```python
import jax
import jax.numpy as jnp
from jax import lax
from jax.sharding import PartitionSpec as P


def unit_rows(raw):
    values = raw.astype(jnp.float32)
    norm = jnp.sqrt(jnp.sum(values * values, axis=1) + 1e-06)
    return (values / norm[:, None], norm)


def project(back, direction, norm):
    return (back - direction * jnp.sum(direction * back, axis=1)[:, None]) / norm[:, None]


def body(image_emb, text_emb, log_scale):
    image_rows = lax.all_gather(image_emb, "txt", axis=0, tiled=True)
    text_rows = lax.all_gather(text_emb, "img", axis=0, tiled=True)
    image_dir, image_norm = unit_rows(image_rows)
    text_dir, text_norm = unit_rows(text_rows)
    own_dir, own_norm = unit_rows(text_emb)
    image_unit = image_dir.astype(jnp.bfloat16)
    text_unit = text_dir.astype(jnp.bfloat16)
    scale = jnp.exp(log_scale[0])
    n_img = lax.axis_size("img")
    n_txt = lax.axis_size("txt")
    img_pos = lax.axis_index("img")
    txt_pos = lax.axis_index("txt")
    nrows = image_unit.shape[0]
    ncols = text_unit.shape[0]
    piece = text_emb.shape[0]
    logits = scale * lax.dot_general(
        image_unit, text_unit, (((1,), (1,)), ((), ())), preferred_element_type=jnp.float32
    )
    row_top = jnp.max(logits, axis=1)
    row_sums = jnp.sum(jnp.exp(logits - row_top[:, None]), axis=1)
    col_top = jnp.max(logits, axis=0)
    col_sums = jnp.sum(jnp.exp(logits - col_top[None, :]), axis=0)
    row_peak = lax.pmax(row_top, "txt")
    row_sums = lax.psum(row_sums * jnp.exp(row_top - row_peak), "txt")
    row_top = row_peak
    col_peak = lax.pmax(col_top, "img")
    col_sums = lax.psum(col_sums * jnp.exp(col_top - col_peak), "img")
    col_top = col_peak
    row_lse = row_top + jnp.log(row_sums)
    col_lse = col_top + jnp.log(col_sums)
    row_ids = img_pos * nrows + jnp.arange(nrows, dtype=jnp.int32)
    col_local = jnp.arange(ncols, dtype=jnp.int32)
    col_block = col_local // piece
    col_ids = col_block * (n_txt * piece) + txt_pos * piece + col_local % piece
    mask = (row_ids[:, None] == col_ids[None, :]).astype(jnp.float32)
    own_rows = jnp.arange(nrows, dtype=jnp.int32) // piece == txt_pos
    own_cols = col_block == img_pos
    partial_loss = (
        jnp.sum(jnp.where(own_rows, row_lse, 0.0))
        + jnp.sum(jnp.where(own_cols, col_lse, 0.0))
        - 2.0 * jnp.sum(logits * mask)
    ) / (2.0 * nrows * n_img)
    loss = lax.psum(partial_loss, ("img", "txt")).reshape(1)
    weights = (
        (jnp.exp(logits - row_lse[:, None]) + jnp.exp(logits - col_lse[None, :]) - 2.0 * mask) * 0.5
    ).astype(jnp.bfloat16)
    image_back = scale * jnp.dot(weights, text_unit, preferred_element_type=jnp.float32)
    image_proj = project(image_back, image_dir, image_norm)
    grad_image = lax.psum_scatter(image_proj, "txt", scatter_dimension=0, tiled=True).astype(
        jnp.bfloat16
    )
    back_dims = (((0,), (0,)), ((), ()))
    text_back = scale * lax.dot_general(
        weights, image_unit, back_dims, preferred_element_type=jnp.float32
    )
    back_piece = lax.psum_scatter(text_back, "img", scatter_dimension=0, tiled=True)
    grad_text = project(back_piece, own_dir, own_norm)
    return (loss, grad_image, grad_text.astype(jnp.bfloat16))


def solution(mesh):
    in_specs = (P(("img", "txt"), None), P(("img", "txt"), None), P())
    out_specs = (P(), P(("img", "txt"), None), P(("img", "txt"), None))
    return jax.shard_map(body, mesh=mesh, in_specs=in_specs, out_specs=out_specs, check_vma=False)
```

profile of v0, /device:TPU:28, one launch (start us, length us, event | category | flops | bytes accessed | tf_op | source)
XLA Modules:
  0.0 446.8 jit_solution(14255167486801409308)
XLA Ops:
  7.2 0.0 all-gather.3.cloned.1.call-start
  7.2 0.7 all-gather.3.cloned.1.call-update
  7.9 0.0 all-gather.5.cloned.1.call-start
  7.9 0.7 all-gather.5.cloned.1.call-update
  8.6 0.0 reduce-scatter.3.cloned.1.call-start
  9.4 42.4 %all-gather.3.cloned.1.call-done = bf16[512,1280]{1,0:T(8,128)(2,1)} async-done(((bf16[64,1280]{1,0:T(8,128)(2,1)}), bf16[512,1280]{1,0:T(8,128)(2,1)}) %all-gather.3.cloned.1.call-update) | async-done | bytes 1310736 | tf_op jit(solution)/shard_map/all_gather | solution.py:18
  51.8 1.6 fusion.6
  53.5 50.0 %all-gather.5.cloned.1.call-done = bf16[2048,1280]{1,0:T(8,128)(2,1)} async-done(((bf16[64,1280]{1,0:T(8,128)(2,1)}), bf16[2048,1280]{1,0:T(8,128)(2,1)}) %all-gather.5.cloned.1.call-update) | async-done | bytes 5242896 | tf_op jit(solution)/shard_map/all_gather | solution.py:19
  103.4 3.7 fusion
  107.2 0.3 copy-done
  107.5 2.2 fusion.1
  109.7 4.6 %fusion.27 = (f32[2048]{0:T(1024)S(1)}, f32[512]{0:T(512)S(1)}, f32[512,2048]{1,0:T(8,128)}) fusion(bf16[2048,1280]{1,0:T(8,128)(2,1)S(1)} %fusion.1, f32[512]{0:T(512)S(1)} %add_sqrt_fusion.1, bf16[512,1280]{1,0:T(8,128)(2,1)S(1)} %copy-done.2, f32[]{:T(128)} %bitcast), kind=kOutput, calls=%fused_computation.60 | convolution fusion | flops 2689463808 | bytes 10760196 | tf_op jit(solution)/shard_map/dot_general | solution.py:33
  114.3 17.4 %pmax.14 = f32[512]{0:T(512)S(1)} all-reduce(f32[512]{0:T(512)S(1)} %get-tuple-element.7), channel_id=1, replica_groups=mesh['img'=32,'txt'=8] {'txt'}, use_global_device_ids=true, to_apply=%region_3.0 | all-reduce | flops 512 | bytes 4096 | tf_op jit(solution)/shard_map/pmax | solution.py:40
  131.7 51.7 %pmax.15 = f32[2048]{0:T(1024)S(1)} all-reduce(f32[2048]{0:T(1024)S(1)} %get-tuple-element.6), channel_id=1, replica_groups=mesh['img'=32,'txt'=8] {'img'}, use_global_device_ids=true, to_apply=%region_8.0 | all-reduce | flops 2048 | bytes 16384 | tf_op jit(solution)/shard_map/pmax | solution.py:43
  183.5 4.6 %fusion.2 = (f32[]{:T(128)}, f32[2048]{0:T(1024)S(1)}, f32[512]{0:T(512)S(1)}) fusion(f32[512,2048]{1,0:T(8,128)} %get-tuple-element.12, s32[2048]{0:T(1024)S(1)} %fusion.16, s32[512]{0:T(512)S(1)} %iota_add_fusion, f32[2048]{0:T(1024)S(1)} %get-tuple-element.6, f32[512]{0:T(512)S(1)} %get-tuple-element.7), kind=kLoop, calls=%fused_computation.7 | loop fusion | flops 7337471 | bytes 4225028 | tf_op jit(solution)/shard_map/reduce_sum | solution.py:58
  188.1 15.0 %psum.21 = f32[512]{0:T(512)S(1)} all-reduce(f32[512]{0:T(512)S(1)} %exponential_multiply_fusion.1), channel_id=1, replica_groups=mesh['img'=32,'txt'=8] {'txt'}, use_global_device_ids=true, to_apply=%region_5.0 | all-reduce | flops 512 | bytes 4096 | tf_op jit(solution)/shard_map/psum | solution.py:41
  203.1 0.6 select_reduce_fusion.1
  203.8 54.8 %psum.22 = f32[2048]{0:T(1024)S(1)} all-reduce(f32[2048]{0:T(1024)S(1)} %exponential_multiply_fusion), channel_id=1, replica_groups=mesh['img'=32,'txt'=8] {'img'}, use_global_device_ids=true, to_apply=%region_10.0 | all-reduce | flops 2048 | bytes 16384 | tf_op jit(solution)/shard_map/psum | solution.py:44
  258.6 0.7 select_reduce_fusion
  259.2 7.5 %multiply_reduce_fusion = (f32[512]{0:T(512)S(1)}, f32[512,1280]{1,0:T(8,128)S(1)}) fusion(f32[512]{0:T(512)S(1)} %add_sqrt_fusion.1, bf16[512,1280]{1,0:T(8,128)(2,1)S(1)} %copy-done.2, bf16[2048,1280]{1,0:T(8,128)(2,1)} %copy-done.1, f32[512,2048]{1,0:T(8,128)} %get-tuple-element.12, f32[2048]{0:T(1024)S(1)} %get-tuple-element.9, ...), kind=kOutput, calls=%fused_computation.19 | convolution fusion | flops 2696019456 | bytes 13393924 | tf_op jit(solution)/shard_map/dot_general | solution.py:64
  266.7 2.0 subtract_divide_fusion
  268.7 0.0 reduce-scatter.3.cloned.1.call-update
  268.8 0.2 reduce-scatter.5.cloned.1.call-start
  269.0 10.1 %convolution_multiply_fusion = f32[2048,1280]{1,0:T(8,128)} fusion(f32[]{:T(128)} %bitcast, bf16[512,1280]{1,0:T(8,128)(2,1)S(1)} %copy-done.2, f32[512]{0:T(512)S(1)} %add_sqrt_fusion.1, f32[512,2048]{1,0:T(8,128)} %get-tuple-element.12, f32[2048]{0:T(1024)S(1)} %get-tuple-element.9, f32[512]{0:T(512)S(1)} %get-tuple-element.11, s32[2048]{0:T(1024)S(1)} %fusion.16, ...), kind=kOutput, calls=%fused_computation.4 | convolution fusion | flops 2697330688 | bytes 16013316 | tf_op jit(solution)/shard_map/dot_general | solution.py:70
  279.1 0.0 reduce-scatter.5.cloned.1.call-update
  279.1 0.9 copy-done.3
  280.0 0.1 fusion.9
  282.1 93.1 %psum.23 = f32[1]{0:T(128)} all-reduce(f32[1]{0:T(128)} %bitcast.1), channel_id=1, replica_groups=mesh['img'=32,'txt'=8] {'img','txt'}, use_global_device_ids=true, to_apply=%region_13.14 | all-reduce | flops 1 | bytes 8 | tf_op jit(solution)/shard_map/psum | solution.py:60
  375.2 1.7 convert_element_type.30
  376.9 60.4 %reduce-scatter.5.cloned.1.call-done = f32[64,1280]{1,0:T(8,128)} async-done(((f32[2048,1280]{1,0:T(8,128)}), f32[64,1280]{1,0:T(8,128)}) %reduce-scatter.5.cloned.1.call-update) | async-done | bytes 327696 | tf_op jit(solution)/shard_map/reduce_scatter | solution.py:73
  437.3 1.2 multiply_reduce_fusion.1
  438.4 1.8 divide_convert_fusion
  (14 shorter events, 0.1 us)
Async XLA Ops:
  7.2 44.7 %all-gather.3.cloned.1.call-start = ((), (), s32[]{:S(2)}) async-start(), calls=%async_computation.2 | async-start | bytes 1474560 | tf_op jit(solution)/shard_map/all_gather | solution.py:18
  7.9 95.5 %all-gather.5.cloned.1.call-start = ((), (), s32[]{:S(2)}) async-start(), calls=%async_computation.3 | async-start | bytes 5406720 | tf_op jit(solution)/shard_map/all_gather | solution.py:19
  8.6 366.6 %reduce-scatter.3.cloned.1.call-start = ((), (), s32[]{:S(2)}) async-start(), calls=%async_computation.4 | async-start | bytes 2949120 | tf_op jit(solution)/shard_map/reduce_scatter | solution.py:66
  103.4 4.0 copy-start
  107.5 2.2 copy-start.2
  109.7 4.6 %copy-start.1 = (bf16[2048,1280]{1,0:T(8,128)(2,1)}, bf16[2048,1280]{1,0:T(8,128)(2,1)S(1)}, u32[]{:S(2)}) copy-start(bf16[2048,1280]{1,0:T(8,128)(2,1)S(1)} %fusion.1) | copy-start | bytes 15728644
  268.8 168.5 %reduce-scatter.5.cloned.1.call-start = ((), (), s32[]{:S(2)}) async-start(), calls=%async_computation.5 | async-start | bytes 10813440 | tf_op jit(solution)/shard_map/reduce_scatter | solution.py:73
  279.1 0.9 copy-start.3
Sparse Core Ops, SparseCore 0:
  9.8 41.9 all-gather.2
  54.4 49.0 all-gather.4
  268.9 61.2 reduce-scatter.2
  334.1 103.1 reduce-scatter.4
where the time goes:
time: 449 us; the launch traced here: 447 us
  blocking collectives  232 us (52%)
  waiting for transfers between devices  154 us (34%)
  matrix products  22.2 us (5%)
  other arithmetic  20.3 us (5%)
  between operations  16.5 us (4%)
    psum x1, blocking collectives, body(): loss = lax.psum(partial_loss, ('img', 'txt')).reshape(1)  93.1 us
    reduce_scatter x1, waiting for transfers between devices, body(): lax.psum_scatter(text_back, 'img', scatter_dimension=0, tiled=True)  60.4 us
    psum x1, blocking collectives, body(): col_sums = lax.psum(col_sums * jnp.exp(col_top - col_peak), 'img')  54.8 us
    pmax x1, blocking collectives, body(): col_peak = lax.pmax(col_top, 'img')  51.7 us
    all_gather x1, waiting for transfers between devices, body(): text_rows = lax.all_gather(text_emb, 'img', axis=0, tiled=True)  50 us
    all_gather x1, waiting for transfers between devices, body(): image_rows = lax.all_gather(image_emb, 'txt', axis=0, tiled=True)  42.4 us
    pmax x1, blocking collectives, body(): row_peak = lax.pmax(row_top, 'txt')  17.4 us
    psum x1, blocking collectives, body(): row_sums = lax.psum(row_sums * jnp.exp(row_top - row_peak), 'txt')  15 us
  transfers between devices with their start and end apart: 4, of which 3 were waited for; matrix products, arithmetic and copies ran while one was open for 3% of the time, Pallas kernels for 0%

commit v1 on v0

v1 whole, which is shorter than its diff:
```python
import functools
import math

import jax
import jax.numpy as jnp
import numpy as np
from jax import lax
from jax.experimental import pallas as pl
from jax.experimental.pallas import tpu as pltpu
from jax.sharding import Mesh, PartitionSpec as P

LOG2E = math.log2(math.e)
LN2 = math.log(2.0)
EPS = 1e-06
VMEM = pltpu.CompilerParams(vmem_limit_bytes=40 * 1024 * 1024)
WHOLE = pl.BlockSpec(memory_space=pltpu.VMEM)
SCALAR = pl.BlockSpec(memory_space=pltpu.SMEM)
F32 = jnp.float32
BF16 = jnp.bfloat16


GRID = (4, 4, 2, 8)
INDEX = np.arange(256).reshape(GRID)
XY = INDEX.transpose(2, 3, 0, 1).reshape(16, 16).tolist()
CZ = INDEX.reshape(16, 16).tolist()
Z = INDEX.reshape(32, 8).tolist()
SWAP = [(int(a), int(b)) for c in (0, 1) for a, b in zip(INDEX[:, :, c].ravel(), INDEX[:, :, 1 - c].ravel())]
PEERS = 16
PIECE = 64
SIDE = PEERS * PIECE
TILE = 256
STEPS = SIDE // TILE


def unit_rows(raw):
    values = raw.astype(F32)
    norm = jnp.sqrt(jnp.sum(values * values, axis=1, keepdims=True) + EPS)
    return values / norm, norm


def image_unit_kernel(raw_ref, out_ref):
    out_ref[...] = unit_rows(raw_ref[...])[0].astype(BF16)


def text_unit_kernel(raw_ref, out_ref):
    unit = unit_rows(raw_ref[...])[0].astype(BF16)
    for k in range(PEERS):
        out_ref[pl.ds(k * PIECE, PIECE), :] = unit


def to_lanes(column):
    wide = jnp.broadcast_to(column, (column.shape[0], 128))
    return wide.T[:1, :]


def to_rows(lanes):
    wide = jnp.broadcast_to(lanes, (128, lanes.shape[1]))
    return wide.T[:, :1]


def logits_kernel(scale_ref, image_ref, text_ref, logits_ref, row_ref, col_ref, top_ref, sum_ref):
    step = pl.program_id(0)
    logits = lax.dot_general(
        image_ref[...], text_ref[...], (((1,), (1,)), ((), ())), preferred_element_type=F32
    ) * (scale_ref[0] * LOG2E)
    logits_ref[...] = logits
    row_top = jnp.max(logits, axis=1, keepdims=True)
    row_sum = jnp.sum(jnp.exp2(logits - row_top), axis=1, keepdims=True)
    row_lse = row_top + jnp.log2(row_sum)
    row_ref[...] = jnp.broadcast_to(to_lanes(row_lse), row_ref.shape)

    @pl.when(step == 0)
    def _():
        top_ref[...] = jnp.full_like(top_ref, -1e30)
        sum_ref[...] = jnp.zeros_like(sum_ref)

    top = jnp.maximum(top_ref[...], jnp.max(logits, axis=0, keepdims=True))
    sums = sum_ref[...] * jnp.exp2(top_ref[...] - top) + jnp.sum(
        jnp.exp2(logits - top), axis=0, keepdims=True
    )
    top_ref[...] = top
    sum_ref[...] = sums

    @pl.when(step == STEPS - 1)
    def _():
        col_ref[...] = jnp.broadcast_to(top + jnp.log2(sums), col_ref.shape)


def join_lse(parts):
    top = jnp.max(parts, axis=0, keepdims=True)
    return top + jnp.log2(jnp.sum(jnp.exp2(parts - top), axis=0, keepdims=True))


def row_tile(step, at_ref):
    return lax.rem(step + 2 * (1 - at_ref[2]), STEPS)


def weights_kernel(
    at_ref, scale_ref, logits_ref, text_ref, rows_ref, cols_ref,
    weights_ref, other_ref, mine_ref, loss_ref, part_ref,
):
    step = pl.program_id(0)
    tile = row_tile(step, at_ref)
    logits = logits_ref[...]
    row_lse = join_lse(rows_ref[...])
    col_lse = join_lse(cols_ref[...])
    row_at = lax.broadcasted_iota(jnp.int32, logits.shape, 0) + (tile * TILE - at_ref[0] * PIECE)
    col_at = lax.broadcasted_iota(jnp.int32, logits.shape, 1) - at_ref[1] * PIECE
    same = (row_at == col_at) & (row_at >= 0) & (row_at < PIECE)
    weights = (
        jnp.exp2(logits - to_rows(row_lse))
        + jnp.exp2(logits - col_lse)
        - jnp.where(same, 2.0, 0.0)
    ) * 0.5
    weights = weights.astype(BF16)
    weights_ref[...] = weights
    back = scale_ref[0] * jnp.dot(weights, text_ref[...], preferred_element_type=F32)

    @pl.when(step < STEPS // 2)
    def _():
        other_ref[...] = back.astype(BF16)

    @pl.when(step >= STEPS // 2)
    def _():
        mine_ref[...] = back

    @pl.when(step == 0)
    def _():
        part_ref[...] = jnp.sum(col_lse, axis=1, keepdims=True) * (1.0 / PEERS)

    part_ref[...] += (
        jnp.sum(row_lse, axis=1, keepdims=True) * (1.0 / PEERS)
        - 2.0 * jnp.sum(jnp.where(same, logits, 0.0), keepdims=True)
    )
    loss_ref[...] = jnp.broadcast_to(part_ref[...], loss_ref.shape)


def text_back_kernel(scale_ref, weights_ref, image_ref, out_ref):
    out_ref[...] = (
        scale_ref[0]
        * lax.dot_general(
            weights_ref[...], image_ref[...], (((0,), (0,)), ((), ())), preferred_element_type=F32
        )
    ).astype(BF16)


def project(back, raw):
    direction, norm = unit_rows(raw)
    along = jnp.sum(direction * back, axis=1, keepdims=True)
    return ((back - direction * along) / norm).astype(BF16)


def text_grad_kernel(parts_ref, raw_ref, out_ref):
    back = parts_ref[pl.ds(0, PIECE), :].astype(F32)
    for k in range(1, PEERS):
        back += parts_ref[pl.ds(k * PIECE, PIECE), :].astype(F32)
    out_ref[...] = project(back, raw_ref[...])


def image_grad_kernel(back_ref, raw_ref, out_ref):
    out_ref[...] = project(back_ref[...], raw_ref[...])


def on_vmem(kernel, shape, dtype, count):
    return pl.pallas_call(
        kernel,
        out_shape=jax.ShapeDtypeStruct(shape, dtype),
        in_specs=[WHOLE] * count,
        out_specs=WHOLE,
        compiler_params=VMEM,
    )


def exchange(x, groups):
    return lax.all_to_all(x, "d", 0, 0, axis_index_groups=groups, tiled=True)


def body(image_emb, text_emb, log_scale):
    width = image_emb.shape[1]
    scale = jnp.exp(log_scale)
    me = lax.axis_index("d")
    core = (me // 8) % 2
    at = jnp.stack([me % 16, me // 16, core]).astype(jnp.int32)

    image_unit = on_vmem(image_unit_kernel, image_emb.shape, BF16, 1)(image_emb)
    image = lax.all_gather(image_unit, "d", axis=0, tiled=True, axis_index_groups=CZ)
    text_units = on_vmem(text_unit_kernel, (SIDE, width), BF16, 1)(text_emb)
    text = exchange(text_units, XY)

    logits, row_part, col_part = pl.pallas_call(
        logits_kernel,
        grid=(STEPS,),
        in_specs=[
            SCALAR,
            pl.BlockSpec((TILE, width), lambda i: (i, 0)),
            pl.BlockSpec((SIDE, width), lambda i: (0, 0)),
        ],
        out_specs=[
            pl.BlockSpec((TILE, SIDE), lambda i: (i, 0)),
            pl.BlockSpec((PEERS, TILE), lambda i: (0, i)),
            pl.BlockSpec((PEERS, SIDE), lambda i: (0, 0)),
        ],
        out_shape=[
            jax.ShapeDtypeStruct((SIDE, SIDE), F32),
            jax.ShapeDtypeStruct((PEERS, SIDE), F32),
            jax.ShapeDtypeStruct((PEERS, SIDE), F32),
        ],
        scratch_shapes=[pltpu.VMEM((1, SIDE), F32), pltpu.VMEM((1, SIDE), F32)],
        compiler_params=VMEM,
    )(scale, image, text)

    rows = exchange(row_part, CZ)
    cols = exchange(col_part, XY)

    weights, other, mine, loss_part = pl.pallas_call(
        weights_kernel,
        grid_spec=pltpu.PrefetchScalarGridSpec(
            num_scalar_prefetch=1,
            grid=(STEPS,),
            in_specs=[
                SCALAR,
                pl.BlockSpec((TILE, SIDE), lambda i, at: (row_tile(i, at), 0)),
                pl.BlockSpec((SIDE, width), lambda i, at: (0, 0)),
                pl.BlockSpec((PEERS, TILE), lambda i, at: (0, row_tile(i, at))),
                pl.BlockSpec((PEERS, SIDE), lambda i, at: (0, 0)),
            ],
            out_specs=[
                pl.BlockSpec((TILE, SIDE), lambda i, at: (row_tile(i, at), 0)),
                pl.BlockSpec((TILE, width), lambda i, at: (jnp.minimum(i, STEPS // 2 - 1), 0)),
                pl.BlockSpec((TILE, width), lambda i, at: (jnp.maximum(i - STEPS // 2, 0), 0)),
                pl.BlockSpec((PEERS, 128), lambda i, at: (0, 0)),
            ],
            scratch_shapes=[pltpu.VMEM((1, 1), F32)],
        ),
        out_shape=[
            jax.ShapeDtypeStruct((SIDE, SIDE), BF16),
            jax.ShapeDtypeStruct((SIDE // 2, width), BF16),
            jax.ShapeDtypeStruct((SIDE // 2, width), F32),
            jax.ShapeDtypeStruct((PEERS, 128), F32),
        ],
        compiler_params=VMEM,
    )(at, scale, logits, text, rows, cols)

    swapped = lax.ppermute(other, "d", SWAP)
    text_parts = pl.pallas_call(
        text_back_kernel,
        grid=(STEPS,),
        in_specs=[
            SCALAR,
            pl.BlockSpec((SIDE, TILE), lambda j: (0, j)),
            pl.BlockSpec((SIDE, width), lambda j: (0, 0)),
        ],
        out_specs=pl.BlockSpec((TILE, width), lambda j: (j, 0)),
        out_shape=jax.ShapeDtypeStruct((SIDE, width), BF16),
        compiler_params=VMEM,
    )(scale, weights, image)
    image_sum = mine + swapped.astype(F32)
    image_back = lax.psum_scatter(
        image_sum, "d", scatter_dimension=0, axis_index_groups=Z, tiled=True
    )
    text_back = exchange(text_parts, XY)

    loss = exchange(loss_part, XY)
    loss = jnp.broadcast_to(jnp.sum(loss, axis=0, keepdims=True), loss.shape)
    loss = jnp.sum(exchange(loss, CZ), axis=0)[:1] * (LN2 / (2.0 * SIDE * PEERS))

    grad_image = on_vmem(image_grad_kernel, image_emb.shape, BF16, 2)(image_back, image_emb)
    grad_text = on_vmem(text_grad_kernel, text_emb.shape, BF16, 2)(text_back, text_emb)
    return loss, grad_image, grad_text


def solution(mesh):
    flat = Mesh(mesh.devices.reshape(-1), ("d",))
    return jax.shard_map(
        body,
        mesh=flat,
        in_specs=(P("d", None), P("d", None), P()),
        out_specs=(P(), P("d", None), P("d", None)),
        check_vma=False,
    )
```

time: 449 us -> 186 us (0.41)
  blocking collectives: 232 us -> 10.8 us
  waiting for transfers between devices: 154 us -> 84.6 us
  starting transfers between devices: 0.34 us -> 33.5 us
  matrix products: 22.2 us -> 0 us
  Pallas kernels: 0 us -> 20.7 us
  other arithmetic: 20.3 us -> 1.91 us
  local copies, waits for them, and re-layouts: 1.2 us -> 16.8 us
    psum x3 -> x0, blocking collectives: 163 us -> none  [the longest x1 93.1 us: body(): loss = lax.psum(partial_loss, ('img', 'txt')).reshape(1)]
    all_gather x2 -> x1, waiting for transfers between devices: 92.4 us -> 0.37 us  [body(): lax.all_gather(image_unit, 'd', axis=0, tiled=True, axis_index_groups=CZ)]
    all_to_all x0 -> x5, waiting for transfers between devices: none -> 81.2 us  [exchange(): return lax.all_to_all(x, 'd', 0, 0, axis_index_groups=groups, tiled=True)]
    pmax x2 -> x0, blocking collectives: 69.2 us -> none  [the longest x1 51.7 us: body(): col_peak = lax.pmax(col_top, 'img')]
    reduce_scatter x2 -> x1, waiting for transfers between devices: 60.4 us -> 0.01 us  [body(): lax.psum_scatter(image_sum, 'd', scatter_dimension=0, axis_index_groups=Z...]
    all_to_all x0 -> x5, starting transfers between devices: none -> 33.4 us  [exchange(): return lax.all_to_all(x, 'd', 0, 0, axis_index_groups=groups, tiled=True)]
    dot_general x3 -> x0, matrix products: 22.2 us -> none  [the longest x1 10.1 us: body(): lax.dot_general(weights, image_unit, back_dims, preferred_element_type=jn...]
    pallas_call x0 -> x7, Pallas kernels: none -> 20.7 us  [the longest x1 8.07 us: body(): pl.pallas_call(weights_kernel, grid_spec=pltpu.PrefetchScalarGridSpec(num...]
  transfers between devices with their start and end apart: 4 -> 8, of which waited for: 3 -> 7; matrix products, arithmetic and copies ran while one was open for 3% -> 1% of each run, Pallas kernels for 0% -> 3%
where the time goes in v1:
time: 186 us; the launch traced here: 184 us
  waiting for transfers between devices  84.6 us (45%)
  starting transfers between devices  33.5 us (18%)
  Pallas kernels  20.7 us (11%)
  local copies, waits for them, and re-layouts  16.8 us (9%)
  between operations  16.1 us (9%)
  blocking collectives  10.8 us (6%)
  other arithmetic  1.91 us (1%)
    all_to_all x5, waiting for transfers between devices, exchange(): return lax.all_to_all(x, 'd', 0, 0, axis_index_groups=groups, tiled=True)  81.2 us
    all_to_all x5, starting transfers between devices, exchange(): return lax.all_to_all(x, 'd', 0, 0, axis_index_groups=groups, tiled=True)  33.4 us
    unnamed x28, local copies, waits for them, and re-layouts  14.8 us
    all_to_all x1, blocking collectives, exchange(): return lax.all_to_all(x, 'd', 0, 0, axis_index_groups=groups, tiled=True)  10.8 us
    pallas_call x1, Pallas kernels, body(): pl.pallas_call(weights_kernel, grid_spec=pltpu.PrefetchScalarGridSpec(num...  8.07 us
    pallas_call x1, Pallas kernels, body(): pl.pallas_call(logits_kernel, grid=(STEPS,), in_specs=[SCALAR, pl.BlockSp...  5.59 us
    pallas_call x1, Pallas kernels, body(): pl.pallas_call(text_back_kernel, grid=(STEPS,), in_specs=[SCALAR, pl.Bloc...  3.9 us
  transfers between devices with their start and end apart: 8, of which 7 were waited for; matrix products, arithmetic and copies ran while one was open for 1% of the time, Pallas kernels for 3%

profile of v1, /device:TPU:28, one launch (start us, length us, event | category | flops | bytes accessed | tf_op | source)
XLA Modules:
  0.0 184.4 jit_solution(11885923529603879977)
XLA Ops:
  7.2 0.9 copy-done.10
  8.1 0.8 shard_map.58
  9.0 0.9 copy-done.8
  10.2 1.5 copy-done
  11.7 7.1 %all-to-all-start = ((bf16[16,64,1280]{2,1,0:T(8,128)(2,1)}), bf16[16,64,1280]{2,1,0:T(8,128)(2,1)S(1)}, u32[]{:S(2)}, u32[]{:S(2)}) async-start(bf16[16,64,1280]{2,1,0:T(8,128)(2,1)} %bitcast.23), calls=%async_computation | async-start | bytes 5242880 | tf_op jit(solution)/shard_map/all_to_all | solution.py:175
  19.5 33.7 %all-to-all-done = bf16[16,64,1280]{2,1,0:T(8,128)(2,1)S(1)} async-done(((bf16[16,64,1280]{2,1,0:T(8,128)(2,1)}), bf16[16,64,1280]{2,1,0:T(8,128)(2,1)S(1)}, u32[]{:S(2)}, u32[]{:S(2)}) %all-to-all-start) | async-done | bytes 2621472 | tf_op jit(solution)/shard_map/all_to_all | solution.py:175
  53.2 0.4 all-gather.2.cloned.1.call-done.image_ref
  53.5 1.7 copy-done.2
  55.3 5.6 %shard_map.60 = (f32[1024,1024]{1,0:T(8,128)S(1)}, f32[16,1024]{1,0:T(8,128)S(1)}, f32[16,1024]{1,0:T(8,128)S(1)}) custom-call(f32[1]{0:T(128)S(6)} %exp.3.scale_ref, bf16[1024,1280]{1,0:T(8,128)(2,1)S(1)} %copy-done.2, bf16[1024,1280]{1,0:T(8,128)(2,1)S(1)} %bitcast.20), custom_call_target="tpu_custom_call" | custom-call | tf_op jit(solution)/shard_map/pallas_call | solution.py:190
  60.9 2.0 %copy-done.4 = f32[1024,1024]{1,0:T(8,128)} copy-done((f32[1024,1024]{1,0:T(8,128)}, f32[1024,1024]{1,0:T(8,128)S(1)}, u32[]{:S(2)}) %copy-start.4) | copy-done | bytes 4194328
  62.9 0.7 copy.13
  63.6 7.2 %all-to-all-start.2 = ((f32[16,1,1024]{2,1,0:T(1,128)}), f32[16,1,1024]{2,1,0:T(1,128)S(1)}, u32[]{:S(2)}, u32[]{:S(2)}) async-start(f32[16,1,1024]{2,1,0:T(1,128)} %copy.13), calls=%async_computation.2 | async-start | bytes 131072 | tf_op jit(solution)/shard_map/all_to_all | solution.py:175
  70.8 0.7 copy.12
  71.5 3.3 %all-to-all-done.2 = f32[16,1,1024]{2,1,0:T(1,128)S(1)} async-done(((f32[16,1,1024]{2,1,0:T(1,128)}), f32[16,1,1024]{2,1,0:T(1,128)S(1)}, u32[]{:S(2)}, u32[]{:S(2)}) %all-to-all-start.2) | async-done | bytes 65568 | tf_op jit(solution)/shard_map/all_to_all | solution.py:175
  74.8 7.9 %all-to-all-start.1 = ((f32[16,1,1024]{2,1,0:T(1,128)}), f32[16,1,1024]{2,1,0:T(1,128)S(1)}, u32[]{:S(2)}, u32[]{:S(2)}) async-start(f32[16,1,1024]{2,1,0:T(1,128)} %copy.12), calls=%async_computation.1 | async-start | bytes 131072 | tf_op jit(solution)/shard_map/all_to_all | solution.py:175
  82.9 7.8 %all-to-all-done.1 = f32[16,1,1024]{2,1,0:T(1,128)S(1)} async-done(((f32[16,1,1024]{2,1,0:T(1,128)}), f32[16,1,1024]{2,1,0:T(1,128)S(1)}, u32[]{:S(2)}, u32[]{:S(2)}) %all-to-all-start.1) | async-done | bytes 65568 | tf_op jit(solution)/shard_map/all_to_all | solution.py:175
  90.8 2.2 %copy-done.5 = f32[1024,1024]{1,0:T(8,128)S(1)} copy-done((f32[1024,1024]{1,0:T(8,128)S(1)}, f32[1024,1024]{1,0:T(8,128)}, u32[]{:S(2)}) %copy-start.5) | copy-done | bytes 4194328
  92.9 8.1 %shard_map.61 = (bf16[1024,1024]{1,0:T(8,128)(2,1)S(1)}, bf16[512,1280]{1,0:T(8,128)(2,1)S(1)}, f32[512,1280]{1,0:T(8,128)S(1)}, f32[16,128]{1,0:T(8,128)S(1)}) custom-call(s32[3]{0:T(128)S(1)} %pad_add_fusion.at_ref, f32[1]{0:T(128)S(6)} %exp.3.scale_ref, f32[1024,1024]{1,0:T(8,128)S(1)} %copy-done.5, bf16[1024,1280]{1,0:T(8,128)(2,1)S(1)} %bitcast.21, ...), custom_call_target="tpu_custom_call" | custom-call | tf_op jit(solution)/shard_map/pallas_call | solution.py:215
  101.0 1.3 copy-done.6
  102.3 3.0 %collective-permute-done = bf16[512,1280]{1,0:T(8,128)(2,1)S(1)} collective-permute-done((bf16[512,1280]{1,0:T(8,128)(2,1)S(1)}, bf16[512,1280]{1,0:T(8,128)(2,1)S(1)}, u32[]{:S(2)}, u32[]{:S(2)}) %collective-permute-start) | collective-permute-done | bytes 1310752 | tf_op jit(solution)/shard_map/ppermute | solution.py:244
  105.4 1.8 convert_add_fusion
  107.2 10.8 %all_to_all.59 = f32[16,1,128]{2,1,0:T(1,128)S(1)} all-to-all(f32[16,1,128]{2,1,0:T(1,128)S(1)} %bitcast.29), channel_id=1, replica_groups={{0,16,32,48,64,80,96,112,128,144,160,176,192,208,224,240},{1,17,33,49,6..., dimensions={0} | all-to-all | bytes 16384 | tf_op jit(solution)/shard_map/all_to_all | solution.py:175
  118.0 0.6 broadcast_in_dim.2
  118.6 3.5 %all-to-all-start.4 = ((f32[16,1,128]{2,1,0:T(1,128)}), f32[16,1,128]{2,1,0:T(1,128)S(1)}, u32[]{:S(2)}, u32[]{:S(2)}) async-start(f32[16,1,128]{2,1,0:T(1,128)} %broadcast_in_dim.2), calls=%async_computation.4 | async-start | bytes 16384 | tf_op jit(solution)/shard_map/all_to_all | solution.py:175
  122.1 1.6 copy-done.7
  123.8 3.9 %shard_map.63 = bf16[1024,1280]{1,0:T(8,128)(2,1)S(1)} custom-call(f32[1]{0:T(128)S(6)} %exp.3.scale_ref, bf16[1024,1024]{1,0:T(8,128)(2,1)S(1)} %copy-done.7, bf16[1024,1280]{1,0:T(8,128)(2,1)S(1)} %copy-done.3), custom_call_target="tpu_custom_call" | custom-call | tf_op jit(solution)/shard_map/pallas_call | solution.py:245
  127.7 1.5 copy-done.1
  129.5 7.7 %all-to-all-start.5 = ((bf16[16,64,1280]{2,1,0:T(8,128)(2,1)}), bf16[16,64,1280]{2,1,0:T(8,128)(2,1)S(1)}, u32[]{:S(2)}, u32[]{:S(2)}) async-start(bf16[16,64,1280]{2,1,0:T(8,128)(2,1)} %bitcast.24), calls=%async_computation.6 | async-start | bytes 5242880 | tf_op jit(solution)/shard_map/all_to_all | solution.py:175
  137.3 36.1 %all-to-all-done.5 = bf16[16,64,1280]{2,1,0:T(8,128)(2,1)S(1)} async-done(((bf16[16,64,1280]{2,1,0:T(8,128)(2,1)}), bf16[16,64,1280]{2,1,0:T(8,128)(2,1)S(1)}, u32[]{:S(2)}, u32[]{:S(2)}) %all-to-all-start.5) | async-done | bytes 2621472 | tf_op jit(solution)/shard_map/all_to_all | solution.py:175
  173.4 1.2 shard_map.64
  174.6 1.0 copy-done.12
  175.5 0.9 shard_map.62
  (29 shorter events, 0.9 us)
Async XLA Ops:
  7.2 46.4 %all-gather.2.cloned.1.call-start = ((), (), s32[]{:S(2)}) async-start(), calls=%async_computation.7 | async-start | bytes 2785280 | tf_op jit(solution)/shard_map/all_gather | solution.py:186
  7.2 0.9 copy-start.10
  8.9 0.9 copy-start.8
  10.2 1.5 copy-start
  11.7 41.5 %all-to-all-start = ((bf16[16,64,1280]{2,1,0:T(8,128)(2,1)}), bf16[16,64,1280]{2,1,0:T(8,128)(2,1)S(1)}, u32[]{:S(2)}, u32[]{:S(2)}) async-start(bf16[16,64,1280]{2,1,0:T(8,128)(2,1)} %bitcast.23), calls=%async_computation | async-start | bytes 5242880 | tf_op jit(solution)/shard_map/all_to_all | solution.py:175
  53.5 1.7 copy-start.2
  60.9 2.0 %copy-start.4 = (f32[1024,1024]{1,0:T(8,128)}, f32[1024,1024]{1,0:T(8,128)S(1)}, u32[]{:S(2)}) copy-start(f32[1024,1024]{1,0:T(8,128)S(1)} %get-tuple-element.10.logits_ref) | copy-start | bytes 12582916
  63.6 11.2 %all-to-all-start.2 = ((f32[16,1,1024]{2,1,0:T(1,128)}), f32[16,1,1024]{2,1,0:T(1,128)S(1)}, u32[]{:S(2)}, u32[]{:S(2)}) async-start(f32[16,1,1024]{2,1,0:T(1,128)} %copy.13), calls=%async_computation.2 | async-start | bytes 131072 | tf_op jit(solution)/shard_map/all_to_all | solution.py:175
  74.8 15.9 %all-to-all-start.1 = ((f32[16,1,1024]{2,1,0:T(1,128)}), f32[16,1,1024]{2,1,0:T(1,128)S(1)}, u32[]{:S(2)}, u32[]{:S(2)}) async-start(f32[16,1,1024]{2,1,0:T(1,128)} %copy.12), calls=%async_computation.1 | async-start | bytes 131072 | tf_op jit(solution)/shard_map/all_to_all | solution.py:175
  82.8 91.8 %reduce-scatter.2.cloned.1.call-start = ((), (), s32[]{:S(2)}) async-start(), calls=%async_computation.8 | async-start | bytes 2949120 | tf_op jit(solution)/shard_map/reduce_scatter | solution.py:258
  90.7 2.2 %copy-start.5 = (f32[1024,1024]{1,0:T(8,128)S(1)}, f32[1024,1024]{1,0:T(8,128)}, u32[]{:S(2)}) copy-start(f32[1024,1024]{1,0:T(8,128)} %copy-done.4) | copy-start | bytes 12582916
  101.0 1.3 copy-start.6
  102.3 3.0 %collective-permute-start = (bf16[512,1280]{1,0:T(8,128)(2,1)S(1)}, bf16[512,1280]{1,0:T(8,128)(2,1)S(1)}, u32[]{:S(2)}, u32[]{:S(2)}) collective-permute-start(bf16[512,1280]{1,0:T(8,128)(2,1)S(1)} %get-tuple-element.15), channel_id=1, source_target_pairs={{0,8},{1,9},{2,10},{3,11},{4,12},{5,13},{6,14},{7,15},{16,24},{17,... | collective-permute-start | bytes 3932168 | tf_op jit(solution)/shard_map/ppermute | solution.py:244
  107.2 15.0 %copy-start.3 = (bf16[1024,1280]{1,0:T(8,128)(2,1)S(1)}, bf16[1024,1280]{1,0:T(8,128)(2,1)}, u32[]{:S(2)}) copy-start(bf16[1024,1280]{1,0:T(8,128)(2,1)} %all-gather.2.cloned.1.call-done.image_ref) | copy-start | bytes 7864324
  118.6 10.9 %all-to-all-start.4 = ((f32[16,1,128]{2,1,0:T(1,128)}), f32[16,1,128]{2,1,0:T(1,128)S(1)}, u32[]{:S(2)}, u32[]{:S(2)}) async-start(f32[16,1,128]{2,1,0:T(1,128)} %broadcast_in_dim.2), calls=%async_computation.4 | async-start | bytes 16384 | tf_op jit(solution)/shard_map/all_to_all | solution.py:175
  122.1 1.6 copy-start.7
  127.7 1.5 copy-start.1
  129.5 43.9 %copy-start.9 = (bf16[64,1280]{1,0:T(8,128)(2,1)S(1)}, bf16[64,1280]{1,0:T(8,128)(2,1)}, u32[]{:S(2)}) copy-start(bf16[64,1280]{1,0:T(8,128)(2,1)} %raw_ref.7) | copy-start | bytes 491524
  129.5 43.9 %all-to-all-start.5 = ((bf16[16,64,1280]{2,1,0:T(8,128)(2,1)}), bf16[16,64,1280]{2,1,0:T(8,128)(2,1)S(1)}, u32[]{:S(2)}, u32[]{:S(2)}) async-start(bf16[16,64,1280]{2,1,0:T(8,128)(2,1)} %bitcast.24), calls=%async_computation.6 | async-start | bytes 5242880 | tf_op jit(solution)/shard_map/all_to_all | solution.py:175
  137.2 37.3 %copy-start.11 = (bf16[64,1280]{1,0:T(8,128)(2,1)S(1)}, bf16[64,1280]{1,0:T(8,128)(2,1)}, u32[]{:S(2)}) copy-start(bf16[64,1280]{1,0:T(8,128)(2,1)} %raw_ref.6) | copy-start | bytes 491524
  174.6 1.0 copy-start.12
Sparse Core Ops, SparseCore 0:
  10.4 43.1 all-gather.1
  107.3 40.5 reduce-scatter.1

commit v2 on v0

v2 whole, which is shorter than its diff:
```python
import functools
import math
import typing

import jax
import jax.numpy as jnp
import numpy as np
from jax import lax
from jax.experimental import pallas as pl
from jax.experimental.pallas import tpu as pltpu
from jax.sharding import Mesh, PartitionSpec as P

LOG2E = math.log2(math.e)
LN2 = math.log(2.0)
EPS = 1e-06
LOW = -1e30
PARAMS = pltpu.CompilerParams(vmem_limit_bytes=24 * 1024 * 1024)
HBM = pl.BlockSpec(memory_space=pl.ANY)
WHOLE = pl.BlockSpec(memory_space=pltpu.VMEM)
SCALAR = pl.BlockSpec(memory_space=pltpu.SMEM)
F32 = jnp.float32
BF16 = jnp.bfloat16

INDEX = np.arange(256).reshape(4, 4, 2, 8)
AXES = {"x": 0, "y": 1, "c": 2, "z": 3}
XY = INDEX.transpose(2, 3, 0, 1).reshape(16, 16).tolist()
MIXED = INDEX[:, :, 0, :].transpose(2, 0, 1).reshape(8, 16).tolist() + (
    INDEX[:, :, 1, :].reshape(2, 2, 4, 8).transpose(0, 2, 1, 3).reshape(8, 16).tolist()
)
PEERS = 16
PIECE = 64
SIDE = PEERS * PIECE
TILE = 256
STEPS = SIDE // TILE
DEEP = 8
LINES = 4 * STEPS


def shift(axis, by):
    to = np.roll(INDEX, -by, AXES[axis])
    return [(int(a), int(b)) for a, b in zip(INDEX.ravel(), to.ravel())]


def send(x, axis, by):
    return lax.ppermute(x, "d", shift(axis, by))


def exchange(x, groups):
    return lax.all_to_all(x, "d", 0, 0, axis_index_groups=groups, tiled=True)


def array(shape, dtype):
    return pltpu.HBM(shape, dtype)


def local(shape, dtype):
    return pltpu.VMEM(shape, dtype)


def call(kernel, outputs, *operands, scratch=(), aliases={}):
    specs, arrays = [], []
    for x in operands:
        if isinstance(x, Outside):
            specs.append(HBM)
            arrays.append(pltpu.with_memory_space_constraint(x.array, pltpu.HBM))
        elif x.size <= 8:
            specs.append(SCALAR)
            arrays.append(x)
        else:
            specs.append(WHOLE)
            arrays.append(pltpu.with_memory_space_constraint(x, pltpu.VMEM))
    return pl.pallas_call(
        kernel,
        out_shape=outputs,
        in_specs=specs,
        out_specs=jax.tree.map(lambda s: WHOLE if s.memory_space == pltpu.VMEM else HBM, outputs),
        scratch_shapes=list(scratch),
        input_output_aliases=aliases,
        compiler_params=PARAMS,
    )(*arrays)


class Outside(typing.NamedTuple):
    array: typing.Any


def run(copies):
    for copy in copies:
        copy.start()
    return copies


def wait(copies):
    for copy in copies:
        copy.wait()


def unit_rows(raw):
    values = raw.astype(F32)
    norm = jnp.sqrt(jnp.sum(values * values, axis=1, keepdims=True) + EPS)
    return values / norm, norm


def image_unit_kernel(raw_ref, out_ref, raw, unit, sem):
    wait(run([pltpu.make_async_copy(raw_ref, raw, sem.at[0])]))
    unit[...] = unit_rows(raw[...])[0].astype(BF16)
    wait(run([pltpu.make_async_copy(unit, out_ref, sem.at[0])]))


def text_units_kernel(raw_ref, out_ref, raw, unit, sem):
    wait(run([pltpu.make_async_copy(raw_ref, raw, sem.at[0])]))
    unit[...] = unit_rows(raw[...])[0].astype(BF16)
    wait(run([
        pltpu.make_async_copy(unit, out_ref.at[pl.ds(k * PIECE, PIECE), :], sem.at[k])
        for k in range(PEERS)
    ]))


def to_lanes(column):
    return jnp.broadcast_to(column, (column.shape[0], 128)).T[:1, :]


def to_rows(lanes):
    return jnp.broadcast_to(lanes, (128, lanes.shape[1])).T[:, :1]


def diagonal(at_ref):
    rows = pl.ds(pl.multiple_of(at_ref[0] * PIECE, PIECE), PIECE)
    cols = pl.ds(pl.multiple_of((at_ref[1] // 2) * 128, 128), 128)
    shape = (PIECE, 128)
    odd = lax.rem(at_ref[1], 2)
    at_row = lax.broadcasted_iota(jnp.int32, shape, 0) + odd * PIECE
    return rows, cols, at_row == lax.broadcasted_iota(jnp.int32, shape, 1)


def logits_kernel(plan, at_ref, scale_ref, text_ref, *refs):
    pieces = refs[: len(plan)]
    image_out, logits_ref, keep_ref, give_ref, image_ref, sem, out_sem = refs[len(plan) :]
    core = at_ref[2]
    copies = []
    for k, (piece, (flip, by, start, rows)) in enumerate(zip(pieces, plan)):
        block = lax.rem(core + flip, 2) * DEEP + lax.rem(at_ref[3] + by + DEEP, DEEP)
        first = pl.multiple_of(block * PIECE + start, 32)
        copies.append(pltpu.make_async_copy(piece, image_ref.at[pl.ds(first, rows), :], sem.at[k]))
    wait(run(copies))
    out = run([pltpu.make_async_copy(image_ref, image_out, out_sem.at[0])])
    text = text_ref[...]
    scale = scale_ref[0] * LOG2E
    top = jnp.full((1, SIDE), LOW, F32)
    sums = jnp.zeros((1, SIDE), F32)
    row_lse = []
    for k in range(STEPS):
        tile = slice(k * TILE, (k + 1) * TILE)
        logits = scale * lax.dot_general(
            image_ref[tile, :], text, (((1,), (1,)), ((), ())), preferred_element_type=F32
        )
        logits_ref[tile, :] = logits
        row_top = jnp.max(logits, axis=1, keepdims=True)
        row_sum = jnp.sum(jnp.exp2(logits - row_top), axis=1, keepdims=True)
        row_lse.append(to_lanes(row_top + jnp.log2(row_sum)))
        new = jnp.maximum(top, jnp.max(logits, axis=0, keepdims=True))
        sums = sums * jnp.exp2(top - new) + jnp.sum(jnp.exp2(logits - new), axis=0, keepdims=True)
        top = new
    col_lse = top + jnp.log2(sums)
    rows, cols, same = diagonal(at_ref)
    pairs = jnp.sum(jnp.where(same, logits_ref[rows, cols], 0.0), keepdims=True)
    first = core == 0
    for k in range(STEPS):
        part = col_lse[:, k * TILE : (k + 1) * TILE]
        keep_ref[k : k + 1, :] = jnp.where(first, part, row_lse[k])
        give_ref[k : k + 1, :] = jnp.where(first, row_lse[k], part)
    both = jnp.broadcast_to(pairs, (STEPS, TILE))
    keep_ref[STEPS:, :] = both
    give_ref[STEPS:, :] = both
    wait(out)


def spread_kernel(at_ref, keep_ref, recv_ref, out_ref):
    keep, recv = keep_ref[:STEPS, :], recv_ref[:STEPS, :]
    top = jnp.maximum(keep, recv)
    both = top + jnp.log2(jnp.exp2(keep - top) + jnp.exp2(recv - top))
    pairs = keep_ref[STEPS:, :] + recv_ref[STEPS:, :]
    first = at_ref[2] == 0
    block = jnp.concatenate(
        [jnp.where(first, keep, both), jnp.where(first, recv, both), pairs, pairs], axis=0
    )
    for k in range(PEERS):
        out_ref[pl.ds(k * LINES, LINES), :] = block


def join_kernel(at_ref, parts_ref, keep_ref, give_ref, loss_ref):
    parts = parts_ref[...].reshape(PEERS, LINES, TILE)
    pairs = jnp.sum(parts[:, 2 * STEPS : 2 * STEPS + 1, :1], axis=0)
    parts = parts[:, : 2 * STEPS, :]
    half = lax.broadcasted_iota(jnp.int32, parts.shape, 0) // DEEP
    first = at_ref[2] == 0
    parts = jnp.where(first | (half == at_ref[4]), parts, LOW)
    top = jnp.max(parts, axis=0)
    lse = top + jnp.log2(jnp.sum(jnp.exp2(parts - top[None]), axis=0))
    keep_ref[...] = lse[:STEPS]
    give_ref[...] = jnp.where(first, lse[STEPS:], lse[:STEPS])
    low = jnp.sum(lse[:STEPS], keepdims=True)
    high = jnp.sum(lse[STEPS:], keepdims=True)
    loss_ref[...] = jnp.broadcast_to(jnp.where(first, low + high - 2.0 * pairs, low), loss_ref.shape)


def weights_kernel(
    at_ref, scale_ref, logits_ref, text_ref, keep_ref, recv_ref,
    weights_ref, other_ref, mine_out, mine, sem,
):
    first = at_ref[2] == 0
    keep, recv = keep_ref[...], recv_ref[...]
    cols = jnp.where(first, keep, recv)
    col_lse = jnp.concatenate([cols[k : k + 1] for k in range(STEPS)], axis=1)
    rows = jnp.where(first, recv, keep)
    row_lse = [to_rows(rows[k : k + 1]) for k in range(STEPS)]
    for k in range(STEPS):
        tile = slice(k * TILE, (k + 1) * TILE)
        logits = logits_ref[tile, :]
        weights_ref[tile, :] = (
            (jnp.exp2(logits - row_lse[k]) + jnp.exp2(logits - col_lse)) * 0.5
        ).astype(BF16)

    own_rows, own_cols, same = diagonal(at_ref)
    logits = logits_ref[own_rows, own_cols]
    at_row = jnp.zeros((PIECE, 1), F32)
    for k in range(SIDE // PIECE):
        part = row_lse[k // STEPS][(k % STEPS) * PIECE : (k % STEPS + 1) * PIECE]
        at_row = jnp.where(at_ref[0] == k, part, at_row)
    at_col = jnp.zeros((1, 128), F32)
    for k in range(SIDE // 128):
        at_col = jnp.where(at_ref[1] // 2 == k, col_lse[:, k * 128 : (k + 1) * 128], at_col)
    weights_ref[own_rows, own_cols] = (
        (jnp.exp2(logits - at_row) + jnp.exp2(logits - at_col) - jnp.where(same, 2.0, 0.0)) * 0.5
    ).astype(BF16)

    text = text_ref[...]
    for k in range(STEPS // 2):
        tile = slice(k * TILE, (k + 1) * TILE)
        theirs = pl.ds(pl.multiple_of((1 - at_ref[2]) * (SIDE // 2) + k * TILE, TILE), TILE)
        other_ref[tile, :] = (
            scale_ref[0] * jnp.dot(weights_ref[theirs, :], text, preferred_element_type=F32)
        ).astype(BF16)


    copies = []
    for k in range(STEPS // 2):
        tile = slice(k * TILE, (k + 1) * TILE)
        ours = pl.ds(pl.multiple_of(at_ref[2] * (SIDE // 2) + k * TILE, TILE), TILE)
        mine[tile, :] = scale_ref[0] * jnp.dot(weights_ref[ours, :], text, preferred_element_type=F32)
        copies += run([pltpu.make_async_copy(mine.at[tile, :], mine_out.at[tile, :], sem.at[k])])
    wait(copies)


def back_tile(k, scale_ref, weights_ref, image, back, out_ref, sem):
    tile = slice(k * TILE, (k + 1) * TILE)
    back[tile, :] = (
        scale_ref[0]
        * lax.dot_general(
            weights_ref[:, tile], image, (((0,), (0,)), ((), ())), preferred_element_type=F32
        )
    ).astype(BF16)
    return run([pltpu.make_async_copy(back.at[tile, :], out_ref.at[tile, :], sem.at[k])])


def text_back_kernel(scale_ref, weights_ref, image_ref, out_ref, back, sem):
    image = image_ref[...]
    copies = []
    for k in range(STEPS - 1):
        copies += back_tile(k, scale_ref, weights_ref, image, back, out_ref, sem)
    wait(copies)


def pieces_kernel(at_ref, scale_ref, weights_ref, image_ref, swapped_ref, mine_ref, begun_ref, *refs):
    out_ref, own_ref, *out_refs, mine, back, sem = refs
    loads = run([pltpu.make_async_copy(mine_ref, mine, sem.at[0])])
    copies = back_tile(STEPS - 1, scale_ref, weights_ref, image_ref[...], back, out_ref, sem)
    wait(loads)
    for k in range(DEEP):
        block = pl.ds(pl.multiple_of(lax.rem(at_ref[3] + k, DEEP) * PIECE, PIECE), PIECE)
        total = mine[block, :] + swapped_ref[block, :].astype(F32)
        if k == 0:
            own_ref[...] = total
        else:
            out_refs[k - 1][...] = total.astype(BF16)
    wait(copies)


def project(back, raw):
    direction, norm = unit_rows(raw)
    along = jnp.sum(direction * back, axis=1, keepdims=True)
    return ((back - direction * along) / norm).astype(BF16)


def text_grad_kernel(raw_ref, parts_ref, out_ref, raw, grad, sem):
    wait(run([pltpu.make_async_copy(raw_ref, raw, sem.at[0])]))
    back = parts_ref[pl.ds(0, PIECE), :].astype(F32)
    for k in range(1, PEERS):
        back += parts_ref[pl.ds(k * PIECE, PIECE), :].astype(F32)
    grad[...] = project(back, raw[...])
    wait(run([pltpu.make_async_copy(grad, out_ref, sem.at[0])]))


def image_grad_kernel(raw_ref, own_ref, part_ref, *refs):
    pieces, (out_ref, loss_ref, raw, grad, sem) = refs[:-5], refs[-5:]
    loss_ref[...] = part_ref[...]
    wait(run([pltpu.make_async_copy(raw_ref, raw, sem.at[0])]))
    back = own_ref[...]
    for ref in pieces:
        back += ref[...].astype(F32)
    grad[...] = project(back, raw[...])
    wait(run([pltpu.make_async_copy(grad, out_ref, sem.at[0])]))


def gather_image(unit):
    plan, arrays = [(0, 0, 0, PIECE)], [unit]
    up, down, half = unit, unit, PIECE // 2
    for by in range(1, DEEP // 2):
        up, down = send(up, "z", 1), send(down, "z", -1)
        plan += [(0, -by, 0, PIECE), (0, by, 0, PIECE)]
        arrays += [up, down]
    plan += [(0, -(DEEP // 2), 0, half), (0, DEEP // 2, half, half)]
    arrays += [send(up[:half], "z", 1), send(down[half:], "z", -1)]
    plan += [(1, *rest) for _, *rest in plan]
    arrays += [send(a, "c", 1) for a in arrays]
    return plan, arrays


def sum_step(part, first, second):
    held = []
    for k in range(3):
        pairs = [(a, b) for a, b in shift(second, k + 1) if a // 8 % 2 == 1]
        if k < len(first):
            pairs += [(a, b) for a, b in shift("z", first[k]) if a // 8 % 2 == 0]
        held.append(lax.ppermute(part, "d", pairs))
    return (part + held[1]) + (held[0] + held[2])


def body(image_emb, text_emb, log_scale):
    width = image_emb.shape[1]
    scale = jnp.exp(log_scale)
    me = lax.axis_index("d")
    z, core, x = me % 8, (me // 8) % 2, me // 64
    at = jnp.stack([me % 16, me // 16, core, z, x % 2]).astype(jnp.int32)
    piece = local((PIECE, width), BF16)
    side = local((SIDE, width), BF16)
    outside = array((SIDE, width), BF16)
    raw = pltpu.VMEM((PIECE, width), BF16)
    sems = pltpu.SemaphoreType.DMA

    image_unit = call(image_unit_kernel, array((PIECE, width), BF16), Outside(image_emb), scratch=[raw, raw, sems((1,))])
    plan, pieces = gather_image(image_unit)
    text_units = call(text_units_kernel, outside, Outside(text_emb), scratch=[raw, raw, sems((PEERS,))])
    text = exchange(text_units, XY)

    lines = local((2 * STEPS, TILE), F32)
    image, logits, keep, give = call(
        functools.partial(logits_kernel, plan), [outside, local((SIDE, SIDE), F32), lines, lines],
        at, scale, text, *map(Outside, pieces),
        scratch=[pltpu.VMEM((SIDE, width), BF16), sems((len(plan),)), sems((1,))],
    )
    spread = call(spread_kernel, local((PEERS * LINES, TILE), F32), at, keep, send(give, "c", 1))
    lines = local((STEPS, TILE), F32)
    keep, give, part = call(join_kernel, [lines, lines, local((8, 128), F32)], at, exchange(spread, MIXED))
    recv = send(give, "c", 1)

    half = pltpu.VMEM((SIDE // 2, width), F32)
    weights, other, mine = call(
        weights_kernel,
        [local((SIDE, SIDE), BF16), local((SIDE // 2, width), BF16), array((SIDE // 2, width), F32)],
        at, scale, logits, text, keep, recv,
        scratch=[half, sems((STEPS // 2,))],
    )
    swapped = send(other, "c", 1)
    back = [pltpu.VMEM((SIDE, width), BF16), sems((STEPS,))]
    text_parts = call(text_back_kernel, outside, scale, weights, image, scratch=back)
    text_parts, own, *away = call(
        pieces_kernel, [outside, local((PIECE, width), F32)] + [piece] * (DEEP - 1),
        at, scale, weights, image, swapped, Outside(mine), Outside(text_parts),
        scratch=[half, *back], aliases={6: 0},
    )
    text_back = exchange(text_parts, XY)
    image_back = [send(a, "z", k + 1) for k, a in enumerate(away)]

    grad = array((PIECE, width), BF16)
    extra = [raw, raw, sems((1,))]
    grad_image, part = call(
        image_grad_kernel, [grad, local((8, 128), F32)], Outside(image_emb), own, part, *image_back, scratch=extra
    )
    part = sum_step(sum_step(part, (2, 4, 6), "x"), (1,), "y")
    loss = (part + send(part, "c", 1))[0, :1] * (LN2 / (2.0 * SIDE * PEERS))
    grad_text = call(text_grad_kernel, grad, Outside(text_emb), text_back, scratch=extra)
    return loss, grad_image, grad_text


def solution(mesh):
    flat = Mesh(mesh.devices.reshape(-1), ("d",))
    return jax.shard_map(
        body,
        mesh=flat,
        in_specs=(P("d", None), P("d", None), P()),
        out_specs=(P(), P("d", None), P("d", None)),
        check_vma=False,
    )
```

time: 449 us -> 157 us (0.35)
  blocking collectives: 232 us -> 12.2 us
  waiting for transfers between devices: 154 us -> 49 us
  starting transfers between devices: 0.34 us -> 58.6 us
  Pallas kernels: 0 us -> 29 us
  matrix products: 22.2 us -> 0 us
  other arithmetic: 20.3 us -> 0.01 us
  between operations: 16.5 us -> 3.41 us
    psum x3 -> x0, blocking collectives: 163 us -> none  [the longest x1 93.1 us: body(): loss = lax.psum(partial_loss, ('img', 'txt')).reshape(1)]
    all_gather x2 -> x0, waiting for transfers between devices: 92.4 us -> none  [the longest x1 50 us: body(): text_rows = lax.all_gather(text_emb, 'img', axis=0, tiled=True)]
    pmax x2 -> x0, blocking collectives: 69.2 us -> none  [the longest x1 51.7 us: body(): col_peak = lax.pmax(col_top, 'img')]
    reduce_scatter x2 -> x0, waiting for transfers between devices: 60.4 us -> none  [the longest x1 60.4 us: body(): lax.psum_scatter(text_back, 'img', scatter_dimension=0, tiled=True)]
    ppermute x0 -> x34, waiting for transfers between devices: none -> 49 us  [the longest x28 42.8 us: send(): return lax.ppermute(x, 'd', shift(axis, by))]
    ppermute x0 -> x34, starting transfers between devices: none -> 44.5 us  [the longest x28 34.1 us: send(): return lax.ppermute(x, 'd', shift(axis, by))]
    pallas_call x0 -> x10, Pallas kernels: none -> 29 us  [call(): pl.pallas_call(kernel, out_shape=outputs, in_specs=specs, out_specs=jax.t...]
    dot_general x3 -> x0, matrix products: 22.2 us -> none  [the longest x1 10.1 us: body(): lax.dot_general(weights, image_unit, back_dims, preferred_element_type=jn...]
  transfers between devices with their start and end apart: 4 -> 36, of which waited for: 3 -> 20; matrix products, arithmetic and copies ran while one was open for 3% -> 0% of each run, Pallas kernels for 0% -> 4%
where the time goes in v2:
time: 157 us; the launch traced here: 155 us
  starting transfers between devices  58.6 us (37%)
  waiting for transfers between devices  49 us (31%)
  Pallas kernels  29 us (18%)
  blocking collectives  12.2 us (8%)
  between operations  3.41 us (2%)
  local copies, waits for them, and re-layouts  3.29 us (2%)
    ppermute x28, waiting for transfers between devices, send(): return lax.ppermute(x, 'd', shift(axis, by))  42.8 us
    ppermute x28, starting transfers between devices, send(): return lax.ppermute(x, 'd', shift(axis, by))  34.1 us
    pallas_call x10, Pallas kernels, call(): pl.pallas_call(kernel, out_shape=outputs, in_specs=specs, out_specs=jax.t...  29 us
    all_to_all x2, starting transfers between devices, exchange(): return lax.all_to_all(x, 'd', 0, 0, axis_index_groups=groups, tiled=True)  14.1 us
    all_to_all x1, blocking collectives, exchange(): return lax.all_to_all(x, 'd', 0, 0, axis_index_groups=groups, tiled=True)  12.2 us
    ppermute x6, starting transfers between devices, sum_step(): held.append(lax.ppermute(part, 'd', pairs))  10.4 us
    ppermute x6, waiting for transfers between devices, sum_step(): held.append(lax.ppermute(part, 'd', pairs))  6.24 us
  transfers between devices with their start and end apart: 36, of which 20 were waited for; matrix products, arithmetic and copies ran while one was open for 0% of the time, Pallas kernels for 4%

profile of v2, /device:TPU:28, one launch (start us, length us, event | category | flops | bytes accessed | tf_op | source)
XLA Modules:
  0.0 155.5 jit_solution(16155307826522871669)
XLA Ops:
  0.6 2.7 %shard_map.58 = bf16[1024,1280]{1,0:T(8,128)(2,1)} custom-call(bf16[64,1280]{1,0:T(8,128)(2,1)} %raw_ref.7), custom_call_target="tpu_custom_call" | custom-call | tf_op jit(solution)/shard_map/pallas_call | solution.py:72
  3.3 7.1 %all-to-all-start = ((bf16[16,64,1280]{2,1,0:T(8,128)(2,1)}), bf16[16,64,1280]{2,1,0:T(8,128)(2,1)S(1)}, u32[]{:S(2)}, u32[]{:S(2)}) async-start(bf16[16,64,1280]{2,1,0:T(8,128)(2,1)} %bitcast.18), calls=%async_computation | async-start | bytes 5242880 | tf_op jit(solution)/shard_map/all_to_all | solution.py:49
  12.2 5.9 %collective-permute-start.1 = (bf16[64,1280]{1,0:T(8,128)(2,1)}, bf16[64,1280]{1,0:T(8,128)(2,1)S(1)}, u32[]{:S(2)}, u32[]{:S(2)}) collective-permute-start(bf16[64,1280]{1,0:T(8,128)(2,1)} %shard_map.59.refs_0_), channel_id=1, source_target_pairs={{0,7},{1,0},{2,1},{3,2},{4,3},{5,4},{6,5},{7,6},{8,15},{9,8},{10,9... | collective-permute-start | bytes 491528 | tf_op jit(solution)/shard_map/ppermute | solution.py:45
  18.1 3.2 %collective-permute-done.1.refs_2_ = bf16[64,1280]{1,0:T(8,128)(2,1)S(1)} collective-permute-done((bf16[64,1280]{1,0:T(8,128)(2,1)}, bf16[64,1280]{1,0:T(8,128)(2,1)S(1)}, u32[]{:S(2)}, u32[]{:S(2)}) %collective-permute-start.1) | collective-permute-done | bytes 163872 | tf_op jit(solution)/shard_map/ppermute | solution.py:45
  21.3 3.6 %collective-permute-start.3 = (bf16[64,1280]{1,0:T(8,128)(2,1)S(1)}, bf16[64,1280]{1,0:T(8,128)(2,1)S(1)}, u32[]{:S(2)}, u32[]{:S(2)}) collective-permute-start(bf16[64,1280]{1,0:T(8,128)(2,1)S(1)} %collective-permute-done.1.refs_2_), channel_id=1, source_target_pairs={{0,7},{1,0},{2,1},{3,2},{4,3},{5,4},{6,5},{7,6},{8,15},{9,8},{10,9... | collective-permute-start | bytes 491528 | tf_op jit(solution)/shard_map/ppermute | solution.py:45
  24.9 2.8 %collective-permute-done.3.refs_4_ = bf16[64,1280]{1,0:T(8,128)(2,1)S(1)} collective-permute-done((bf16[64,1280]{1,0:T(8,128)(2,1)S(1)}, bf16[64,1280]{1,0:T(8,128)(2,1)S(1)}, u32[]{:S(2)}, u32[]{:S(2)}) %collective-permute-start.3) | collective-permute-done | bytes 163872 | tf_op jit(solution)/shard_map/ppermute | solution.py:45
  27.7 3.7 %collective-permute-start.5 = (bf16[64,1280]{1,0:T(8,128)(2,1)S(1)}, bf16[64,1280]{1,0:T(8,128)(2,1)S(1)}, u32[]{:S(2)}, u32[]{:S(2)}) collective-permute-start(bf16[64,1280]{1,0:T(8,128)(2,1)S(1)} %collective-permute-done.3.refs_4_), channel_id=1, source_target_pairs={{0,7},{1,0},{2,1},{3,2},{4,3},{5,4},{6,5},{7,6},{8,15},{9,8},{10,9... | collective-permute-start | bytes 491528 | tf_op jit(solution)/shard_map/ppermute | solution.py:45
  32.1 2.2 %collective-permute-done.5.refs_6_ = bf16[64,1280]{1,0:T(8,128)(2,1)S(1)} collective-permute-done((bf16[64,1280]{1,0:T(8,128)(2,1)S(1)}, bf16[64,1280]{1,0:T(8,128)(2,1)S(1)}, u32[]{:S(2)}, u32[]{:S(2)}) %collective-permute-start.5) | collective-permute-done | bytes 163872 | tf_op jit(solution)/shard_map/ppermute | solution.py:45
  34.3 4.0 %collective-permute-done.4.refs_5_ = bf16[64,1280]{1,0:T(8,128)(2,1)S(1)} collective-permute-done((bf16[64,1280]{1,0:T(8,128)(2,1)}, bf16[64,1280]{1,0:T(8,128)(2,1)S(1)}, u32[]{:S(2)}, u32[]{:S(2)}) %collective-permute-start.4) | collective-permute-done | bytes 163872 | tf_op jit(solution)/shard_map/ppermute | solution.py:45
  41.0 2.2 %collective-permute-done.7.refs_8_ = bf16[32,1280]{1,0:T(8,128)(2,1)S(1)} collective-permute-done((bf16[32,1280]{1,0:T(8,128)(2,1)S(1)}, bf16[32,1280]{1,0:T(8,128)(2,1)S(1)}, u32[]{:S(2)}, u32[]{:S(2)}) %collective-permute-start.7) | collective-permute-done | bytes 81952 | tf_op jit(solution)/shard_map/ppermute | solution.py:45
  46.3 6.9 %shard_map.60 = (bf16[1024,1280]{1,0:T(8,128)(2,1)}, f32[1024,1024]{1,0:T(8,128)S(1)}, f32[8,256]{1,0:T(8,128)S(1)}, f32[8,256]{1,0:T(8,128)S(1)}) custom-call(s32[5]{0:T(128)S(1)} %stack.23.at_ref, f32[1]{0:T(128)S(6)} %exp.3.scale_ref, bf16[1024,1280]{1,0:T(8,128)(2,1)S(1)} %bitcast.12, bf16[64,1280]{1,0:T(8,128)(2,1)} %shard_map.59.refs_0_, ...), custom_call_target="tpu_custom_call" | custom-call | tf_op jit(solution)/shard_map/pallas_call | solution.py:72
  55.0 12.2 %all_to_all.33 = f32[16,16,256]{2,1,0:T(8,128)S(1)} all-to-all(f32[16,16,256]{2,1,0:T(8,128)S(1)} %bitcast.16), channel_id=1, replica_groups={{0,16,32,48,64,80,96,112,128,144,160,176,192,208,224,240},{1,17,33,49,6..., dimensions={0} | all-to-all | bytes 524288 | tf_op jit(solution)/shard_map/all_to_all | solution.py:49
  68.0 2.4 %collective-permute-start.18 = (f32[4,256]{1,0:T(4,128)S(1)}, f32[4,256]{1,0:T(4,128)S(1)}, u32[]{:S(2)}, u32[]{:S(2)}) collective-permute-start(f32[4,256]{1,0:T(4,128)S(1)} %get-tuple-element.28), channel_id=1, source_target_pairs={{0,8},{1,9},{2,10},{3,11},{4,12},{5,13},{6,14},{7,15},{8,0},{9,1},... | collective-permute-start | bytes 12296 | tf_op jit(solution)/shard_map/ppermute | solution.py:45
  71.2 5.8 %shard_map.63 = (bf16[1024,1024]{1,0:T(8,128)(2,1)S(1)}, bf16[512,1280]{1,0:T(8,128)(2,1)S(1)}, f32[512,1280]{1,0:T(8,128)}) custom-call(s32[5]{0:T(128)S(1)} %stack.23.at_ref, f32[1]{0:T(128)S(6)} %exp.3.scale_ref, f32[1024,1024]{1,0:T(8,128)S(1)} %get-tuple-element.24.logits_ref, bf16[1024,1280]{1,0:T(8,128)(2,1)S(1)} %bitcast.13, ...), custom_call_target="tpu_custom_call" | custom-call | tf_op jit(solution)/shard_map/pallas_call | solution.py:72
  77.5 3.2 %shard_map.64.begun_ref = bf16[1024,1280]{1,0:T(8,128)(2,1)} custom-call(f32[1]{0:T(128)S(6)} %exp.3.scale_ref, bf16[1024,1024]{1,0:T(8,128)(2,1)S(1)} %get-tuple-element.29.weights_ref, bf16[1024,1280]{1,0:T(8,128)(2,1)S(1)} %copy-done), custom_call_target="tpu_custom_call" | custom-call | tf_op jit(solution)/shard_map/pallas_call | solution.py:72
  80.7 3.4 %shard_map.65 = (bf16[1024,1280]{1,0:T(8,128)(2,1)}, f32[64,1280]{1,0:T(8,128)S(1)}, bf16[64,1280]{1,0:T(8,128)(2,1)S(1)}, bf16[64,1280]{1,0:T(8,128)(2,1)S(1)},...) custom-call(s32[5]{0:T(128)S(1)} %stack.23.at_ref, ...), custom_call_target="tpu_custom_call", output_to_operand_aliasing={{0}: (6, {})} | custom-call | tf_op jit(solution)/shard_map/pallas_call | solution.py:72
  86.8 6.9 %all-to-all-start.2 = ((bf16[16,64,1280]{2,1,0:T(8,128)(2,1)}), bf16[16,64,1280]{2,1,0:T(8,128)(2,1)S(1)}, u32[]{:S(2)}, u32[]{:S(2)}) async-start(bf16[16,64,1280]{2,1,0:T(8,128)(2,1)} %bitcast.17), calls=%async_computation.2 | async-start | bytes 5242880 | tf_op jit(solution)/shard_map/all_to_all | solution.py:49
  93.7 2.1 %collective-permute-start.20 = (bf16[64,1280]{1,0:T(8,128)(2,1)}, bf16[64,1280]{1,0:T(8,128)(2,1)S(1)}, u32[]{:S(2)}, u32[]{:S(2)}) collective-permute-start(bf16[64,1280]{1,0:T(8,128)(2,1)} %copy-done.4), channel_id=1, source_target_pairs={{0,1},{1,2},{2,3},{3,4},{4,5},{5,6},{6,7},{7,0},{8,9},{9,10},{10,1... | collective-permute-start | bytes 491528 | tf_op jit(solution)/shard_map/ppermute | solution.py:45
  96.6 3.4 %collective-permute-start.22 = (bf16[64,1280]{1,0:T(8,128)(2,1)}, bf16[64,1280]{1,0:T(8,128)(2,1)S(1)}, u32[]{:S(2)}, u32[]{:S(2)}) collective-permute-start(bf16[64,1280]{1,0:T(8,128)(2,1)} %copy-done.2), channel_id=1, source_target_pairs={{0,3},{1,4},{2,5},{3,6},{4,7},{5,0},{6,1},{7,2},{8,11},{9,12},{10,... | collective-permute-start | bytes 491528 | tf_op jit(solution)/shard_map/ppermute | solution.py:45
  100.0 2.0 %collective-permute-start.23 = (bf16[64,1280]{1,0:T(8,128)(2,1)}, bf16[64,1280]{1,0:T(8,128)(2,1)S(1)}, u32[]{:S(2)}, u32[]{:S(2)}) collective-permute-start(bf16[64,1280]{1,0:T(8,128)(2,1)} %copy-done.1), channel_id=1, source_target_pairs={{0,4},{1,5},{2,6},{3,7},{4,0},{5,1},{6,2},{7,3},{8,12},{9,13},{10,... | collective-permute-start | bytes 491528 | tf_op jit(solution)/shard_map/ppermute | solution.py:45
  102.0 3.3 %collective-permute-start.24 = (bf16[64,1280]{1,0:T(8,128)(2,1)S(1)}, bf16[64,1280]{1,0:T(8,128)(2,1)S(1)}, u32[]{:S(2)}, u32[]{:S(2)}) collective-permute-start(bf16[64,1280]{1,0:T(8,128)(2,1)S(1)} %get-tuple-element.39), channel_id=1, source_target_pairs={{0,5},{1,6},{2,7},{3,0},{4,1},{5,2},{6,3},{7,4},{8,13},{9,14},{10,... | collective-permute-start | bytes 491528 | tf_op jit(solution)/shard_map/ppermute | solution.py:45
  105.3 2.9 %collective-permute-start.25 = (bf16[64,1280]{1,0:T(8,128)(2,1)S(1)}, bf16[64,1280]{1,0:T(8,128)(2,1)S(1)}, u32[]{:S(2)}, u32[]{:S(2)}) collective-permute-start(bf16[64,1280]{1,0:T(8,128)(2,1)S(1)} %get-tuple-element.40), channel_id=1, source_target_pairs={{0,6},{1,7},{2,0},{3,1},{4,2},{5,3},{6,4},{7,5},{8,14},{9,15},{10,... | collective-permute-start | bytes 491528 | tf_op jit(solution)/shard_map/ppermute | solution.py:45
  108.1 8.8 %collective-permute-done.21.refs_1_ = bf16[64,1280]{1,0:T(8,128)(2,1)S(1)} collective-permute-done((bf16[64,1280]{1,0:T(8,128)(2,1)}, bf16[64,1280]{1,0:T(8,128)(2,1)S(1)}, u32[]{:S(2)}, u32[]{:S(2)}) %collective-permute-start.21) | collective-permute-done | bytes 163872 | tf_op jit(solution)/shard_map/ppermute | solution.py:45
  118.4 4.8 %collective-permute-done.23.refs_3_ = bf16[64,1280]{1,0:T(8,128)(2,1)S(1)} collective-permute-done((bf16[64,1280]{1,0:T(8,128)(2,1)}, bf16[64,1280]{1,0:T(8,128)(2,1)S(1)}, u32[]{:S(2)}, u32[]{:S(2)}) %collective-permute-start.23) | collective-permute-done | bytes 163872 | tf_op jit(solution)/shard_map/ppermute | solution.py:45
  123.3 6.5 %collective-permute-done.25.refs_5_ = bf16[64,1280]{1,0:T(8,128)(2,1)S(1)} collective-permute-done((bf16[64,1280]{1,0:T(8,128)(2,1)S(1)}, bf16[64,1280]{1,0:T(8,128)(2,1)S(1)}, u32[]{:S(2)}, u32[]{:S(2)}) %collective-permute-start.25) | collective-permute-done | bytes 163872 | tf_op jit(solution)/shard_map/ppermute | solution.py:45
  131.2 1.9 %shard_map.66 = (bf16[64,1280]{1,0:T(8,128)(2,1)}, f32[8,128]{1,0:T(8,128)S(1)}) custom-call(bf16[64,1280]{1,0:T(8,128)(2,1)} %raw_ref.6, f32[64,1280]{1,0:T(8,128)S(1)} %get-tuple-element.33.own_ref, f32[8,128]{1,0:T(8,128)S(1)} %get-tuple-element.34.part_ref, bf16[64,1280]{1,0:T(8,128)(2,1)S(1)} %collective-permute-done.20.refs_0_, ...), custom_call_target="tpu_custom_call" | custom-call | tf_op jit(solution)/shard_map/pallas_call | solution.py:72
  133.1 2.9 %collective-permute-start.29 = (f32[8,128]{1,0:T(8,128)S(1)}, f32[8,128]{1,0:T(8,128)S(1)}, u32[]{:S(2)}, u32[]{:S(2)}) collective-permute-start(f32[8,128]{1,0:T(8,128)S(1)} %get-tuple-element.42), channel_id=1, source_target_pairs={{8,200},{9,201},{10,202},{11,203},{12,204},{13,205},{14,206},{15,2... | collective-permute-start | bytes 12296 | tf_op jit(solution)/shard_map/ppermute | solution.py:335
  136.1 3.4 %collective-permute-start.27 = (f32[8,128]{1,0:T(8,128)S(1)}, f32[8,128]{1,0:T(8,128)S(1)}, u32[]{:S(2)}, u32[]{:S(2)}) collective-permute-start(f32[8,128]{1,0:T(8,128)S(1)} %get-tuple-element.42), channel_id=1, source_target_pairs={{8,136},{9,137},{10,138},{11,139},{12,140},{13,141},{14,142},{15,1... | collective-permute-start | bytes 12296 | tf_op jit(solution)/shard_map/ppermute | solution.py:335
  139.5 2.3 %collective-permute-done.28 = f32[8,128]{1,0:T(8,128)S(1)} collective-permute-done((f32[8,128]{1,0:T(8,128)S(1)}, f32[8,128]{1,0:T(8,128)S(1)}, u32[]{:S(2)}, u32[]{:S(2)}) %collective-permute-start.28) | collective-permute-done | bytes 4128 | tf_op jit(solution)/shard_map/ppermute | solution.py:335
  144.3 2.7 %collective-permute-start.31 = (f32[8,128]{1,0:T(8,128)S(1)}, f32[8,128]{1,0:T(8,128)S(1)}, u32[]{:S(2)}, u32[]{:S(2)}) collective-permute-start(f32[8,128]{1,0:T(8,128)S(1)} %add_add_fusion.1), channel_id=1, source_target_pairs={{8,24},{9,25},{10,26},{11,27},{12,28},{13,29},{14,30},{15,31},{24,... | collective-permute-start | bytes 12296 | tf_op jit(solution)/shard_map/ppermute | solution.py:335
  147.7 2.1 %collective-permute-done.31 = f32[8,128]{1,0:T(8,128)S(1)} collective-permute-done((f32[8,128]{1,0:T(8,128)S(1)}, f32[8,128]{1,0:T(8,128)S(1)}, u32[]{:S(2)}, u32[]{:S(2)}) %collective-permute-start.31) | collective-permute-done | bytes 4128 | tf_op jit(solution)/shard_map/ppermute | solution.py:335
  152.3 2.1 %shard_map.67 = bf16[64,1280]{1,0:T(8,128)(2,1)} custom-call(bf16[64,1280]{1,0:T(8,128)(2,1)} %raw_ref.7, bf16[1024,1280]{1,0:T(8,128)(2,1)S(1)} %bitcast.14), custom_call_target="tpu_custom_call" | custom-call | tf_op jit(solution)/shard_map/pallas_call | solution.py:72
  (88 shorter events, 22.7 us)
Async XLA Ops:
  3.3 43.0 %all-to-all-start = ((bf16[16,64,1280]{2,1,0:T(8,128)(2,1)}), bf16[16,64,1280]{2,1,0:T(8,128)(2,1)S(1)}, u32[]{:S(2)}, u32[]{:S(2)}) async-start(bf16[16,64,1280]{2,1,0:T(8,128)(2,1)} %bitcast.18), calls=%async_computation | async-start | bytes 5242880 | tf_op jit(solution)/shard_map/all_to_all | solution.py:49
  12.2 9.1 %collective-permute-start.1 = (bf16[64,1280]{1,0:T(8,128)(2,1)}, bf16[64,1280]{1,0:T(8,128)(2,1)S(1)}, u32[]{:S(2)}, u32[]{:S(2)}) collective-permute-start(bf16[64,1280]{1,0:T(8,128)(2,1)} %shard_map.59.refs_0_), channel_id=1, source_target_pairs={{0,7},{1,0},{2,1},{3,2},{4,3},{5,4},{6,5},{7,6},{8,15},{9,8},{10,9... | collective-permute-start | bytes 491528 | tf_op jit(solution)/shard_map/ppermute | solution.py:45
  18.1 6.8 %collective-permute-start = (bf16[64,1280]{1,0:T(8,128)(2,1)}, bf16[64,1280]{1,0:T(8,128)(2,1)S(1)}, u32[]{:S(2)}, u32[]{:S(2)}) collective-permute-start(bf16[64,1280]{1,0:T(8,128)(2,1)} %shard_map.59.refs_0_), channel_id=1, source_target_pairs={{0,1},{1,2},{2,3},{3,4},{4,5},{5,6},{6,7},{7,0},{8,9},{9,10},{10,1... | collective-permute-start | bytes 491528 | tf_op jit(solution)/shard_map/ppermute | solution.py:45
  21.3 6.4 %collective-permute-start.3 = (bf16[64,1280]{1,0:T(8,128)(2,1)S(1)}, bf16[64,1280]{1,0:T(8,128)(2,1)S(1)}, u32[]{:S(2)}, u32[]{:S(2)}) collective-permute-start(bf16[64,1280]{1,0:T(8,128)(2,1)S(1)} %collective-permute-done.1.refs_2_), channel_id=1, source_target_pairs={{0,7},{1,0},{2,1},{3,2},{4,3},{5,4},{6,5},{7,6},{8,15},{9,8},{10,9... | collective-permute-start | bytes 491528 | tf_op jit(solution)/shard_map/ppermute | solution.py:45
  24.9 6.6 %collective-permute-start.2 = (bf16[64,1280]{1,0:T(8,128)(2,1)S(1)}, bf16[64,1280]{1,0:T(8,128)(2,1)}, u32[]{:S(2)}, u32[]{:S(2)}) collective-permute-start(bf16[64,1280]{1,0:T(8,128)(2,1)S(1)} %collective-permute-done.refs_1_), channel_id=1, source_target_pairs={{0,1},{1,2},{2,3},{3,4},{4,5},{5,6},{6,7},{7,0},{8,9},{9,10},{10,1... | collective-permute-start | bytes 491528 | tf_op jit(solution)/shard_map/ppermute | solution.py:45
  27.7 6.5 %collective-permute-start.5 = (bf16[64,1280]{1,0:T(8,128)(2,1)S(1)}, bf16[64,1280]{1,0:T(8,128)(2,1)S(1)}, u32[]{:S(2)}, u32[]{:S(2)}) collective-permute-start(bf16[64,1280]{1,0:T(8,128)(2,1)S(1)} %collective-permute-done.3.refs_4_), channel_id=1, source_target_pairs={{0,7},{1,0},{2,1},{3,2},{4,3},{5,4},{6,5},{7,6},{8,15},{9,8},{10,9... | collective-permute-start | bytes 491528 | tf_op jit(solution)/shard_map/ppermute | solution.py:45
  31.5 6.7 %collective-permute-start.4 = (bf16[64,1280]{1,0:T(8,128)(2,1)}, bf16[64,1280]{1,0:T(8,128)(2,1)S(1)}, u32[]{:S(2)}, u32[]{:S(2)}) collective-permute-start(bf16[64,1280]{1,0:T(8,128)(2,1)} %collective-permute-done.2.refs_3_), channel_id=1, source_target_pairs={{0,1},{1,2},{2,3},{3,4},{4,5},{5,6},{6,7},{7,0},{8,9},{9,10},{10,1... | collective-permute-start | bytes 491528 | tf_op jit(solution)/shard_map/ppermute | solution.py:45
  31.5 6.8 %collective-permute-start.8 = (bf16[64,1280]{1,0:T(8,128)(2,1)}, bf16[64,1280]{1,0:T(8,128)(2,1)S(1)}, u32[]{:S(2)}, u32[]{:S(2)}) collective-permute-start(bf16[64,1280]{1,0:T(8,128)(2,1)} %shard_map.59.refs_0_), channel_id=1, source_target_pairs={{0,8},{1,9},{2,10},{3,11},{4,12},{5,13},{6,14},{7,15},{8,0},{9,1},... | collective-permute-start | bytes 491528 | tf_op jit(solution)/shard_map/ppermute | solution.py:45
  31.5 7.1 %collective-permute-start.10 = (bf16[64,1280]{1,0:T(8,128)(2,1)S(1)}, bf16[64,1280]{1,0:T(8,128)(2,1)S(1)}, u32[]{:S(2)}, u32[]{:S(2)}) collective-permute-start(bf16[64,1280]{1,0:T(8,128)(2,1)S(1)} %collective-permute-done.1.refs_2_), channel_id=1, source_target_pairs={{0,8},{1,9},{2,10},{3,11},{4,12},{5,13},{6,14},{7,15},{8,0},{9,1},... | collective-permute-start | bytes 491528 | tf_op jit(solution)/shard_map/ppermute | solution.py:45
  32.0 8.4 %collective-permute-start.9 = (bf16[64,1280]{1,0:T(8,128)(2,1)S(1)}, bf16[64,1280]{1,0:T(8,128)(2,1)S(1)}, u32[]{:S(2)}, u32[]{:S(2)}) collective-permute-start(bf16[64,1280]{1,0:T(8,128)(2,1)S(1)} %collective-permute-done.refs_1_), channel_id=1, source_target_pairs={{0,8},{1,9},{2,10},{3,11},{4,12},{5,13},{6,14},{7,15},{8,0},{9,1},... | collective-permute-start | bytes 491528 | tf_op jit(solution)/shard_map/ppermute | solution.py:45
  34.3 6.2 %collective-permute-start.12 = (bf16[64,1280]{1,0:T(8,128)(2,1)S(1)}, bf16[64,1280]{1,0:T(8,128)(2,1)S(1)}, u32[]{:S(2)}, u32[]{:S(2)}) collective-permute-start(bf16[64,1280]{1,0:T(8,128)(2,1)S(1)} %collective-permute-done.3.refs_4_), channel_id=1, source_target_pairs={{0,8},{1,9},{2,10},{3,11},{4,12},{5,13},{6,14},{7,15},{8,0},{9,1},... | collective-permute-start | bytes 491528 | tf_op jit(solution)/shard_map/ppermute | solution.py:45
  38.3 7.2 %collective-permute-start.11 = (bf16[64,1280]{1,0:T(8,128)(2,1)}, bf16[64,1280]{1,0:T(8,128)(2,1)}, u32[]{:S(2)}, u32[]{:S(2)}) collective-permute-start(bf16[64,1280]{1,0:T(8,128)(2,1)} %collective-permute-done.2.refs_3_), channel_id=1, source_target_pairs={{0,8},{1,9},{2,10},{3,11},{4,12},{5,13},{6,14},{7,15},{8,0},{9,1},... | collective-permute-start | bytes 491528 | tf_op jit(solution)/shard_map/ppermute | solution.py:45
  38.3 4.9 %collective-permute-start.7 = (bf16[32,1280]{1,0:T(8,128)(2,1)S(1)}, bf16[32,1280]{1,0:T(8,128)(2,1)S(1)}, u32[]{:S(2)}, u32[]{:S(2)}) collective-permute-start(bf16[32,1280]{1,0:T(8,128)(2,1)S(1)} %slice.13), channel_id=1, source_target_pairs={{0,7},{1,0},{2,1},{3,2},{4,3},{5,4},{6,5},{7,6},{8,15},{9,8},{10,9... | collective-permute-start | bytes 245768 | tf_op jit(solution)/shard_map/ppermute | solution.py:45
  38.7 6.0 %collective-permute-start.6 = (bf16[32,1280]{1,0:T(8,128)(2,1)S(1)}, bf16[32,1280]{1,0:T(8,128)(2,1)}, u32[]{:S(2)}, u32[]{:S(2)}) collective-permute-start(bf16[32,1280]{1,0:T(8,128)(2,1)S(1)} %slice.12), channel_id=1, source_target_pairs={{0,1},{1,2},{2,3},{3,4},{4,5},{5,6},{6,7},{7,0},{8,9},{9,10},{10,1... | collective-permute-start | bytes 245768 | tf_op jit(solution)/shard_map/ppermute | solution.py:45
  40.4 5.0 %collective-permute-start.14 = (bf16[64,1280]{1,0:T(8,128)(2,1)S(1)}, bf16[64,1280]{1,0:T(8,128)(2,1)}, u32[]{:S(2)}, u32[]{:S(2)}) collective-permute-start(bf16[64,1280]{1,0:T(8,128)(2,1)S(1)} %collective-permute-done.5.refs_6_), channel_id=1, source_target_pairs={{0,8},{1,9},{2,10},{3,11},{4,12},{5,13},{6,14},{7,15},{8,0},{9,1},... | collective-permute-start | bytes 491528 | tf_op jit(solution)/shard_map/ppermute | solution.py:45
  40.5 5.8 %collective-permute-start.13 = (bf16[64,1280]{1,0:T(8,128)(2,1)S(1)}, bf16[64,1280]{1,0:T(8,128)(2,1)}, u32[]{:S(2)}, u32[]{:S(2)}) collective-permute-start(bf16[64,1280]{1,0:T(8,128)(2,1)S(1)} %collective-permute-done.4.refs_5_), channel_id=1, source_target_pairs={{0,8},{1,9},{2,10},{3,11},{4,12},{5,13},{6,14},{7,15},{8,0},{9,1},... | collective-permute-start | bytes 491528 | tf_op jit(solution)/shard_map/ppermute | solution.py:45
  68.0 3.3 %collective-permute-start.18 = (f32[4,256]{1,0:T(4,128)S(1)}, f32[4,256]{1,0:T(4,128)S(1)}, u32[]{:S(2)}, u32[]{:S(2)}) collective-permute-start(f32[4,256]{1,0:T(4,128)S(1)} %get-tuple-element.28), channel_id=1, source_target_pairs={{0,8},{1,9},{2,10},{3,11},{4,12},{5,13},{6,14},{7,15},{8,0},{9,1},... | collective-permute-start | bytes 12296 | tf_op jit(solution)/shard_map/ppermute | solution.py:45
  77.0 3.6 %collective-permute-start.19 = (bf16[512,1280]{1,0:T(8,128)(2,1)S(1)}, bf16[512,1280]{1,0:T(8,128)(2,1)S(1)}, u32[]{:S(2)}, u32[]{:S(2)}) collective-permute-start(bf16[512,1280]{1,0:T(8,128)(2,1)S(1)} %get-tuple-element.31), channel_id=1, source_target_pairs={{0,8},{1,9},{2,10},{3,11},{4,12},{5,13},{6,14},{7,15},{8,0},{9,1},... | collective-permute-start | bytes 3932168 | tf_op jit(solution)/shard_map/ppermute | solution.py:45
  86.8 65.5 %all-to-all-start.2 = ((bf16[16,64,1280]{2,1,0:T(8,128)(2,1)}), bf16[16,64,1280]{2,1,0:T(8,128)(2,1)S(1)}, u32[]{:S(2)}, u32[]{:S(2)}) async-start(bf16[16,64,1280]{2,1,0:T(8,128)(2,1)} %bitcast.17), calls=%async_computation.2 | async-start | bytes 5242880 | tf_op jit(solution)/shard_map/all_to_all | solution.py:49
  93.7 11.6 %collective-permute-start.20 = (bf16[64,1280]{1,0:T(8,128)(2,1)}, bf16[64,1280]{1,0:T(8,128)(2,1)S(1)}, u32[]{:S(2)}, u32[]{:S(2)}) collective-permute-start(bf16[64,1280]{1,0:T(8,128)(2,1)} %copy-done.4), channel_id=1, source_target_pairs={{0,1},{1,2},{2,3},{3,4},{4,5},{5,6},{6,7},{7,0},{8,9},{9,10},{10,1... | collective-permute-start | bytes 491528 | tf_op jit(solution)/shard_map/ppermute | solution.py:45
  95.8 21.2 %collective-permute-start.21 = (bf16[64,1280]{1,0:T(8,128)(2,1)}, bf16[64,1280]{1,0:T(8,128)(2,1)S(1)}, u32[]{:S(2)}, u32[]{:S(2)}) collective-permute-start(bf16[64,1280]{1,0:T(8,128)(2,1)} %copy-done.3), channel_id=1, source_target_pairs={{0,2},{1,3},{2,4},{3,5},{4,6},{5,7},{6,0},{7,1},{8,10},{9,11},{10,... | collective-permute-start | bytes 491528 | tf_op jit(solution)/shard_map/ppermute | solution.py:45
  96.6 21.8 %collective-permute-start.22 = (bf16[64,1280]{1,0:T(8,128)(2,1)}, bf16[64,1280]{1,0:T(8,128)(2,1)S(1)}, u32[]{:S(2)}, u32[]{:S(2)}) collective-permute-start(bf16[64,1280]{1,0:T(8,128)(2,1)} %copy-done.2), channel_id=1, source_target_pairs={{0,3},{1,4},{2,5},{3,6},{4,7},{5,0},{6,1},{7,2},{8,11},{9,12},{10,... | collective-permute-start | bytes 491528 | tf_op jit(solution)/shard_map/ppermute | solution.py:45
  100.0 23.2 %collective-permute-start.23 = (bf16[64,1280]{1,0:T(8,128)(2,1)}, bf16[64,1280]{1,0:T(8,128)(2,1)S(1)}, u32[]{:S(2)}, u32[]{:S(2)}) collective-permute-start(bf16[64,1280]{1,0:T(8,128)(2,1)} %copy-done.1), channel_id=1, source_target_pairs={{0,4},{1,5},{2,6},{3,7},{4,0},{5,1},{6,2},{7,3},{8,12},{9,13},{10,... | collective-permute-start | bytes 491528 | tf_op jit(solution)/shard_map/ppermute | solution.py:45
  102.0 21.3 %collective-permute-start.24 = (bf16[64,1280]{1,0:T(8,128)(2,1)S(1)}, bf16[64,1280]{1,0:T(8,128)(2,1)S(1)}, u32[]{:S(2)}, u32[]{:S(2)}) collective-permute-start(bf16[64,1280]{1,0:T(8,128)(2,1)S(1)} %get-tuple-element.39), channel_id=1, source_target_pairs={{0,5},{1,6},{2,7},{3,0},{4,1},{5,2},{6,3},{7,4},{8,13},{9,14},{10,... | collective-permute-start | bytes 491528 | tf_op jit(solution)/shard_map/ppermute | solution.py:45
  105.3 24.5 %collective-permute-start.25 = (bf16[64,1280]{1,0:T(8,128)(2,1)S(1)}, bf16[64,1280]{1,0:T(8,128)(2,1)S(1)}, u32[]{:S(2)}, u32[]{:S(2)}) collective-permute-start(bf16[64,1280]{1,0:T(8,128)(2,1)S(1)} %get-tuple-element.40), channel_id=1, source_target_pairs={{0,6},{1,7},{2,0},{3,1},{4,2},{5,3},{6,4},{7,5},{8,14},{9,15},{10,... | collective-permute-start | bytes 491528 | tf_op jit(solution)/shard_map/ppermute | solution.py:45
  116.9 14.2 %collective-permute-start.26 = (bf16[64,1280]{1,0:T(8,128)(2,1)S(1)}, bf16[64,1280]{1,0:T(8,128)(2,1)S(1)}, u32[]{:S(2)}, u32[]{:S(2)}) collective-permute-start(bf16[64,1280]{1,0:T(8,128)(2,1)S(1)} %get-tuple-element.41), channel_id=1, source_target_pairs={{0,7},{1,0},{2,1},{3,2},{4,3},{5,4},{6,5},{7,6},{8,15},{9,8},{10,9... | collective-permute-start | bytes 491528 | tf_op jit(solution)/shard_map/ppermute | solution.py:45
  133.1 6.4 %collective-permute-start.29 = (f32[8,128]{1,0:T(8,128)S(1)}, f32[8,128]{1,0:T(8,128)S(1)}, u32[]{:S(2)}, u32[]{:S(2)}) collective-permute-start(f32[8,128]{1,0:T(8,128)S(1)} %get-tuple-element.42), channel_id=1, source_target_pairs={{8,200},{9,201},{10,202},{11,203},{12,204},{13,205},{14,206},{15,2... | collective-permute-start | bytes 12296 | tf_op jit(solution)/shard_map/ppermute | solution.py:335
  136.1 5.7 %collective-permute-start.28 = (f32[8,128]{1,0:T(8,128)S(1)}, f32[8,128]{1,0:T(8,128)S(1)}, u32[]{:S(2)}, u32[]{:S(2)}) collective-permute-start(f32[8,128]{1,0:T(8,128)S(1)} %get-tuple-element.42), channel_id=1, source_target_pairs={{8,72},{9,73},{10,74},{11,75},{12,76},{13,77},{14,78},{15,79},{24,... | collective-permute-start | bytes 12296 | tf_op jit(solution)/shard_map/ppermute | solution.py:335
  136.1 7.5 %collective-permute-start.27 = (f32[8,128]{1,0:T(8,128)S(1)}, f32[8,128]{1,0:T(8,128)S(1)}, u32[]{:S(2)}, u32[]{:S(2)}) collective-permute-start(f32[8,128]{1,0:T(8,128)S(1)} %get-tuple-element.42), channel_id=1, source_target_pairs={{8,136},{9,137},{10,138},{11,139},{12,140},{13,141},{14,142},{15,1... | collective-permute-start | bytes 12296 | tf_op jit(solution)/shard_map/ppermute | solution.py:335
  143.6 4.1 %collective-permute-start.32 = (f32[8,128]{1,0:T(8,128)S(1)}, f32[8,128]{1,0:T(8,128)S(1)}, u32[]{:S(2)}, u32[]{:S(2)}) collective-permute-start(f32[8,128]{1,0:T(8,128)S(1)} %add_add_fusion.1), channel_id=1, source_target_pairs={{8,56},{9,57},{10,58},{11,59},{12,60},{13,61},{14,62},{15,63},{24,... | collective-permute-start | bytes 12296 | tf_op jit(solution)/shard_map/ppermute | solution.py:335
  144.3 5.5 %collective-permute-start.31 = (f32[8,128]{1,0:T(8,128)S(1)}, f32[8,128]{1,0:T(8,128)S(1)}, u32[]{:S(2)}, u32[]{:S(2)}) collective-permute-start(f32[8,128]{1,0:T(8,128)S(1)} %add_add_fusion.1), channel_id=1, source_target_pairs={{8,24},{9,25},{10,26},{11,27},{12,28},{13,29},{14,30},{15,31},{24,... | collective-permute-start | bytes 12296 | tf_op jit(solution)/shard_map/ppermute | solution.py:335
  147.0 2.8 %collective-permute-start.30 = (f32[8,128]{1,0:T(8,128)S(1)}, f32[8,128]{1,0:T(8,128)S(1)}, u32[]{:S(2)}, u32[]{:S(2)}) collective-permute-start(f32[8,128]{1,0:T(8,128)S(1)} %add_add_fusion.1), channel_id=1, source_target_pairs={{8,40},{9,41},{10,42},{11,43},{12,44},{13,45},{14,46},{15,47},{24,... | collective-permute-start | bytes 12296 | tf_op jit(solution)/shard_map/ppermute | solution.py:335
  (19 other events, 113.6 us)

commit v3 on v2

--- a/solution.py
+++ b/solution.py
@@ -34,6 +34,8 @@
 STEPS = SIDE // TILE
 DEEP = 8
 LINES = 4 * STEPS
+WIDTH = 1280
+WIDER = WIDTH + 128
 
 
 def shift(axis, by):
@@ -73,7 +75,7 @@
         kernel,
         out_shape=outputs,
         in_specs=specs,
-        out_specs=jax.tree.map(lambda s: WHOLE if s.memory_space == pltpu.VMEM else HBM, outputs),
+        out_specs=jax.tree.map(lambda s: {pltpu.VMEM: WHOLE, pltpu.SMEM: SCALAR}.get(s.memory_space, HBM), outputs),
         scratch_shapes=list(scratch),
         input_output_aliases=aliases,
         compiler_params=PARAMS,
@@ -142,15 +144,19 @@
         block = lax.rem(core + flip, 2) * DEEP + lax.rem(at_ref[3] + by + DEEP, DEEP)
         first = pl.multiple_of(block * PIECE + start, 32)
         copies.append(pltpu.make_async_copy(piece, image_ref.at[pl.ds(first, rows), :], sem.at[k]))
-    wait(run(copies))
-    out = run([pltpu.make_async_copy(image_ref, image_out, out_sem.at[0])])
+    run(copies)
+    near = len(plan) // 2
+    wait(copies[:near])
     text = text_ref[...]
     scale = scale_ref[0] * LOG2E
     top = jnp.full((1, SIDE), LOW, F32)
     sums = jnp.zeros((1, SIDE), F32)
     row_lse = []
     for k in range(STEPS):
-        tile = slice(k * TILE, (k + 1) * TILE)
+        if k == STEPS // 2:
+            wait(copies[near:])
+            out = run([pltpu.make_async_copy(image_ref, image_out, out_sem.at[0])])
+        tile = pl.ds(pl.multiple_of(lax.rem(core * 2 + k, STEPS) * TILE, TILE), TILE)
         logits = scale * lax.dot_general(
             image_ref[tile, :], text, (((1,), (1,)), ((), ())), preferred_element_type=F32
         )
@@ -165,6 +171,7 @@
     rows, cols, same = diagonal(at_ref)
     pairs = jnp.sum(jnp.where(same, logits_ref[rows, cols], 0.0), keepdims=True)
     first = core == 0
+    row_lse = [jnp.where(first, row_lse[k], row_lse[(k + 2) % STEPS]) for k in range(STEPS)]
     for k in range(STEPS):
         part = col_lse[:, k * TILE : (k + 1) * TILE]
         keep_ref[k : k + 1, :] = jnp.where(first, part, row_lse[k])
@@ -188,7 +195,7 @@
         out_ref[pl.ds(k * LINES, LINES), :] = block
 
 
-def join_kernel(at_ref, parts_ref, keep_ref, give_ref, loss_ref):
+def join_kernel(at_ref, parts_ref, keep_ref, give_ref):
     parts = parts_ref[...].reshape(PEERS, LINES, TILE)
     pairs = jnp.sum(parts[:, 2 * STEPS : 2 * STEPS + 1, :1], axis=0)
     parts = parts[:, : 2 * STEPS, :]
@@ -197,22 +204,41 @@
     parts = jnp.where(first | (half == at_ref[4]), parts, LOW)
     top = jnp.max(parts, axis=0)
     lse = top + jnp.log2(jnp.sum(jnp.exp2(parts - top[None]), axis=0))
-    keep_ref[...] = lse[:STEPS]
-    give_ref[...] = jnp.where(first, lse[STEPS:], lse[:STEPS])
-    low = jnp.sum(lse[:STEPS], keepdims=True)
-    high = jnp.sum(lse[STEPS:], keepdims=True)
-    loss_ref[...] = jnp.broadcast_to(jnp.where(first, low + high - 2.0 * pairs, low), loss_ref.shape)
+    columns = jnp.broadcast_to(jnp.sum(lse, keepdims=True) - 2.0 * pairs, (STEPS, TILE))
+    keep_ref[:STEPS, :] = lse[:STEPS]
+    keep_ref[STEPS:, :] = columns
+    give_ref[:STEPS, :] = jnp.where(first, lse[STEPS:], lse[:STEPS])
+    give_ref[STEPS:, :] = columns
+
+
+def tag(term):
+    term = jnp.broadcast_to(term, (PIECE, 128))
+    high = term.astype(BF16)
+    rest = term - high.astype(F32)
+    middle = rest.astype(BF16)
+    low = (rest - middle.astype(F32)).astype(BF16)
+    row = lax.broadcasted_iota(jnp.int32, (PIECE, 128), 0)
+    return jnp.where(
+        row < 16, high.astype(F32), jnp.where(row < 32, middle.astype(F32), low.astype(F32))
+    ).astype(BF16)
+
+
+def untag(block):
+    block = block.astype(F32)
+    return (block[0:1, :1] + block[16:17, :1]) + block[32:33, :1]
 
 
 def weights_kernel(
     at_ref, scale_ref, logits_ref, text_ref, keep_ref, recv_ref,
-    weights_ref, other_ref, mine_out, mine, sem,
+    weights_ref, other_ref, sums_ref, mine_out, mine, sem,
 ):
     first = at_ref[2] == 0
-    keep, recv = keep_ref[...], recv_ref[...]
+    keep, recv = keep_ref[:STEPS, :], recv_ref[:STEPS, :]
     cols = jnp.where(first, keep, recv)
     col_lse = jnp.concatenate([cols[k : k + 1] for k in range(STEPS)], axis=1)
     rows = jnp.where(first, recv, keep)
+    sums_ref[:STEPS, :] = jnp.broadcast_to(jnp.sum(rows, keepdims=True), (STEPS, 128))
+    sums_ref[STEPS:, :] = jnp.where(first, keep_ref[STEPS:, :128], recv_ref[STEPS:, :128])
     row_lse = [to_rows(rows[k : k + 1]) for k in range(STEPS)]
     for k in range(STEPS):
         tile = slice(k * TILE, (k + 1) * TILE)
@@ -252,29 +278,36 @@
     wait(copies)
 
 
-def back_tile(k, scale_ref, weights_ref, image, back, out_ref, sem):
+def back_tile(k, scale_ref, weights_ref, image, mark, back, out_ref, sem):
     tile = slice(k * TILE, (k + 1) * TILE)
-    back[tile, :] = (
+    back[tile, :WIDTH] = (
         scale_ref[0]
         * lax.dot_general(
             weights_ref[:, tile], image, (((0,), (0,)), ((), ())), preferred_element_type=F32
         )
     ).astype(BF16)
+    back[tile, WIDTH:] = jnp.concatenate([mark] * (TILE // PIECE), axis=0)
     return run([pltpu.make_async_copy(back.at[tile, :], out_ref.at[tile, :], sem.at[k])])
 
 
-def text_back_kernel(scale_ref, weights_ref, image_ref, out_ref, back, sem):
+def text_back_kernel(scale_ref, weights_ref, image_ref, sums_ref, out_ref, back, sem):
     image = image_ref[...]
+    mark = tag(sums_ref[:1, :1])
     copies = []
     for k in range(STEPS - 1):
-        copies += back_tile(k, scale_ref, weights_ref, image, back, out_ref, sem)
+        copies += back_tile(k, scale_ref, weights_ref, image, mark, back, out_ref, sem)
     wait(copies)
 
 
-def pieces_kernel(at_ref, scale_ref, weights_ref, image_ref, swapped_ref, mine_ref, begun_ref, *refs):
-    out_ref, own_ref, *out_refs, mine, back, sem = refs
-    loads = run([pltpu.make_async_copy(mine_ref, mine, sem.at[0])])
-    copies = back_tile(STEPS - 1, scale_ref, weights_ref, image_ref[...], back, out_ref, sem)
+def pieces_kernel(
+    at_ref, scale_ref, weights_ref, image_ref, sums_ref, swapped_ref, mine_ref, begun_ref, *refs
+):
+    out_ref, own_ref, *out_refs, mine, parts, back, mine_sem, sem, back_sem = refs
+    loads = run([pltpu.make_async_copy(mine_ref, mine, mine_sem.at[0])])
+    copies = back_tile(
+        STEPS - 1, scale_ref, weights_ref, image_ref[...], tag(sums_ref[:1, :1]), back, out_ref, back_sem
+    )
+    mark = tag(sums_ref[STEPS : STEPS + 1, :1])
     wait(loads)
     for k in range(DEEP):
         block = pl.ds(pl.multiple_of(lax.rem(at_ref[3] + k, DEEP) * PIECE, PIECE), PIECE)
@@ -282,7 +315,9 @@
         if k == 0:
             own_ref[...] = total
         else:
-            out_refs[k - 1][...] = total.astype(BF16)
+            parts[k - 1, :, :WIDTH] = total.astype(BF16)
+            parts[k - 1, :, WIDTH:] = mark
+            copies += run([pltpu.make_async_copy(parts.at[k - 1], out_refs[k - 1], sem.at[k - 1])])
     wait(copies)
 
 
@@ -292,22 +327,33 @@
     return ((back - direction * along) / norm).astype(BF16)
 
 
-def text_grad_kernel(raw_ref, parts_ref, out_ref, raw, grad, sem):
-    wait(run([pltpu.make_async_copy(raw_ref, raw, sem.at[0])]))
-    back = parts_ref[pl.ds(0, PIECE), :].astype(F32)
-    for k in range(1, PEERS):
-        back += parts_ref[pl.ds(k * PIECE, PIECE), :].astype(F32)
+def text_grad_kernel(raw_ref, loss_ref, parts_ref, out_ref, total_ref, raw, grad, sem):
+    copies = run([pltpu.make_async_copy(raw_ref, raw, sem.at[0])])
+    back = jnp.zeros((PIECE, WIDTH), F32)
+    total = loss_ref[:1, :1]
+    for k in range(PEERS):
+        block = pl.ds(k * PIECE, PIECE)
+        back += parts_ref[block, :WIDTH].astype(F32)
+        total += untag(parts_ref[block, WIDTH:])
+    total_ref[0] = (total * (LN2 / (2.0 * SIDE * PEERS)))[0, 0]
+    wait(copies)
     grad[...] = project(back, raw[...])
     wait(run([pltpu.make_async_copy(grad, out_ref, sem.at[0])]))
 
 
-def image_grad_kernel(raw_ref, own_ref, part_ref, *refs):
+def image_grad_kernel(raw_ref, own_ref, sums_ref, *refs):
     pieces, (out_ref, loss_ref, raw, grad, sem) = refs[:-5], refs[-5:]
-    loss_ref[...] = part_ref[...]
-    wait(run([pltpu.make_async_copy(raw_ref, raw, sem.at[0])]))
+    copies = run([pltpu.make_async_copy(raw_ref, raw, sem.at[0])])
     back = own_ref[...]
+    held = [sums_ref[STEPS : STEPS + 1, :1]]
     for ref in pieces:
-        back += ref[...].astype(F32)
+        back += ref[:, :WIDTH].astype(F32)
+        held.append(untag(ref[:, WIDTH:]))
+    while len(held) > 1:
+        half = len(held) // 2
+        held = [held[k] + held[k + half] for k in range(half)]
+    loss_ref[...] = jnp.broadcast_to(held[0], loss_ref.shape)
+    wait(copies)
     grad[...] = project(back, raw[...])
     wait(run([pltpu.make_async_copy(grad, out_ref, sem.at[0])]))
 
@@ -326,16 +372,6 @@
     return plan, arrays
 
 
-def sum_step(part, first, second):
-    held = []
-    for k in range(3):
-        pairs = [(a, b) for a, b in shift(second, k + 1) if a // 8 % 2 == 1]
-        if k < len(first):
-            pairs += [(a, b) for a, b in shift("z", first[k]) if a // 8 % 2 == 0]
-        held.append(lax.ppermute(part, "d", pairs))
-    return (part + held[1]) + (held[0] + held[2])
-
-
 def body(image_emb, text_emb, log_scale):
     width = image_emb.shape[1]
     scale = jnp.exp(log_scale)
@@ -360,24 +396,35 @@
         scratch=[pltpu.VMEM((SIDE, width), BF16), sems((len(plan),)), sems((1,))],
     )
     spread = call(spread_kernel, local((PEERS * LINES, TILE), F32), at, keep, send(give, "c", 1))
-    lines = local((STEPS, TILE), F32)
-    keep, give, part = call(join_kernel, [lines, lines, local((8, 128), F32)], at, exchange(spread, MIXED))
+    keep, give = call(join_kernel, [lines, lines], at, exchange(spread, MIXED))
     recv = send(give, "c", 1)
 
     half = pltpu.VMEM((SIDE // 2, width), F32)
-    weights, other, mine = call(
+    weights, other, sums, mine = call(
         weights_kernel,
-        [local((SIDE, SIDE), BF16), local((SIDE // 2, width), BF16), array((SIDE // 2, width), F32)],
+        [
+            local((SIDE, SIDE), BF16),
+            local((SIDE // 2, width), BF16),
+            local((2 * STEPS, 128), F32),
+            array((SIDE // 2, width), F32),
+        ],
         at, scale, logits, text, keep, recv,
         scratch=[half, sems((STEPS // 2,))],
     )
     swapped = send(other, "c", 1)
-    back = [pltpu.VMEM((SIDE, width), BF16), sems((STEPS,))]
-    text_parts = call(text_back_kernel, outside, scale, weights, image, scratch=back)
+    back = pltpu.VMEM((SIDE, WIDER), BF16)
+    wide = array((SIDE, WIDER), BF16)
+    text_parts = call(
+        text_back_kernel, wide, scale, weights, image, sums, scratch=[back, sems((STEPS,))]
+    )
     text_parts, own, *away = call(
-        pieces_kernel, [outside, local((PIECE, width), F32)] + [piece] * (DEEP - 1),
-        at, scale, weights, image, swapped, Outside(mine), Outside(text_parts),
-        scratch=[half, *back], aliases={6: 0},
+        pieces_kernel,
+        [wide, local((PIECE, width), F32)] + [array((PIECE, WIDER), BF16)] * (DEEP - 1),
+        at, scale, weights, image, sums, swapped, Outside(mine), Outside(text_parts),
+        scratch=[
+            half, pltpu.VMEM((DEEP - 1, PIECE, WIDER), BF16), back, sems((1,)), sems((DEEP - 1,)), sems((STEPS,))
+        ],
+        aliases={7: 0},
     )
     text_back = exchange(text_parts, XY)
     image_back = [send(a, "z", k + 1) for k, a in enumerate(away)]
@@ -385,11 +432,11 @@
     grad = array((PIECE, width), BF16)
     extra = [raw, raw, sems((1,))]
     grad_image, part = call(
-        image_grad_kernel, [grad, local((8, 128), F32)], Outside(image_emb), own, part, *image_back, scratch=extra
-    )
-    part = sum_step(sum_step(part, (2, 4, 6), "x"), (1,), "y")
-    loss = (part + send(part, "c", 1))[0, :1] * (LN2 / (2.0 * SIDE * PEERS))
-    grad_text = call(text_grad_kernel, grad, Outside(text_emb), text_back, scratch=extra)
+        image_grad_kernel, [grad, local((8, 128), F32)], Outside(image_emb), own, sums, *image_back, scratch=extra
+    )
+    grad_text, loss = call(
+        text_grad_kernel, [grad, pltpu.SMEM((1,), F32)], Outside(text_emb), part, text_back, scratch=extra
+    )
     return loss, grad_image, grad_text
 
 

time: 157 us -> 139 us (0.89)
  starting transfers between devices: 58.6 us -> 48.1 us
  waiting for transfers between devices: 49 us -> 44.3 us
  local copies, waits for them, and re-layouts: 3.29 us -> 0.14 us
    ppermute x6 -> x0, starting transfers between devices: 10.4 us -> none  [sum_step(): held.append(lax.ppermute(part, 'd', pairs))]
    ppermute x6 -> x0, waiting for transfers between devices: 6.24 us -> none  [sum_step(): held.append(lax.ppermute(part, 'd', pairs))]
    unnamed x30 -> x24, local copies, waits for them, and re-layouts: 2.68 us -> 0.05 us
    ppermute x28 -> x27, waiting for transfers between devices: 42.8 us -> 44.3 us  [send(): return lax.ppermute(x, 'd', shift(axis, by))]
    ppermute x28 -> x27, starting transfers between devices: 34.1 us -> 33.9 us  [send(): return lax.ppermute(x, 'd', shift(axis, by))]
  transfers between devices with their start and end apart: 36 -> 29, of which waited for: 20 -> 15; matrix products, arithmetic and copies ran while one was open for 0% -> 0% of each run, Pallas kernels for 4% -> 5%
where the time goes in v3:
time: 139 us; the launch traced here: 137 us
  starting transfers between devices  48.1 us (35%)
  waiting for transfers between devices  44.3 us (32%)
  Pallas kernels  30.4 us (22%)
  blocking collectives  12.2 us (9%)
  between operations  2.28 us (2%)
    ppermute x27, waiting for transfers between devices, send(): return lax.ppermute(x, 'd', shift(axis, by))  44.3 us
    ppermute x27, starting transfers between devices, send(): return lax.ppermute(x, 'd', shift(axis, by))  33.9 us
    pallas_call x10, Pallas kernels, call(): pl.pallas_call(kernel, out_shape=outputs, in_specs=specs, out_specs=jax.t...  30.4 us
    all_to_all x2, starting transfers between devices, exchange(): return lax.all_to_all(x, 'd', 0, 0, axis_index_groups=groups, tiled=True)  14.2 us
    all_to_all x1, blocking collectives, exchange(): return lax.all_to_all(x, 'd', 0, 0, axis_index_groups=groups, tiled=True)  12.2 us
  transfers between devices with their start and end apart: 29, of which 15 were waited for; matrix products, arithmetic and copies ran while one was open for 0% of the time, Pallas kernels for 5%

profile of v3, /device:TPU:28, one launch (start us, length us, event | category | flops | bytes accessed | tf_op | source)
XLA Modules:
  0.0 137.4 jit_solution(3146914598678876037)
XLA Ops:
  0.6 2.7 %shard_map.58 = bf16[1024,1280]{1,0:T(8,128)(2,1)} custom-call(bf16[64,1280]{1,0:T(8,128)(2,1)} %raw_ref.7), custom_call_target="tpu_custom_call" | custom-call | tf_op jit(solution)/shard_map/pallas_call | solution.py:74
  3.3 7.1 %all-to-all-start = ((bf16[16,64,1280]{2,1,0:T(8,128)(2,1)}), bf16[16,64,1280]{2,1,0:T(8,128)(2,1)S(1)}, u32[]{:S(2)}, u32[]{:S(2)}) async-start(bf16[16,64,1280]{2,1,0:T(8,128)(2,1)} %bitcast.17), calls=%async_computation | async-start | bytes 5242880 | tf_op jit(solution)/shard_map/all_to_all | solution.py:51
  10.5 1.7 %shard_map.59.refs_0_ = bf16[64,1280]{1,0:T(8,128)(2,1)} custom-call(bf16[64,1280]{1,0:T(8,128)(2,1)} %raw_ref.6), custom_call_target="tpu_custom_call" | custom-call | tf_op jit(solution)/shard_map/pallas_call | solution.py:74
  12.2 5.9 %collective-permute-start.1 = (bf16[64,1280]{1,0:T(8,128)(2,1)}, bf16[64,1280]{1,0:T(8,128)(2,1)S(1)}, u32[]{:S(2)}, u32[]{:S(2)}) collective-permute-start(bf16[64,1280]{1,0:T(8,128)(2,1)} %shard_map.59.refs_0_), channel_id=1, source_target_pairs={{0,7},{1,0},{2,1},{3,2},{4,3},{5,4},{6,5},{7,6},{8,15},{9,8},{10,9... | collective-permute-start | bytes 491528 | tf_op jit(solution)/shard_map/ppermute | solution.py:47
  18.1 3.2 %collective-permute-done.1.refs_2_ = bf16[64,1280]{1,0:T(8,128)(2,1)S(1)} collective-permute-done((bf16[64,1280]{1,0:T(8,128)(2,1)}, bf16[64,1280]{1,0:T(8,128)(2,1)S(1)}, u32[]{:S(2)}, u32[]{:S(2)}) %collective-permute-start.1) | collective-permute-done | bytes 163872 | tf_op jit(solution)/shard_map/ppermute | solution.py:47
  21.3 3.6 %collective-permute-start.3 = (bf16[64,1280]{1,0:T(8,128)(2,1)S(1)}, bf16[64,1280]{1,0:T(8,128)(2,1)S(1)}, u32[]{:S(2)}, u32[]{:S(2)}) collective-permute-start(bf16[64,1280]{1,0:T(8,128)(2,1)S(1)} %collective-permute-done.1.refs_2_), channel_id=1, source_target_pairs={{0,7},{1,0},{2,1},{3,2},{4,3},{5,4},{6,5},{7,6},{8,15},{9,8},{10,9... | collective-permute-start | bytes 491528 | tf_op jit(solution)/shard_map/ppermute | solution.py:47
  24.9 2.8 %collective-permute-done.3.refs_4_ = bf16[64,1280]{1,0:T(8,128)(2,1)S(1)} collective-permute-done((bf16[64,1280]{1,0:T(8,128)(2,1)S(1)}, bf16[64,1280]{1,0:T(8,128)(2,1)S(1)}, u32[]{:S(2)}, u32[]{:S(2)}) %collective-permute-start.3) | collective-permute-done | bytes 163872 | tf_op jit(solution)/shard_map/ppermute | solution.py:47
  27.8 3.7 %collective-permute-start.5 = (bf16[64,1280]{1,0:T(8,128)(2,1)S(1)}, bf16[64,1280]{1,0:T(8,128)(2,1)S(1)}, u32[]{:S(2)}, u32[]{:S(2)}) collective-permute-start(bf16[64,1280]{1,0:T(8,128)(2,1)S(1)} %collective-permute-done.3.refs_4_), channel_id=1, source_target_pairs={{0,7},{1,0},{2,1},{3,2},{4,3},{5,4},{6,5},{7,6},{8,15},{9,8},{10,9... | collective-permute-start | bytes 491528 | tf_op jit(solution)/shard_map/ppermute | solution.py:47
  32.1 2.2 %collective-permute-done.5.refs_6_ = bf16[64,1280]{1,0:T(8,128)(2,1)S(1)} collective-permute-done((bf16[64,1280]{1,0:T(8,128)(2,1)S(1)}, bf16[64,1280]{1,0:T(8,128)(2,1)S(1)}, u32[]{:S(2)}, u32[]{:S(2)}) %collective-permute-start.5) | collective-permute-done | bytes 163872 | tf_op jit(solution)/shard_map/ppermute | solution.py:47
  34.3 4.0 %collective-permute-done.4.refs_5_ = bf16[64,1280]{1,0:T(8,128)(2,1)S(1)} collective-permute-done((bf16[64,1280]{1,0:T(8,128)(2,1)}, bf16[64,1280]{1,0:T(8,128)(2,1)S(1)}, u32[]{:S(2)}, u32[]{:S(2)}) %collective-permute-start.4) | collective-permute-done | bytes 163872 | tf_op jit(solution)/shard_map/ppermute | solution.py:47
  38.7 1.7 %collective-permute-start.6 = (bf16[32,1280]{1,0:T(8,128)(2,1)S(1)}, bf16[32,1280]{1,0:T(8,128)(2,1)}, u32[]{:S(2)}, u32[]{:S(2)}) collective-permute-start(bf16[32,1280]{1,0:T(8,128)(2,1)S(1)} %slice.8), channel_id=1, source_target_pairs={{0,1},{1,2},{2,3},{3,4},{4,5},{5,6},{6,7},{7,0},{8,9},{9,10},{10,1... | collective-permute-start | bytes 245768 | tf_op jit(solution)/shard_map/ppermute | solution.py:47
  41.1 2.2 %collective-permute-done.7.refs_8_ = bf16[32,1280]{1,0:T(8,128)(2,1)S(1)} collective-permute-done((bf16[32,1280]{1,0:T(8,128)(2,1)S(1)}, bf16[32,1280]{1,0:T(8,128)(2,1)S(1)}, u32[]{:S(2)}, u32[]{:S(2)}) %collective-permute-start.7) | collective-permute-done | bytes 81952 | tf_op jit(solution)/shard_map/ppermute | solution.py:47
  43.3 1.4 %collective-permute-done.6.refs_7_ = bf16[32,1280]{1,0:T(8,128)(2,1)} collective-permute-done((bf16[32,1280]{1,0:T(8,128)(2,1)S(1)}, bf16[32,1280]{1,0:T(8,128)(2,1)}, u32[]{:S(2)}, u32[]{:S(2)}) %collective-permute-start.6) | collective-permute-done | bytes 81952 | tf_op jit(solution)/shard_map/ppermute | solution.py:47
  46.4 7.4 %shard_map.60 = (bf16[1024,1280]{1,0:T(8,128)(2,1)}, f32[1024,1024]{1,0:T(8,128)S(1)}, f32[8,256]{1,0:T(8,128)S(1)}, f32[8,256]{1,0:T(8,128)S(1)}) custom-call(s32[5]{0:T(128)S(1)} %stack.23.at_ref, f32[1]{0:T(128)S(6)} %exp.3.scale_ref, bf16[1024,1280]{1,0:T(8,128)(2,1)S(1)} %bitcast.11, bf16[64,1280]{1,0:T(8,128)(2,1)} %shard_map.59.refs_0_, ...), custom_call_target="tpu_custom_call" | custom-call | tf_op jit(solution)/shard_map/pallas_call | solution.py:74
  55.6 12.2 %all_to_all.33 = f32[16,16,256]{2,1,0:T(8,128)S(1)} all-to-all(f32[16,16,256]{2,1,0:T(8,128)S(1)} %bitcast.15), channel_id=1, replica_groups={{0,16,32,48,64,80,96,112,128,144,160,176,192,208,224,240},{1,17,33,49,6..., dimensions={0} | all-to-all | bytes 524288 | tf_op jit(solution)/shard_map/all_to_all | solution.py:51
  68.5 2.5 %collective-permute-start.18 = (f32[8,256]{1,0:T(8,128)S(1)}, f32[8,256]{1,0:T(8,128)S(1)}, u32[]{:S(2)}, u32[]{:S(2)}) collective-permute-start(f32[8,256]{1,0:T(8,128)S(1)} %get-tuple-element.30), channel_id=1, source_target_pairs={{0,8},{1,9},{2,10},{3,11},{4,12},{5,13},{6,14},{7,15},{8,0},{9,1},... | collective-permute-start | bytes 24584 | tf_op jit(solution)/shard_map/ppermute | solution.py:47
  71.8 5.9 %shard_map.63 = (bf16[1024,1024]{1,0:T(8,128)(2,1)S(1)}, bf16[512,1280]{1,0:T(8,128)(2,1)S(1)}, f32[8,128]{1,0:T(8,128)S(1)}, f32[512,1280]{1,0:T(8,128)}) custom-call(s32[5]{0:T(128)S(1)} %stack.23.at_ref, f32[1]{0:T(128)S(6)} %exp.3.scale_ref, f32[1024,1024]{1,0:T(8,128)S(1)} %get-tuple-element.26.logits_ref, bf16[1024,1280]{1,0:T(8,128)(2,1)S(1)} %bitcast.12, ...), custom_call_target="tpu_custom_call" | custom-call | tf_op jit(solution)/shard_map/pallas_call | solution.py:74
  78.1 3.2 %shard_map.64.begun_ref = bf16[1024,1408]{1,0:T(8,128)(2,1)} custom-call(f32[1]{0:T(128)S(6)} %exp.3.scale_ref, bf16[1024,1024]{1,0:T(8,128)(2,1)S(1)} %get-tuple-element.31.weights_ref, bf16[1024,1280]{1,0:T(8,128)(2,1)S(1)} %copy-done, f32[8,128]{1,0:T(8,128)S(1)} %get-tuple-element.33.sums_ref), custom_call_target="tpu_custom_call" | custom-call | tf_op jit(solution)/shard_map/pallas_call | solution.py:74
  81.4 4.5 %shard_map.65 = (bf16[1024,1408]{1,0:T(8,128)(2,1)}, f32[64,1280]{1,0:T(8,128)S(1)}, bf16[64,1408]{1,0:T(8,128)(2,1)}, bf16[64,1408]{1,0:T(8,128)(2,1)}, bf16[64...) custom-call(s32[5]{0:T(128)S(1)} %stack.23.at_ref, ...), custom_call_target="tpu_custom_call", output_to_operand_aliasing={{0}: (7, {})} | custom-call | tf_op jit(solution)/shard_map/pallas_call | solution.py:74
  85.9 7.1 %all-to-all-start.2 = ((bf16[16,64,1408]{2,1,0:T(8,128)(2,1)}), bf16[16,64,1408]{2,1,0:T(8,128)(2,1)S(1)}, u32[]{:S(2)}, u32[]{:S(2)}) async-start(bf16[16,64,1408]{2,1,0:T(8,128)(2,1)} %bitcast.16), calls=%async_computation.2 | async-start | bytes 5767168 | tf_op jit(solution)/shard_map/all_to_all | solution.py:51
  93.0 2.1 %collective-permute-start.20 = (bf16[64,1408]{1,0:T(8,128)(2,1)}, bf16[64,1408]{1,0:T(8,128)(2,1)S(1)}, u32[]{:S(2)}, u32[]{:S(2)}) collective-permute-start(bf16[64,1408]{1,0:T(8,128)(2,1)} %get-tuple-element.37), channel_id=1, source_target_pairs={{0,1},{1,2},{2,3},{3,4},{4,5},{5,6},{6,7},{7,0},{8,9},{9,10},{10,1... | collective-permute-start | bytes 540680 | tf_op jit(solution)/shard_map/ppermute | solution.py:47
  95.8 3.3 %collective-permute-start.22 = (bf16[64,1408]{1,0:T(8,128)(2,1)}, bf16[64,1408]{1,0:T(8,128)(2,1)S(1)}, u32[]{:S(2)}, u32[]{:S(2)}) collective-permute-start(bf16[64,1408]{1,0:T(8,128)(2,1)} %get-tuple-element.39), channel_id=1, source_target_pairs={{0,3},{1,4},{2,5},{3,6},{4,7},{5,0},{6,1},{7,2},{8,11},{9,12},{10,... | collective-permute-start | bytes 540680 | tf_op jit(solution)/shard_map/ppermute | solution.py:47
  99.2 2.1 %collective-permute-start.23 = (bf16[64,1408]{1,0:T(8,128)(2,1)}, bf16[64,1408]{1,0:T(8,128)(2,1)S(1)}, u32[]{:S(2)}, u32[]{:S(2)}) collective-permute-start(bf16[64,1408]{1,0:T(8,128)(2,1)} %get-tuple-element.40), channel_id=1, source_target_pairs={{0,4},{1,5},{2,6},{3,7},{4,0},{5,1},{6,2},{7,3},{8,12},{9,13},{10,... | collective-permute-start | bytes 540680 | tf_op jit(solution)/shard_map/ppermute | solution.py:47
  101.2 3.2 %collective-permute-start.24 = (bf16[64,1408]{1,0:T(8,128)(2,1)}, bf16[64,1408]{1,0:T(8,128)(2,1)S(1)}, u32[]{:S(2)}, u32[]{:S(2)}) collective-permute-start(bf16[64,1408]{1,0:T(8,128)(2,1)} %get-tuple-element.41), channel_id=1, source_target_pairs={{0,5},{1,6},{2,7},{3,0},{4,1},{5,2},{6,3},{7,4},{8,13},{9,14},{10,... | collective-permute-start | bytes 540680 | tf_op jit(solution)/shard_map/ppermute | solution.py:47
  104.5 2.9 %collective-permute-start.25 = (bf16[64,1408]{1,0:T(8,128)(2,1)}, bf16[64,1408]{1,0:T(8,128)(2,1)S(1)}, u32[]{:S(2)}, u32[]{:S(2)}) collective-permute-start(bf16[64,1408]{1,0:T(8,128)(2,1)} %get-tuple-element.42), channel_id=1, source_target_pairs={{0,6},{1,7},{2,0},{3,1},{4,2},{5,3},{6,4},{7,5},{8,14},{9,15},{10,... | collective-permute-start | bytes 540680 | tf_op jit(solution)/shard_map/ppermute | solution.py:47
  107.3 9.6 %collective-permute-done.21.refs_1_ = bf16[64,1408]{1,0:T(8,128)(2,1)S(1)} collective-permute-done((bf16[64,1408]{1,0:T(8,128)(2,1)}, bf16[64,1408]{1,0:T(8,128)(2,1)S(1)}, u32[]{:S(2)}, u32[]{:S(2)}) %collective-permute-start.21) | collective-permute-done | bytes 180256 | tf_op jit(solution)/shard_map/ppermute | solution.py:47
  116.9 2.4 %collective-permute-done.22.refs_2_ = bf16[64,1408]{1,0:T(8,128)(2,1)S(1)} collective-permute-done((bf16[64,1408]{1,0:T(8,128)(2,1)}, bf16[64,1408]{1,0:T(8,128)(2,1)S(1)}, u32[]{:S(2)}, u32[]{:S(2)}) %collective-permute-start.22) | collective-permute-done | bytes 180256 | tf_op jit(solution)/shard_map/ppermute | solution.py:47
  119.4 5.6 %collective-permute-done.23.refs_3_ = bf16[64,1408]{1,0:T(8,128)(2,1)S(1)} collective-permute-done((bf16[64,1408]{1,0:T(8,128)(2,1)}, bf16[64,1408]{1,0:T(8,128)(2,1)S(1)}, u32[]{:S(2)}, u32[]{:S(2)}) %collective-permute-start.23) | collective-permute-done | bytes 180256 | tf_op jit(solution)/shard_map/ppermute | solution.py:47
  125.0 6.6 %collective-permute-done.25.refs_5_ = bf16[64,1408]{1,0:T(8,128)(2,1)S(1)} collective-permute-done((bf16[64,1408]{1,0:T(8,128)(2,1)}, bf16[64,1408]{1,0:T(8,128)(2,1)S(1)}, u32[]{:S(2)}, u32[]{:S(2)}) %collective-permute-start.25) | collective-permute-done | bytes 180256 | tf_op jit(solution)/shard_map/ppermute | solution.py:47
  131.6 1.5 %collective-permute-done.26.refs_6_ = bf16[64,1408]{1,0:T(8,128)(2,1)S(1)} collective-permute-done((bf16[64,1408]{1,0:T(8,128)(2,1)S(1)}, bf16[64,1408]{1,0:T(8,128)(2,1)S(1)}, u32[]{:S(2)}, u32[]{:S(2)}) %collective-permute-start.26) | collective-permute-done | bytes 180256 | tf_op jit(solution)/shard_map/ppermute | solution.py:47
  133.1 1.8 %shard_map.66 = (bf16[64,1280]{1,0:T(8,128)(2,1)}, f32[8,128]{1,0:T(8,128)S(1)}) custom-call(bf16[64,1280]{1,0:T(8,128)(2,1)} %raw_ref.6, f32[64,1280]{1,0:T(8,128)S(1)} %get-tuple-element.36.own_ref, f32[8,128]{1,0:T(8,128)S(1)} %get-tuple-element.33.sums_ref, bf16[64,1408]{1,0:T(8,128)(2,1)S(1)} %collective-permute-done.20.refs_0_, ...), custom_call_target="tpu_custom_call" | custom-call | tf_op jit(solution)/shard_map/pallas_call | solution.py:74
  134.9 1.8 %shard_map.67 = (bf16[64,1280]{1,0:T(8,128)(2,1)}, f32[1]{0:T(128)S(4)}) custom-call(bf16[64,1280]{1,0:T(8,128)(2,1)} %raw_ref.7, f32[8,128]{1,0:T(8,128)S(1)} %get-tuple-element.44.loss_ref, bf16[1024,1408]{1,0:T(8,128)(2,1)S(1)} %bitcast.13), custom_call_target="tpu_custom_call" | custom-call | tf_op jit(solution)/shard_map/pallas_call | solution.py:74
  (64 shorter events, 7.2 us)
Async XLA Ops:
  3.3 43.0 %all-to-all-start = ((bf16[16,64,1280]{2,1,0:T(8,128)(2,1)}), bf16[16,64,1280]{2,1,0:T(8,128)(2,1)S(1)}, u32[]{:S(2)}, u32[]{:S(2)}) async-start(bf16[16,64,1280]{2,1,0:T(8,128)(2,1)} %bitcast.17), calls=%async_computation | async-start | bytes 5242880 | tf_op jit(solution)/shard_map/all_to_all | solution.py:51
  12.2 9.1 %collective-permute-start.1 = (bf16[64,1280]{1,0:T(8,128)(2,1)}, bf16[64,1280]{1,0:T(8,128)(2,1)S(1)}, u32[]{:S(2)}, u32[]{:S(2)}) collective-permute-start(bf16[64,1280]{1,0:T(8,128)(2,1)} %shard_map.59.refs_0_), channel_id=1, source_target_pairs={{0,7},{1,0},{2,1},{3,2},{4,3},{5,4},{6,5},{7,6},{8,15},{9,8},{10,9... | collective-permute-start | bytes 491528 | tf_op jit(solution)/shard_map/ppermute | solution.py:47
  18.1 6.8 %collective-permute-start = (bf16[64,1280]{1,0:T(8,128)(2,1)}, bf16[64,1280]{1,0:T(8,128)(2,1)S(1)}, u32[]{:S(2)}, u32[]{:S(2)}) collective-permute-start(bf16[64,1280]{1,0:T(8,128)(2,1)} %shard_map.59.refs_0_), channel_id=1, source_target_pairs={{0,1},{1,2},{2,3},{3,4},{4,5},{5,6},{6,7},{7,0},{8,9},{9,10},{10,1... | collective-permute-start | bytes 491528 | tf_op jit(solution)/shard_map/ppermute | solution.py:47
  21.3 25.0 %copy-start.3 = (bf16[64,1280]{1,0:T(8,128)(2,1)}, bf16[64,1280]{1,0:T(8,128)(2,1)S(1)}, u32[]{:S(2)}) copy-start(bf16[64,1280]{1,0:T(8,128)(2,1)S(1)} %collective-permute-done.1.refs_2_) | copy-start | bytes 491524
  21.3 6.4 %collective-permute-start.3 = (bf16[64,1280]{1,0:T(8,128)(2,1)S(1)}, bf16[64,1280]{1,0:T(8,128)(2,1)S(1)}, u32[]{:S(2)}, u32[]{:S(2)}) collective-permute-start(bf16[64,1280]{1,0:T(8,128)(2,1)S(1)} %collective-permute-done.1.refs_2_), channel_id=1, source_target_pairs={{0,7},{1,0},{2,1},{3,2},{4,3},{5,4},{6,5},{7,6},{8,15},{9,8},{10,9... | collective-permute-start | bytes 491528 | tf_op jit(solution)/shard_map/ppermute | solution.py:47
  24.9 21.4 %copy-start.4 = (bf16[64,1280]{1,0:T(8,128)(2,1)}, bf16[64,1280]{1,0:T(8,128)(2,1)S(1)}, u32[]{:S(2)}) copy-start(bf16[64,1280]{1,0:T(8,128)(2,1)S(1)} %collective-permute-done.refs_1_) | copy-start | bytes 491524
  24.9 6.6 %collective-permute-start.2 = (bf16[64,1280]{1,0:T(8,128)(2,1)S(1)}, bf16[64,1280]{1,0:T(8,128)(2,1)}, u32[]{:S(2)}, u32[]{:S(2)}) collective-permute-start(bf16[64,1280]{1,0:T(8,128)(2,1)S(1)} %collective-permute-done.refs_1_), channel_id=1, source_target_pairs={{0,1},{1,2},{2,3},{3,4},{4,5},{5,6},{6,7},{7,0},{8,9},{9,10},{10,1... | collective-permute-start | bytes 491528 | tf_op jit(solution)/shard_map/ppermute | solution.py:47
  27.8 6.5 %collective-permute-start.5 = (bf16[64,1280]{1,0:T(8,128)(2,1)S(1)}, bf16[64,1280]{1,0:T(8,128)(2,1)S(1)}, u32[]{:S(2)}, u32[]{:S(2)}) collective-permute-start(bf16[64,1280]{1,0:T(8,128)(2,1)S(1)} %collective-permute-done.3.refs_4_), channel_id=1, source_target_pairs={{0,7},{1,0},{2,1},{3,2},{4,3},{5,4},{6,5},{7,6},{8,15},{9,8},{10,9... | collective-permute-start | bytes 491528 | tf_op jit(solution)/shard_map/ppermute | solution.py:47
  31.6 6.7 %collective-permute-start.4 = (bf16[64,1280]{1,0:T(8,128)(2,1)}, bf16[64,1280]{1,0:T(8,128)(2,1)S(1)}, u32[]{:S(2)}, u32[]{:S(2)}) collective-permute-start(bf16[64,1280]{1,0:T(8,128)(2,1)} %collective-permute-done.2.refs_3_), channel_id=1, source_target_pairs={{0,1},{1,2},{2,3},{3,4},{4,5},{5,6},{6,7},{7,0},{8,9},{9,10},{10,1... | collective-permute-start | bytes 491528 | tf_op jit(solution)/shard_map/ppermute | solution.py:47
  31.6 6.8 %collective-permute-start.8 = (bf16[64,1280]{1,0:T(8,128)(2,1)}, bf16[64,1280]{1,0:T(8,128)(2,1)S(1)}, u32[]{:S(2)}, u32[]{:S(2)}) collective-permute-start(bf16[64,1280]{1,0:T(8,128)(2,1)} %shard_map.59.refs_0_), channel_id=1, source_target_pairs={{0,8},{1,9},{2,10},{3,11},{4,12},{5,13},{6,14},{7,15},{8,0},{9,1},... | collective-permute-start | bytes 491528 | tf_op jit(solution)/shard_map/ppermute | solution.py:47
  31.6 7.1 %collective-permute-start.10 = (bf16[64,1280]{1,0:T(8,128)(2,1)S(1)}, bf16[64,1280]{1,0:T(8,128)(2,1)S(1)}, u32[]{:S(2)}, u32[]{:S(2)}) collective-permute-start(bf16[64,1280]{1,0:T(8,128)(2,1)S(1)} %collective-permute-done.1.refs_2_), channel_id=1, source_target_pairs={{0,8},{1,9},{2,10},{3,11},{4,12},{5,13},{6,14},{7,15},{8,0},{9,1},... | collective-permute-start | bytes 491528 | tf_op jit(solution)/shard_map/ppermute | solution.py:47
  32.1 8.4 %collective-permute-start.9 = (bf16[64,1280]{1,0:T(8,128)(2,1)S(1)}, bf16[64,1280]{1,0:T(8,128)(2,1)S(1)}, u32[]{:S(2)}, u32[]{:S(2)}) collective-permute-start(bf16[64,1280]{1,0:T(8,128)(2,1)S(1)} %collective-permute-done.refs_1_), channel_id=1, source_target_pairs={{0,8},{1,9},{2,10},{3,11},{4,12},{5,13},{6,14},{7,15},{8,0},{9,1},... | collective-permute-start | bytes 491528 | tf_op jit(solution)/shard_map/ppermute | solution.py:47
  34.3 6.2 %collective-permute-start.12 = (bf16[64,1280]{1,0:T(8,128)(2,1)S(1)}, bf16[64,1280]{1,0:T(8,128)(2,1)S(1)}, u32[]{:S(2)}, u32[]{:S(2)}) collective-permute-start(bf16[64,1280]{1,0:T(8,128)(2,1)S(1)} %collective-permute-done.3.refs_4_), channel_id=1, source_target_pairs={{0,8},{1,9},{2,10},{3,11},{4,12},{5,13},{6,14},{7,15},{8,0},{9,1},... | collective-permute-start | bytes 491528 | tf_op jit(solution)/shard_map/ppermute | solution.py:47
  38.3 7.2 %collective-permute-start.11 = (bf16[64,1280]{1,0:T(8,128)(2,1)}, bf16[64,1280]{1,0:T(8,128)(2,1)}, u32[]{:S(2)}, u32[]{:S(2)}) collective-permute-start(bf16[64,1280]{1,0:T(8,128)(2,1)} %collective-permute-done.2.refs_3_), channel_id=1, source_target_pairs={{0,8},{1,9},{2,10},{3,11},{4,12},{5,13},{6,14},{7,15},{8,0},{9,1},... | collective-permute-start | bytes 491528 | tf_op jit(solution)/shard_map/ppermute | solution.py:47
  38.3 4.9 %collective-permute-start.7 = (bf16[32,1280]{1,0:T(8,128)(2,1)S(1)}, bf16[32,1280]{1,0:T(8,128)(2,1)S(1)}, u32[]{:S(2)}, u32[]{:S(2)}) collective-permute-start(bf16[32,1280]{1,0:T(8,128)(2,1)S(1)} %slice.9), channel_id=1, source_target_pairs={{0,7},{1,0},{2,1},{3,2},{4,3},{5,4},{6,5},{7,6},{8,15},{9,8},{10,9... | collective-permute-start | bytes 245768 | tf_op jit(solution)/shard_map/ppermute | solution.py:47
  38.7 6.0 %collective-permute-start.6 = (bf16[32,1280]{1,0:T(8,128)(2,1)S(1)}, bf16[32,1280]{1,0:T(8,128)(2,1)}, u32[]{:S(2)}, u32[]{:S(2)}) collective-permute-start(bf16[32,1280]{1,0:T(8,128)(2,1)S(1)} %slice.8), channel_id=1, source_target_pairs={{0,1},{1,2},{2,3},{3,4},{4,5},{5,6},{6,7},{7,0},{8,9},{9,10},{10,1... | collective-permute-start | bytes 245768 | tf_op jit(solution)/shard_map/ppermute | solution.py:47
  40.4 5.0 %collective-permute-start.14 = (bf16[64,1280]{1,0:T(8,128)(2,1)S(1)}, bf16[64,1280]{1,0:T(8,128)(2,1)}, u32[]{:S(2)}, u32[]{:S(2)}) collective-permute-start(bf16[64,1280]{1,0:T(8,128)(2,1)S(1)} %collective-permute-done.5.refs_6_), channel_id=1, source_target_pairs={{0,8},{1,9},{2,10},{3,11},{4,12},{5,13},{6,14},{7,15},{8,0},{9,1},... | collective-permute-start | bytes 491528 | tf_op jit(solution)/shard_map/ppermute | solution.py:47
  40.5 5.8 %collective-permute-start.13 = (bf16[64,1280]{1,0:T(8,128)(2,1)S(1)}, bf16[64,1280]{1,0:T(8,128)(2,1)}, u32[]{:S(2)}, u32[]{:S(2)}) collective-permute-start(bf16[64,1280]{1,0:T(8,128)(2,1)S(1)} %collective-permute-done.4.refs_5_), channel_id=1, source_target_pairs={{0,8},{1,9},{2,10},{3,11},{4,12},{5,13},{6,14},{7,15},{8,0},{9,1},... | collective-permute-start | bytes 491528 | tf_op jit(solution)/shard_map/ppermute | solution.py:47
  43.3 2.2 %collective-permute-start.16 = (bf16[32,1280]{1,0:T(8,128)(2,1)S(1)}, bf16[32,1280]{1,0:T(8,128)(2,1)}, u32[]{:S(2)}, u32[]{:S(2)}) collective-permute-start(bf16[32,1280]{1,0:T(8,128)(2,1)S(1)} %collective-permute-done.7.refs_8_), channel_id=1, source_target_pairs={{0,8},{1,9},{2,10},{3,11},{4,12},{5,13},{6,14},{7,15},{8,0},{9,1},... | collective-permute-start | bytes 245768 | tf_op jit(solution)/shard_map/ppermute | solution.py:47
  44.7 1.6 %collective-permute-start.15 = (bf16[32,1280]{1,0:T(8,128)(2,1)}, bf16[32,1280]{1,0:T(8,128)(2,1)}, u32[]{:S(2)}, u32[]{:S(2)}) collective-permute-start(bf16[32,1280]{1,0:T(8,128)(2,1)} %collective-permute-done.6.refs_7_), channel_id=1, source_target_pairs={{0,8},{1,9},{2,10},{3,11},{4,12},{5,13},{6,14},{7,15},{8,0},{9,1},... | collective-permute-start | bytes 245768 | tf_op jit(solution)/shard_map/ppermute | solution.py:47
  53.8 1.3 collective-permute-start.17
  68.5 3.3 %collective-permute-start.18 = (f32[8,256]{1,0:T(8,128)S(1)}, f32[8,256]{1,0:T(8,128)S(1)}, u32[]{:S(2)}, u32[]{:S(2)}) collective-permute-start(f32[8,256]{1,0:T(8,128)S(1)} %get-tuple-element.30), channel_id=1, source_target_pairs={{0,8},{1,9},{2,10},{3,11},{4,12},{5,13},{6,14},{7,15},{8,0},{9,1},... | collective-permute-start | bytes 24584 | tf_op jit(solution)/shard_map/ppermute | solution.py:47
  77.7 3.7 %collective-permute-start.19 = (bf16[512,1280]{1,0:T(8,128)(2,1)S(1)}, bf16[512,1280]{1,0:T(8,128)(2,1)S(1)}, u32[]{:S(2)}, u32[]{:S(2)}) collective-permute-start(bf16[512,1280]{1,0:T(8,128)(2,1)S(1)} %get-tuple-element.34), channel_id=1, source_target_pairs={{0,8},{1,9},{2,10},{3,11},{4,12},{5,13},{6,14},{7,15},{8,0},{9,1},... | collective-permute-start | bytes 3932168 | tf_op jit(solution)/shard_map/ppermute | solution.py:47
  85.9 31.0 %copy-start.11 = (bf16[64,1408]{1,0:T(8,128)(2,1)S(1)}, bf16[64,1408]{1,0:T(8,128)(2,1)}, u32[]{:S(2)}) copy-start(bf16[64,1408]{1,0:T(8,128)(2,1)} %get-tuple-element.43) | copy-start | bytes 540676
  85.9 49.0 %all-to-all-start.2 = ((bf16[16,64,1408]{2,1,0:T(8,128)(2,1)}), bf16[16,64,1408]{2,1,0:T(8,128)(2,1)S(1)}, u32[]{:S(2)}, u32[]{:S(2)}) async-start(bf16[16,64,1408]{2,1,0:T(8,128)(2,1)} %bitcast.16), calls=%async_computation.2 | async-start | bytes 5767168 | tf_op jit(solution)/shard_map/all_to_all | solution.py:51
  93.0 11.5 %collective-permute-start.20 = (bf16[64,1408]{1,0:T(8,128)(2,1)}, bf16[64,1408]{1,0:T(8,128)(2,1)S(1)}, u32[]{:S(2)}, u32[]{:S(2)}) collective-permute-start(bf16[64,1408]{1,0:T(8,128)(2,1)} %get-tuple-element.37), channel_id=1, source_target_pairs={{0,1},{1,2},{2,3},{3,4},{4,5},{5,6},{6,7},{7,0},{8,9},{9,10},{10,1... | collective-permute-start | bytes 540680 | tf_op jit(solution)/shard_map/ppermute | solution.py:47
  95.0 21.9 %collective-permute-start.21 = (bf16[64,1408]{1,0:T(8,128)(2,1)}, bf16[64,1408]{1,0:T(8,128)(2,1)S(1)}, u32[]{:S(2)}, u32[]{:S(2)}) collective-permute-start(bf16[64,1408]{1,0:T(8,128)(2,1)} %get-tuple-element.38), channel_id=1, source_target_pairs={{0,2},{1,3},{2,4},{3,5},{4,6},{5,7},{6,0},{7,1},{8,10},{9,11},{10,... | collective-permute-start | bytes 540680 | tf_op jit(solution)/shard_map/ppermute | solution.py:47
  95.8 23.5 %collective-permute-start.22 = (bf16[64,1408]{1,0:T(8,128)(2,1)}, bf16[64,1408]{1,0:T(8,128)(2,1)S(1)}, u32[]{:S(2)}, u32[]{:S(2)}) collective-permute-start(bf16[64,1408]{1,0:T(8,128)(2,1)} %get-tuple-element.39), channel_id=1, source_target_pairs={{0,3},{1,4},{2,5},{3,6},{4,7},{5,0},{6,1},{7,2},{8,11},{9,12},{10,... | collective-permute-start | bytes 540680 | tf_op jit(solution)/shard_map/ppermute | solution.py:47
  99.2 25.8 %collective-permute-start.23 = (bf16[64,1408]{1,0:T(8,128)(2,1)}, bf16[64,1408]{1,0:T(8,128)(2,1)S(1)}, u32[]{:S(2)}, u32[]{:S(2)}) collective-permute-start(bf16[64,1408]{1,0:T(8,128)(2,1)} %get-tuple-element.40), channel_id=1, source_target_pairs={{0,4},{1,5},{2,6},{3,7},{4,0},{5,1},{6,2},{7,3},{8,12},{9,13},{10,... | collective-permute-start | bytes 540680 | tf_op jit(solution)/shard_map/ppermute | solution.py:47
  101.2 23.7 %collective-permute-start.24 = (bf16[64,1408]{1,0:T(8,128)(2,1)}, bf16[64,1408]{1,0:T(8,128)(2,1)S(1)}, u32[]{:S(2)}, u32[]{:S(2)}) collective-permute-start(bf16[64,1408]{1,0:T(8,128)(2,1)} %get-tuple-element.41), channel_id=1, source_target_pairs={{0,5},{1,6},{2,7},{3,0},{4,1},{5,2},{6,3},{7,4},{8,13},{9,14},{10,... | collective-permute-start | bytes 540680 | tf_op jit(solution)/shard_map/ppermute | solution.py:47
  104.5 27.1 %collective-permute-start.25 = (bf16[64,1408]{1,0:T(8,128)(2,1)}, bf16[64,1408]{1,0:T(8,128)(2,1)S(1)}, u32[]{:S(2)}, u32[]{:S(2)}) collective-permute-start(bf16[64,1408]{1,0:T(8,128)(2,1)} %get-tuple-element.42), channel_id=1, source_target_pairs={{0,6},{1,7},{2,0},{3,1},{4,2},{5,3},{6,4},{7,5},{8,14},{9,15},{10,... | collective-permute-start | bytes 540680 | tf_op jit(solution)/shard_map/ppermute | solution.py:47
  116.9 16.2 %collective-permute-start.26 = (bf16[64,1408]{1,0:T(8,128)(2,1)S(1)}, bf16[64,1408]{1,0:T(8,128)(2,1)S(1)}, u32[]{:S(2)}, u32[]{:S(2)}) collective-permute-start(bf16[64,1408]{1,0:T(8,128)(2,1)S(1)} %copy-done.11), channel_id=1, source_target_pairs={{0,7},{1,0},{2,1},{3,2},{4,3},{5,4},{6,5},{7,6},{8,15},{9,8},{10,9... | collective-permute-start | bytes 540680 | tf_op jit(solution)/shard_map/ppermute | solution.py:47
  (9 other events, 58.2 us)

commit v4 on v3

v4 whole, which is shorter than its diff:
```python
import functools
import math
import typing

import jax
import jax.numpy as jnp
import numpy as np
from jax import lax
from jax.experimental import pallas as pl
from jax.experimental.pallas import tpu as pltpu
from jax.sharding import Mesh, PartitionSpec as P

LOG2E = math.log2(math.e)
LN2 = math.log(2.0)
EPS = 1e-06
LOW = -1e30
PARAMS = pltpu.CompilerParams(vmem_limit_bytes=24 * 1024 * 1024)
HBM = pl.BlockSpec(memory_space=pl.ANY)
WHOLE = pl.BlockSpec(memory_space=pltpu.VMEM)
SCALAR = pl.BlockSpec(memory_space=pltpu.SMEM)
F32 = jnp.float32
BF16 = jnp.bfloat16

INDEX = np.arange(256).reshape(4, 4, 2, 8)
AXES = {"x": 0, "y": 1, "c": 2, "z": 3}
XY = INDEX.transpose(2, 3, 0, 1).reshape(16, 16).tolist()
MIXED = INDEX[:, :, 0, :].transpose(2, 0, 1).reshape(8, 16).tolist() + (
    INDEX[:, :, 1, :].reshape(2, 2, 4, 8).transpose(0, 2, 1, 3).reshape(8, 16).tolist()
)
PEERS = 16
PIECE = 64
SIDE = PEERS * PIECE
TILE = 256
STEPS = SIDE // TILE
DEEP = 8
LINES = 4 * STEPS
WIDTH = 1280
WIDER = WIDTH + 128
MARK = 16
PART = PIECE * (WIDTH // 128) + MARK


def shift(axis, by):
    to = np.roll(INDEX, -by, AXES[axis])
    return [(int(a), int(b)) for a, b in zip(INDEX.ravel(), to.ravel())]


def send(x, axis, by):
    return lax.ppermute(x, "d", shift(axis, by))


def exchange(x, groups):
    return lax.all_to_all(x, "d", 0, 0, axis_index_groups=groups, tiled=True)


def array(shape, dtype):
    return pltpu.HBM(shape, dtype)


def local(shape, dtype):
    return pltpu.VMEM(shape, dtype)


def call(kernel, outputs, *operands, scratch=(), aliases={}):
    specs, arrays = [], []
    for x in operands:
        if isinstance(x, Outside):
            specs.append(HBM)
            arrays.append(pltpu.with_memory_space_constraint(x.array, pltpu.HBM))
        elif x.size <= 8:
            specs.append(SCALAR)
            arrays.append(x)
        else:
            specs.append(WHOLE)
            arrays.append(pltpu.with_memory_space_constraint(x, pltpu.VMEM))
    return pl.pallas_call(
        kernel,
        out_shape=outputs,
        in_specs=specs,
        out_specs=jax.tree.map(lambda s: {pltpu.VMEM: WHOLE, pltpu.SMEM: SCALAR}.get(s.memory_space, HBM), outputs),
        scratch_shapes=list(scratch),
        input_output_aliases=aliases,
        compiler_params=PARAMS,
    )(*arrays)


class Outside(typing.NamedTuple):
    array: typing.Any


def run(copies):
    for copy in copies:
        copy.start()
    return copies


def wait(copies):
    for copy in copies:
        copy.wait()


def unit_rows(raw):
    values = raw.astype(F32)
    norm = jnp.sqrt(jnp.sum(values * values, axis=1, keepdims=True) + EPS)
    return values / norm, norm


def image_unit_kernel(scale_ref, raw_ref, text_ref, out_ref, pairs_ref, raw, text, unit, sem):
    copies = run([
        pltpu.make_async_copy(raw_ref, raw, sem.at[0]), pltpu.make_async_copy(text_ref, text, sem.at[1])
    ])
    copies[0].wait()
    unit[...] = unit_rows(raw[...])[0].astype(BF16)
    out = run([pltpu.make_async_copy(unit, out_ref, sem.at[2])])
    copies[1].wait()
    other = unit_rows(text[...])[0].astype(BF16)
    total = jnp.sum(unit[...].astype(F32) * other.astype(F32), keepdims=True)
    pairs_ref[...] = jnp.broadcast_to(total * (scale_ref[0] * LOG2E), pairs_ref.shape)
    wait(out)


def text_units_kernel(raw_ref, out_ref, raw, unit, sem):
    wait(run([pltpu.make_async_copy(raw_ref, raw, sem.at[0])]))
    unit[...] = unit_rows(raw[...])[0].astype(BF16)
    wait(run([
        pltpu.make_async_copy(unit, out_ref.at[pl.ds(k * PIECE, PIECE), :], sem.at[k])
        for k in range(PEERS)
    ]))


def to_lanes(column):
    return jnp.broadcast_to(column, (column.shape[0], 128)).T[:1, :]


def to_rows(lanes):
    return jnp.broadcast_to(lanes, (128, lanes.shape[1])).T[:, :1]


def logits_kernel(plan, at_ref, scale_ref, text_ref, *refs):
    pieces = refs[: len(plan)]
    image_out, logits_ref, keep_ref, give_ref, image_ref, sem, out_sem = refs[len(plan) :]
    core = at_ref[2]
    copies = []
    for k, (piece, (flip, by, start, rows)) in enumerate(zip(pieces, plan)):
        block = lax.rem(at_ref[3] + by + DEEP, DEEP)
        first = pl.multiple_of(flip * (SIDE // 2) + block * PIECE + start, 32)
        copies.append(pltpu.make_async_copy(piece, image_ref.at[pl.ds(first, rows), :], sem.at[k]))
    near = len(plan) // 2
    halves = [pl.ds(k * (SIDE // 2), SIDE // 2) for k in range(2)]
    out = [pltpu.make_async_copy(image_ref.at[h, :], image_out.at[h, :], out_sem.at[k]) for k, h in enumerate(halves)]
    wait(run(copies[:near]))
    run(copies[near:] + out[:1])
    text = text_ref[...]
    scale = scale_ref[0] * LOG2E
    top = jnp.full((1, SIDE), LOW, F32)
    sums = jnp.zeros((1, SIDE), F32)
    row_lse = []
    for k in range(STEPS):
        if k == STEPS // 2:
            wait(copies[near:])
            run(out[1:])
        tile = slice(k * TILE, (k + 1) * TILE)
        logits = scale * lax.dot_general(
            image_ref[tile, :], text, (((1,), (1,)), ((), ())), preferred_element_type=F32
        )
        logits_ref[tile, :] = logits
        row_top = jnp.max(logits, axis=1, keepdims=True)
        row_sum = jnp.sum(jnp.exp2(logits - row_top), axis=1, keepdims=True)
        row_lse.append(to_lanes(row_top + jnp.log2(row_sum)))
        new = jnp.maximum(top, jnp.max(logits, axis=0, keepdims=True))
        sums = sums * jnp.exp2(top - new) + jnp.sum(jnp.exp2(logits - new), axis=0, keepdims=True)
        top = new
    col_lse = top + jnp.log2(sums)
    first = core == 0
    for k in range(STEPS):
        part = col_lse[:, k * TILE : (k + 1) * TILE]
        keep_ref[k : k + 1, :] = jnp.where(first, part, row_lse[k])
        give_ref[k : k + 1, :] = jnp.where(first, row_lse[(k + STEPS // 2) % STEPS], part)
    wait(out)


def spread_kernel(at_ref, keep_ref, recv_ref, ours_ref, theirs_ref, out_ref):
    keep, recv = keep_ref[...], recv_ref[...]
    top = jnp.maximum(keep, recv)
    both = top + jnp.log2(jnp.exp2(keep - top) + jnp.exp2(recv - top))
    pairs = jnp.broadcast_to(ours_ref[:1, :1] + theirs_ref[:1, :1], (2 * STEPS, TILE))
    first = at_ref[2] == 0
    block = jnp.concatenate([jnp.where(first, keep, both), jnp.where(first, recv, both), pairs], axis=0)
    for k in range(PEERS):
        out_ref[pl.ds(k * LINES, LINES), :] = block


def join_kernel(at_ref, parts_ref, keep_ref, give_ref):
    parts = parts_ref[...].reshape(PEERS, LINES, TILE)
    pairs = jnp.sum(parts[:, 2 * STEPS : 2 * STEPS + 1, :1], axis=0)
    parts = parts[:, : 2 * STEPS, :]
    half = lax.broadcasted_iota(jnp.int32, parts.shape, 0) // DEEP
    first = at_ref[2] == 0
    parts = jnp.where(first | (half == at_ref[4]), parts, LOW)
    top = jnp.max(parts, axis=0)
    lse = top + jnp.log2(jnp.sum(jnp.exp2(parts - top[None]), axis=0))
    columns = jnp.broadcast_to(jnp.sum(lse, keepdims=True) - 2.0 * pairs, (STEPS, TILE))
    keep_ref[:STEPS, :] = lse[:STEPS]
    keep_ref[STEPS:, :] = columns
    turned = jnp.concatenate([lse[STEPS // 2 : STEPS], lse[: STEPS // 2]], axis=0)
    give_ref[:STEPS, :] = jnp.where(first, lse[STEPS:], turned)
    give_ref[STEPS:, :] = columns


def tag(term, rows=PIECE):
    term = jnp.broadcast_to(term, (rows, 128))
    high = term.astype(BF16).astype(F32)
    middle = (term - high).astype(BF16).astype(F32)
    low = (term - high) - middle
    lane = lax.rem(lax.broadcasted_iota(jnp.int32, (rows, 128), 1), 4)
    return jnp.where(lane == 0, high, jnp.where(lane == 1, middle, low)).astype(BF16)


def place_tag(at_ref, sums_ref):
    lane = lax.broadcasted_iota(jnp.int32, (1, 128), 1)
    mark = tag(sums_ref[STEPS : STEPS + 1, :1], 16).astype(F32)[:1]
    return jnp.where(lane // 4 == at_ref[3], mark, 0.0)


def untag(row, lane=0):
    return (row[:, lane : lane + 1] + row[:, lane + 1 : lane + 2]) + row[:, lane + 2 : lane + 3]


def weights_kernel(
    at_ref, scale_ref, logits_ref, text_ref, keep_ref, recv_ref,
    weights_ref, turned_ref, other_ref, sums_ref,
):
    first = at_ref[2] == 0
    keep, recv = keep_ref[:STEPS, :], recv_ref[:STEPS, :]
    cols = jnp.where(first, keep, recv)
    col_lse = jnp.concatenate([cols[k : k + 1] for k in range(STEPS)], axis=1)
    rows = jnp.where(first, recv, keep)
    sums_ref[:STEPS, :] = jnp.broadcast_to(jnp.sum(rows, keepdims=True), (STEPS, 128))
    sums_ref[STEPS:, :] = jnp.where(first, keep_ref[STEPS:, :128], recv_ref[STEPS:, :128])
    row_at = lax.broadcasted_iota(jnp.int32, (TILE, 1), 0) - at_ref[3] * PIECE
    col_at = lax.broadcasted_iota(jnp.int32, (1, SIDE), 1) - at_ref[1] * PIECE
    col_at = jnp.where((col_at >= 0) & (col_at < PIECE), col_at, -SIDE)
    text = text_ref[...]
    for k in (2, 3, 0, 1):
        tile = slice(k * TILE, (k + 1) * TILE)
        logits = logits_ref[tile, :]
        weights = jnp.exp2(logits - to_rows(rows[k : k + 1])) + jnp.exp2(logits - col_lse)
        if k < STEPS // 2:
            weights -= jnp.where(row_at + k * TILE == col_at, 2.0, 0.0)
        weights = (weights * 0.5).astype(BF16)
        turned_ref[:, tile] = weights.T
        if k < STEPS // 2:
            weights_ref[tile, :] = weights
        else:
            other_ref[(k - 2) * TILE : (k - 1) * TILE, :] = (
                scale_ref[0] * jnp.dot(weights, text, preferred_element_type=F32)
            ).astype(BF16)


def back_tile(k, scale_ref, turned_ref, image, mark, out_ref):
    tile = slice(k * TILE, (k + 1) * TILE)
    term = (
        scale_ref[0] * jnp.dot(turned_ref[tile, :], image, preferred_element_type=F32)
    ).astype(BF16)
    peers = TILE // PIECE
    for p in range(peers):
        start = (k * peers + p) * PART
        for b in range(WIDTH // 128):
            out_ref[start + b * PIECE : start + (b + 1) * PIECE, :] = (
                term[p * PIECE : (p + 1) * PIECE, b * 128 : (b + 1) * 128]
            )
        out_ref[start + PART - MARK : start + PART, :] = mark


EARLY = 3
SPLIT = EARLY * (TILE // PIECE) * PART


def text_back_kernel(scale_ref, turned_ref, image_ref, sums_ref, out_ref):
    image = image_ref[...]
    mark = tag(sums_ref[:1, :1], MARK)
    for k in range(EARLY):
        back_tile(k, scale_ref, turned_ref, image, mark, out_ref)


HALF = PIECE // 2
AWAY = (3, 2, 1, -3, -2, -1)


def pieces_kernel(
    at_ref, scale_ref, weights_ref, turned_ref, image_ref, text_ref, sums_ref, swapped_ref, begun_ref, out_ref, *refs
):
    own_out, up_out, down_out, *away_refs, mine, parts, ends, back, sem, back_sem = refs
    begun = run([pltpu.make_async_copy(begun_ref, out_ref.at[pl.ds(0, SPLIT), :], back_sem.at[0])])
    mine[...] = scale_ref[0] * jnp.dot(
        weights_ref[...], text_ref[...], preferred_element_type=F32
    ) + swapped_ref[...].astype(F32)

    def block(by):
        return pl.ds(pl.multiple_of(lax.rem(at_ref[3] + by + DEEP, DEEP) * PIECE, PIECE), PIECE)

    ends[:, :WIDTH] = mine[block(4), :].astype(BF16)
    ends[:, WIDTH:] = jnp.broadcast_to(place_tag(at_ref, sums_ref), (PIECE, 128)).astype(BF16)
    copies = run([
        pltpu.make_async_copy(ends.at[pl.ds(0, HALF), :], up_out, sem.at[0]),
        pltpu.make_async_copy(ends.at[pl.ds(HALF, HALF), :], down_out, sem.at[1]),
        pltpu.make_async_copy(mine.at[block(0), :], own_out, sem.at[2]),
    ])
    for k, (by, ref) in enumerate(zip(AWAY, away_refs)):
        parts[k] = mine[block(by), :].astype(BF16)
        copies += run([pltpu.make_async_copy(parts.at[k], ref, sem.at[3 + k])])
    for k in range(EARLY, STEPS):
        back_tile(k - EARLY, scale_ref, turned_ref.at[pl.ds(EARLY * TILE, SIDE - EARLY * TILE), :], image_ref[...], tag(sums_ref[:1, :1], MARK), back)
    begun += run([
        pltpu.make_async_copy(back, out_ref.at[pl.ds(SPLIT, PEERS * PART - SPLIT), :], back_sem.at[1])
    ])
    wait(begun + copies)


def relay_kernel(
    at_ref, sums_ref, up_ref, down_ref, below_ref, above_ref, up_out, down_out, up, down, sem
):
    copies = run([pltpu.make_async_copy(up_ref, up, sem.at[0]), pltpu.make_async_copy(down_ref, down, sem.at[1])])
    mark = place_tag(at_ref, sums_ref)
    for k, (copy, ours, theirs, out) in enumerate(
        zip(copies, (up, down), (below_ref, above_ref), (up_out, down_out))
    ):
        came = theirs[:, :WIDTH].astype(F32)
        if came.shape[0] == HALF:
            rest = jnp.zeros_like(came)
            came = jnp.concatenate([came, rest] if k == 0 else [rest, came], axis=0)
        marks = theirs[:16, WIDTH:].astype(F32)[:1] + mark
        out[:, WIDTH:] = jnp.broadcast_to(marks, (PIECE, 128)).astype(BF16)
        copy.wait()
        out[:, :WIDTH] = (ours[...].astype(F32) + came).astype(BF16)


def project(back, raw):
    direction, norm = unit_rows(raw)
    along = jnp.sum(direction * back, axis=1, keepdims=True)
    return ((back - direction * along) / norm).astype(BF16)


def text_grad_kernel(raw_ref, loss_ref, parts_ref, out_ref, total_ref, raw, grad, sem):
    copies = run([pltpu.make_async_copy(raw_ref, raw, sem.at[0])])
    total = loss_ref[:1, :1]
    for k in range(PEERS):
        total += untag(parts_ref[(k + 1) * PART - MARK : (k + 1) * PART, :].astype(F32)[:1])
    total_ref[0] = (total * (LN2 / (2.0 * SIDE * PEERS)))[0, 0]
    columns = []
    for b in range(WIDTH // 128):
        column = jnp.zeros((PIECE, 128), F32)
        for k in range(PEERS):
            start = k * PART + b * PIECE
            column += parts_ref[start : start + PIECE, :].astype(F32)
        columns.append(column)
    wait(copies)
    grad[...] = project(jnp.concatenate(columns, axis=1), raw[...])
    wait(run([pltpu.make_async_copy(grad, out_ref, sem.at[0])]))


def image_grad_kernel(at_ref, sums_ref, raw_ref, own_ref, below_ref, above_ref, out_ref, loss_ref, raw, own, grad, sem):
    copies = run([
        pltpu.make_async_copy(raw_ref, raw, sem.at[0]), pltpu.make_async_copy(own_ref, own, sem.at[1])
    ])
    twice = lax.rem(at_ref[3] + DEEP // 2, DEEP)
    lane = lax.broadcasted_iota(jnp.int32, (1, 128), 1)
    marks = place_tag(at_ref, sums_ref) + below_ref[:16, WIDTH:].astype(F32)[:1]
    marks += jnp.where(lane // 4 == twice, 0.0, above_ref[:16, WIDTH:].astype(F32)[:1])
    total = jnp.zeros((1, 1), F32)
    for k in range(DEEP):
        total += untag(marks, 4 * k)
    loss_ref[...] = jnp.broadcast_to(total, loss_ref.shape)
    wait(copies)
    back = own[...] + below_ref[:, :WIDTH].astype(F32) + above_ref[:, :WIDTH].astype(F32)
    grad[...] = project(back, raw[...])
    wait(run([pltpu.make_async_copy(grad, out_ref, sem.at[0])]))


def gather_image(unit):
    plan, arrays = [(0, 0, 0, PIECE)], [unit]
    up, down, half = unit, unit, PIECE // 2
    for by in range(1, DEEP // 2):
        up, down = send(up, "z", 1), send(down, "z", -1)
        plan += [(0, -by, 0, PIECE), (0, by, 0, PIECE)]
        arrays += [up, down]
    plan += [(0, -(DEEP // 2), 0, half), (0, DEEP // 2, half, half)]
    arrays += [send(up[:half], "z", 1), send(down[half:], "z", -1)]
    plan += [(1, *rest) for _, *rest in plan]
    arrays += [send(a, "c", 1) for a in arrays]
    return plan, arrays


def body(image_emb, text_emb, log_scale):
    width = image_emb.shape[1]
    scale = jnp.exp(log_scale)
    me = lax.axis_index("d")
    z, core, x = me % 8, (me // 8) % 2, me // 64
    at = jnp.stack([me % 16, me // 16, core, z, x % 2]).astype(jnp.int32)
    piece = local((PIECE, width), BF16)
    side = local((SIDE, width), BF16)
    outside = array((SIDE, width), BF16)
    raw = pltpu.VMEM((PIECE, width), BF16)
    sems = pltpu.SemaphoreType.DMA

    image_unit, pairs = call(
        image_unit_kernel, [array((PIECE, width), BF16), local((8, 128), F32)],
        scale, Outside(image_emb), Outside(text_emb), scratch=[raw, raw, raw, sems((3,))],
    )
    plan, pieces = gather_image(image_unit)
    text_units = call(text_units_kernel, outside, Outside(text_emb), scratch=[raw, raw, sems((PEERS,))])
    text = exchange(text_units, XY)

    pairs = [pairs, send(pairs, "c", 1)]

    lines = local((STEPS, TILE), F32)
    image, logits, keep, give = call(
        functools.partial(logits_kernel, plan), [outside, local((SIDE, SIDE), F32), lines, lines],
        at, scale, text, *map(Outside, pieces),
        scratch=[pltpu.VMEM((SIDE, width), BF16), sems((len(plan),)), sems((2,))],
    )
    spread = call(spread_kernel, local((PEERS * LINES, TILE), F32), at, keep, send(give, "c", 1), *pairs)
    lines = local((2 * STEPS, TILE), F32)
    keep, give = call(join_kernel, [lines, lines], at, exchange(spread, MIXED))
    recv = send(give, "c", 1)

    half = (SIDE // 2, width)
    weights, turned, other, sums = call(
        weights_kernel,
        [local((SIDE // 2, SIDE), BF16), local((SIDE, SIDE), BF16), local(half, BF16), local((2 * STEPS, 128), F32)],
        at, scale, logits, text, keep, recv,
    )
    swapped = send(other, "c", 1)
    text_parts = call(text_back_kernel, local((SPLIT, 128), BF16), scale, turned, image, sums)
    end = array((HALF, WIDER), BF16)
    away = [array((PIECE, width), BF16)] * len(AWAY)
    text_parts, own, up, down, *away = call(
        pieces_kernel, [array((PEERS * PART, 128), BF16), array((PIECE, width), F32), end, end, *away],
        at, scale, weights, turned, image, text, sums, swapped, text_parts,
        scratch=[
            pltpu.VMEM(half, F32),
            pltpu.VMEM((len(AWAY), PIECE, width), BF16),
            pltpu.VMEM((PIECE, WIDER), BF16),
            pltpu.VMEM((PEERS * PART - SPLIT, 128), BF16),
            sems((3 + len(AWAY),)),
            sems((2,)),
        ],
    )
    text_back = exchange(text_parts, XY)
    below, above = send(up, "z", 1), send(down, "z", -1)
    whole = local((PIECE, WIDER), BF16)
    for k in range(3):
        up, down = call(
            relay_kernel, [whole] * 2, at, sums, Outside(away[k]), Outside(away[k + 3]), below, above,
            scratch=[raw, raw, sems((2,))],
        )
        below, above = send(up, "z", 1), send(down, "z", -1)

    grad = array((PIECE, width), BF16)
    grad_image, part = call(
        image_grad_kernel, [grad, local((8, 128), F32)],
        at, sums, Outside(image_emb), Outside(own), below, above,
        scratch=[raw, pltpu.VMEM((PIECE, width), F32), raw, sems((2,))],
    )
    grad_text, loss = call(
        text_grad_kernel, [grad, pltpu.SMEM((1,), F32)], Outside(text_emb), part, text_back,
        scratch=[raw, raw, sems((1,))],
    )
    return loss, grad_image, grad_text


def solution(mesh):
    flat = Mesh(mesh.devices.reshape(-1), ("d",))
    return jax.shard_map(
        body,
        mesh=flat,
        in_specs=(P("d", None), P("d", None), P()),
        out_specs=(P(), P("d", None), P("d", None)),
        check_vma=False,
    )
```

time: 139 us -> 129 us (0.928)
  waiting for transfers between devices: 44.3 us -> 35.8 us
    ppermute x27 -> x29, waiting for transfers between devices: 44.3 us -> 34.3 us  [send(): return lax.ppermute(x, 'd', shift(axis, by))]
    all_to_all x2, waiting for transfers between devices: 0.01 us -> 1.49 us  [exchange(): return lax.all_to_all(x, 'd', 0, 0, axis_index_groups=groups, tiled=True)]
    ppermute x27 -> x29, starting transfers between devices: 33.9 us -> 33.1 us  [send(): return lax.ppermute(x, 'd', shift(axis, by))]
    pallas_call x10 -> x13, Pallas kernels: 30.4 us -> 30.7 us  [call(): pl.pallas_call(kernel, out_shape=outputs, in_specs=specs, out_specs=jax.t...]
  transfers between devices with their start and end apart: 29 -> 31, of which waited for: 15 -> 19; matrix products, arithmetic and copies ran while one was open for 0% -> 0% of each run, Pallas kernels for 5% -> 14%
where the time goes in v4:
time: 129 us; the launch traced here: 128 us
  starting transfers between devices  47.3 us (37%)
  waiting for transfers between devices  35.8 us (28%)
  Pallas kernels  30.7 us (24%)
  blocking collectives  12.2 us (9%)
  between operations  2.26 us (2%)
    ppermute x29, waiting for transfers between devices, send(): return lax.ppermute(x, 'd', shift(axis, by))  34.3 us
    ppermute x29, starting transfers between devices, send(): return lax.ppermute(x, 'd', shift(axis, by))  33.1 us
    pallas_call x13, Pallas kernels, call(): pl.pallas_call(kernel, out_shape=outputs, in_specs=specs, out_specs=jax.t...  30.7 us
    all_to_all x2, starting transfers between devices, exchange(): return lax.all_to_all(x, 'd', 0, 0, axis_index_groups=groups, tiled=True)  14.2 us
    all_to_all x1, blocking collectives, exchange(): return lax.all_to_all(x, 'd', 0, 0, axis_index_groups=groups, tiled=True)  12.2 us
  transfers between devices with their start and end apart: 31, of which 19 were waited for; matrix products, arithmetic and copies ran while one was open for 0% of the time, Pallas kernels for 14%

profile of v4, /device:TPU:28, one launch (start us, length us, event | category | flops | bytes accessed | tf_op | source)
XLA Modules:
  0.0 128.4 jit_solution(11037659115919606114)
XLA Ops:
  0.6 2.7 %shard_map.58 = bf16[1024,1280]{1,0:T(8,128)(2,1)} custom-call(bf16[64,1280]{1,0:T(8,128)(2,1)} %raw_ref.7), custom_call_target="tpu_custom_call" | custom-call | tf_op jit(solution)/shard_map/pallas_call | solution.py:76
  3.3 7.1 %all-to-all-start = ((bf16[16,64,1280]{2,1,0:T(8,128)(2,1)}), bf16[16,64,1280]{2,1,0:T(8,128)(2,1)S(1)}, u32[]{:S(2)}, u32[]{:S(2)}) async-start(bf16[16,64,1280]{2,1,0:T(8,128)(2,1)} %bitcast.17), calls=%async_computation | async-start | bytes 5242880 | tf_op jit(solution)/shard_map/all_to_all | solution.py:53
  11.1 1.7 %shard_map.59 = (bf16[64,1280]{1,0:T(8,128)(2,1)}, f32[8,128]{1,0:T(8,128)S(1)}) custom-call(f32[1]{0:T(128)S(6)} %exp.3.scale_ref, bf16[64,1280]{1,0:T(8,128)(2,1)} %raw_ref.6, bf16[64,1280]{1,0:T(8,128)(2,1)} %raw_ref.7), custom_call_target="tpu_custom_call" | custom-call | tf_op jit(solution)/shard_map/pallas_call | solution.py:76
  12.9 5.9 %collective-permute-start.1 = (bf16[64,1280]{1,0:T(8,128)(2,1)}, bf16[64,1280]{1,0:T(8,128)(2,1)S(1)}, u32[]{:S(2)}, u32[]{:S(2)}) collective-permute-start(bf16[64,1280]{1,0:T(8,128)(2,1)} %get-tuple-element.35.refs_0_), channel_id=1, source_target_pairs={{0,7},{1,0},{2,1},{3,2},{4,3},{5,4},{6,5},{7,6},{8,15},{9,8},{10,9... | collective-permute-start | bytes 491528 | tf_op jit(solution)/shard_map/ppermute | solution.py:49
  18.8 3.2 %collective-permute-done.1.refs_2_ = bf16[64,1280]{1,0:T(8,128)(2,1)S(1)} collective-permute-done((bf16[64,1280]{1,0:T(8,128)(2,1)}, bf16[64,1280]{1,0:T(8,128)(2,1)S(1)}, u32[]{:S(2)}, u32[]{:S(2)}) %collective-permute-start.1) | collective-permute-done | bytes 163872 | tf_op jit(solution)/shard_map/ppermute | solution.py:49
  22.0 3.6 %collective-permute-start.3 = (bf16[64,1280]{1,0:T(8,128)(2,1)S(1)}, bf16[64,1280]{1,0:T(8,128)(2,1)S(1)}, u32[]{:S(2)}, u32[]{:S(2)}) collective-permute-start(bf16[64,1280]{1,0:T(8,128)(2,1)S(1)} %collective-permute-done.1.refs_2_), channel_id=1, source_target_pairs={{0,7},{1,0},{2,1},{3,2},{4,3},{5,4},{6,5},{7,6},{8,15},{9,8},{10,9... | collective-permute-start | bytes 491528 | tf_op jit(solution)/shard_map/ppermute | solution.py:49
  25.6 2.8 %collective-permute-done.3.refs_4_ = bf16[64,1280]{1,0:T(8,128)(2,1)S(1)} collective-permute-done((bf16[64,1280]{1,0:T(8,128)(2,1)S(1)}, bf16[64,1280]{1,0:T(8,128)(2,1)S(1)}, u32[]{:S(2)}, u32[]{:S(2)}) %collective-permute-start.3) | collective-permute-done | bytes 163872 | tf_op jit(solution)/shard_map/ppermute | solution.py:49
  28.5 3.7 %collective-permute-start.5 = (bf16[64,1280]{1,0:T(8,128)(2,1)S(1)}, bf16[64,1280]{1,0:T(8,128)(2,1)S(1)}, u32[]{:S(2)}, u32[]{:S(2)}) collective-permute-start(bf16[64,1280]{1,0:T(8,128)(2,1)S(1)} %collective-permute-done.3.refs_4_), channel_id=1, source_target_pairs={{0,7},{1,0},{2,1},{3,2},{4,3},{5,4},{6,5},{7,6},{8,15},{9,8},{10,9... | collective-permute-start | bytes 491528 | tf_op jit(solution)/shard_map/ppermute | solution.py:49
  32.8 2.2 %collective-permute-done.5.refs_6_ = bf16[64,1280]{1,0:T(8,128)(2,1)S(1)} collective-permute-done((bf16[64,1280]{1,0:T(8,128)(2,1)S(1)}, bf16[64,1280]{1,0:T(8,128)(2,1)S(1)}, u32[]{:S(2)}, u32[]{:S(2)}) %collective-permute-start.5) | collective-permute-done | bytes 163872 | tf_op jit(solution)/shard_map/ppermute | solution.py:49
  35.0 4.0 %collective-permute-done.4.refs_5_ = bf16[64,1280]{1,0:T(8,128)(2,1)S(1)} collective-permute-done((bf16[64,1280]{1,0:T(8,128)(2,1)}, bf16[64,1280]{1,0:T(8,128)(2,1)S(1)}, u32[]{:S(2)}, u32[]{:S(2)}) %collective-permute-start.4) | collective-permute-done | bytes 163872 | tf_op jit(solution)/shard_map/ppermute | solution.py:49
  39.4 1.7 %collective-permute-start.6 = (bf16[32,1280]{1,0:T(8,128)(2,1)S(1)}, bf16[32,1280]{1,0:T(8,128)(2,1)}, u32[]{:S(2)}, u32[]{:S(2)}) collective-permute-start(bf16[32,1280]{1,0:T(8,128)(2,1)S(1)} %slice.8), channel_id=1, source_target_pairs={{0,1},{1,2},{2,3},{3,4},{4,5},{5,6},{6,7},{7,0},{8,9},{9,10},{10,1... | collective-permute-start | bytes 245768 | tf_op jit(solution)/shard_map/ppermute | solution.py:49
  41.8 2.3 %collective-permute-done.7.refs_8_ = bf16[32,1280]{1,0:T(8,128)(2,1)} collective-permute-done((bf16[32,1280]{1,0:T(8,128)(2,1)S(1)}, bf16[32,1280]{1,0:T(8,128)(2,1)}, u32[]{:S(2)}, u32[]{:S(2)}) %collective-permute-start.7) | collective-permute-done | bytes 81952 | tf_op jit(solution)/shard_map/ppermute | solution.py:49
  47.1 6.4 %shard_map.60 = (bf16[1024,1280]{1,0:T(8,128)(2,1)}, f32[1024,1024]{1,0:T(8,128)S(1)}, f32[4,256]{1,0:T(4,128)S(1)}, f32[4,256]{1,0:T(4,128)S(1)}) custom-call(s32[5]{0:T(128)S(1)} %stack.23.at_ref, f32[1]{0:T(128)S(6)} %exp.3.scale_ref, bf16[1024,1280]{1,0:T(8,128)(2,1)S(1)} %bitcast.11, bf16[64,1280]{1,0:T(8,128)(2,1)} %get-tuple-element.35.refs_0_, ...), custom_call_target="tpu_custom_call" | custom-call | tf_op jit(solution)/shard_map/pallas_call | solution.py:76
  55.3 12.2 %all_to_all.33 = f32[16,16,256]{2,1,0:T(8,128)S(1)} all-to-all(f32[16,16,256]{2,1,0:T(8,128)S(1)} %bitcast.15), channel_id=1, replica_groups={{0,16,32,48,64,80,96,112,128,144,160,176,192,208,224,240},{1,17,33,49,6..., dimensions={0} | all-to-all | bytes 524288 | tf_op jit(solution)/shard_map/all_to_all | solution.py:53
  68.2 1.7 %collective-permute-start.19 = (f32[8,256]{1,0:T(8,128)S(1)}, f32[8,256]{1,0:T(8,128)S(1)}, u32[]{:S(2)}, u32[]{:S(2)}) collective-permute-start(f32[8,256]{1,0:T(8,128)S(1)} %get-tuple-element.41), channel_id=1, source_target_pairs={{0,8},{1,9},{2,10},{3,11},{4,12},{5,13},{6,14},{7,15},{8,0},{9,1},... | collective-permute-start | bytes 24584 | tf_op jit(solution)/shard_map/ppermute | solution.py:49
  70.7 2.9 %shard_map.63 = (bf16[512,1024]{1,0:T(8,128)(2,1)S(1)}, bf16[1024,1024]{1,0:T(8,128)(2,1)S(1)}, bf16[512,1280]{1,0:T(8,128)(2,1)S(1)}, f32[8,128]{1,0:T(8,128)S(1)}) custom-call(s32[5]{0:T(128)S(1)} %stack.23.at_ref, f32[1]{0:T(128)S(6)} %exp.3.scale_ref, f32[1024,1024]{1,0:T(8,128)S(1)} %get-tuple-element.36.logits_ref, bf16[1024,1280]{1,0:T(8,128)(2,1)S(1)} %bitcast.12, ...), custom_call_target="tpu_custom_call" | custom-call | tf_op jit(solution)/shard_map/pallas_call | solution.py:76
  74.1 2.2 %shard_map.64.begun_ref = bf16[7872,128]{1,0:T(8,128)(2,1)S(1)} custom-call(f32[1]{0:T(128)S(6)} %exp.3.scale_ref, bf16[1024,1024]{1,0:T(8,128)(2,1)S(1)} %get-tuple-element.44.turned_ref, bf16[1024,1280]{1,0:T(8,128)(2,1)S(1)} %copy-done, f32[8,128]{1,0:T(8,128)S(1)} %get-tuple-element.42.sums_ref), custom_call_target="tpu_custom_call" | custom-call | tf_op jit(solution)/shard_map/pallas_call | solution.py:76
  76.7 4.4 %shard_map.65 = (bf16[10496,128]{1,0:T(8,128)(2,1)}, f32[64,1280]{1,0:T(8,128)}, bf16[32,1408]{1,0:T(8,128)(2,1)}, bf16[32,1408]{1,0:T(8,128)(2,1)}, bf16[64,128...) custom-call(s32[5]{0:T(128)S(1)} %stack.23.at_ref, ...), custom_call_target="tpu_custom_call" | custom-call | tf_op jit(solution)/shard_map/pallas_call | solution.py:76
  81.2 7.1 %all-to-all-start.2 = ((bf16[16,656,128]{2,1,0:T(8,128)(2,1)}), bf16[16,656,128]{2,1,0:T(8,128)(2,1)S(1)}, u32[]{:S(2)}, u32[]{:S(2)}) async-start(bf16[16,656,128]{2,1,0:T(8,128)(2,1)} %bitcast.18), calls=%async_computation.2 | async-start | bytes 5373952 | tf_op jit(solution)/shard_map/all_to_all | solution.py:53
  88.2 2.4 %collective-permute-start.21 = (bf16[32,1408]{1,0:T(8,128)(2,1)S(1)}, bf16[32,1408]{1,0:T(8,128)(2,1)S(1)}, u32[]{:S(2)}, u32[]{:S(2)}) collective-permute-start(bf16[32,1408]{1,0:T(8,128)(2,1)S(1)} %copy-done.11), channel_id=1, source_target_pairs={{0,1},{1,2},{2,3},{3,4},{4,5},{5,6},{6,7},{7,0},{8,9},{9,10},{10,1... | collective-permute-start | bytes 270344 | tf_op jit(solution)/shard_map/ppermute | solution.py:49
  91.8 2.5 %collective-permute-done.21.below_ref = bf16[32,1408]{1,0:T(8,128)(2,1)S(1)} collective-permute-done((bf16[32,1408]{1,0:T(8,128)(2,1)S(1)}, bf16[32,1408]{1,0:T(8,128)(2,1)S(1)}, u32[]{:S(2)}, u32[]{:S(2)}) %collective-permute-start.21) | collective-permute-done | bytes 90144 | tf_op jit(solution)/shard_map/ppermute | solution.py:49
  95.1 1.6 %shard_map.66 = (bf16[64,1408]{1,0:T(8,128)(2,1)S(1)}, bf16[64,1408]{1,0:T(8,128)(2,1)S(1)}) custom-call(s32[5]{0:T(128)S(1)} %stack.23.at_ref, f32[8,128]{1,0:T(8,128)S(1)} %get-tuple-element.42.sums_ref, bf16[64,1280]{1,0:T(8,128)(2,1)} %get-tuple-element.52.up_ref, bf16[64,1280]{1,0:T(8,128)(2,1)} %get-tuple-element.53.down_ref, ...), custom_call_target="tpu_custom_call" | custom-call | tf_op jit(solution)/shard_map/pallas_call | solution.py:76
  97.1 3.0 %collective-permute-start.24 = (bf16[64,1408]{1,0:T(8,128)(2,1)S(1)}, bf16[64,1408]{1,0:T(8,128)(2,1)S(1)}, u32[]{:S(2)}, u32[]{:S(2)}) collective-permute-start(bf16[64,1408]{1,0:T(8,128)(2,1)S(1)} %get-tuple-element.57), channel_id=1, source_target_pairs={{0,7},{1,0},{2,1},{3,2},{4,3},{5,4},{6,5},{7,6},{8,15},{9,8},{10,9... | collective-permute-start | bytes 540680 | tf_op jit(solution)/shard_map/ppermute | solution.py:49
  100.0 3.5 %collective-permute-done.23.below_ref = bf16[64,1408]{1,0:T(8,128)(2,1)S(1)} collective-permute-done((bf16[64,1408]{1,0:T(8,128)(2,1)S(1)}, bf16[64,1408]{1,0:T(8,128)(2,1)S(1)}, u32[]{:S(2)}, u32[]{:S(2)}) %collective-permute-start.23) | collective-permute-done | bytes 180256 | tf_op jit(solution)/shard_map/ppermute | solution.py:49
  103.5 1.6 %shard_map.67 = (bf16[64,1408]{1,0:T(8,128)(2,1)S(1)}, bf16[64,1408]{1,0:T(8,128)(2,1)S(1)}) custom-call(s32[5]{0:T(128)S(1)} %stack.23.at_ref, f32[8,128]{1,0:T(8,128)S(1)} %get-tuple-element.42.sums_ref, bf16[64,1280]{1,0:T(8,128)(2,1)} %get-tuple-element.50.up_ref, bf16[64,1280]{1,0:T(8,128)(2,1)} %get-tuple-element.51.down_ref, ...), custom_call_target="tpu_custom_call" | custom-call | tf_op jit(solution)/shard_map/pallas_call | solution.py:76
  105.1 2.1 %collective-permute-start.25 = (bf16[64,1408]{1,0:T(8,128)(2,1)S(1)}, bf16[64,1408]{1,0:T(8,128)(2,1)S(1)}, u32[]{:S(2)}, u32[]{:S(2)}) collective-permute-start(bf16[64,1408]{1,0:T(8,128)(2,1)S(1)} %get-tuple-element.58), channel_id=1, source_target_pairs={{0,1},{1,2},{2,3},{3,4},{4,5},{5,6},{6,7},{7,0},{8,9},{9,10},{10,1... | collective-permute-start | bytes 540680 | tf_op jit(solution)/shard_map/ppermute | solution.py:49
  108.5 3.4 %collective-permute-done.25.below_ref = bf16[64,1408]{1,0:T(8,128)(2,1)S(1)} collective-permute-done((bf16[64,1408]{1,0:T(8,128)(2,1)S(1)}, bf16[64,1408]{1,0:T(8,128)(2,1)S(1)}, u32[]{:S(2)}, u32[]{:S(2)}) %collective-permute-start.25) | collective-permute-done | bytes 180256 | tf_op jit(solution)/shard_map/ppermute | solution.py:49
  112.7 1.6 %shard_map.68 = (bf16[64,1408]{1,0:T(8,128)(2,1)S(1)}, bf16[64,1408]{1,0:T(8,128)(2,1)S(1)}) custom-call(s32[5]{0:T(128)S(1)} %stack.23.at_ref, f32[8,128]{1,0:T(8,128)S(1)} %get-tuple-element.42.sums_ref, bf16[64,1280]{1,0:T(8,128)(2,1)} %get-tuple-element.48.up_ref, bf16[64,1280]{1,0:T(8,128)(2,1)} %get-tuple-element.49.down_ref, ...), custom_call_target="tpu_custom_call" | custom-call | tf_op jit(solution)/shard_map/pallas_call | solution.py:76
  114.3 2.1 %collective-permute-start.27 = (bf16[64,1408]{1,0:T(8,128)(2,1)S(1)}, bf16[64,1408]{1,0:T(8,128)(2,1)S(1)}, u32[]{:S(2)}, u32[]{:S(2)}) collective-permute-start(bf16[64,1408]{1,0:T(8,128)(2,1)S(1)} %get-tuple-element.60), channel_id=1, source_target_pairs={{0,1},{1,2},{2,3},{3,4},{4,5},{5,6},{6,7},{7,0},{8,9},{9,10},{10,1... | collective-permute-start | bytes 540680 | tf_op jit(solution)/shard_map/ppermute | solution.py:49
  117.6 3.5 %collective-permute-done.27.below_ref = bf16[64,1408]{1,0:T(8,128)(2,1)S(1)} collective-permute-done((bf16[64,1408]{1,0:T(8,128)(2,1)S(1)}, bf16[64,1408]{1,0:T(8,128)(2,1)S(1)}, u32[]{:S(2)}, u32[]{:S(2)}) %collective-permute-start.27) | collective-permute-done | bytes 180256 | tf_op jit(solution)/shard_map/ppermute | solution.py:49
  121.9 2.5 %shard_map.69 = (bf16[64,1280]{1,0:T(8,128)(2,1)}, f32[8,128]{1,0:T(8,128)S(1)}) custom-call(s32[5]{0:T(128)S(1)} %stack.23.at_ref, f32[8,128]{1,0:T(8,128)S(1)} %get-tuple-element.42.sums_ref, bf16[64,1280]{1,0:T(8,128)(2,1)} %raw_ref.6, f32[64,1280]{1,0:T(8,128)} %get-tuple-element.47.own_ref, bf16[64,1408]{1,0:T(8,128)(2,1)S(1)} %collective-permute-done.27.below_ref, ...), custom_call_target="tpu_custom_call" | custom-call | tf_op jit(solution)/shard_map/pallas_call | solution.py:76
  125.9 1.8 %shard_map.70 = (bf16[64,1280]{1,0:T(8,128)(2,1)}, f32[1]{0:T(128)S(4)}) custom-call(bf16[64,1280]{1,0:T(8,128)(2,1)} %raw_ref.7, f32[8,128]{1,0:T(8,128)S(1)} %get-tuple-element.62.loss_ref, bf16[10496,128]{1,0:T(8,128)(2,1)S(1)} %bitcast.14), custom_call_target="tpu_custom_call" | custom-call | tf_op jit(solution)/shard_map/pallas_call | solution.py:76
  (71 shorter events, 16.9 us)
Async XLA Ops:
  3.3 43.7 %all-to-all-start = ((bf16[16,64,1280]{2,1,0:T(8,128)(2,1)}), bf16[16,64,1280]{2,1,0:T(8,128)(2,1)S(1)}, u32[]{:S(2)}, u32[]{:S(2)}) async-start(bf16[16,64,1280]{2,1,0:T(8,128)(2,1)} %bitcast.17), calls=%async_computation | async-start | bytes 5242880 | tf_op jit(solution)/shard_map/all_to_all | solution.py:53
  12.9 9.1 %collective-permute-start.1 = (bf16[64,1280]{1,0:T(8,128)(2,1)}, bf16[64,1280]{1,0:T(8,128)(2,1)S(1)}, u32[]{:S(2)}, u32[]{:S(2)}) collective-permute-start(bf16[64,1280]{1,0:T(8,128)(2,1)} %get-tuple-element.35.refs_0_), channel_id=1, source_target_pairs={{0,7},{1,0},{2,1},{3,2},{4,3},{5,4},{6,5},{7,6},{8,15},{9,8},{10,9... | collective-permute-start | bytes 491528 | tf_op jit(solution)/shard_map/ppermute | solution.py:49
  18.8 6.8 %collective-permute-start = (bf16[64,1280]{1,0:T(8,128)(2,1)}, bf16[64,1280]{1,0:T(8,128)(2,1)S(1)}, u32[]{:S(2)}, u32[]{:S(2)}) collective-permute-start(bf16[64,1280]{1,0:T(8,128)(2,1)} %get-tuple-element.35.refs_0_), channel_id=1, source_target_pairs={{0,1},{1,2},{2,3},{3,4},{4,5},{5,6},{6,7},{7,0},{8,9},{9,10},{10,1... | collective-permute-start | bytes 491528 | tf_op jit(solution)/shard_map/ppermute | solution.py:49
  22.0 25.0 %copy-start.3 = (bf16[64,1280]{1,0:T(8,128)(2,1)}, bf16[64,1280]{1,0:T(8,128)(2,1)S(1)}, u32[]{:S(2)}) copy-start(bf16[64,1280]{1,0:T(8,128)(2,1)S(1)} %collective-permute-done.1.refs_2_) | copy-start | bytes 491524
  22.0 6.4 %collective-permute-start.3 = (bf16[64,1280]{1,0:T(8,128)(2,1)S(1)}, bf16[64,1280]{1,0:T(8,128)(2,1)S(1)}, u32[]{:S(2)}, u32[]{:S(2)}) collective-permute-start(bf16[64,1280]{1,0:T(8,128)(2,1)S(1)} %collective-permute-done.1.refs_2_), channel_id=1, source_target_pairs={{0,7},{1,0},{2,1},{3,2},{4,3},{5,4},{6,5},{7,6},{8,15},{9,8},{10,9... | collective-permute-start | bytes 491528 | tf_op jit(solution)/shard_map/ppermute | solution.py:49
  25.6 6.6 %collective-permute-start.2 = (bf16[64,1280]{1,0:T(8,128)(2,1)S(1)}, bf16[64,1280]{1,0:T(8,128)(2,1)}, u32[]{:S(2)}, u32[]{:S(2)}) collective-permute-start(bf16[64,1280]{1,0:T(8,128)(2,1)S(1)} %collective-permute-done.refs_1_), channel_id=1, source_target_pairs={{0,1},{1,2},{2,3},{3,4},{4,5},{5,6},{6,7},{7,0},{8,9},{9,10},{10,1... | collective-permute-start | bytes 491528 | tf_op jit(solution)/shard_map/ppermute | solution.py:49
  28.5 6.5 %collective-permute-start.5 = (bf16[64,1280]{1,0:T(8,128)(2,1)S(1)}, bf16[64,1280]{1,0:T(8,128)(2,1)S(1)}, u32[]{:S(2)}, u32[]{:S(2)}) collective-permute-start(bf16[64,1280]{1,0:T(8,128)(2,1)S(1)} %collective-permute-done.3.refs_4_), channel_id=1, source_target_pairs={{0,7},{1,0},{2,1},{3,2},{4,3},{5,4},{6,5},{7,6},{8,15},{9,8},{10,9... | collective-permute-start | bytes 491528 | tf_op jit(solution)/shard_map/ppermute | solution.py:49
  32.3 6.7 %collective-permute-start.4 = (bf16[64,1280]{1,0:T(8,128)(2,1)}, bf16[64,1280]{1,0:T(8,128)(2,1)S(1)}, u32[]{:S(2)}, u32[]{:S(2)}) collective-permute-start(bf16[64,1280]{1,0:T(8,128)(2,1)} %collective-permute-done.2.refs_3_), channel_id=1, source_target_pairs={{0,1},{1,2},{2,3},{3,4},{4,5},{5,6},{6,7},{7,0},{8,9},{9,10},{10,1... | collective-permute-start | bytes 491528 | tf_op jit(solution)/shard_map/ppermute | solution.py:49
  32.3 6.8 %collective-permute-start.8 = (bf16[64,1280]{1,0:T(8,128)(2,1)}, bf16[64,1280]{1,0:T(8,128)(2,1)S(1)}, u32[]{:S(2)}, u32[]{:S(2)}) collective-permute-start(bf16[64,1280]{1,0:T(8,128)(2,1)} %get-tuple-element.35.refs_0_), channel_id=1, source_target_pairs={{0,8},{1,9},{2,10},{3,11},{4,12},{5,13},{6,14},{7,15},{8,0},{9,1},... | collective-permute-start | bytes 491528 | tf_op jit(solution)/shard_map/ppermute | solution.py:49
  32.3 7.1 %collective-permute-start.10 = (bf16[64,1280]{1,0:T(8,128)(2,1)S(1)}, bf16[64,1280]{1,0:T(8,128)(2,1)S(1)}, u32[]{:S(2)}, u32[]{:S(2)}) collective-permute-start(bf16[64,1280]{1,0:T(8,128)(2,1)S(1)} %collective-permute-done.1.refs_2_), channel_id=1, source_target_pairs={{0,8},{1,9},{2,10},{3,11},{4,12},{5,13},{6,14},{7,15},{8,0},{9,1},... | collective-permute-start | bytes 491528 | tf_op jit(solution)/shard_map/ppermute | solution.py:49
  32.8 8.4 %collective-permute-start.9 = (bf16[64,1280]{1,0:T(8,128)(2,1)S(1)}, bf16[64,1280]{1,0:T(8,128)(2,1)S(1)}, u32[]{:S(2)}, u32[]{:S(2)}) collective-permute-start(bf16[64,1280]{1,0:T(8,128)(2,1)S(1)} %collective-permute-done.refs_1_), channel_id=1, source_target_pairs={{0,8},{1,9},{2,10},{3,11},{4,12},{5,13},{6,14},{7,15},{8,0},{9,1},... | collective-permute-start | bytes 491528 | tf_op jit(solution)/shard_map/ppermute | solution.py:49
  35.0 6.2 %collective-permute-start.12 = (bf16[64,1280]{1,0:T(8,128)(2,1)S(1)}, bf16[64,1280]{1,0:T(8,128)(2,1)S(1)}, u32[]{:S(2)}, u32[]{:S(2)}) collective-permute-start(bf16[64,1280]{1,0:T(8,128)(2,1)S(1)} %collective-permute-done.3.refs_4_), channel_id=1, source_target_pairs={{0,8},{1,9},{2,10},{3,11},{4,12},{5,13},{6,14},{7,15},{8,0},{9,1},... | collective-permute-start | bytes 491528 | tf_op jit(solution)/shard_map/ppermute | solution.py:49
  39.0 6.5 %collective-permute-start.11 = (bf16[64,1280]{1,0:T(8,128)(2,1)}, bf16[64,1280]{1,0:T(8,128)(2,1)}, u32[]{:S(2)}, u32[]{:S(2)}) collective-permute-start(bf16[64,1280]{1,0:T(8,128)(2,1)} %collective-permute-done.2.refs_3_), channel_id=1, source_target_pairs={{0,8},{1,9},{2,10},{3,11},{4,12},{5,13},{6,14},{7,15},{8,0},{9,1},... | collective-permute-start | bytes 491528 | tf_op jit(solution)/shard_map/ppermute | solution.py:49
  39.0 5.0 %collective-permute-start.7 = (bf16[32,1280]{1,0:T(8,128)(2,1)S(1)}, bf16[32,1280]{1,0:T(8,128)(2,1)}, u32[]{:S(2)}, u32[]{:S(2)}) collective-permute-start(bf16[32,1280]{1,0:T(8,128)(2,1)S(1)} %slice.9), channel_id=1, source_target_pairs={{0,7},{1,0},{2,1},{3,2},{4,3},{5,4},{6,5},{7,6},{8,15},{9,8},{10,9... | collective-permute-start | bytes 245768 | tf_op jit(solution)/shard_map/ppermute | solution.py:49
  39.4 6.0 %collective-permute-start.6 = (bf16[32,1280]{1,0:T(8,128)(2,1)S(1)}, bf16[32,1280]{1,0:T(8,128)(2,1)}, u32[]{:S(2)}, u32[]{:S(2)}) collective-permute-start(bf16[32,1280]{1,0:T(8,128)(2,1)S(1)} %slice.8), channel_id=1, source_target_pairs={{0,1},{1,2},{2,3},{3,4},{4,5},{5,6},{6,7},{7,0},{8,9},{9,10},{10,1... | collective-permute-start | bytes 245768 | tf_op jit(solution)/shard_map/ppermute | solution.py:49
  41.2 5.0 %collective-permute-start.14 = (bf16[64,1280]{1,0:T(8,128)(2,1)S(1)}, bf16[64,1280]{1,0:T(8,128)(2,1)}, u32[]{:S(2)}, u32[]{:S(2)}) collective-permute-start(bf16[64,1280]{1,0:T(8,128)(2,1)S(1)} %collective-permute-done.5.refs_6_), channel_id=1, source_target_pairs={{0,8},{1,9},{2,10},{3,11},{4,12},{5,13},{6,14},{7,15},{8,0},{9,1},... | collective-permute-start | bytes 491528 | tf_op jit(solution)/shard_map/ppermute | solution.py:49
  41.2 5.8 %collective-permute-start.13 = (bf16[64,1280]{1,0:T(8,128)(2,1)S(1)}, bf16[64,1280]{1,0:T(8,128)(2,1)}, u32[]{:S(2)}, u32[]{:S(2)}) collective-permute-start(bf16[64,1280]{1,0:T(8,128)(2,1)S(1)} %collective-permute-done.4.refs_5_), channel_id=1, source_target_pairs={{0,8},{1,9},{2,10},{3,11},{4,12},{5,13},{6,14},{7,15},{8,0},{9,1},... | collective-permute-start | bytes 491528 | tf_op jit(solution)/shard_map/ppermute | solution.py:49
  44.1 2.1 %collective-permute-start.16 = (bf16[32,1280]{1,0:T(8,128)(2,1)}, bf16[32,1280]{1,0:T(8,128)(2,1)}, u32[]{:S(2)}, u32[]{:S(2)}) collective-permute-start(bf16[32,1280]{1,0:T(8,128)(2,1)} %collective-permute-done.7.refs_8_), channel_id=1, source_target_pairs={{0,8},{1,9},{2,10},{3,11},{4,12},{5,13},{6,14},{7,15},{8,0},{9,1},... | collective-permute-start | bytes 245768 | tf_op jit(solution)/shard_map/ppermute | solution.py:49
  45.4 1.6 %collective-permute-start.15 = (bf16[32,1280]{1,0:T(8,128)(2,1)}, bf16[32,1280]{1,0:T(8,128)(2,1)}, u32[]{:S(2)}, u32[]{:S(2)}) collective-permute-start(bf16[32,1280]{1,0:T(8,128)(2,1)} %collective-permute-done.6.refs_7_), channel_id=1, source_target_pairs={{0,8},{1,9},{2,10},{3,11},{4,12},{5,13},{6,14},{7,15},{8,0},{9,1},... | collective-permute-start | bytes 245768 | tf_op jit(solution)/shard_map/ppermute | solution.py:49
  45.5 8.2 %collective-permute-start.18 = (f32[8,128]{1,0:T(8,128)S(1)}, f32[8,128]{1,0:T(8,128)S(1)}, u32[]{:S(2)}, u32[]{:S(2)}) collective-permute-start(f32[8,128]{1,0:T(8,128)S(1)} %get-tuple-element.39.ours_ref), channel_id=1, source_target_pairs={{0,8},{1,9},{2,10},{3,11},{4,12},{5,13},{6,14},{7,15},{8,0},{9,1},... | collective-permute-start | bytes 12296 | tf_op jit(solution)/shard_map/ppermute | solution.py:49
  53.4 1.3 collective-permute-start.17
  68.2 2.5 %collective-permute-start.19 = (f32[8,256]{1,0:T(8,128)S(1)}, f32[8,256]{1,0:T(8,128)S(1)}, u32[]{:S(2)}, u32[]{:S(2)}) collective-permute-start(f32[8,256]{1,0:T(8,128)S(1)} %get-tuple-element.41), channel_id=1, source_target_pairs={{0,8},{1,9},{2,10},{3,11},{4,12},{5,13},{6,14},{7,15},{8,0},{9,1},... | collective-permute-start | bytes 24584 | tf_op jit(solution)/shard_map/ppermute | solution.py:49
  73.6 3.1 %collective-permute-start.20 = (bf16[512,1280]{1,0:T(8,128)(2,1)S(1)}, bf16[512,1280]{1,0:T(8,128)(2,1)S(1)}, u32[]{:S(2)}, u32[]{:S(2)}) collective-permute-start(bf16[512,1280]{1,0:T(8,128)(2,1)S(1)} %get-tuple-element.46), channel_id=1, source_target_pairs={{0,8},{1,9},{2,10},{3,11},{4,12},{5,13},{6,14},{7,15},{8,0},{9,1},... | collective-permute-start | bytes 3932168 | tf_op jit(solution)/shard_map/ppermute | solution.py:49
  81.2 44.7 %all-to-all-start.2 = ((bf16[16,656,128]{2,1,0:T(8,128)(2,1)}), bf16[16,656,128]{2,1,0:T(8,128)(2,1)S(1)}, u32[]{:S(2)}, u32[]{:S(2)}) async-start(bf16[16,656,128]{2,1,0:T(8,128)(2,1)} %bitcast.18), calls=%async_computation.2 | async-start | bytes 5373952 | tf_op jit(solution)/shard_map/all_to_all | solution.py:53
  88.2 6.0 %collective-permute-start.21 = (bf16[32,1408]{1,0:T(8,128)(2,1)S(1)}, bf16[32,1408]{1,0:T(8,128)(2,1)S(1)}, u32[]{:S(2)}, u32[]{:S(2)}) collective-permute-start(bf16[32,1408]{1,0:T(8,128)(2,1)S(1)} %copy-done.11), channel_id=1, source_target_pairs={{0,1},{1,2},{2,3},{3,4},{4,5},{5,6},{6,7},{7,0},{8,9},{9,10},{10,1... | collective-permute-start | bytes 270344 | tf_op jit(solution)/shard_map/ppermute | solution.py:49
  90.6 4.5 %collective-permute-start.22 = (bf16[32,1408]{1,0:T(8,128)(2,1)S(1)}, bf16[32,1408]{1,0:T(8,128)(2,1)S(1)}, u32[]{:S(2)}, u32[]{:S(2)}) collective-permute-start(bf16[32,1408]{1,0:T(8,128)(2,1)S(1)} %copy-done.10), channel_id=1, source_target_pairs={{0,7},{1,0},{2,1},{3,2},{4,3},{5,4},{6,5},{7,6},{8,15},{9,8},{10,9... | collective-permute-start | bytes 270344 | tf_op jit(solution)/shard_map/ppermute | solution.py:49
  96.7 6.8 %collective-permute-start.23 = (bf16[64,1408]{1,0:T(8,128)(2,1)S(1)}, bf16[64,1408]{1,0:T(8,128)(2,1)S(1)}, u32[]{:S(2)}, u32[]{:S(2)}) collective-permute-start(bf16[64,1408]{1,0:T(8,128)(2,1)S(1)} %get-tuple-element.56), channel_id=1, source_target_pairs={{0,1},{1,2},{2,3},{3,4},{4,5},{5,6},{6,7},{7,0},{8,9},{9,10},{10,1... | collective-permute-start | bytes 540680 | tf_op jit(solution)/shard_map/ppermute | solution.py:49
  97.1 6.5 %collective-permute-start.24 = (bf16[64,1408]{1,0:T(8,128)(2,1)S(1)}, bf16[64,1408]{1,0:T(8,128)(2,1)S(1)}, u32[]{:S(2)}, u32[]{:S(2)}) collective-permute-start(bf16[64,1408]{1,0:T(8,128)(2,1)S(1)} %get-tuple-element.57), channel_id=1, source_target_pairs={{0,7},{1,0},{2,1},{3,2},{4,3},{5,4},{6,5},{7,6},{8,15},{9,8},{10,9... | collective-permute-start | bytes 540680 | tf_op jit(solution)/shard_map/ppermute | solution.py:49
  105.1 6.8 %collective-permute-start.25 = (bf16[64,1408]{1,0:T(8,128)(2,1)S(1)}, bf16[64,1408]{1,0:T(8,128)(2,1)S(1)}, u32[]{:S(2)}, u32[]{:S(2)}) collective-permute-start(bf16[64,1408]{1,0:T(8,128)(2,1)S(1)} %get-tuple-element.58), channel_id=1, source_target_pairs={{0,1},{1,2},{2,3},{3,4},{4,5},{5,6},{6,7},{7,0},{8,9},{9,10},{10,1... | collective-permute-start | bytes 540680 | tf_op jit(solution)/shard_map/ppermute | solution.py:49
  107.2 5.5 %collective-permute-start.26 = (bf16[64,1408]{1,0:T(8,128)(2,1)S(1)}, bf16[64,1408]{1,0:T(8,128)(2,1)S(1)}, u32[]{:S(2)}, u32[]{:S(2)}) collective-permute-start(bf16[64,1408]{1,0:T(8,128)(2,1)S(1)} %get-tuple-element.59), channel_id=1, source_target_pairs={{0,7},{1,0},{2,1},{3,2},{4,3},{5,4},{6,5},{7,6},{8,15},{9,8},{10,9... | collective-permute-start | bytes 540680 | tf_op jit(solution)/shard_map/ppermute | solution.py:49
  114.3 6.8 %collective-permute-start.27 = (bf16[64,1408]{1,0:T(8,128)(2,1)S(1)}, bf16[64,1408]{1,0:T(8,128)(2,1)S(1)}, u32[]{:S(2)}, u32[]{:S(2)}) collective-permute-start(bf16[64,1408]{1,0:T(8,128)(2,1)S(1)} %get-tuple-element.60), channel_id=1, source_target_pairs={{0,1},{1,2},{2,3},{3,4},{4,5},{5,6},{6,7},{7,0},{8,9},{9,10},{10,1... | collective-permute-start | bytes 540680 | tf_op jit(solution)/shard_map/ppermute | solution.py:49
  116.4 5.5 %collective-permute-start.28 = (bf16[64,1408]{1,0:T(8,128)(2,1)S(1)}, bf16[64,1408]{1,0:T(8,128)(2,1)S(1)}, u32[]{:S(2)}, u32[]{:S(2)}) collective-permute-start(bf16[64,1408]{1,0:T(8,128)(2,1)S(1)} %get-tuple-element.61), channel_id=1, source_target_pairs={{0,7},{1,0},{2,1},{3,2},{4,3},{5,4},{6,5},{7,6},{8,15},{9,8},{10,9... | collective-permute-start | bytes 540680 | tf_op jit(solution)/shard_map/ppermute | solution.py:49
  (11 other events, 90.3 us)

commit v5 on v4

--- a/solution.py
+++ b/solution.py
@@ -33,7 +33,7 @@
 TILE = 256
 STEPS = SIDE // TILE
 DEEP = 8
-LINES = 4 * STEPS
+LINES = 2 * STEPS
 WIDTH = 1280
 WIDER = WIDTH + 128
 MARK = 16
@@ -183,28 +183,30 @@
     keep, recv = keep_ref[...], recv_ref[...]
     top = jnp.maximum(keep, recv)
     both = top + jnp.log2(jnp.exp2(keep - top) + jnp.exp2(recv - top))
-    pairs = jnp.broadcast_to(ours_ref[:1, :1] + theirs_ref[:1, :1], (2 * STEPS, TILE))
+    pairs = jnp.broadcast_to(ours_ref[:1, :1] + theirs_ref[:1, :1], (STEPS, TILE))
     first = at_ref[2] == 0
-    block = jnp.concatenate([jnp.where(first, keep, both), jnp.where(first, recv, both), pairs], axis=0)
+    block = jnp.concatenate([jnp.where(first, keep, both), jnp.where(first, recv, pairs)], axis=0)
     for k in range(PEERS):
         out_ref[pl.ds(k * LINES, LINES), :] = block
 
 
 def join_kernel(at_ref, parts_ref, keep_ref, give_ref):
     parts = parts_ref[...].reshape(PEERS, LINES, TILE)
-    pairs = jnp.sum(parts[:, 2 * STEPS : 2 * STEPS + 1, :1], axis=0)
-    parts = parts[:, : 2 * STEPS, :]
     half = lax.broadcasted_iota(jnp.int32, parts.shape, 0) // DEEP
     first = at_ref[2] == 0
-    parts = jnp.where(first | (half == at_ref[4]), parts, LOW)
+    used = first | (half == at_ref[4])
+    pairs = jnp.sum(jnp.where(used, parts, 0.0)[:, STEPS:, :1], axis=0)[:1]
+    parts = jnp.where(used, parts, LOW)
     top = jnp.max(parts, axis=0)
     lse = top + jnp.log2(jnp.sum(jnp.exp2(parts - top[None]), axis=0))
-    columns = jnp.broadcast_to(jnp.sum(lse, keepdims=True) - 2.0 * pairs, (STEPS, TILE))
+    low = jnp.sum(lse[:STEPS], keepdims=True)
+    high = jnp.sum(lse[STEPS:], keepdims=True)
+    term = jnp.broadcast_to(jnp.where(first, low + high, low - 2.0 * pairs), (STEPS, TILE))
     keep_ref[:STEPS, :] = lse[:STEPS]
-    keep_ref[STEPS:, :] = columns
+    keep_ref[STEPS:, :] = term
     turned = jnp.concatenate([lse[STEPS // 2 : STEPS], lse[: STEPS // 2]], axis=0)
     give_ref[:STEPS, :] = jnp.where(first, lse[STEPS:], turned)
-    give_ref[STEPS:, :] = columns
+    give_ref[STEPS:, :] = term
 
 
 def tag(term, rows=PIECE):
@@ -235,7 +237,7 @@
     cols = jnp.where(first, keep, recv)
     col_lse = jnp.concatenate([cols[k : k + 1] for k in range(STEPS)], axis=1)
     rows = jnp.where(first, recv, keep)
-    sums_ref[:STEPS, :] = jnp.broadcast_to(jnp.sum(rows, keepdims=True), (STEPS, 128))
+    sums_ref[:STEPS, :] = jnp.where(first, recv_ref[STEPS:, :128], keep_ref[STEPS:, :128])
     sums_ref[STEPS:, :] = jnp.where(first, keep_ref[STEPS:, :128], recv_ref[STEPS:, :128])
     row_at = lax.broadcasted_iota(jnp.int32, (TILE, 1), 0) - at_ref[3] * PIECE
     col_at = lax.broadcasted_iota(jnp.int32, (1, SIDE), 1) - at_ref[1] * PIECE
@@ -272,7 +274,7 @@
         out_ref[start + PART - MARK : start + PART, :] = mark
 
 
-EARLY = 3
+EARLY = 4
 SPLIT = EARLY * (TILE // PIECE) * PART
 
 
@@ -288,10 +290,10 @@
 
 
 def pieces_kernel(
-    at_ref, scale_ref, weights_ref, turned_ref, image_ref, text_ref, sums_ref, swapped_ref, begun_ref, out_ref, *refs
+    at_ref, scale_ref, weights_ref, text_ref, sums_ref, swapped_ref, begun_ref, out_ref, *refs
 ):
-    own_out, up_out, down_out, *away_refs, mine, parts, ends, back, sem, back_sem = refs
-    begun = run([pltpu.make_async_copy(begun_ref, out_ref.at[pl.ds(0, SPLIT), :], back_sem.at[0])])
+    own_out, up_out, down_out, *away_refs, mine, parts, ends, sem, back_sem = refs
+    begun = run([pltpu.make_async_copy(begun_ref, out_ref, back_sem.at[0])])
     mine[...] = scale_ref[0] * jnp.dot(
         weights_ref[...], text_ref[...], preferred_element_type=F32
     ) + swapped_ref[...].astype(F32)
@@ -309,11 +311,6 @@
     for k, (by, ref) in enumerate(zip(AWAY, away_refs)):
         parts[k] = mine[block(by), :].astype(BF16)
         copies += run([pltpu.make_async_copy(parts.at[k], ref, sem.at[3 + k])])
-    for k in range(EARLY, STEPS):
-        back_tile(k - EARLY, scale_ref, turned_ref.at[pl.ds(EARLY * TILE, SIDE - EARLY * TILE), :], image_ref[...], tag(sums_ref[:1, :1], MARK), back)
-    begun += run([
-        pltpu.make_async_copy(back, out_ref.at[pl.ds(SPLIT, PEERS * PART - SPLIT), :], back_sem.at[1])
-    ])
     wait(begun + copies)
 
 
@@ -436,14 +433,13 @@
     away = [array((PIECE, width), BF16)] * len(AWAY)
     text_parts, own, up, down, *away = call(
         pieces_kernel, [array((PEERS * PART, 128), BF16), array((PIECE, width), F32), end, end, *away],
-        at, scale, weights, turned, image, text, sums, swapped, text_parts,
+        at, scale, weights, text, sums, swapped, text_parts,
         scratch=[
             pltpu.VMEM(half, F32),
             pltpu.VMEM((len(AWAY), PIECE, width), BF16),
             pltpu.VMEM((PIECE, WIDER), BF16),
-            pltpu.VMEM((PEERS * PART - SPLIT, 128), BF16),
             sems((3 + len(AWAY),)),
-            sems((2,)),
+            sems((1,)),
         ],
     )
     text_back = exchange(text_parts, XY)

time: 129 us -> 128 us (level)
    ppermute x29, waiting for transfers between devices: 34.3 us -> 32.8 us  [send(): return lax.ppermute(x, 'd', shift(axis, by))]
  transfers between devices with their start and end apart: 31 -> 31, of which waited for: 19 -> 18; matrix products, arithmetic and copies ran while one was open for 0% -> 0% of each run, Pallas kernels for 14% -> 14%
where the time goes in v5:
time: 128 us
  starting transfers between devices  47.9 us (37%)
  waiting for transfers between devices  34.8 us (27%)
  Pallas kernels  31.1 us (24%)
  blocking collectives  11.3 us (9%)
  between operations  2.27 us (2%)
    ppermute x29, starting transfers between devices, send(): return lax.ppermute(x, 'd', shift(axis, by))  33.7 us
    ppermute x29, waiting for transfers between devices, send(): return lax.ppermute(x, 'd', shift(axis, by))  32.8 us
    pallas_call x13, Pallas kernels, call(): pl.pallas_call(kernel, out_shape=outputs, in_specs=specs, out_specs=jax.t...  31.1 us
    all_to_all x2, starting transfers between devices, exchange(): return lax.all_to_all(x, 'd', 0, 0, axis_index_groups=groups, tiled=True)  14.2 us
    all_to_all x1, blocking collectives, exchange(): return lax.all_to_all(x, 'd', 0, 0, axis_index_groups=groups, tiled=True)  11.3 us
  transfers between devices with their start and end apart: 31, of which 18 were waited for; matrix products, arithmetic and copies ran while one was open for 0% of the time, Pallas kernels for 14%

profile of v5, /device:TPU:28, one launch (start us, length us, event | category | flops | bytes accessed | tf_op | source)
XLA Modules:
  0.0 127.5 jit_solution(17734604399138869819)
XLA Ops:
  0.6 2.7 %shard_map.58 = bf16[1024,1280]{1,0:T(8,128)(2,1)} custom-call(bf16[64,1280]{1,0:T(8,128)(2,1)} %raw_ref.7), custom_call_target="tpu_custom_call" | custom-call | tf_op jit(solution)/shard_map/pallas_call | solution.py:76
  3.3 7.1 %all-to-all-start = ((bf16[16,64,1280]{2,1,0:T(8,128)(2,1)}), bf16[16,64,1280]{2,1,0:T(8,128)(2,1)S(1)}, u32[]{:S(2)}, u32[]{:S(2)}) async-start(bf16[16,64,1280]{2,1,0:T(8,128)(2,1)} %bitcast.17), calls=%async_computation | async-start | bytes 5242880 | tf_op jit(solution)/shard_map/all_to_all | solution.py:53
  11.1 1.7 %shard_map.59 = (bf16[64,1280]{1,0:T(8,128)(2,1)}, f32[8,128]{1,0:T(8,128)S(1)}) custom-call(f32[1]{0:T(128)S(6)} %exp.3.scale_ref, bf16[64,1280]{1,0:T(8,128)(2,1)} %raw_ref.6, bf16[64,1280]{1,0:T(8,128)(2,1)} %raw_ref.7), custom_call_target="tpu_custom_call" | custom-call | tf_op jit(solution)/shard_map/pallas_call | solution.py:76
  12.9 5.9 %collective-permute-start.1 = (bf16[64,1280]{1,0:T(8,128)(2,1)}, bf16[64,1280]{1,0:T(8,128)(2,1)S(1)}, u32[]{:S(2)}, u32[]{:S(2)}) collective-permute-start(bf16[64,1280]{1,0:T(8,128)(2,1)} %get-tuple-element.35.refs_0_), channel_id=1, source_target_pairs={{0,7},{1,0},{2,1},{3,2},{4,3},{5,4},{6,5},{7,6},{8,15},{9,8},{10,9... | collective-permute-start | bytes 491528 | tf_op jit(solution)/shard_map/ppermute | solution.py:49
  18.8 3.2 %collective-permute-done.1.refs_2_ = bf16[64,1280]{1,0:T(8,128)(2,1)S(1)} collective-permute-done((bf16[64,1280]{1,0:T(8,128)(2,1)}, bf16[64,1280]{1,0:T(8,128)(2,1)S(1)}, u32[]{:S(2)}, u32[]{:S(2)}) %collective-permute-start.1) | collective-permute-done | bytes 163872 | tf_op jit(solution)/shard_map/ppermute | solution.py:49
  22.0 3.6 %collective-permute-start.3 = (bf16[64,1280]{1,0:T(8,128)(2,1)S(1)}, bf16[64,1280]{1,0:T(8,128)(2,1)S(1)}, u32[]{:S(2)}, u32[]{:S(2)}) collective-permute-start(bf16[64,1280]{1,0:T(8,128)(2,1)S(1)} %collective-permute-done.1.refs_2_), channel_id=1, source_target_pairs={{0,7},{1,0},{2,1},{3,2},{4,3},{5,4},{6,5},{7,6},{8,15},{9,8},{10,9... | collective-permute-start | bytes 491528 | tf_op jit(solution)/shard_map/ppermute | solution.py:49
  25.6 2.8 %collective-permute-done.3.refs_4_ = bf16[64,1280]{1,0:T(8,128)(2,1)S(1)} collective-permute-done((bf16[64,1280]{1,0:T(8,128)(2,1)S(1)}, bf16[64,1280]{1,0:T(8,128)(2,1)S(1)}, u32[]{:S(2)}, u32[]{:S(2)}) %collective-permute-start.3) | collective-permute-done | bytes 163872 | tf_op jit(solution)/shard_map/ppermute | solution.py:49
  28.5 3.7 %collective-permute-start.5 = (bf16[64,1280]{1,0:T(8,128)(2,1)S(1)}, bf16[64,1280]{1,0:T(8,128)(2,1)S(1)}, u32[]{:S(2)}, u32[]{:S(2)}) collective-permute-start(bf16[64,1280]{1,0:T(8,128)(2,1)S(1)} %collective-permute-done.3.refs_4_), channel_id=1, source_target_pairs={{0,7},{1,0},{2,1},{3,2},{4,3},{5,4},{6,5},{7,6},{8,15},{9,8},{10,9... | collective-permute-start | bytes 491528 | tf_op jit(solution)/shard_map/ppermute | solution.py:49
  32.8 2.2 %collective-permute-done.5.refs_6_ = bf16[64,1280]{1,0:T(8,128)(2,1)S(1)} collective-permute-done((bf16[64,1280]{1,0:T(8,128)(2,1)S(1)}, bf16[64,1280]{1,0:T(8,128)(2,1)S(1)}, u32[]{:S(2)}, u32[]{:S(2)}) %collective-permute-start.5) | collective-permute-done | bytes 163872 | tf_op jit(solution)/shard_map/ppermute | solution.py:49
  35.0 4.0 %collective-permute-done.4.refs_5_ = bf16[64,1280]{1,0:T(8,128)(2,1)S(1)} collective-permute-done((bf16[64,1280]{1,0:T(8,128)(2,1)}, bf16[64,1280]{1,0:T(8,128)(2,1)S(1)}, u32[]{:S(2)}, u32[]{:S(2)}) %collective-permute-start.4) | collective-permute-done | bytes 163872 | tf_op jit(solution)/shard_map/ppermute | solution.py:49
  39.4 1.7 %collective-permute-start.6 = (bf16[32,1280]{1,0:T(8,128)(2,1)S(1)}, bf16[32,1280]{1,0:T(8,128)(2,1)}, u32[]{:S(2)}, u32[]{:S(2)}) collective-permute-start(bf16[32,1280]{1,0:T(8,128)(2,1)S(1)} %slice.8), channel_id=1, source_target_pairs={{0,1},{1,2},{2,3},{3,4},{4,5},{5,6},{6,7},{7,0},{8,9},{9,10},{10,1... | collective-permute-start | bytes 245768 | tf_op jit(solution)/shard_map/ppermute | solution.py:49
  41.8 2.3 %collective-permute-done.7.refs_8_ = bf16[32,1280]{1,0:T(8,128)(2,1)} collective-permute-done((bf16[32,1280]{1,0:T(8,128)(2,1)S(1)}, bf16[32,1280]{1,0:T(8,128)(2,1)}, u32[]{:S(2)}, u32[]{:S(2)}) %collective-permute-start.7) | collective-permute-done | bytes 81952 | tf_op jit(solution)/shard_map/ppermute | solution.py:49
  47.1 6.3 %shard_map.60 = (bf16[1024,1280]{1,0:T(8,128)(2,1)}, f32[1024,1024]{1,0:T(8,128)S(1)}, f32[4,256]{1,0:T(4,128)S(1)}, f32[4,256]{1,0:T(4,128)S(1)}) custom-call(s32[5]{0:T(128)S(1)} %stack.23.at_ref, f32[1]{0:T(128)S(6)} %exp.3.scale_ref, bf16[1024,1280]{1,0:T(8,128)(2,1)S(1)} %bitcast.11, bf16[64,1280]{1,0:T(8,128)(2,1)} %get-tuple-element.35.refs_0_, ...), custom_call_target="tpu_custom_call" | custom-call | tf_op jit(solution)/shard_map/pallas_call | solution.py:76
  55.2 11.3 %all_to_all.33 = f32[16,8,256]{2,1,0:T(8,128)S(1)} all-to-all(f32[16,8,256]{2,1,0:T(8,128)S(1)} %bitcast.15), channel_id=1, replica_groups={{0,16,32,48,64,80,96,112,128,144,160,176,192,208,224,240},{1,17,33,49,6..., dimensions={0} | all-to-all | bytes 262144 | tf_op jit(solution)/shard_map/all_to_all | solution.py:53
  67.2 2.3 %collective-permute-start.19 = (f32[8,256]{1,0:T(8,128)S(1)}, f32[8,256]{1,0:T(8,128)S(1)}, u32[]{:S(2)}, u32[]{:S(2)}) collective-permute-start(f32[8,256]{1,0:T(8,128)S(1)} %get-tuple-element.41), channel_id=1, source_target_pairs={{0,8},{1,9},{2,10},{3,11},{4,12},{5,13},{6,14},{7,15},{8,0},{9,1},... | collective-permute-start | bytes 24584 | tf_op jit(solution)/shard_map/ppermute | solution.py:49
  70.4 2.9 %shard_map.63 = (bf16[512,1024]{1,0:T(8,128)(2,1)S(1)}, bf16[1024,1024]{1,0:T(8,128)(2,1)S(1)}, bf16[512,1280]{1,0:T(8,128)(2,1)S(1)}, f32[8,128]{1,0:T(8,128)S(1)}) custom-call(s32[5]{0:T(128)S(1)} %stack.23.at_ref, f32[1]{0:T(128)S(6)} %exp.3.scale_ref, f32[1024,1024]{1,0:T(8,128)S(1)} %get-tuple-element.36.logits_ref, bf16[1024,1280]{1,0:T(8,128)(2,1)S(1)} %bitcast.12, ...), custom_call_target="tpu_custom_call" | custom-call | tf_op jit(solution)/shard_map/pallas_call | solution.py:76
  73.7 2.9 %shard_map.64.begun_ref = bf16[10496,128]{1,0:T(8,128)(2,1)S(1)} custom-call(f32[1]{0:T(128)S(6)} %exp.3.scale_ref, bf16[1024,1024]{1,0:T(8,128)(2,1)S(1)} %get-tuple-element.45.turned_ref, bf16[1024,1280]{1,0:T(8,128)(2,1)S(1)} %copy-done, f32[8,128]{1,0:T(8,128)S(1)} %get-tuple-element.42.sums_ref), custom_call_target="tpu_custom_call" | custom-call | tf_op jit(solution)/shard_map/pallas_call | solution.py:76
  76.6 4.2 %shard_map.65 = (bf16[10496,128]{1,0:T(8,128)(2,1)}, f32[64,1280]{1,0:T(8,128)}, bf16[32,1408]{1,0:T(8,128)(2,1)}, bf16[32,1408]{1,0:T(8,128)(2,1)}, bf16[64,128...) custom-call(s32[5]{0:T(128)S(1)} %stack.23.at_ref, ...), custom_call_target="tpu_custom_call" | custom-call | tf_op jit(solution)/shard_map/pallas_call | solution.py:76
  80.8 7.1 %all-to-all-start.2 = ((bf16[16,656,128]{2,1,0:T(8,128)(2,1)}), bf16[16,656,128]{2,1,0:T(8,128)(2,1)S(1)}, u32[]{:S(2)}, u32[]{:S(2)}) async-start(bf16[16,656,128]{2,1,0:T(8,128)(2,1)} %bitcast.18), calls=%async_computation.2 | async-start | bytes 5373952 | tf_op jit(solution)/shard_map/all_to_all | solution.py:53
  87.9 1.7 %collective-permute-start.21 = (bf16[32,1408]{1,0:T(8,128)(2,1)S(1)}, bf16[32,1408]{1,0:T(8,128)(2,1)S(1)}, u32[]{:S(2)}, u32[]{:S(2)}) collective-permute-start(bf16[32,1408]{1,0:T(8,128)(2,1)S(1)} %copy-done.11), channel_id=1, source_target_pairs={{0,1},{1,2},{2,3},{3,4},{4,5},{5,6},{6,7},{7,0},{8,9},{9,10},{10,1... | collective-permute-start | bytes 270344 | tf_op jit(solution)/shard_map/ppermute | solution.py:49
  89.6 1.9 %collective-permute-start.22 = (bf16[32,1408]{1,0:T(8,128)(2,1)S(1)}, bf16[32,1408]{1,0:T(8,128)(2,1)S(1)}, u32[]{:S(2)}, u32[]{:S(2)}) collective-permute-start(bf16[32,1408]{1,0:T(8,128)(2,1)S(1)} %copy-done.10), channel_id=1, source_target_pairs={{0,7},{1,0},{2,1},{3,2},{4,3},{5,4},{6,5},{7,6},{8,15},{9,8},{10,9... | collective-permute-start | bytes 270344 | tf_op jit(solution)/shard_map/ppermute | solution.py:49
  91.4 2.5 %collective-permute-done.21.below_ref = bf16[32,1408]{1,0:T(8,128)(2,1)S(1)} collective-permute-done((bf16[32,1408]{1,0:T(8,128)(2,1)S(1)}, bf16[32,1408]{1,0:T(8,128)(2,1)S(1)}, u32[]{:S(2)}, u32[]{:S(2)}) %collective-permute-start.21) | collective-permute-done | bytes 90144 | tf_op jit(solution)/shard_map/ppermute | solution.py:49
  96.5 2.5 %collective-permute-start.24 = (bf16[64,1408]{1,0:T(8,128)(2,1)S(1)}, bf16[64,1408]{1,0:T(8,128)(2,1)S(1)}, u32[]{:S(2)}, u32[]{:S(2)}) collective-permute-start(bf16[64,1408]{1,0:T(8,128)(2,1)S(1)} %get-tuple-element.57), channel_id=1, source_target_pairs={{0,7},{1,0},{2,1},{3,2},{4,3},{5,4},{6,5},{7,6},{8,15},{9,8},{10,9... | collective-permute-start | bytes 540680 | tf_op jit(solution)/shard_map/ppermute | solution.py:49
  99.0 3.5 %collective-permute-done.23.below_ref = bf16[64,1408]{1,0:T(8,128)(2,1)S(1)} collective-permute-done((bf16[64,1408]{1,0:T(8,128)(2,1)S(1)}, bf16[64,1408]{1,0:T(8,128)(2,1)S(1)}, u32[]{:S(2)}, u32[]{:S(2)}) %collective-permute-start.23) | collective-permute-done | bytes 180256 | tf_op jit(solution)/shard_map/ppermute | solution.py:49
  104.1 1.7 %collective-permute-start.25 = (bf16[64,1408]{1,0:T(8,128)(2,1)S(1)}, bf16[64,1408]{1,0:T(8,128)(2,1)S(1)}, u32[]{:S(2)}, u32[]{:S(2)}) collective-permute-start(bf16[64,1408]{1,0:T(8,128)(2,1)S(1)} %get-tuple-element.58), channel_id=1, source_target_pairs={{0,1},{1,2},{2,3},{3,4},{4,5},{5,6},{6,7},{7,0},{8,9},{9,10},{10,1... | collective-permute-start | bytes 540680 | tf_op jit(solution)/shard_map/ppermute | solution.py:49
  105.7 1.7 %collective-permute-start.26 = (bf16[64,1408]{1,0:T(8,128)(2,1)S(1)}, bf16[64,1408]{1,0:T(8,128)(2,1)S(1)}, u32[]{:S(2)}, u32[]{:S(2)}) collective-permute-start(bf16[64,1408]{1,0:T(8,128)(2,1)S(1)} %get-tuple-element.59), channel_id=1, source_target_pairs={{0,7},{1,0},{2,1},{3,2},{4,3},{5,4},{6,5},{7,6},{8,15},{9,8},{10,9... | collective-permute-start | bytes 540680 | tf_op jit(solution)/shard_map/ppermute | solution.py:49
  107.5 3.4 %collective-permute-done.25.below_ref = bf16[64,1408]{1,0:T(8,128)(2,1)S(1)} collective-permute-done((bf16[64,1408]{1,0:T(8,128)(2,1)S(1)}, bf16[64,1408]{1,0:T(8,128)(2,1)S(1)}, u32[]{:S(2)}, u32[]{:S(2)}) %collective-permute-start.25) | collective-permute-done | bytes 180256 | tf_op jit(solution)/shard_map/ppermute | solution.py:49
  112.8 2.1 %collective-permute-start.27 = (bf16[64,1408]{1,0:T(8,128)(2,1)S(1)}, bf16[64,1408]{1,0:T(8,128)(2,1)S(1)}, u32[]{:S(2)}, u32[]{:S(2)}) collective-permute-start(bf16[64,1408]{1,0:T(8,128)(2,1)S(1)} %get-tuple-element.60), channel_id=1, source_target_pairs={{0,1},{1,2},{2,3},{3,4},{4,5},{5,6},{6,7},{7,0},{8,9},{9,10},{10,1... | collective-permute-start | bytes 540680 | tf_op jit(solution)/shard_map/ppermute | solution.py:49
  116.1 3.5 %collective-permute-done.27.below_ref = bf16[64,1408]{1,0:T(8,128)(2,1)S(1)} collective-permute-done((bf16[64,1408]{1,0:T(8,128)(2,1)S(1)}, bf16[64,1408]{1,0:T(8,128)(2,1)S(1)}, u32[]{:S(2)}, u32[]{:S(2)}) %collective-permute-start.27) | collective-permute-done | bytes 180256 | tf_op jit(solution)/shard_map/ppermute | solution.py:49
  120.4 2.5 %shard_map.69 = (bf16[64,1280]{1,0:T(8,128)(2,1)}, f32[8,128]{1,0:T(8,128)S(1)}) custom-call(s32[5]{0:T(128)S(1)} %stack.23.at_ref, f32[8,128]{1,0:T(8,128)S(1)} %get-tuple-element.42.sums_ref, bf16[64,1280]{1,0:T(8,128)(2,1)} %raw_ref.6, f32[64,1280]{1,0:T(8,128)} %get-tuple-element.47.own_ref, bf16[64,1408]{1,0:T(8,128)(2,1)S(1)} %collective-permute-done.27.below_ref, ...), custom_call_target="tpu_custom_call" | custom-call | tf_op jit(solution)/shard_map/pallas_call | solution.py:76
  123.0 2.1 %all-to-all-done.2 = bf16[16,656,128]{2,1,0:T(8,128)(2,1)S(1)} async-done(((bf16[16,656,128]{2,1,0:T(8,128)(2,1)}), bf16[16,656,128]{2,1,0:T(8,128)(2,1)S(1)}, u32[]{:S(2)}, u32[]{:S(2)}) %all-to-all-start.2) | async-done | bytes 2687008 | tf_op jit(solution)/shard_map/all_to_all | solution.py:53
  125.0 1.8 %shard_map.70 = (bf16[64,1280]{1,0:T(8,128)(2,1)}, f32[1]{0:T(128)S(4)}) custom-call(bf16[64,1280]{1,0:T(8,128)(2,1)} %raw_ref.7, f32[8,128]{1,0:T(8,128)S(1)} %get-tuple-element.62.loss_ref, bf16[10496,128]{1,0:T(8,128)(2,1)S(1)} %bitcast.14), custom_call_target="tpu_custom_call" | custom-call | tf_op jit(solution)/shard_map/pallas_call | solution.py:76
  (71 shorter events, 16.6 us)
Async XLA Ops:
  3.3 43.7 %all-to-all-start = ((bf16[16,64,1280]{2,1,0:T(8,128)(2,1)}), bf16[16,64,1280]{2,1,0:T(8,128)(2,1)S(1)}, u32[]{:S(2)}, u32[]{:S(2)}) async-start(bf16[16,64,1280]{2,1,0:T(8,128)(2,1)} %bitcast.17), calls=%async_computation | async-start | bytes 5242880 | tf_op jit(solution)/shard_map/all_to_all | solution.py:53
  12.9 9.1 %collective-permute-start.1 = (bf16[64,1280]{1,0:T(8,128)(2,1)}, bf16[64,1280]{1,0:T(8,128)(2,1)S(1)}, u32[]{:S(2)}, u32[]{:S(2)}) collective-permute-start(bf16[64,1280]{1,0:T(8,128)(2,1)} %get-tuple-element.35.refs_0_), channel_id=1, source_target_pairs={{0,7},{1,0},{2,1},{3,2},{4,3},{5,4},{6,5},{7,6},{8,15},{9,8},{10,9... | collective-permute-start | bytes 491528 | tf_op jit(solution)/shard_map/ppermute | solution.py:49
  18.8 6.8 %collective-permute-start = (bf16[64,1280]{1,0:T(8,128)(2,1)}, bf16[64,1280]{1,0:T(8,128)(2,1)S(1)}, u32[]{:S(2)}, u32[]{:S(2)}) collective-permute-start(bf16[64,1280]{1,0:T(8,128)(2,1)} %get-tuple-element.35.refs_0_), channel_id=1, source_target_pairs={{0,1},{1,2},{2,3},{3,4},{4,5},{5,6},{6,7},{7,0},{8,9},{9,10},{10,1... | collective-permute-start | bytes 491528 | tf_op jit(solution)/shard_map/ppermute | solution.py:49
  22.0 25.0 %copy-start.3 = (bf16[64,1280]{1,0:T(8,128)(2,1)}, bf16[64,1280]{1,0:T(8,128)(2,1)S(1)}, u32[]{:S(2)}) copy-start(bf16[64,1280]{1,0:T(8,128)(2,1)S(1)} %collective-permute-done.1.refs_2_) | copy-start | bytes 491524
  22.0 6.4 %collective-permute-start.3 = (bf16[64,1280]{1,0:T(8,128)(2,1)S(1)}, bf16[64,1280]{1,0:T(8,128)(2,1)S(1)}, u32[]{:S(2)}, u32[]{:S(2)}) collective-permute-start(bf16[64,1280]{1,0:T(8,128)(2,1)S(1)} %collective-permute-done.1.refs_2_), channel_id=1, source_target_pairs={{0,7},{1,0},{2,1},{3,2},{4,3},{5,4},{6,5},{7,6},{8,15},{9,8},{10,9... | collective-permute-start | bytes 491528 | tf_op jit(solution)/shard_map/ppermute | solution.py:49
  25.6 6.6 %collective-permute-start.2 = (bf16[64,1280]{1,0:T(8,128)(2,1)S(1)}, bf16[64,1280]{1,0:T(8,128)(2,1)}, u32[]{:S(2)}, u32[]{:S(2)}) collective-permute-start(bf16[64,1280]{1,0:T(8,128)(2,1)S(1)} %collective-permute-done.refs_1_), channel_id=1, source_target_pairs={{0,1},{1,2},{2,3},{3,4},{4,5},{5,6},{6,7},{7,0},{8,9},{9,10},{10,1... | collective-permute-start | bytes 491528 | tf_op jit(solution)/shard_map/ppermute | solution.py:49
  28.5 6.5 %collective-permute-start.5 = (bf16[64,1280]{1,0:T(8,128)(2,1)S(1)}, bf16[64,1280]{1,0:T(8,128)(2,1)S(1)}, u32[]{:S(2)}, u32[]{:S(2)}) collective-permute-start(bf16[64,1280]{1,0:T(8,128)(2,1)S(1)} %collective-permute-done.3.refs_4_), channel_id=1, source_target_pairs={{0,7},{1,0},{2,1},{3,2},{4,3},{5,4},{6,5},{7,6},{8,15},{9,8},{10,9... | collective-permute-start | bytes 491528 | tf_op jit(solution)/shard_map/ppermute | solution.py:49
  32.3 6.7 %collective-permute-start.4 = (bf16[64,1280]{1,0:T(8,128)(2,1)}, bf16[64,1280]{1,0:T(8,128)(2,1)S(1)}, u32[]{:S(2)}, u32[]{:S(2)}) collective-permute-start(bf16[64,1280]{1,0:T(8,128)(2,1)} %collective-permute-done.2.refs_3_), channel_id=1, source_target_pairs={{0,1},{1,2},{2,3},{3,4},{4,5},{5,6},{6,7},{7,0},{8,9},{9,10},{10,1... | collective-permute-start | bytes 491528 | tf_op jit(solution)/shard_map/ppermute | solution.py:49
  32.3 6.8 %collective-permute-start.8 = (bf16[64,1280]{1,0:T(8,128)(2,1)}, bf16[64,1280]{1,0:T(8,128)(2,1)S(1)}, u32[]{:S(2)}, u32[]{:S(2)}) collective-permute-start(bf16[64,1280]{1,0:T(8,128)(2,1)} %get-tuple-element.35.refs_0_), channel_id=1, source_target_pairs={{0,8},{1,9},{2,10},{3,11},{4,12},{5,13},{6,14},{7,15},{8,0},{9,1},... | collective-permute-start | bytes 491528 | tf_op jit(solution)/shard_map/ppermute | solution.py:49
  32.3 7.1 %collective-permute-start.10 = (bf16[64,1280]{1,0:T(8,128)(2,1)S(1)}, bf16[64,1280]{1,0:T(8,128)(2,1)S(1)}, u32[]{:S(2)}, u32[]{:S(2)}) collective-permute-start(bf16[64,1280]{1,0:T(8,128)(2,1)S(1)} %collective-permute-done.1.refs_2_), channel_id=1, source_target_pairs={{0,8},{1,9},{2,10},{3,11},{4,12},{5,13},{6,14},{7,15},{8,0},{9,1},... | collective-permute-start | bytes 491528 | tf_op jit(solution)/shard_map/ppermute | solution.py:49
  32.8 8.4 %collective-permute-start.9 = (bf16[64,1280]{1,0:T(8,128)(2,1)S(1)}, bf16[64,1280]{1,0:T(8,128)(2,1)S(1)}, u32[]{:S(2)}, u32[]{:S(2)}) collective-permute-start(bf16[64,1280]{1,0:T(8,128)(2,1)S(1)} %collective-permute-done.refs_1_), channel_id=1, source_target_pairs={{0,8},{1,9},{2,10},{3,11},{4,12},{5,13},{6,14},{7,15},{8,0},{9,1},... | collective-permute-start | bytes 491528 | tf_op jit(solution)/shard_map/ppermute | solution.py:49
  35.0 6.2 %collective-permute-start.12 = (bf16[64,1280]{1,0:T(8,128)(2,1)S(1)}, bf16[64,1280]{1,0:T(8,128)(2,1)S(1)}, u32[]{:S(2)}, u32[]{:S(2)}) collective-permute-start(bf16[64,1280]{1,0:T(8,128)(2,1)S(1)} %collective-permute-done.3.refs_4_), channel_id=1, source_target_pairs={{0,8},{1,9},{2,10},{3,11},{4,12},{5,13},{6,14},{7,15},{8,0},{9,1},... | collective-permute-start | bytes 491528 | tf_op jit(solution)/shard_map/ppermute | solution.py:49
  39.0 6.5 %collective-permute-start.11 = (bf16[64,1280]{1,0:T(8,128)(2,1)}, bf16[64,1280]{1,0:T(8,128)(2,1)}, u32[]{:S(2)}, u32[]{:S(2)}) collective-permute-start(bf16[64,1280]{1,0:T(8,128)(2,1)} %collective-permute-done.2.refs_3_), channel_id=1, source_target_pairs={{0,8},{1,9},{2,10},{3,11},{4,12},{5,13},{6,14},{7,15},{8,0},{9,1},... | collective-permute-start | bytes 491528 | tf_op jit(solution)/shard_map/ppermute | solution.py:49
  39.0 5.0 %collective-permute-start.7 = (bf16[32,1280]{1,0:T(8,128)(2,1)S(1)}, bf16[32,1280]{1,0:T(8,128)(2,1)}, u32[]{:S(2)}, u32[]{:S(2)}) collective-permute-start(bf16[32,1280]{1,0:T(8,128)(2,1)S(1)} %slice.9), channel_id=1, source_target_pairs={{0,7},{1,0},{2,1},{3,2},{4,3},{5,4},{6,5},{7,6},{8,15},{9,8},{10,9... | collective-permute-start | bytes 245768 | tf_op jit(solution)/shard_map/ppermute | solution.py:49
  39.4 6.0 %collective-permute-start.6 = (bf16[32,1280]{1,0:T(8,128)(2,1)S(1)}, bf16[32,1280]{1,0:T(8,128)(2,1)}, u32[]{:S(2)}, u32[]{:S(2)}) collective-permute-start(bf16[32,1280]{1,0:T(8,128)(2,1)S(1)} %slice.8), channel_id=1, source_target_pairs={{0,1},{1,2},{2,3},{3,4},{4,5},{5,6},{6,7},{7,0},{8,9},{9,10},{10,1... | collective-permute-start | bytes 245768 | tf_op jit(solution)/shard_map/ppermute | solution.py:49
  41.2 5.0 %collective-permute-start.14 = (bf16[64,1280]{1,0:T(8,128)(2,1)S(1)}, bf16[64,1280]{1,0:T(8,128)(2,1)}, u32[]{:S(2)}, u32[]{:S(2)}) collective-permute-start(bf16[64,1280]{1,0:T(8,128)(2,1)S(1)} %collective-permute-done.5.refs_6_), channel_id=1, source_target_pairs={{0,8},{1,9},{2,10},{3,11},{4,12},{5,13},{6,14},{7,15},{8,0},{9,1},... | collective-permute-start | bytes 491528 | tf_op jit(solution)/shard_map/ppermute | solution.py:49
  41.2 5.8 %collective-permute-start.13 = (bf16[64,1280]{1,0:T(8,128)(2,1)S(1)}, bf16[64,1280]{1,0:T(8,128)(2,1)}, u32[]{:S(2)}, u32[]{:S(2)}) collective-permute-start(bf16[64,1280]{1,0:T(8,128)(2,1)S(1)} %collective-permute-done.4.refs_5_), channel_id=1, source_target_pairs={{0,8},{1,9},{2,10},{3,11},{4,12},{5,13},{6,14},{7,15},{8,0},{9,1},... | collective-permute-start | bytes 491528 | tf_op jit(solution)/shard_map/ppermute | solution.py:49
  44.1 2.1 %collective-permute-start.16 = (bf16[32,1280]{1,0:T(8,128)(2,1)}, bf16[32,1280]{1,0:T(8,128)(2,1)}, u32[]{:S(2)}, u32[]{:S(2)}) collective-permute-start(bf16[32,1280]{1,0:T(8,128)(2,1)} %collective-permute-done.7.refs_8_), channel_id=1, source_target_pairs={{0,8},{1,9},{2,10},{3,11},{4,12},{5,13},{6,14},{7,15},{8,0},{9,1},... | collective-permute-start | bytes 245768 | tf_op jit(solution)/shard_map/ppermute | solution.py:49
  45.4 1.6 %collective-permute-start.15 = (bf16[32,1280]{1,0:T(8,128)(2,1)}, bf16[32,1280]{1,0:T(8,128)(2,1)}, u32[]{:S(2)}, u32[]{:S(2)}) collective-permute-start(bf16[32,1280]{1,0:T(8,128)(2,1)} %collective-permute-done.6.refs_7_), channel_id=1, source_target_pairs={{0,8},{1,9},{2,10},{3,11},{4,12},{5,13},{6,14},{7,15},{8,0},{9,1},... | collective-permute-start | bytes 245768 | tf_op jit(solution)/shard_map/ppermute | solution.py:49
  45.5 8.1 %collective-permute-start.18 = (f32[8,128]{1,0:T(8,128)S(1)}, f32[8,128]{1,0:T(8,128)S(1)}, u32[]{:S(2)}, u32[]{:S(2)}) collective-permute-start(f32[8,128]{1,0:T(8,128)S(1)} %get-tuple-element.39.ours_ref), channel_id=1, source_target_pairs={{0,8},{1,9},{2,10},{3,11},{4,12},{5,13},{6,14},{7,15},{8,0},{9,1},... | collective-permute-start | bytes 12296 | tf_op jit(solution)/shard_map/ppermute | solution.py:49
  53.4 1.3 collective-permute-start.17
  67.2 3.1 %collective-permute-start.19 = (f32[8,256]{1,0:T(8,128)S(1)}, f32[8,256]{1,0:T(8,128)S(1)}, u32[]{:S(2)}, u32[]{:S(2)}) collective-permute-start(f32[8,256]{1,0:T(8,128)S(1)} %get-tuple-element.41), channel_id=1, source_target_pairs={{0,8},{1,9},{2,10},{3,11},{4,12},{5,13},{6,14},{7,15},{8,0},{9,1},... | collective-permute-start | bytes 24584 | tf_op jit(solution)/shard_map/ppermute | solution.py:49
  73.2 3.4 %collective-permute-start.20 = (bf16[512,1280]{1,0:T(8,128)(2,1)S(1)}, bf16[512,1280]{1,0:T(8,128)(2,1)S(1)}, u32[]{:S(2)}, u32[]{:S(2)}) collective-permute-start(bf16[512,1280]{1,0:T(8,128)(2,1)S(1)} %get-tuple-element.44), channel_id=1, source_target_pairs={{0,8},{1,9},{2,10},{3,11},{4,12},{5,13},{6,14},{7,15},{8,0},{9,1},... | collective-permute-start | bytes 3932168 | tf_op jit(solution)/shard_map/ppermute | solution.py:49
  80.8 44.2 %all-to-all-start.2 = ((bf16[16,656,128]{2,1,0:T(8,128)(2,1)}), bf16[16,656,128]{2,1,0:T(8,128)(2,1)S(1)}, u32[]{:S(2)}, u32[]{:S(2)}) async-start(bf16[16,656,128]{2,1,0:T(8,128)(2,1)} %bitcast.18), calls=%async_computation.2 | async-start | bytes 5373952 | tf_op jit(solution)/shard_map/all_to_all | solution.py:53
  87.9 6.0 %collective-permute-start.21 = (bf16[32,1408]{1,0:T(8,128)(2,1)S(1)}, bf16[32,1408]{1,0:T(8,128)(2,1)S(1)}, u32[]{:S(2)}, u32[]{:S(2)}) collective-permute-start(bf16[32,1408]{1,0:T(8,128)(2,1)S(1)} %copy-done.11), channel_id=1, source_target_pairs={{0,1},{1,2},{2,3},{3,4},{4,5},{5,6},{6,7},{7,0},{8,9},{9,10},{10,1... | collective-permute-start | bytes 270344 | tf_op jit(solution)/shard_map/ppermute | solution.py:49
  89.6 4.5 %collective-permute-start.22 = (bf16[32,1408]{1,0:T(8,128)(2,1)S(1)}, bf16[32,1408]{1,0:T(8,128)(2,1)S(1)}, u32[]{:S(2)}, u32[]{:S(2)}) collective-permute-start(bf16[32,1408]{1,0:T(8,128)(2,1)S(1)} %copy-done.10), channel_id=1, source_target_pairs={{0,7},{1,0},{2,1},{3,2},{4,3},{5,4},{6,5},{7,6},{8,15},{9,8},{10,9... | collective-permute-start | bytes 270344 | tf_op jit(solution)/shard_map/ppermute | solution.py:49
  95.7 6.8 %collective-permute-start.23 = (bf16[64,1408]{1,0:T(8,128)(2,1)S(1)}, bf16[64,1408]{1,0:T(8,128)(2,1)S(1)}, u32[]{:S(2)}, u32[]{:S(2)}) collective-permute-start(bf16[64,1408]{1,0:T(8,128)(2,1)S(1)} %get-tuple-element.56), channel_id=1, source_target_pairs={{0,1},{1,2},{2,3},{3,4},{4,5},{5,6},{6,7},{7,0},{8,9},{9,10},{10,1... | collective-permute-start | bytes 540680 | tf_op jit(solution)/shard_map/ppermute | solution.py:49
  96.5 6.0 %collective-permute-start.24 = (bf16[64,1408]{1,0:T(8,128)(2,1)S(1)}, bf16[64,1408]{1,0:T(8,128)(2,1)S(1)}, u32[]{:S(2)}, u32[]{:S(2)}) collective-permute-start(bf16[64,1408]{1,0:T(8,128)(2,1)S(1)} %get-tuple-element.57), channel_id=1, source_target_pairs={{0,7},{1,0},{2,1},{3,2},{4,3},{5,4},{6,5},{7,6},{8,15},{9,8},{10,9... | collective-permute-start | bytes 540680 | tf_op jit(solution)/shard_map/ppermute | solution.py:49
  104.1 6.8 %collective-permute-start.25 = (bf16[64,1408]{1,0:T(8,128)(2,1)S(1)}, bf16[64,1408]{1,0:T(8,128)(2,1)S(1)}, u32[]{:S(2)}, u32[]{:S(2)}) collective-permute-start(bf16[64,1408]{1,0:T(8,128)(2,1)S(1)} %get-tuple-element.58), channel_id=1, source_target_pairs={{0,1},{1,2},{2,3},{3,4},{4,5},{5,6},{6,7},{7,0},{8,9},{9,10},{10,1... | collective-permute-start | bytes 540680 | tf_op jit(solution)/shard_map/ppermute | solution.py:49
  105.7 5.5 %collective-permute-start.26 = (bf16[64,1408]{1,0:T(8,128)(2,1)S(1)}, bf16[64,1408]{1,0:T(8,128)(2,1)S(1)}, u32[]{:S(2)}, u32[]{:S(2)}) collective-permute-start(bf16[64,1408]{1,0:T(8,128)(2,1)S(1)} %get-tuple-element.59), channel_id=1, source_target_pairs={{0,7},{1,0},{2,1},{3,2},{4,3},{5,4},{6,5},{7,6},{8,15},{9,8},{10,9... | collective-permute-start | bytes 540680 | tf_op jit(solution)/shard_map/ppermute | solution.py:49
  112.8 6.8 %collective-permute-start.27 = (bf16[64,1408]{1,0:T(8,128)(2,1)S(1)}, bf16[64,1408]{1,0:T(8,128)(2,1)S(1)}, u32[]{:S(2)}, u32[]{:S(2)}) collective-permute-start(bf16[64,1408]{1,0:T(8,128)(2,1)S(1)} %get-tuple-element.60), channel_id=1, source_target_pairs={{0,1},{1,2},{2,3},{3,4},{4,5},{5,6},{6,7},{7,0},{8,9},{9,10},{10,1... | collective-permute-start | bytes 540680 | tf_op jit(solution)/shard_map/ppermute | solution.py:49
  114.9 5.5 %collective-permute-start.28 = (bf16[64,1408]{1,0:T(8,128)(2,1)S(1)}, bf16[64,1408]{1,0:T(8,128)(2,1)S(1)}, u32[]{:S(2)}, u32[]{:S(2)}) collective-permute-start(bf16[64,1408]{1,0:T(8,128)(2,1)S(1)} %get-tuple-element.61), channel_id=1, source_target_pairs={{0,7},{1,0},{2,1},{3,2},{4,3},{5,4},{6,5},{7,6},{8,15},{9,8},{10,9... | collective-permute-start | bytes 540680 | tf_op jit(solution)/shard_map/ppermute | solution.py:49
  (11 other events, 89.6 us)

commit v6 on v5

--- a/solution.py
+++ b/solution.py
@@ -35,7 +35,6 @@
 DEEP = 8
 LINES = 2 * STEPS
 WIDTH = 1280
-WIDER = WIDTH + 128
 MARK = 16
 PART = PIECE * (WIDTH // 128) + MARK
 
@@ -136,7 +135,7 @@
     return jnp.broadcast_to(lanes, (128, lanes.shape[1])).T[:, :1]
 
 
-def logits_kernel(plan, at_ref, scale_ref, text_ref, *refs):
+def logits_kernel(plan, at_ref, scale_ref, pairs_ref, text_ref, *refs):
     pieces = refs[: len(plan)]
     image_out, logits_ref, keep_ref, give_ref, image_ref, sem, out_sem = refs[len(plan) :]
     core = at_ref[2]
@@ -176,14 +175,15 @@
         part = col_lse[:, k * TILE : (k + 1) * TILE]
         keep_ref[k : k + 1, :] = jnp.where(first, part, row_lse[k])
         give_ref[k : k + 1, :] = jnp.where(first, row_lse[(k + STEPS // 2) % STEPS], part)
+    give_ref[STEPS:, :] = jnp.broadcast_to(pairs_ref[:1, :1], (STEPS, TILE))
     wait(out)
 
 
-def spread_kernel(at_ref, keep_ref, recv_ref, ours_ref, theirs_ref, out_ref):
-    keep, recv = keep_ref[...], recv_ref[...]
+def spread_kernel(at_ref, keep_ref, recv_ref, pairs_ref, out_ref):
+    keep, recv = keep_ref[...], recv_ref[:STEPS, :]
     top = jnp.maximum(keep, recv)
     both = top + jnp.log2(jnp.exp2(keep - top) + jnp.exp2(recv - top))
-    pairs = jnp.broadcast_to(ours_ref[:1, :1] + theirs_ref[:1, :1], (STEPS, TILE))
+    pairs = recv_ref[STEPS:, :] + pairs_ref[:1, :1]
     first = at_ref[2] == 0
     block = jnp.concatenate([jnp.where(first, keep, both), jnp.where(first, recv, pairs)], axis=0)
     for k in range(PEERS):
@@ -259,59 +259,56 @@
             ).astype(BF16)
 
 
-def back_tile(k, scale_ref, turned_ref, image, mark, out_ref):
-    tile = slice(k * TILE, (k + 1) * TILE)
-    term = (
-        scale_ref[0] * jnp.dot(turned_ref[tile, :], image, preferred_element_type=F32)
-    ).astype(BF16)
-    peers = TILE // PIECE
-    for p in range(peers):
-        start = (k * peers + p) * PART
-        for b in range(WIDTH // 128):
-            out_ref[start + b * PIECE : start + (b + 1) * PIECE, :] = (
-                term[p * PIECE : (p + 1) * PIECE, b * 128 : (b + 1) * 128]
-            )
-        out_ref[start + PART - MARK : start + PART, :] = mark
-
-
-EARLY = 4
-SPLIT = EARLY * (TILE // PIECE) * PART
-
-
-def text_back_kernel(scale_ref, turned_ref, image_ref, sums_ref, out_ref):
+def text_back_kernel(scale_ref, weights_ref, turned_ref, image_ref, text_ref, sums_ref, out_ref, mine_ref, back, sem):
     image = image_ref[...]
     mark = tag(sums_ref[:1, :1], MARK)
-    for k in range(EARLY):
-        back_tile(k, scale_ref, turned_ref, image, mark, out_ref)
+    half = PEERS // 2
+    copies = []
+    for h in range(2):
+        term = (
+            scale_ref[0]
+            * jnp.dot(turned_ref[h * half * PIECE : (h + 1) * half * PIECE, :], image, preferred_element_type=F32)
+        ).astype(BF16)
+        for p in range(half):
+            start = (h * half + p) * PART
+            for b in range(WIDTH // 128):
+                back[start + b * PIECE : start + (b + 1) * PIECE, :] = (
+                    term[p * PIECE : (p + 1) * PIECE, b * 128 : (b + 1) * 128]
+                )
+            back[start + PART - MARK : start + PART, :] = mark
+        span = pl.ds(h * half * PART, half * PART)
+        copies += run([pltpu.make_async_copy(back.at[span, :], out_ref.at[span, :], sem.at[h])])
+    mine_ref[...] = scale_ref[0] * jnp.dot(weights_ref[...], text_ref[...], preferred_element_type=F32)
+    wait(copies)
 
 
 HALF = PIECE // 2
+FIRST = HALF * (WIDTH // 128) + MARK
 AWAY = (3, 2, 1, -3, -2, -1)
 
 
-def pieces_kernel(
-    at_ref, scale_ref, weights_ref, text_ref, sums_ref, swapped_ref, begun_ref, out_ref, *refs
-):
-    own_out, up_out, down_out, *away_refs, mine, parts, ends, sem, back_sem = refs
-    begun = run([pltpu.make_async_copy(begun_ref, out_ref, back_sem.at[0])])
-    mine[...] = scale_ref[0] * jnp.dot(
-        weights_ref[...], text_ref[...], preferred_element_type=F32
-    ) + swapped_ref[...].astype(F32)
+def pieces_kernel(at_ref, sums_ref, mine_ref, swapped_ref, begun_ref, out_ref, *refs):
+    own_out, up_out, down_out, *away_refs, mine, parts, ends, sem = refs
+    mine[...] = mine_ref[...] + swapped_ref[...].astype(F32)
 
     def block(by):
         return pl.ds(pl.multiple_of(lax.rem(at_ref[3] + by + DEEP, DEEP) * PIECE, PIECE), PIECE)
 
-    ends[:, :WIDTH] = mine[block(4), :].astype(BF16)
-    ends[:, WIDTH:] = jnp.broadcast_to(place_tag(at_ref, sums_ref), (PIECE, 128)).astype(BF16)
+    across = mine[block(4), :].astype(BF16)
+    mark = jnp.broadcast_to(place_tag(at_ref, sums_ref), (MARK, 128)).astype(BF16)
+    for h in range(2):
+        for b in range(WIDTH // 128):
+            ends[h, b * HALF : (b + 1) * HALF, :] = across[h * HALF : (h + 1) * HALF, b * 128 : (b + 1) * 128]
+        ends[h, FIRST - MARK :, :] = mark
     copies = run([
-        pltpu.make_async_copy(ends.at[pl.ds(0, HALF), :], up_out, sem.at[0]),
-        pltpu.make_async_copy(ends.at[pl.ds(HALF, HALF), :], down_out, sem.at[1]),
+        pltpu.make_async_copy(ends.at[0], up_out, sem.at[0]),
+        pltpu.make_async_copy(ends.at[1], down_out, sem.at[1]),
         pltpu.make_async_copy(mine.at[block(0), :], own_out, sem.at[2]),
     ])
     for k, (by, ref) in enumerate(zip(AWAY, away_refs)):
         parts[k] = mine[block(by), :].astype(BF16)
         copies += run([pltpu.make_async_copy(parts.at[k], ref, sem.at[3 + k])])
-    wait(begun + copies)
+    wait(copies)
 
 
 def relay_kernel(
@@ -322,14 +319,18 @@
     for k, (copy, ours, theirs, out) in enumerate(
         zip(copies, (up, down), (below_ref, above_ref), (up_out, down_out))
     ):
-        came = theirs[:, :WIDTH].astype(F32)
-        if came.shape[0] == HALF:
-            rest = jnp.zeros_like(came)
-            came = jnp.concatenate([came, rest] if k == 0 else [rest, came], axis=0)
-        marks = theirs[:16, WIDTH:].astype(F32)[:1] + mark
-        out[:, WIDTH:] = jnp.broadcast_to(marks, (PIECE, 128)).astype(BF16)
+        size = theirs.shape[0]
+        rows = (size - MARK) // (WIDTH // 128)
+        marks = theirs[size - MARK :, :].astype(F32)[:1] + mark
+        out[PART - MARK :, :] = jnp.broadcast_to(marks, (MARK, 128)).astype(BF16)
         copy.wait()
-        out[:, :WIDTH] = (ours[...].astype(F32) + came).astype(BF16)
+        for b in range(WIDTH // 128):
+            block = ours[:, b * 128 : (b + 1) * 128].astype(F32)
+            came = theirs[b * rows : (b + 1) * rows, :].astype(F32)
+            if rows < PIECE:
+                rest = jnp.zeros_like(came)
+                came = jnp.concatenate([came, rest] if k == 0 else [rest, came], axis=0)
+            out[b * PIECE : (b + 1) * PIECE, :] = (block + came).astype(BF16)
 
 
 def project(back, raw):
@@ -362,14 +363,18 @@
     ])
     twice = lax.rem(at_ref[3] + DEEP // 2, DEEP)
     lane = lax.broadcasted_iota(jnp.int32, (1, 128), 1)
-    marks = place_tag(at_ref, sums_ref) + below_ref[:16, WIDTH:].astype(F32)[:1]
-    marks += jnp.where(lane // 4 == twice, 0.0, above_ref[:16, WIDTH:].astype(F32)[:1])
+    marks = place_tag(at_ref, sums_ref) + below_ref[PART - MARK :, :].astype(F32)[:1]
+    marks += jnp.where(lane // 4 == twice, 0.0, above_ref[PART - MARK :, :].astype(F32)[:1])
     total = jnp.zeros((1, 1), F32)
     for k in range(DEEP):
         total += untag(marks, 4 * k)
     loss_ref[...] = jnp.broadcast_to(total, loss_ref.shape)
     wait(copies)
-    back = own[...] + below_ref[:, :WIDTH].astype(F32) + above_ref[:, :WIDTH].astype(F32)
+    came = [
+        below_ref[b * PIECE : (b + 1) * PIECE, :].astype(F32) + above_ref[b * PIECE : (b + 1) * PIECE, :].astype(F32)
+        for b in range(WIDTH // 128)
+    ]
+    back = own[...] + jnp.concatenate(came, axis=1)
     grad[...] = project(back, raw[...])
     wait(run([pltpu.make_async_copy(grad, out_ref, sem.at[0])]))
 
@@ -408,15 +413,14 @@
     text_units = call(text_units_kernel, outside, Outside(text_emb), scratch=[raw, raw, sems((PEERS,))])
     text = exchange(text_units, XY)
 
-    pairs = [pairs, send(pairs, "c", 1)]
 
     lines = local((STEPS, TILE), F32)
     image, logits, keep, give = call(
-        functools.partial(logits_kernel, plan), [outside, local((SIDE, SIDE), F32), lines, lines],
-        at, scale, text, *map(Outside, pieces),
+        functools.partial(logits_kernel, plan), [outside, local((SIDE, SIDE), F32), lines, local((2 * STEPS, TILE), F32)],
+        at, scale, pairs, text, *map(Outside, pieces),
         scratch=[pltpu.VMEM((SIDE, width), BF16), sems((len(plan),)), sems((2,))],
     )
-    spread = call(spread_kernel, local((PEERS * LINES, TILE), F32), at, keep, send(give, "c", 1), *pairs)
+    spread = call(spread_kernel, local((PEERS * LINES, TILE), F32), at, keep, send(give, "c", 1), pairs)
     lines = local((2 * STEPS, TILE), F32)
     keep, give = call(join_kernel, [lines, lines], at, exchange(spread, MIXED))
     recv = send(give, "c", 1)
@@ -428,23 +432,27 @@
         at, scale, logits, text, keep, recv,
     )
     swapped = send(other, "c", 1)
-    text_parts = call(text_back_kernel, local((SPLIT, 128), BF16), scale, turned, image, sums)
-    end = array((HALF, WIDER), BF16)
+    parts = array((PEERS * PART, 128), BF16)
+    text_parts, mine = call(
+        text_back_kernel, [parts, local(half, F32)], scale, weights, turned, image, text, sums,
+        scratch=[pltpu.VMEM(parts.shape, BF16), sems((2,))],
+    )
+    end = array((FIRST, 128), BF16)
     away = [array((PIECE, width), BF16)] * len(AWAY)
     text_parts, own, up, down, *away = call(
-        pieces_kernel, [array((PEERS * PART, 128), BF16), array((PIECE, width), F32), end, end, *away],
-        at, scale, weights, text, sums, swapped, text_parts,
+        pieces_kernel, [parts, array((PIECE, width), F32), end, end, *away],
+        at, sums, mine, swapped, Outside(text_parts),
         scratch=[
             pltpu.VMEM(half, F32),
             pltpu.VMEM((len(AWAY), PIECE, width), BF16),
-            pltpu.VMEM((PIECE, WIDER), BF16),
+            pltpu.VMEM((2, FIRST, 128), BF16),
             sems((3 + len(AWAY),)),
-            sems((1,)),
         ],
+        aliases={4: 0},
     )
     text_back = exchange(text_parts, XY)
     below, above = send(up, "z", 1), send(down, "z", -1)
-    whole = local((PIECE, WIDER), BF16)
+    whole = local((PART, 128), BF16)
     for k in range(3):
         up, down = call(
             relay_kernel, [whole] * 2, at, sums, Outside(away[k]), Outside(away[k + 3]), below, above,

time: 128 us -> 127 us (level)
    ppermute x29 -> x28, starting transfers between devices: 33.7 us -> 33 us  [send(): return lax.ppermute(x, 'd', shift(axis, by))]
    ppermute x29 -> x28, waiting for transfers between devices: 32.8 us -> 33.1 us  [send(): return lax.ppermute(x, 'd', shift(axis, by))]
  transfers between devices with their start and end apart: 31 -> 30, of which waited for: 18 -> 19; matrix products, arithmetic and copies ran while one was open for 0% -> 0% of each run, Pallas kernels for 14% -> 11%
where the time goes in v6:
time: 127 us
  starting transfers between devices  47.2 us (37%)
  waiting for transfers between devices  35.5 us (28%)
  Pallas kernels  30.4 us (24%)
  blocking collectives  11.3 us (9%)
  between operations  2.27 us (2%)
    ppermute x28, waiting for transfers between devices, send(): return lax.ppermute(x, 'd', shift(axis, by))  33.1 us
    ppermute x28, starting transfers between devices, send(): return lax.ppermute(x, 'd', shift(axis, by))  33 us
    pallas_call x13, Pallas kernels, call(): pl.pallas_call(kernel, out_shape=outputs, in_specs=specs, out_specs=jax.t...  30.4 us
    all_to_all x2, starting transfers between devices, exchange(): return lax.all_to_all(x, 'd', 0, 0, axis_index_groups=groups, tiled=True)  14.2 us
    all_to_all x1, blocking collectives, exchange(): return lax.all_to_all(x, 'd', 0, 0, axis_index_groups=groups, tiled=True)  11.3 us
  transfers between devices with their start and end apart: 30, of which 19 were waited for; matrix products, arithmetic and copies ran while one was open for 0% of the time, Pallas kernels for 11%

profile of v6, /device:TPU:28, one launch (start us, length us, event | category | flops | bytes accessed | tf_op | source)
XLA Modules:
  0.0 126.8 jit_solution(18098084777257920446)
XLA Ops:
  0.6 2.7 %shard_map.59 = bf16[1024,1280]{1,0:T(8,128)(2,1)} custom-call(bf16[64,1280]{1,0:T(8,128)(2,1)} %raw_ref.7), custom_call_target="tpu_custom_call" | custom-call | tf_op jit(solution)/shard_map/pallas_call | solution.py:75
  3.3 7.1 %all-to-all-start = ((bf16[16,64,1280]{2,1,0:T(8,128)(2,1)}), bf16[16,64,1280]{2,1,0:T(8,128)(2,1)S(1)}, u32[]{:S(2)}, u32[]{:S(2)}) async-start(bf16[16,64,1280]{2,1,0:T(8,128)(2,1)} %bitcast.18), calls=%async_computation | async-start | bytes 5242880 | tf_op jit(solution)/shard_map/all_to_all | solution.py:52
  11.1 1.7 %shard_map.58 = (bf16[64,1280]{1,0:T(8,128)(2,1)}, f32[8,128]{1,0:T(8,128)S(1)}) custom-call(f32[1]{0:T(128)S(6)} %exp.3.scale_ref, bf16[64,1280]{1,0:T(8,128)(2,1)} %raw_ref.6, bf16[64,1280]{1,0:T(8,128)(2,1)} %raw_ref.7), custom_call_target="tpu_custom_call" | custom-call | tf_op jit(solution)/shard_map/pallas_call | solution.py:75
  12.9 5.9 %collective-permute-start.1 = (bf16[64,1280]{1,0:T(8,128)(2,1)}, bf16[64,1280]{1,0:T(8,128)(2,1)S(1)}, u32[]{:S(2)}, u32[]{:S(2)}) collective-permute-start(bf16[64,1280]{1,0:T(8,128)(2,1)} %get-tuple-element.38.refs_0_), channel_id=1, source_target_pairs={{0,7},{1,0},{2,1},{3,2},{4,3},{5,4},{6,5},{7,6},{8,15},{9,8},{10,9... | collective-permute-start | bytes 491528 | tf_op jit(solution)/shard_map/ppermute | solution.py:48
  18.8 3.2 %collective-permute-done.1.refs_2_ = bf16[64,1280]{1,0:T(8,128)(2,1)S(1)} collective-permute-done((bf16[64,1280]{1,0:T(8,128)(2,1)}, bf16[64,1280]{1,0:T(8,128)(2,1)S(1)}, u32[]{:S(2)}, u32[]{:S(2)}) %collective-permute-start.1) | collective-permute-done | bytes 163872 | tf_op jit(solution)/shard_map/ppermute | solution.py:48
  22.0 3.6 %collective-permute-start.3 = (bf16[64,1280]{1,0:T(8,128)(2,1)S(1)}, bf16[64,1280]{1,0:T(8,128)(2,1)S(1)}, u32[]{:S(2)}, u32[]{:S(2)}) collective-permute-start(bf16[64,1280]{1,0:T(8,128)(2,1)S(1)} %collective-permute-done.1.refs_2_), channel_id=1, source_target_pairs={{0,7},{1,0},{2,1},{3,2},{4,3},{5,4},{6,5},{7,6},{8,15},{9,8},{10,9... | collective-permute-start | bytes 491528 | tf_op jit(solution)/shard_map/ppermute | solution.py:48
  25.6 2.8 %collective-permute-done.3.refs_4_ = bf16[64,1280]{1,0:T(8,128)(2,1)S(1)} collective-permute-done((bf16[64,1280]{1,0:T(8,128)(2,1)S(1)}, bf16[64,1280]{1,0:T(8,128)(2,1)S(1)}, u32[]{:S(2)}, u32[]{:S(2)}) %collective-permute-start.3) | collective-permute-done | bytes 163872 | tf_op jit(solution)/shard_map/ppermute | solution.py:48
  28.5 3.7 %collective-permute-start.5 = (bf16[64,1280]{1,0:T(8,128)(2,1)S(1)}, bf16[64,1280]{1,0:T(8,128)(2,1)S(1)}, u32[]{:S(2)}, u32[]{:S(2)}) collective-permute-start(bf16[64,1280]{1,0:T(8,128)(2,1)S(1)} %collective-permute-done.3.refs_4_), channel_id=1, source_target_pairs={{0,7},{1,0},{2,1},{3,2},{4,3},{5,4},{6,5},{7,6},{8,15},{9,8},{10,9... | collective-permute-start | bytes 491528 | tf_op jit(solution)/shard_map/ppermute | solution.py:48
  32.8 2.2 %collective-permute-done.5.refs_6_ = bf16[64,1280]{1,0:T(8,128)(2,1)S(1)} collective-permute-done((bf16[64,1280]{1,0:T(8,128)(2,1)S(1)}, bf16[64,1280]{1,0:T(8,128)(2,1)S(1)}, u32[]{:S(2)}, u32[]{:S(2)}) %collective-permute-start.5) | collective-permute-done | bytes 163872 | tf_op jit(solution)/shard_map/ppermute | solution.py:48
  35.0 4.0 %collective-permute-done.4.refs_5_ = bf16[64,1280]{1,0:T(8,128)(2,1)S(1)} collective-permute-done((bf16[64,1280]{1,0:T(8,128)(2,1)}, bf16[64,1280]{1,0:T(8,128)(2,1)S(1)}, u32[]{:S(2)}, u32[]{:S(2)}) %collective-permute-start.4) | collective-permute-done | bytes 163872 | tf_op jit(solution)/shard_map/ppermute | solution.py:48
  39.4 1.7 %collective-permute-start.6 = (bf16[32,1280]{1,0:T(8,128)(2,1)S(1)}, bf16[32,1280]{1,0:T(8,128)(2,1)}, u32[]{:S(2)}, u32[]{:S(2)}) collective-permute-start(bf16[32,1280]{1,0:T(8,128)(2,1)S(1)} %slice.8), channel_id=1, source_target_pairs={{0,1},{1,2},{2,3},{3,4},{4,5},{5,6},{6,7},{7,0},{8,9},{9,10},{10,1... | collective-permute-start | bytes 245768 | tf_op jit(solution)/shard_map/ppermute | solution.py:48
  41.8 2.3 %collective-permute-done.7.refs_8_ = bf16[32,1280]{1,0:T(8,128)(2,1)} collective-permute-done((bf16[32,1280]{1,0:T(8,128)(2,1)S(1)}, bf16[32,1280]{1,0:T(8,128)(2,1)}, u32[]{:S(2)}, u32[]{:S(2)}) %collective-permute-start.7) | collective-permute-done | bytes 81952 | tf_op jit(solution)/shard_map/ppermute | solution.py:48
  47.1 6.3 %shard_map.60 = (bf16[1024,1280]{1,0:T(8,128)(2,1)}, f32[1024,1024]{1,0:T(8,128)S(1)}, f32[4,256]{1,0:T(4,128)S(1)}, f32[8,256]{1,0:T(8,128)S(1)}) custom-call(s32[5]{0:T(128)S(1)} %stack.23.at_ref, f32[1]{0:T(128)S(6)} %exp.3.scale_ref, f32[8,128]{1,0:T(8,128)S(1)} %get-tuple-element.37.pairs_ref, bf16[1024,1280]{1,0:T(8,128)(2,1)S(1)} %bitcast.11, ...), custom_call_target="tpu_custom_call" | custom-call | tf_op jit(solution)/shard_map/pallas_call | solution.py:75
  55.2 11.3 %all_to_all.33 = f32[16,8,256]{2,1,0:T(8,128)S(1)} all-to-all(f32[16,8,256]{2,1,0:T(8,128)S(1)} %bitcast.15), channel_id=1, replica_groups={{0,16,32,48,64,80,96,112,128,144,160,176,192,208,224,240},{1,17,33,49,6..., dimensions={0} | all-to-all | bytes 262144 | tf_op jit(solution)/shard_map/all_to_all | solution.py:52
  67.3 2.3 %collective-permute-start.18 = (f32[8,256]{1,0:T(8,128)S(1)}, f32[8,256]{1,0:T(8,128)S(1)}, u32[]{:S(2)}, u32[]{:S(2)}) collective-permute-start(f32[8,256]{1,0:T(8,128)S(1)} %get-tuple-element.43), channel_id=1, source_target_pairs={{0,8},{1,9},{2,10},{3,11},{4,12},{5,13},{6,14},{7,15},{8,0},{9,1},... | collective-permute-start | bytes 24584 | tf_op jit(solution)/shard_map/ppermute | solution.py:48
  70.4 2.9 %shard_map.63 = (bf16[512,1024]{1,0:T(8,128)(2,1)S(1)}, bf16[1024,1024]{1,0:T(8,128)(2,1)S(1)}, bf16[512,1280]{1,0:T(8,128)(2,1)S(1)}, f32[8,128]{1,0:T(8,128)S(1)}) custom-call(s32[5]{0:T(128)S(1)} %stack.23.at_ref, f32[1]{0:T(128)S(6)} %exp.3.scale_ref, f32[1024,1024]{1,0:T(8,128)S(1)} %get-tuple-element.39.logits_ref, bf16[1024,1280]{1,0:T(8,128)(2,1)S(1)} %bitcast.12, ...), custom_call_target="tpu_custom_call" | custom-call | tf_op jit(solution)/shard_map/pallas_call | solution.py:75
  73.7 4.3 %shard_map.64 = (bf16[10496,128]{1,0:T(8,128)(2,1)}, f32[512,1280]{1,0:T(8,128)S(1)}) custom-call(f32[1]{0:T(128)S(6)} %exp.3.scale_ref, bf16[512,1024]{1,0:T(8,128)(2,1)S(1)} %get-tuple-element.45.weights_ref, bf16[1024,1024]{1,0:T(8,128)(2,1)S(1)} %get-tuple-element.46.turned_ref, bf16[1024,1280]{1,0:T(8,128)(2,1)S(1)} %copy-done, ...), custom_call_target="tpu_custom_call" | custom-call | tf_op jit(solution)/shard_map/pallas_call | solution.py:75
  78.0 2.1 %shard_map.65 = (bf16[10496,128]{1,0:T(8,128)(2,1)}, f32[64,1280]{1,0:T(8,128)}, bf16[336,128]{1,0:T(8,128)(2,1)}, bf16[336,128]{1,0:T(8,128)(2,1)}, bf16[64,128...) custom-call(s32[5]{0:T(128)S(1)} %stack.23.at_ref, ...), custom_call_target="tpu_custom_call", output_to_operand_aliasing={{0}: (4, {})} | custom-call | tf_op jit(solution)/shard_map/pallas_call | solution.py:75
  80.1 7.1 %all-to-all-start.2 = ((bf16[16,656,128]{2,1,0:T(8,128)(2,1)}), bf16[16,656,128]{2,1,0:T(8,128)(2,1)S(1)}, u32[]{:S(2)}, u32[]{:S(2)}) async-start(bf16[16,656,128]{2,1,0:T(8,128)(2,1)} %bitcast.17), calls=%async_computation.2 | async-start | bytes 5373952 | tf_op jit(solution)/shard_map/all_to_all | solution.py:52
  87.2 1.7 %collective-permute-start.20 = (bf16[336,128]{1,0:T(8,128)(2,1)S(1)}, bf16[336,128]{1,0:T(8,128)(2,1)S(1)}, u32[]{:S(2)}, u32[]{:S(2)}) collective-permute-start(bf16[336,128]{1,0:T(8,128)(2,1)S(1)} %copy-done.11), channel_id=1, source_target_pairs={{0,1},{1,2},{2,3},{3,4},{4,5},{5,6},{6,7},{7,0},{8,9},{9,10},{10,1... | collective-permute-start | bytes 258056 | tf_op jit(solution)/shard_map/ppermute | solution.py:48
  88.8 1.9 %collective-permute-start.21 = (bf16[336,128]{1,0:T(8,128)(2,1)S(1)}, bf16[336,128]{1,0:T(8,128)(2,1)S(1)}, u32[]{:S(2)}, u32[]{:S(2)}) collective-permute-start(bf16[336,128]{1,0:T(8,128)(2,1)S(1)} %copy-done.10), channel_id=1, source_target_pairs={{0,7},{1,0},{2,1},{3,2},{4,3},{5,4},{6,5},{7,6},{8,15},{9,8},{10,9... | collective-permute-start | bytes 258056 | tf_op jit(solution)/shard_map/ppermute | solution.py:48
  90.7 2.5 %collective-permute-done.20.below_ref = bf16[336,128]{1,0:T(8,128)(2,1)S(1)} collective-permute-done((bf16[336,128]{1,0:T(8,128)(2,1)S(1)}, bf16[336,128]{1,0:T(8,128)(2,1)S(1)}, u32[]{:S(2)}, u32[]{:S(2)}) %collective-permute-start.20) | collective-permute-done | bytes 86048 | tf_op jit(solution)/shard_map/ppermute | solution.py:48
  95.7 2.5 %collective-permute-start.23 = (bf16[656,128]{1,0:T(8,128)(2,1)S(1)}, bf16[656,128]{1,0:T(8,128)(2,1)S(1)}, u32[]{:S(2)}, u32[]{:S(2)}) collective-permute-start(bf16[656,128]{1,0:T(8,128)(2,1)S(1)} %get-tuple-element.61), channel_id=1, source_target_pairs={{0,7},{1,0},{2,1},{3,2},{4,3},{5,4},{6,5},{7,6},{8,15},{9,8},{10,9... | collective-permute-start | bytes 503816 | tf_op jit(solution)/shard_map/ppermute | solution.py:48
  98.2 3.3 %collective-permute-done.22.below_ref = bf16[656,128]{1,0:T(8,128)(2,1)S(1)} collective-permute-done((bf16[656,128]{1,0:T(8,128)(2,1)S(1)}, bf16[656,128]{1,0:T(8,128)(2,1)S(1)}, u32[]{:S(2)}, u32[]{:S(2)}) %collective-permute-start.22) | collective-permute-done | bytes 167968 | tf_op jit(solution)/shard_map/ppermute | solution.py:48
  103.2 1.7 %collective-permute-start.24 = (bf16[656,128]{1,0:T(8,128)(2,1)S(1)}, bf16[656,128]{1,0:T(8,128)(2,1)S(1)}, u32[]{:S(2)}, u32[]{:S(2)}) collective-permute-start(bf16[656,128]{1,0:T(8,128)(2,1)S(1)} %get-tuple-element.62), channel_id=1, source_target_pairs={{0,1},{1,2},{2,3},{3,4},{4,5},{5,6},{6,7},{7,0},{8,9},{9,10},{10,1... | collective-permute-start | bytes 503816 | tf_op jit(solution)/shard_map/ppermute | solution.py:48
  104.8 1.7 %collective-permute-start.25 = (bf16[656,128]{1,0:T(8,128)(2,1)S(1)}, bf16[656,128]{1,0:T(8,128)(2,1)S(1)}, u32[]{:S(2)}, u32[]{:S(2)}) collective-permute-start(bf16[656,128]{1,0:T(8,128)(2,1)S(1)} %get-tuple-element.63), channel_id=1, source_target_pairs={{0,7},{1,0},{2,1},{3,2},{4,3},{5,4},{6,5},{7,6},{8,15},{9,8},{10,9... | collective-permute-start | bytes 503816 | tf_op jit(solution)/shard_map/ppermute | solution.py:48
  106.6 3.3 %collective-permute-done.24.below_ref = bf16[656,128]{1,0:T(8,128)(2,1)S(1)} collective-permute-done((bf16[656,128]{1,0:T(8,128)(2,1)S(1)}, bf16[656,128]{1,0:T(8,128)(2,1)S(1)}, u32[]{:S(2)}, u32[]{:S(2)}) %collective-permute-start.24) | collective-permute-done | bytes 167968 | tf_op jit(solution)/shard_map/ppermute | solution.py:48
  111.8 2.1 %collective-permute-start.26 = (bf16[656,128]{1,0:T(8,128)(2,1)S(1)}, bf16[656,128]{1,0:T(8,128)(2,1)S(1)}, u32[]{:S(2)}, u32[]{:S(2)}) collective-permute-start(bf16[656,128]{1,0:T(8,128)(2,1)S(1)} %get-tuple-element.64), channel_id=1, source_target_pairs={{0,1},{1,2},{2,3},{3,4},{4,5},{5,6},{6,7},{7,0},{8,9},{9,10},{10,1... | collective-permute-start | bytes 503816 | tf_op jit(solution)/shard_map/ppermute | solution.py:48
  115.1 3.3 %collective-permute-done.26.below_ref = bf16[656,128]{1,0:T(8,128)(2,1)S(1)} collective-permute-done((bf16[656,128]{1,0:T(8,128)(2,1)S(1)}, bf16[656,128]{1,0:T(8,128)(2,1)S(1)}, u32[]{:S(2)}, u32[]{:S(2)}) %collective-permute-start.26) | collective-permute-done | bytes 167968 | tf_op jit(solution)/shard_map/ppermute | solution.py:48
  119.3 2.5 %shard_map.69 = (bf16[64,1280]{1,0:T(8,128)(2,1)}, f32[8,128]{1,0:T(8,128)S(1)}) custom-call(s32[5]{0:T(128)S(1)} %stack.23.at_ref, f32[8,128]{1,0:T(8,128)S(1)} %get-tuple-element.44.sums_ref, bf16[64,1280]{1,0:T(8,128)(2,1)} %raw_ref.6, f32[64,1280]{1,0:T(8,128)} %get-tuple-element.51.own_ref, bf16[656,128]{1,0:T(8,128)(2,1)S(1)} %collective-permute-done.26.below_ref, ...), custom_call_target="tpu_custom_call" | custom-call | tf_op jit(solution)/shard_map/pallas_call | solution.py:75
  121.8 2.4 %all-to-all-done.2 = bf16[16,656,128]{2,1,0:T(8,128)(2,1)S(1)} async-done(((bf16[16,656,128]{2,1,0:T(8,128)(2,1)}), bf16[16,656,128]{2,1,0:T(8,128)(2,1)S(1)}, u32[]{:S(2)}, u32[]{:S(2)}) %all-to-all-start.2) | async-done | bytes 2687008 | tf_op jit(solution)/shard_map/all_to_all | solution.py:52
  124.2 1.8 %shard_map.70 = (bf16[64,1280]{1,0:T(8,128)(2,1)}, f32[1]{0:T(128)S(4)}) custom-call(bf16[64,1280]{1,0:T(8,128)(2,1)} %raw_ref.7, f32[8,128]{1,0:T(8,128)S(1)} %get-tuple-element.66.loss_ref, bf16[10496,128]{1,0:T(8,128)(2,1)S(1)} %bitcast.14), custom_call_target="tpu_custom_call" | custom-call | tf_op jit(solution)/shard_map/pallas_call | solution.py:75
  (69 shorter events, 16.6 us)
Async XLA Ops:
  3.3 43.7 %all-to-all-start = ((bf16[16,64,1280]{2,1,0:T(8,128)(2,1)}), bf16[16,64,1280]{2,1,0:T(8,128)(2,1)S(1)}, u32[]{:S(2)}, u32[]{:S(2)}) async-start(bf16[16,64,1280]{2,1,0:T(8,128)(2,1)} %bitcast.18), calls=%async_computation | async-start | bytes 5242880 | tf_op jit(solution)/shard_map/all_to_all | solution.py:52
  12.9 9.1 %collective-permute-start.1 = (bf16[64,1280]{1,0:T(8,128)(2,1)}, bf16[64,1280]{1,0:T(8,128)(2,1)S(1)}, u32[]{:S(2)}, u32[]{:S(2)}) collective-permute-start(bf16[64,1280]{1,0:T(8,128)(2,1)} %get-tuple-element.38.refs_0_), channel_id=1, source_target_pairs={{0,7},{1,0},{2,1},{3,2},{4,3},{5,4},{6,5},{7,6},{8,15},{9,8},{10,9... | collective-permute-start | bytes 491528 | tf_op jit(solution)/shard_map/ppermute | solution.py:48
  18.8 6.8 %collective-permute-start = (bf16[64,1280]{1,0:T(8,128)(2,1)}, bf16[64,1280]{1,0:T(8,128)(2,1)S(1)}, u32[]{:S(2)}, u32[]{:S(2)}) collective-permute-start(bf16[64,1280]{1,0:T(8,128)(2,1)} %get-tuple-element.38.refs_0_), channel_id=1, source_target_pairs={{0,1},{1,2},{2,3},{3,4},{4,5},{5,6},{6,7},{7,0},{8,9},{9,10},{10,1... | collective-permute-start | bytes 491528 | tf_op jit(solution)/shard_map/ppermute | solution.py:48
  22.0 25.0 %copy-start.3 = (bf16[64,1280]{1,0:T(8,128)(2,1)}, bf16[64,1280]{1,0:T(8,128)(2,1)S(1)}, u32[]{:S(2)}) copy-start(bf16[64,1280]{1,0:T(8,128)(2,1)S(1)} %collective-permute-done.1.refs_2_) | copy-start | bytes 491524
  22.0 6.4 %collective-permute-start.3 = (bf16[64,1280]{1,0:T(8,128)(2,1)S(1)}, bf16[64,1280]{1,0:T(8,128)(2,1)S(1)}, u32[]{:S(2)}, u32[]{:S(2)}) collective-permute-start(bf16[64,1280]{1,0:T(8,128)(2,1)S(1)} %collective-permute-done.1.refs_2_), channel_id=1, source_target_pairs={{0,7},{1,0},{2,1},{3,2},{4,3},{5,4},{6,5},{7,6},{8,15},{9,8},{10,9... | collective-permute-start | bytes 491528 | tf_op jit(solution)/shard_map/ppermute | solution.py:48
  25.6 21.4 %copy-start.4 = (bf16[64,1280]{1,0:T(8,128)(2,1)}, bf16[64,1280]{1,0:T(8,128)(2,1)S(1)}, u32[]{:S(2)}) copy-start(bf16[64,1280]{1,0:T(8,128)(2,1)S(1)} %collective-permute-done.refs_1_) | copy-start | bytes 491524
  25.6 6.6 %collective-permute-start.2 = (bf16[64,1280]{1,0:T(8,128)(2,1)S(1)}, bf16[64,1280]{1,0:T(8,128)(2,1)}, u32[]{:S(2)}, u32[]{:S(2)}) collective-permute-start(bf16[64,1280]{1,0:T(8,128)(2,1)S(1)} %collective-permute-done.refs_1_), channel_id=1, source_target_pairs={{0,1},{1,2},{2,3},{3,4},{4,5},{5,6},{6,7},{7,0},{8,9},{9,10},{10,1... | collective-permute-start | bytes 491528 | tf_op jit(solution)/shard_map/ppermute | solution.py:48
  28.5 6.5 %collective-permute-start.5 = (bf16[64,1280]{1,0:T(8,128)(2,1)S(1)}, bf16[64,1280]{1,0:T(8,128)(2,1)S(1)}, u32[]{:S(2)}, u32[]{:S(2)}) collective-permute-start(bf16[64,1280]{1,0:T(8,128)(2,1)S(1)} %collective-permute-done.3.refs_4_), channel_id=1, source_target_pairs={{0,7},{1,0},{2,1},{3,2},{4,3},{5,4},{6,5},{7,6},{8,15},{9,8},{10,9... | collective-permute-start | bytes 491528 | tf_op jit(solution)/shard_map/ppermute | solution.py:48
  32.3 6.7 %collective-permute-start.4 = (bf16[64,1280]{1,0:T(8,128)(2,1)}, bf16[64,1280]{1,0:T(8,128)(2,1)S(1)}, u32[]{:S(2)}, u32[]{:S(2)}) collective-permute-start(bf16[64,1280]{1,0:T(8,128)(2,1)} %collective-permute-done.2.refs_3_), channel_id=1, source_target_pairs={{0,1},{1,2},{2,3},{3,4},{4,5},{5,6},{6,7},{7,0},{8,9},{9,10},{10,1... | collective-permute-start | bytes 491528 | tf_op jit(solution)/shard_map/ppermute | solution.py:48
  32.3 6.8 %collective-permute-start.8 = (bf16[64,1280]{1,0:T(8,128)(2,1)}, bf16[64,1280]{1,0:T(8,128)(2,1)S(1)}, u32[]{:S(2)}, u32[]{:S(2)}) collective-permute-start(bf16[64,1280]{1,0:T(8,128)(2,1)} %get-tuple-element.38.refs_0_), channel_id=1, source_target_pairs={{0,8},{1,9},{2,10},{3,11},{4,12},{5,13},{6,14},{7,15},{8,0},{9,1},... | collective-permute-start | bytes 491528 | tf_op jit(solution)/shard_map/ppermute | solution.py:48
  32.3 7.1 %collective-permute-start.10 = (bf16[64,1280]{1,0:T(8,128)(2,1)S(1)}, bf16[64,1280]{1,0:T(8,128)(2,1)S(1)}, u32[]{:S(2)}, u32[]{:S(2)}) collective-permute-start(bf16[64,1280]{1,0:T(8,128)(2,1)S(1)} %collective-permute-done.1.refs_2_), channel_id=1, source_target_pairs={{0,8},{1,9},{2,10},{3,11},{4,12},{5,13},{6,14},{7,15},{8,0},{9,1},... | collective-permute-start | bytes 491528 | tf_op jit(solution)/shard_map/ppermute | solution.py:48
  32.8 8.4 %collective-permute-start.9 = (bf16[64,1280]{1,0:T(8,128)(2,1)S(1)}, bf16[64,1280]{1,0:T(8,128)(2,1)S(1)}, u32[]{:S(2)}, u32[]{:S(2)}) collective-permute-start(bf16[64,1280]{1,0:T(8,128)(2,1)S(1)} %collective-permute-done.refs_1_), channel_id=1, source_target_pairs={{0,8},{1,9},{2,10},{3,11},{4,12},{5,13},{6,14},{7,15},{8,0},{9,1},... | collective-permute-start | bytes 491528 | tf_op jit(solution)/shard_map/ppermute | solution.py:48
  35.0 6.2 %collective-permute-start.12 = (bf16[64,1280]{1,0:T(8,128)(2,1)S(1)}, bf16[64,1280]{1,0:T(8,128)(2,1)S(1)}, u32[]{:S(2)}, u32[]{:S(2)}) collective-permute-start(bf16[64,1280]{1,0:T(8,128)(2,1)S(1)} %collective-permute-done.3.refs_4_), channel_id=1, source_target_pairs={{0,8},{1,9},{2,10},{3,11},{4,12},{5,13},{6,14},{7,15},{8,0},{9,1},... | collective-permute-start | bytes 491528 | tf_op jit(solution)/shard_map/ppermute | solution.py:48
  39.0 6.5 %collective-permute-start.11 = (bf16[64,1280]{1,0:T(8,128)(2,1)}, bf16[64,1280]{1,0:T(8,128)(2,1)}, u32[]{:S(2)}, u32[]{:S(2)}) collective-permute-start(bf16[64,1280]{1,0:T(8,128)(2,1)} %collective-permute-done.2.refs_3_), channel_id=1, source_target_pairs={{0,8},{1,9},{2,10},{3,11},{4,12},{5,13},{6,14},{7,15},{8,0},{9,1},... | collective-permute-start | bytes 491528 | tf_op jit(solution)/shard_map/ppermute | solution.py:48
  39.0 5.0 %collective-permute-start.7 = (bf16[32,1280]{1,0:T(8,128)(2,1)S(1)}, bf16[32,1280]{1,0:T(8,128)(2,1)}, u32[]{:S(2)}, u32[]{:S(2)}) collective-permute-start(bf16[32,1280]{1,0:T(8,128)(2,1)S(1)} %slice.9), channel_id=1, source_target_pairs={{0,7},{1,0},{2,1},{3,2},{4,3},{5,4},{6,5},{7,6},{8,15},{9,8},{10,9... | collective-permute-start | bytes 245768 | tf_op jit(solution)/shard_map/ppermute | solution.py:48
  39.4 6.0 %collective-permute-start.6 = (bf16[32,1280]{1,0:T(8,128)(2,1)S(1)}, bf16[32,1280]{1,0:T(8,128)(2,1)}, u32[]{:S(2)}, u32[]{:S(2)}) collective-permute-start(bf16[32,1280]{1,0:T(8,128)(2,1)S(1)} %slice.8), channel_id=1, source_target_pairs={{0,1},{1,2},{2,3},{3,4},{4,5},{5,6},{6,7},{7,0},{8,9},{9,10},{10,1... | collective-permute-start | bytes 245768 | tf_op jit(solution)/shard_map/ppermute | solution.py:48
  41.2 4.5 %collective-permute-start.14 = (bf16[64,1280]{1,0:T(8,128)(2,1)S(1)}, bf16[64,1280]{1,0:T(8,128)(2,1)}, u32[]{:S(2)}, u32[]{:S(2)}) collective-permute-start(bf16[64,1280]{1,0:T(8,128)(2,1)S(1)} %collective-permute-done.5.refs_6_), channel_id=1, source_target_pairs={{0,8},{1,9},{2,10},{3,11},{4,12},{5,13},{6,14},{7,15},{8,0},{9,1},... | collective-permute-start | bytes 491528 | tf_op jit(solution)/shard_map/ppermute | solution.py:48
  41.2 5.8 %collective-permute-start.13 = (bf16[64,1280]{1,0:T(8,128)(2,1)S(1)}, bf16[64,1280]{1,0:T(8,128)(2,1)}, u32[]{:S(2)}, u32[]{:S(2)}) collective-permute-start(bf16[64,1280]{1,0:T(8,128)(2,1)S(1)} %collective-permute-done.4.refs_5_), channel_id=1, source_target_pairs={{0,8},{1,9},{2,10},{3,11},{4,12},{5,13},{6,14},{7,15},{8,0},{9,1},... | collective-permute-start | bytes 491528 | tf_op jit(solution)/shard_map/ppermute | solution.py:48
  44.1 1.6 %collective-permute-start.16 = (bf16[32,1280]{1,0:T(8,128)(2,1)}, bf16[32,1280]{1,0:T(8,128)(2,1)}, u32[]{:S(2)}, u32[]{:S(2)}) collective-permute-start(bf16[32,1280]{1,0:T(8,128)(2,1)} %collective-permute-done.7.refs_8_), channel_id=1, source_target_pairs={{0,8},{1,9},{2,10},{3,11},{4,12},{5,13},{6,14},{7,15},{8,0},{9,1},... | collective-permute-start | bytes 245768 | tf_op jit(solution)/shard_map/ppermute | solution.py:48
  45.4 1.6 %collective-permute-start.15 = (bf16[32,1280]{1,0:T(8,128)(2,1)}, bf16[32,1280]{1,0:T(8,128)(2,1)}, u32[]{:S(2)}, u32[]{:S(2)}) collective-permute-start(bf16[32,1280]{1,0:T(8,128)(2,1)} %collective-permute-done.6.refs_7_), channel_id=1, source_target_pairs={{0,8},{1,9},{2,10},{3,11},{4,12},{5,13},{6,14},{7,15},{8,0},{9,1},... | collective-permute-start | bytes 245768 | tf_op jit(solution)/shard_map/ppermute | solution.py:48
  53.4 1.3 collective-permute-start.17
  67.3 3.1 %collective-permute-start.18 = (f32[8,256]{1,0:T(8,128)S(1)}, f32[8,256]{1,0:T(8,128)S(1)}, u32[]{:S(2)}, u32[]{:S(2)}) collective-permute-start(f32[8,256]{1,0:T(8,128)S(1)} %get-tuple-element.43), channel_id=1, source_target_pairs={{0,8},{1,9},{2,10},{3,11},{4,12},{5,13},{6,14},{7,15},{8,0},{9,1},... | collective-permute-start | bytes 24584 | tf_op jit(solution)/shard_map/ppermute | solution.py:48
  73.2 4.7 %collective-permute-start.19 = (bf16[512,1280]{1,0:T(8,128)(2,1)S(1)}, bf16[512,1280]{1,0:T(8,128)(2,1)S(1)}, u32[]{:S(2)}, u32[]{:S(2)}) collective-permute-start(bf16[512,1280]{1,0:T(8,128)(2,1)S(1)} %get-tuple-element.49), channel_id=1, source_target_pairs={{0,8},{1,9},{2,10},{3,11},{4,12},{5,13},{6,14},{7,15},{8,0},{9,1},... | collective-permute-start | bytes 3932168 | tf_op jit(solution)/shard_map/ppermute | solution.py:48
  80.1 44.1 %all-to-all-start.2 = ((bf16[16,656,128]{2,1,0:T(8,128)(2,1)}), bf16[16,656,128]{2,1,0:T(8,128)(2,1)S(1)}, u32[]{:S(2)}, u32[]{:S(2)}) async-start(bf16[16,656,128]{2,1,0:T(8,128)(2,1)} %bitcast.17), calls=%async_computation.2 | async-start | bytes 5373952 | tf_op jit(solution)/shard_map/all_to_all | solution.py:52
  87.2 6.0 %collective-permute-start.20 = (bf16[336,128]{1,0:T(8,128)(2,1)S(1)}, bf16[336,128]{1,0:T(8,128)(2,1)S(1)}, u32[]{:S(2)}, u32[]{:S(2)}) collective-permute-start(bf16[336,128]{1,0:T(8,128)(2,1)S(1)} %copy-done.11), channel_id=1, source_target_pairs={{0,1},{1,2},{2,3},{3,4},{4,5},{5,6},{6,7},{7,0},{8,9},{9,10},{10,1... | collective-permute-start | bytes 258056 | tf_op jit(solution)/shard_map/ppermute | solution.py:48
  88.8 4.5 %collective-permute-start.21 = (bf16[336,128]{1,0:T(8,128)(2,1)S(1)}, bf16[336,128]{1,0:T(8,128)(2,1)S(1)}, u32[]{:S(2)}, u32[]{:S(2)}) collective-permute-start(bf16[336,128]{1,0:T(8,128)(2,1)S(1)} %copy-done.10), channel_id=1, source_target_pairs={{0,7},{1,0},{2,1},{3,2},{4,3},{5,4},{6,5},{7,6},{8,15},{9,8},{10,9... | collective-permute-start | bytes 258056 | tf_op jit(solution)/shard_map/ppermute | solution.py:48
  94.9 6.7 %collective-permute-start.22 = (bf16[656,128]{1,0:T(8,128)(2,1)S(1)}, bf16[656,128]{1,0:T(8,128)(2,1)S(1)}, u32[]{:S(2)}, u32[]{:S(2)}) collective-permute-start(bf16[656,128]{1,0:T(8,128)(2,1)S(1)} %get-tuple-element.60), channel_id=1, source_target_pairs={{0,1},{1,2},{2,3},{3,4},{4,5},{5,6},{6,7},{7,0},{8,9},{9,10},{10,1... | collective-permute-start | bytes 503816 | tf_op jit(solution)/shard_map/ppermute | solution.py:48
  95.7 5.9 %collective-permute-start.23 = (bf16[656,128]{1,0:T(8,128)(2,1)S(1)}, bf16[656,128]{1,0:T(8,128)(2,1)S(1)}, u32[]{:S(2)}, u32[]{:S(2)}) collective-permute-start(bf16[656,128]{1,0:T(8,128)(2,1)S(1)} %get-tuple-element.61), channel_id=1, source_target_pairs={{0,7},{1,0},{2,1},{3,2},{4,3},{5,4},{6,5},{7,6},{8,15},{9,8},{10,9... | collective-permute-start | bytes 503816 | tf_op jit(solution)/shard_map/ppermute | solution.py:48
  103.2 6.7 %collective-permute-start.24 = (bf16[656,128]{1,0:T(8,128)(2,1)S(1)}, bf16[656,128]{1,0:T(8,128)(2,1)S(1)}, u32[]{:S(2)}, u32[]{:S(2)}) collective-permute-start(bf16[656,128]{1,0:T(8,128)(2,1)S(1)} %get-tuple-element.62), channel_id=1, source_target_pairs={{0,1},{1,2},{2,3},{3,4},{4,5},{5,6},{6,7},{7,0},{8,9},{9,10},{10,1... | collective-permute-start | bytes 503816 | tf_op jit(solution)/shard_map/ppermute | solution.py:48
  104.8 5.4 %collective-permute-start.25 = (bf16[656,128]{1,0:T(8,128)(2,1)S(1)}, bf16[656,128]{1,0:T(8,128)(2,1)S(1)}, u32[]{:S(2)}, u32[]{:S(2)}) collective-permute-start(bf16[656,128]{1,0:T(8,128)(2,1)S(1)} %get-tuple-element.63), channel_id=1, source_target_pairs={{0,7},{1,0},{2,1},{3,2},{4,3},{5,4},{6,5},{7,6},{8,15},{9,8},{10,9... | collective-permute-start | bytes 503816 | tf_op jit(solution)/shard_map/ppermute | solution.py:48
  111.8 6.7 %collective-permute-start.26 = (bf16[656,128]{1,0:T(8,128)(2,1)S(1)}, bf16[656,128]{1,0:T(8,128)(2,1)S(1)}, u32[]{:S(2)}, u32[]{:S(2)}) collective-permute-start(bf16[656,128]{1,0:T(8,128)(2,1)S(1)} %get-tuple-element.64), channel_id=1, source_target_pairs={{0,1},{1,2},{2,3},{3,4},{4,5},{5,6},{6,7},{7,0},{8,9},{9,10},{10,1... | collective-permute-start | bytes 503816 | tf_op jit(solution)/shard_map/ppermute | solution.py:48
  113.9 5.4 %collective-permute-start.27 = (bf16[656,128]{1,0:T(8,128)(2,1)S(1)}, bf16[656,128]{1,0:T(8,128)(2,1)S(1)}, u32[]{:S(2)}, u32[]{:S(2)}) collective-permute-start(bf16[656,128]{1,0:T(8,128)(2,1)S(1)} %get-tuple-element.65), channel_id=1, source_target_pairs={{0,7},{1,0},{2,1},{3,2},{4,3},{5,4},{6,5},{7,6},{8,15},{9,8},{10,9... | collective-permute-start | bytes 503816 | tf_op jit(solution)/shard_map/ppermute | solution.py:48
  (10 other events, 68.2 us)

commit v7 on v6

--- a/solution.py
+++ b/solution.py
@@ -288,26 +288,25 @@
 
 
 def pieces_kernel(at_ref, sums_ref, mine_ref, swapped_ref, begun_ref, out_ref, *refs):
-    own_out, up_out, down_out, *away_refs, mine, parts, ends, sem = refs
-    mine[...] = mine_ref[...] + swapped_ref[...].astype(F32)
+    own_out, up_out, down_out, *away_refs, own, parts, ends, sem = refs
 
     def block(by):
-        return pl.ds(pl.multiple_of(lax.rem(at_ref[3] + by + DEEP, DEEP) * PIECE, PIECE), PIECE)
-
-    across = mine[block(4), :].astype(BF16)
+        rows = pl.ds(pl.multiple_of(lax.rem(at_ref[3] + by + DEEP, DEEP) * PIECE, PIECE), PIECE)
+        return mine_ref[rows, :] + swapped_ref[rows, :].astype(F32)
+
+    copies = []
+    for k, (by, ref) in enumerate(zip(AWAY, away_refs)):
+        parts[k] = block(by).astype(BF16)
+        copies += run([pltpu.make_async_copy(parts.at[k], ref, sem.at[3 + k])])
+    own[...] = block(0)
+    copies += run([pltpu.make_async_copy(own, own_out, sem.at[2])])
+    across = block(4).astype(BF16)
     mark = jnp.broadcast_to(place_tag(at_ref, sums_ref), (MARK, 128)).astype(BF16)
-    for h in range(2):
+    for h, out in enumerate((up_out, down_out)):
         for b in range(WIDTH // 128):
             ends[h, b * HALF : (b + 1) * HALF, :] = across[h * HALF : (h + 1) * HALF, b * 128 : (b + 1) * 128]
         ends[h, FIRST - MARK :, :] = mark
-    copies = run([
-        pltpu.make_async_copy(ends.at[0], up_out, sem.at[0]),
-        pltpu.make_async_copy(ends.at[1], down_out, sem.at[1]),
-        pltpu.make_async_copy(mine.at[block(0), :], own_out, sem.at[2]),
-    ])
-    for k, (by, ref) in enumerate(zip(AWAY, away_refs)):
-        parts[k] = mine[block(by), :].astype(BF16)
-        copies += run([pltpu.make_async_copy(parts.at[k], ref, sem.at[3 + k])])
+        copies += run([pltpu.make_async_copy(ends.at[h], out, sem.at[h])])
     wait(copies)
 
 
@@ -443,7 +442,7 @@
         pieces_kernel, [parts, array((PIECE, width), F32), end, end, *away],
         at, sums, mine, swapped, Outside(text_parts),
         scratch=[
-            pltpu.VMEM(half, F32),
+            pltpu.VMEM((PIECE, width), F32),
             pltpu.VMEM((len(AWAY), PIECE, width), BF16),
             pltpu.VMEM((2, FIRST, 128), BF16),
             sems((3 + len(AWAY),)),

time: 127 us -> 127 us (level)
  no operation moved by 1% of the time
where the time goes in v7:
time: 127 us; the launch traced here: 126 us
  starting transfers between devices  46.9 us (37%)
  waiting for transfers between devices  35.7 us (28%)
  Pallas kernels  30.1 us (24%)
  blocking collectives  11.3 us (9%)
  between operations  2.27 us (2%)
    ppermute x28, waiting for transfers between devices, send(): return lax.ppermute(x, 'd', shift(axis, by))  33.1 us
    ppermute x28, starting transfers between devices, send(): return lax.ppermute(x, 'd', shift(axis, by))  32.7 us
    pallas_call x13, Pallas kernels, call(): pl.pallas_call(kernel, out_shape=outputs, in_specs=specs, out_specs=jax.t...  30.1 us
    all_to_all x2, starting transfers between devices, exchange(): return lax.all_to_all(x, 'd', 0, 0, axis_index_groups=groups, tiled=True)  14.2 us
    all_to_all x1, blocking collectives, exchange(): return lax.all_to_all(x, 'd', 0, 0, axis_index_groups=groups, tiled=True)  11.3 us
    all_to_all x2, waiting for transfers between devices, exchange(): return lax.all_to_all(x, 'd', 0, 0, axis_index_groups=groups, tiled=True)  2.64 us
  transfers between devices with their start and end apart: 30, of which 19 were waited for; matrix products, arithmetic and copies ran while one was open for 0% of the time, Pallas kernels for 11%

profile of v7, /device:TPU:28, one launch (start us, length us, event | category | flops | bytes accessed | tf_op | source)
XLA Modules:
  0.0 126.5 jit_solution(3020755388339911173)
XLA Ops:
  0.6 2.7 %shard_map.59 = bf16[1024,1280]{1,0:T(8,128)(2,1)} custom-call(bf16[64,1280]{1,0:T(8,128)(2,1)} %raw_ref.7), custom_call_target="tpu_custom_call" | custom-call | tf_op jit(solution)/shard_map/pallas_call | solution.py:75
  3.3 7.1 %all-to-all-start = ((bf16[16,64,1280]{2,1,0:T(8,128)(2,1)}), bf16[16,64,1280]{2,1,0:T(8,128)(2,1)S(1)}, u32[]{:S(2)}, u32[]{:S(2)}) async-start(bf16[16,64,1280]{2,1,0:T(8,128)(2,1)} %bitcast.18), calls=%async_computation | async-start | bytes 5242880 | tf_op jit(solution)/shard_map/all_to_all | solution.py:52
  11.1 1.7 %shard_map.58 = (bf16[64,1280]{1,0:T(8,128)(2,1)}, f32[8,128]{1,0:T(8,128)S(1)}) custom-call(f32[1]{0:T(128)S(6)} %exp.3.scale_ref, bf16[64,1280]{1,0:T(8,128)(2,1)} %raw_ref.6, bf16[64,1280]{1,0:T(8,128)(2,1)} %raw_ref.7), custom_call_target="tpu_custom_call" | custom-call | tf_op jit(solution)/shard_map/pallas_call | solution.py:75
  12.9 5.9 %collective-permute-start.1 = (bf16[64,1280]{1,0:T(8,128)(2,1)}, bf16[64,1280]{1,0:T(8,128)(2,1)S(1)}, u32[]{:S(2)}, u32[]{:S(2)}) collective-permute-start(bf16[64,1280]{1,0:T(8,128)(2,1)} %get-tuple-element.38.refs_0_), channel_id=1, source_target_pairs={{0,7},{1,0},{2,1},{3,2},{4,3},{5,4},{6,5},{7,6},{8,15},{9,8},{10,9... | collective-permute-start | bytes 491528 | tf_op jit(solution)/shard_map/ppermute | solution.py:48
  18.8 3.2 %collective-permute-done.1.refs_2_ = bf16[64,1280]{1,0:T(8,128)(2,1)S(1)} collective-permute-done((bf16[64,1280]{1,0:T(8,128)(2,1)}, bf16[64,1280]{1,0:T(8,128)(2,1)S(1)}, u32[]{:S(2)}, u32[]{:S(2)}) %collective-permute-start.1) | collective-permute-done | bytes 163872 | tf_op jit(solution)/shard_map/ppermute | solution.py:48
  22.0 3.6 %collective-permute-start.3 = (bf16[64,1280]{1,0:T(8,128)(2,1)S(1)}, bf16[64,1280]{1,0:T(8,128)(2,1)S(1)}, u32[]{:S(2)}, u32[]{:S(2)}) collective-permute-start(bf16[64,1280]{1,0:T(8,128)(2,1)S(1)} %collective-permute-done.1.refs_2_), channel_id=1, source_target_pairs={{0,7},{1,0},{2,1},{3,2},{4,3},{5,4},{6,5},{7,6},{8,15},{9,8},{10,9... | collective-permute-start | bytes 491528 | tf_op jit(solution)/shard_map/ppermute | solution.py:48
  25.6 2.8 %collective-permute-done.3.refs_4_ = bf16[64,1280]{1,0:T(8,128)(2,1)S(1)} collective-permute-done((bf16[64,1280]{1,0:T(8,128)(2,1)S(1)}, bf16[64,1280]{1,0:T(8,128)(2,1)S(1)}, u32[]{:S(2)}, u32[]{:S(2)}) %collective-permute-start.3) | collective-permute-done | bytes 163872 | tf_op jit(solution)/shard_map/ppermute | solution.py:48
  28.5 3.7 %collective-permute-start.5 = (bf16[64,1280]{1,0:T(8,128)(2,1)S(1)}, bf16[64,1280]{1,0:T(8,128)(2,1)S(1)}, u32[]{:S(2)}, u32[]{:S(2)}) collective-permute-start(bf16[64,1280]{1,0:T(8,128)(2,1)S(1)} %collective-permute-done.3.refs_4_), channel_id=1, source_target_pairs={{0,7},{1,0},{2,1},{3,2},{4,3},{5,4},{6,5},{7,6},{8,15},{9,8},{10,9... | collective-permute-start | bytes 491528 | tf_op jit(solution)/shard_map/ppermute | solution.py:48
  32.8 2.2 %collective-permute-done.5.refs_6_ = bf16[64,1280]{1,0:T(8,128)(2,1)S(1)} collective-permute-done((bf16[64,1280]{1,0:T(8,128)(2,1)S(1)}, bf16[64,1280]{1,0:T(8,128)(2,1)S(1)}, u32[]{:S(2)}, u32[]{:S(2)}) %collective-permute-start.5) | collective-permute-done | bytes 163872 | tf_op jit(solution)/shard_map/ppermute | solution.py:48
  35.0 4.0 %collective-permute-done.4.refs_5_ = bf16[64,1280]{1,0:T(8,128)(2,1)S(1)} collective-permute-done((bf16[64,1280]{1,0:T(8,128)(2,1)}, bf16[64,1280]{1,0:T(8,128)(2,1)S(1)}, u32[]{:S(2)}, u32[]{:S(2)}) %collective-permute-start.4) | collective-permute-done | bytes 163872 | tf_op jit(solution)/shard_map/ppermute | solution.py:48
  39.4 1.7 %collective-permute-start.6 = (bf16[32,1280]{1,0:T(8,128)(2,1)S(1)}, bf16[32,1280]{1,0:T(8,128)(2,1)}, u32[]{:S(2)}, u32[]{:S(2)}) collective-permute-start(bf16[32,1280]{1,0:T(8,128)(2,1)S(1)} %slice.8), channel_id=1, source_target_pairs={{0,1},{1,2},{2,3},{3,4},{4,5},{5,6},{6,7},{7,0},{8,9},{9,10},{10,1... | collective-permute-start | bytes 245768 | tf_op jit(solution)/shard_map/ppermute | solution.py:48
  41.8 2.3 %collective-permute-done.7.refs_8_ = bf16[32,1280]{1,0:T(8,128)(2,1)} collective-permute-done((bf16[32,1280]{1,0:T(8,128)(2,1)S(1)}, bf16[32,1280]{1,0:T(8,128)(2,1)}, u32[]{:S(2)}, u32[]{:S(2)}) %collective-permute-start.7) | collective-permute-done | bytes 81952 | tf_op jit(solution)/shard_map/ppermute | solution.py:48
  47.1 6.3 %shard_map.60 = (bf16[1024,1280]{1,0:T(8,128)(2,1)}, f32[1024,1024]{1,0:T(8,128)S(1)}, f32[4,256]{1,0:T(4,128)S(1)}, f32[8,256]{1,0:T(8,128)S(1)}) custom-call(s32[5]{0:T(128)S(1)} %stack.23.at_ref, f32[1]{0:T(128)S(6)} %exp.3.scale_ref, f32[8,128]{1,0:T(8,128)S(1)} %get-tuple-element.37.pairs_ref, bf16[1024,1280]{1,0:T(8,128)(2,1)S(1)} %bitcast.11, ...), custom_call_target="tpu_custom_call" | custom-call | tf_op jit(solution)/shard_map/pallas_call | solution.py:75
  55.2 11.3 %all_to_all.33 = f32[16,8,256]{2,1,0:T(8,128)S(1)} all-to-all(f32[16,8,256]{2,1,0:T(8,128)S(1)} %bitcast.15), channel_id=1, replica_groups={{0,16,32,48,64,80,96,112,128,144,160,176,192,208,224,240},{1,17,33,49,6..., dimensions={0} | all-to-all | bytes 262144 | tf_op jit(solution)/shard_map/all_to_all | solution.py:52
  67.3 2.3 %collective-permute-start.18 = (f32[8,256]{1,0:T(8,128)S(1)}, f32[8,256]{1,0:T(8,128)S(1)}, u32[]{:S(2)}, u32[]{:S(2)}) collective-permute-start(f32[8,256]{1,0:T(8,128)S(1)} %get-tuple-element.43), channel_id=1, source_target_pairs={{0,8},{1,9},{2,10},{3,11},{4,12},{5,13},{6,14},{7,15},{8,0},{9,1},... | collective-permute-start | bytes 24584 | tf_op jit(solution)/shard_map/ppermute | solution.py:48
  70.4 2.9 %shard_map.63 = (bf16[512,1024]{1,0:T(8,128)(2,1)S(1)}, bf16[1024,1024]{1,0:T(8,128)(2,1)S(1)}, bf16[512,1280]{1,0:T(8,128)(2,1)S(1)}, f32[8,128]{1,0:T(8,128)S(1)}) custom-call(s32[5]{0:T(128)S(1)} %stack.23.at_ref, f32[1]{0:T(128)S(6)} %exp.3.scale_ref, f32[1024,1024]{1,0:T(8,128)S(1)} %get-tuple-element.39.logits_ref, bf16[1024,1280]{1,0:T(8,128)(2,1)S(1)} %bitcast.12, ...), custom_call_target="tpu_custom_call" | custom-call | tf_op jit(solution)/shard_map/pallas_call | solution.py:75
  73.7 4.3 %shard_map.64 = (bf16[10496,128]{1,0:T(8,128)(2,1)}, f32[512,1280]{1,0:T(8,128)S(1)}) custom-call(f32[1]{0:T(128)S(6)} %exp.3.scale_ref, bf16[512,1024]{1,0:T(8,128)(2,1)S(1)} %get-tuple-element.45.weights_ref, bf16[1024,1024]{1,0:T(8,128)(2,1)S(1)} %get-tuple-element.46.turned_ref, bf16[1024,1280]{1,0:T(8,128)(2,1)S(1)} %copy-done, ...), custom_call_target="tpu_custom_call" | custom-call | tf_op jit(solution)/shard_map/pallas_call | solution.py:75
  78.0 1.8 %shard_map.65 = (bf16[10496,128]{1,0:T(8,128)(2,1)}, f32[64,1280]{1,0:T(8,128)}, bf16[336,128]{1,0:T(8,128)(2,1)}, bf16[336,128]{1,0:T(8,128)(2,1)}, bf16[64,128...) custom-call(s32[5]{0:T(128)S(1)} %stack.23.at_ref, ...), custom_call_target="tpu_custom_call", output_to_operand_aliasing={{0}: (4, {})} | custom-call | tf_op jit(solution)/shard_map/pallas_call | solution.py:75
  79.8 7.1 %all-to-all-start.2 = ((bf16[16,656,128]{2,1,0:T(8,128)(2,1)}), bf16[16,656,128]{2,1,0:T(8,128)(2,1)S(1)}, u32[]{:S(2)}, u32[]{:S(2)}) async-start(bf16[16,656,128]{2,1,0:T(8,128)(2,1)} %bitcast.17), calls=%async_computation.2 | async-start | bytes 5373952 | tf_op jit(solution)/shard_map/all_to_all | solution.py:52
  88.3 1.9 %collective-permute-start.21 = (bf16[336,128]{1,0:T(8,128)(2,1)S(1)}, bf16[336,128]{1,0:T(8,128)(2,1)S(1)}, u32[]{:S(2)}, u32[]{:S(2)}) collective-permute-start(bf16[336,128]{1,0:T(8,128)(2,1)S(1)} %copy-done.10), channel_id=1, source_target_pairs={{0,7},{1,0},{2,1},{3,2},{4,3},{5,4},{6,5},{7,6},{8,15},{9,8},{10,9... | collective-permute-start | bytes 258056 | tf_op jit(solution)/shard_map/ppermute | solution.py:48
  90.2 2.5 %collective-permute-done.20.below_ref = bf16[336,128]{1,0:T(8,128)(2,1)S(1)} collective-permute-done((bf16[336,128]{1,0:T(8,128)(2,1)S(1)}, bf16[336,128]{1,0:T(8,128)(2,1)S(1)}, u32[]{:S(2)}, u32[]{:S(2)}) %collective-permute-start.20) | collective-permute-done | bytes 86048 | tf_op jit(solution)/shard_map/ppermute | solution.py:48
  95.2 2.5 %collective-permute-start.23 = (bf16[656,128]{1,0:T(8,128)(2,1)S(1)}, bf16[656,128]{1,0:T(8,128)(2,1)S(1)}, u32[]{:S(2)}, u32[]{:S(2)}) collective-permute-start(bf16[656,128]{1,0:T(8,128)(2,1)S(1)} %get-tuple-element.61), channel_id=1, source_target_pairs={{0,7},{1,0},{2,1},{3,2},{4,3},{5,4},{6,5},{7,6},{8,15},{9,8},{10,9... | collective-permute-start | bytes 503816 | tf_op jit(solution)/shard_map/ppermute | solution.py:48
  97.7 3.3 %collective-permute-done.22.below_ref = bf16[656,128]{1,0:T(8,128)(2,1)S(1)} collective-permute-done((bf16[656,128]{1,0:T(8,128)(2,1)S(1)}, bf16[656,128]{1,0:T(8,128)(2,1)S(1)}, u32[]{:S(2)}, u32[]{:S(2)}) %collective-permute-start.22) | collective-permute-done | bytes 167968 | tf_op jit(solution)/shard_map/ppermute | solution.py:48
  101.1 1.6 %shard_map.67 = (bf16[656,128]{1,0:T(8,128)(2,1)S(1)}, bf16[656,128]{1,0:T(8,128)(2,1)S(1)}) custom-call(s32[5]{0:T(128)S(1)} %stack.23.at_ref, f32[8,128]{1,0:T(8,128)S(1)} %get-tuple-element.44.sums_ref, bf16[64,1280]{1,0:T(8,128)(2,1)} %get-tuple-element.54.up_ref, bf16[64,1280]{1,0:T(8,128)(2,1)} %get-tuple-element.55.down_ref, ...), custom_call_target="tpu_custom_call" | custom-call | tf_op jit(solution)/shard_map/pallas_call | solution.py:75
  102.7 1.7 %collective-permute-start.24 = (bf16[656,128]{1,0:T(8,128)(2,1)S(1)}, bf16[656,128]{1,0:T(8,128)(2,1)S(1)}, u32[]{:S(2)}, u32[]{:S(2)}) collective-permute-start(bf16[656,128]{1,0:T(8,128)(2,1)S(1)} %get-tuple-element.62), channel_id=1, source_target_pairs={{0,1},{1,2},{2,3},{3,4},{4,5},{5,6},{6,7},{7,0},{8,9},{9,10},{10,1... | collective-permute-start | bytes 503816 | tf_op jit(solution)/shard_map/ppermute | solution.py:48
  104.3 1.7 %collective-permute-start.25 = (bf16[656,128]{1,0:T(8,128)(2,1)S(1)}, bf16[656,128]{1,0:T(8,128)(2,1)S(1)}, u32[]{:S(2)}, u32[]{:S(2)}) collective-permute-start(bf16[656,128]{1,0:T(8,128)(2,1)S(1)} %get-tuple-element.63), channel_id=1, source_target_pairs={{0,7},{1,0},{2,1},{3,2},{4,3},{5,4},{6,5},{7,6},{8,15},{9,8},{10,9... | collective-permute-start | bytes 503816 | tf_op jit(solution)/shard_map/ppermute | solution.py:48
  106.1 3.3 %collective-permute-done.24.below_ref = bf16[656,128]{1,0:T(8,128)(2,1)S(1)} collective-permute-done((bf16[656,128]{1,0:T(8,128)(2,1)S(1)}, bf16[656,128]{1,0:T(8,128)(2,1)S(1)}, u32[]{:S(2)}, u32[]{:S(2)}) %collective-permute-start.24) | collective-permute-done | bytes 167968 | tf_op jit(solution)/shard_map/ppermute | solution.py:48
  111.3 2.1 %collective-permute-start.26 = (bf16[656,128]{1,0:T(8,128)(2,1)S(1)}, bf16[656,128]{1,0:T(8,128)(2,1)S(1)}, u32[]{:S(2)}, u32[]{:S(2)}) collective-permute-start(bf16[656,128]{1,0:T(8,128)(2,1)S(1)} %get-tuple-element.64), channel_id=1, source_target_pairs={{0,1},{1,2},{2,3},{3,4},{4,5},{5,6},{6,7},{7,0},{8,9},{9,10},{10,1... | collective-permute-start | bytes 503816 | tf_op jit(solution)/shard_map/ppermute | solution.py:48
  114.6 3.3 %collective-permute-done.26.below_ref = bf16[656,128]{1,0:T(8,128)(2,1)S(1)} collective-permute-done((bf16[656,128]{1,0:T(8,128)(2,1)S(1)}, bf16[656,128]{1,0:T(8,128)(2,1)S(1)}, u32[]{:S(2)}, u32[]{:S(2)}) %collective-permute-start.26) | collective-permute-done | bytes 167968 | tf_op jit(solution)/shard_map/ppermute | solution.py:48
  118.8 2.5 %shard_map.69 = (bf16[64,1280]{1,0:T(8,128)(2,1)}, f32[8,128]{1,0:T(8,128)S(1)}) custom-call(s32[5]{0:T(128)S(1)} %stack.23.at_ref, f32[8,128]{1,0:T(8,128)S(1)} %get-tuple-element.44.sums_ref, bf16[64,1280]{1,0:T(8,128)(2,1)} %raw_ref.6, f32[64,1280]{1,0:T(8,128)} %get-tuple-element.51.own_ref, bf16[656,128]{1,0:T(8,128)(2,1)S(1)} %collective-permute-done.26.below_ref, ...), custom_call_target="tpu_custom_call" | custom-call | tf_op jit(solution)/shard_map/pallas_call | solution.py:75
  121.3 2.6 %all-to-all-done.2 = bf16[16,656,128]{2,1,0:T(8,128)(2,1)S(1)} async-done(((bf16[16,656,128]{2,1,0:T(8,128)(2,1)}), bf16[16,656,128]{2,1,0:T(8,128)(2,1)S(1)}, u32[]{:S(2)}, u32[]{:S(2)}) %all-to-all-start.2) | async-done | bytes 2687008 | tf_op jit(solution)/shard_map/all_to_all | solution.py:52
  123.9 1.8 %shard_map.70 = (bf16[64,1280]{1,0:T(8,128)(2,1)}, f32[1]{0:T(128)S(4)}) custom-call(bf16[64,1280]{1,0:T(8,128)(2,1)} %raw_ref.7, f32[8,128]{1,0:T(8,128)S(1)} %get-tuple-element.66.loss_ref, bf16[10496,128]{1,0:T(8,128)(2,1)S(1)} %bitcast.14), custom_call_target="tpu_custom_call" | custom-call | tf_op jit(solution)/shard_map/pallas_call | solution.py:75
  (69 shorter events, 16.4 us)
Async XLA Ops:
  3.3 43.7 %all-to-all-start = ((bf16[16,64,1280]{2,1,0:T(8,128)(2,1)}), bf16[16,64,1280]{2,1,0:T(8,128)(2,1)S(1)}, u32[]{:S(2)}, u32[]{:S(2)}) async-start(bf16[16,64,1280]{2,1,0:T(8,128)(2,1)} %bitcast.18), calls=%async_computation | async-start | bytes 5242880 | tf_op jit(solution)/shard_map/all_to_all | solution.py:52
  12.9 9.1 %collective-permute-start.1 = (bf16[64,1280]{1,0:T(8,128)(2,1)}, bf16[64,1280]{1,0:T(8,128)(2,1)S(1)}, u32[]{:S(2)}, u32[]{:S(2)}) collective-permute-start(bf16[64,1280]{1,0:T(8,128)(2,1)} %get-tuple-element.38.refs_0_), channel_id=1, source_target_pairs={{0,7},{1,0},{2,1},{3,2},{4,3},{5,4},{6,5},{7,6},{8,15},{9,8},{10,9... | collective-permute-start | bytes 491528 | tf_op jit(solution)/shard_map/ppermute | solution.py:48
  18.8 6.8 %collective-permute-start = (bf16[64,1280]{1,0:T(8,128)(2,1)}, bf16[64,1280]{1,0:T(8,128)(2,1)S(1)}, u32[]{:S(2)}, u32[]{:S(2)}) collective-permute-start(bf16[64,1280]{1,0:T(8,128)(2,1)} %get-tuple-element.38.refs_0_), channel_id=1, source_target_pairs={{0,1},{1,2},{2,3},{3,4},{4,5},{5,6},{6,7},{7,0},{8,9},{9,10},{10,1... | collective-permute-start | bytes 491528 | tf_op jit(solution)/shard_map/ppermute | solution.py:48
  22.0 25.0 %copy-start.3 = (bf16[64,1280]{1,0:T(8,128)(2,1)}, bf16[64,1280]{1,0:T(8,128)(2,1)S(1)}, u32[]{:S(2)}) copy-start(bf16[64,1280]{1,0:T(8,128)(2,1)S(1)} %collective-permute-done.1.refs_2_) | copy-start | bytes 491524
  22.0 6.4 %collective-permute-start.3 = (bf16[64,1280]{1,0:T(8,128)(2,1)S(1)}, bf16[64,1280]{1,0:T(8,128)(2,1)S(1)}, u32[]{:S(2)}, u32[]{:S(2)}) collective-permute-start(bf16[64,1280]{1,0:T(8,128)(2,1)S(1)} %collective-permute-done.1.refs_2_), channel_id=1, source_target_pairs={{0,7},{1,0},{2,1},{3,2},{4,3},{5,4},{6,5},{7,6},{8,15},{9,8},{10,9... | collective-permute-start | bytes 491528 | tf_op jit(solution)/shard_map/ppermute | solution.py:48
  25.6 21.4 %copy-start.4 = (bf16[64,1280]{1,0:T(8,128)(2,1)}, bf16[64,1280]{1,0:T(8,128)(2,1)S(1)}, u32[]{:S(2)}) copy-start(bf16[64,1280]{1,0:T(8,128)(2,1)S(1)} %collective-permute-done.refs_1_) | copy-start | bytes 491524
  25.6 6.6 %collective-permute-start.2 = (bf16[64,1280]{1,0:T(8,128)(2,1)S(1)}, bf16[64,1280]{1,0:T(8,128)(2,1)}, u32[]{:S(2)}, u32[]{:S(2)}) collective-permute-start(bf16[64,1280]{1,0:T(8,128)(2,1)S(1)} %collective-permute-done.refs_1_), channel_id=1, source_target_pairs={{0,1},{1,2},{2,3},{3,4},{4,5},{5,6},{6,7},{7,0},{8,9},{9,10},{10,1... | collective-permute-start | bytes 491528 | tf_op jit(solution)/shard_map/ppermute | solution.py:48
  28.5 6.5 %collective-permute-start.5 = (bf16[64,1280]{1,0:T(8,128)(2,1)S(1)}, bf16[64,1280]{1,0:T(8,128)(2,1)S(1)}, u32[]{:S(2)}, u32[]{:S(2)}) collective-permute-start(bf16[64,1280]{1,0:T(8,128)(2,1)S(1)} %collective-permute-done.3.refs_4_), channel_id=1, source_target_pairs={{0,7},{1,0},{2,1},{3,2},{4,3},{5,4},{6,5},{7,6},{8,15},{9,8},{10,9... | collective-permute-start | bytes 491528 | tf_op jit(solution)/shard_map/ppermute | solution.py:48
  32.3 6.7 %collective-permute-start.4 = (bf16[64,1280]{1,0:T(8,128)(2,1)}, bf16[64,1280]{1,0:T(8,128)(2,1)S(1)}, u32[]{:S(2)}, u32[]{:S(2)}) collective-permute-start(bf16[64,1280]{1,0:T(8,128)(2,1)} %collective-permute-done.2.refs_3_), channel_id=1, source_target_pairs={{0,1},{1,2},{2,3},{3,4},{4,5},{5,6},{6,7},{7,0},{8,9},{9,10},{10,1... | collective-permute-start | bytes 491528 | tf_op jit(solution)/shard_map/ppermute | solution.py:48
  32.3 6.8 %collective-permute-start.8 = (bf16[64,1280]{1,0:T(8,128)(2,1)}, bf16[64,1280]{1,0:T(8,128)(2,1)S(1)}, u32[]{:S(2)}, u32[]{:S(2)}) collective-permute-start(bf16[64,1280]{1,0:T(8,128)(2,1)} %get-tuple-element.38.refs_0_), channel_id=1, source_target_pairs={{0,8},{1,9},{2,10},{3,11},{4,12},{5,13},{6,14},{7,15},{8,0},{9,1},... | collective-permute-start | bytes 491528 | tf_op jit(solution)/shard_map/ppermute | solution.py:48
  32.3 7.1 %collective-permute-start.10 = (bf16[64,1280]{1,0:T(8,128)(2,1)S(1)}, bf16[64,1280]{1,0:T(8,128)(2,1)S(1)}, u32[]{:S(2)}, u32[]{:S(2)}) collective-permute-start(bf16[64,1280]{1,0:T(8,128)(2,1)S(1)} %collective-permute-done.1.refs_2_), channel_id=1, source_target_pairs={{0,8},{1,9},{2,10},{3,11},{4,12},{5,13},{6,14},{7,15},{8,0},{9,1},... | collective-permute-start | bytes 491528 | tf_op jit(solution)/shard_map/ppermute | solution.py:48
  32.8 8.4 %collective-permute-start.9 = (bf16[64,1280]{1,0:T(8,128)(2,1)S(1)}, bf16[64,1280]{1,0:T(8,128)(2,1)S(1)}, u32[]{:S(2)}, u32[]{:S(2)}) collective-permute-start(bf16[64,1280]{1,0:T(8,128)(2,1)S(1)} %collective-permute-done.refs_1_), channel_id=1, source_target_pairs={{0,8},{1,9},{2,10},{3,11},{4,12},{5,13},{6,14},{7,15},{8,0},{9,1},... | collective-permute-start | bytes 491528 | tf_op jit(solution)/shard_map/ppermute | solution.py:48
  35.0 6.2 %collective-permute-start.12 = (bf16[64,1280]{1,0:T(8,128)(2,1)S(1)}, bf16[64,1280]{1,0:T(8,128)(2,1)S(1)}, u32[]{:S(2)}, u32[]{:S(2)}) collective-permute-start(bf16[64,1280]{1,0:T(8,128)(2,1)S(1)} %collective-permute-done.3.refs_4_), channel_id=1, source_target_pairs={{0,8},{1,9},{2,10},{3,11},{4,12},{5,13},{6,14},{7,15},{8,0},{9,1},... | collective-permute-start | bytes 491528 | tf_op jit(solution)/shard_map/ppermute | solution.py:48
  39.0 6.5 %collective-permute-start.11 = (bf16[64,1280]{1,0:T(8,128)(2,1)}, bf16[64,1280]{1,0:T(8,128)(2,1)}, u32[]{:S(2)}, u32[]{:S(2)}) collective-permute-start(bf16[64,1280]{1,0:T(8,128)(2,1)} %collective-permute-done.2.refs_3_), channel_id=1, source_target_pairs={{0,8},{1,9},{2,10},{3,11},{4,12},{5,13},{6,14},{7,15},{8,0},{9,1},... | collective-permute-start | bytes 491528 | tf_op jit(solution)/shard_map/ppermute | solution.py:48
  39.0 5.0 %collective-permute-start.7 = (bf16[32,1280]{1,0:T(8,128)(2,1)S(1)}, bf16[32,1280]{1,0:T(8,128)(2,1)}, u32[]{:S(2)}, u32[]{:S(2)}) collective-permute-start(bf16[32,1280]{1,0:T(8,128)(2,1)S(1)} %slice.9), channel_id=1, source_target_pairs={{0,7},{1,0},{2,1},{3,2},{4,3},{5,4},{6,5},{7,6},{8,15},{9,8},{10,9... | collective-permute-start | bytes 245768 | tf_op jit(solution)/shard_map/ppermute | solution.py:48
  39.4 6.0 %collective-permute-start.6 = (bf16[32,1280]{1,0:T(8,128)(2,1)S(1)}, bf16[32,1280]{1,0:T(8,128)(2,1)}, u32[]{:S(2)}, u32[]{:S(2)}) collective-permute-start(bf16[32,1280]{1,0:T(8,128)(2,1)S(1)} %slice.8), channel_id=1, source_target_pairs={{0,1},{1,2},{2,3},{3,4},{4,5},{5,6},{6,7},{7,0},{8,9},{9,10},{10,1... | collective-permute-start | bytes 245768 | tf_op jit(solution)/shard_map/ppermute | solution.py:48
  41.2 4.5 %collective-permute-start.14 = (bf16[64,1280]{1,0:T(8,128)(2,1)S(1)}, bf16[64,1280]{1,0:T(8,128)(2,1)}, u32[]{:S(2)}, u32[]{:S(2)}) collective-permute-start(bf16[64,1280]{1,0:T(8,128)(2,1)S(1)} %collective-permute-done.5.refs_6_), channel_id=1, source_target_pairs={{0,8},{1,9},{2,10},{3,11},{4,12},{5,13},{6,14},{7,15},{8,0},{9,1},... | collective-permute-start | bytes 491528 | tf_op jit(solution)/shard_map/ppermute | solution.py:48
  41.2 5.8 %collective-permute-start.13 = (bf16[64,1280]{1,0:T(8,128)(2,1)S(1)}, bf16[64,1280]{1,0:T(8,128)(2,1)}, u32[]{:S(2)}, u32[]{:S(2)}) collective-permute-start(bf16[64,1280]{1,0:T(8,128)(2,1)S(1)} %collective-permute-done.4.refs_5_), channel_id=1, source_target_pairs={{0,8},{1,9},{2,10},{3,11},{4,12},{5,13},{6,14},{7,15},{8,0},{9,1},... | collective-permute-start | bytes 491528 | tf_op jit(solution)/shard_map/ppermute | solution.py:48
  44.1 1.6 %collective-permute-start.16 = (bf16[32,1280]{1,0:T(8,128)(2,1)}, bf16[32,1280]{1,0:T(8,128)(2,1)}, u32[]{:S(2)}, u32[]{:S(2)}) collective-permute-start(bf16[32,1280]{1,0:T(8,128)(2,1)} %collective-permute-done.7.refs_8_), channel_id=1, source_target_pairs={{0,8},{1,9},{2,10},{3,11},{4,12},{5,13},{6,14},{7,15},{8,0},{9,1},... | collective-permute-start | bytes 245768 | tf_op jit(solution)/shard_map/ppermute | solution.py:48
  45.4 1.6 %collective-permute-start.15 = (bf16[32,1280]{1,0:T(8,128)(2,1)}, bf16[32,1280]{1,0:T(8,128)(2,1)}, u32[]{:S(2)}, u32[]{:S(2)}) collective-permute-start(bf16[32,1280]{1,0:T(8,128)(2,1)} %collective-permute-done.6.refs_7_), channel_id=1, source_target_pairs={{0,8},{1,9},{2,10},{3,11},{4,12},{5,13},{6,14},{7,15},{8,0},{9,1},... | collective-permute-start | bytes 245768 | tf_op jit(solution)/shard_map/ppermute | solution.py:48
  53.4 1.3 collective-permute-start.17
  67.3 3.1 %collective-permute-start.18 = (f32[8,256]{1,0:T(8,128)S(1)}, f32[8,256]{1,0:T(8,128)S(1)}, u32[]{:S(2)}, u32[]{:S(2)}) collective-permute-start(f32[8,256]{1,0:T(8,128)S(1)} %get-tuple-element.43), channel_id=1, source_target_pairs={{0,8},{1,9},{2,10},{3,11},{4,12},{5,13},{6,14},{7,15},{8,0},{9,1},... | collective-permute-start | bytes 24584 | tf_op jit(solution)/shard_map/ppermute | solution.py:48
  73.2 4.7 %collective-permute-start.19 = (bf16[512,1280]{1,0:T(8,128)(2,1)S(1)}, bf16[512,1280]{1,0:T(8,128)(2,1)S(1)}, u32[]{:S(2)}, u32[]{:S(2)}) collective-permute-start(bf16[512,1280]{1,0:T(8,128)(2,1)S(1)} %get-tuple-element.49), channel_id=1, source_target_pairs={{0,8},{1,9},{2,10},{3,11},{4,12},{5,13},{6,14},{7,15},{8,0},{9,1},... | collective-permute-start | bytes 3932168 | tf_op jit(solution)/shard_map/ppermute | solution.py:48
  79.8 44.1 %all-to-all-start.2 = ((bf16[16,656,128]{2,1,0:T(8,128)(2,1)}), bf16[16,656,128]{2,1,0:T(8,128)(2,1)S(1)}, u32[]{:S(2)}, u32[]{:S(2)}) async-start(bf16[16,656,128]{2,1,0:T(8,128)(2,1)} %bitcast.17), calls=%async_computation.2 | async-start | bytes 5373952 | tf_op jit(solution)/shard_map/all_to_all | solution.py:52
  86.9 5.8 %collective-permute-start.20 = (bf16[336,128]{1,0:T(8,128)(2,1)S(1)}, bf16[336,128]{1,0:T(8,128)(2,1)S(1)}, u32[]{:S(2)}, u32[]{:S(2)}) collective-permute-start(bf16[336,128]{1,0:T(8,128)(2,1)S(1)} %copy-done.11), channel_id=1, source_target_pairs={{0,1},{1,2},{2,3},{3,4},{4,5},{5,6},{6,7},{7,0},{8,9},{9,10},{10,1... | collective-permute-start | bytes 258056 | tf_op jit(solution)/shard_map/ppermute | solution.py:48
  88.3 4.5 %collective-permute-start.21 = (bf16[336,128]{1,0:T(8,128)(2,1)S(1)}, bf16[336,128]{1,0:T(8,128)(2,1)S(1)}, u32[]{:S(2)}, u32[]{:S(2)}) collective-permute-start(bf16[336,128]{1,0:T(8,128)(2,1)S(1)} %copy-done.10), channel_id=1, source_target_pairs={{0,7},{1,0},{2,1},{3,2},{4,3},{5,4},{6,5},{7,6},{8,15},{9,8},{10,9... | collective-permute-start | bytes 258056 | tf_op jit(solution)/shard_map/ppermute | solution.py:48
  94.4 6.7 %collective-permute-start.22 = (bf16[656,128]{1,0:T(8,128)(2,1)S(1)}, bf16[656,128]{1,0:T(8,128)(2,1)S(1)}, u32[]{:S(2)}, u32[]{:S(2)}) collective-permute-start(bf16[656,128]{1,0:T(8,128)(2,1)S(1)} %get-tuple-element.60), channel_id=1, source_target_pairs={{0,1},{1,2},{2,3},{3,4},{4,5},{5,6},{6,7},{7,0},{8,9},{9,10},{10,1... | collective-permute-start | bytes 503816 | tf_op jit(solution)/shard_map/ppermute | solution.py:48
  95.2 5.9 %collective-permute-start.23 = (bf16[656,128]{1,0:T(8,128)(2,1)S(1)}, bf16[656,128]{1,0:T(8,128)(2,1)S(1)}, u32[]{:S(2)}, u32[]{:S(2)}) collective-permute-start(bf16[656,128]{1,0:T(8,128)(2,1)S(1)} %get-tuple-element.61), channel_id=1, source_target_pairs={{0,7},{1,0},{2,1},{3,2},{4,3},{5,4},{6,5},{7,6},{8,15},{9,8},{10,9... | collective-permute-start | bytes 503816 | tf_op jit(solution)/shard_map/ppermute | solution.py:48
  102.7 6.7 %collective-permute-start.24 = (bf16[656,128]{1,0:T(8,128)(2,1)S(1)}, bf16[656,128]{1,0:T(8,128)(2,1)S(1)}, u32[]{:S(2)}, u32[]{:S(2)}) collective-permute-start(bf16[656,128]{1,0:T(8,128)(2,1)S(1)} %get-tuple-element.62), channel_id=1, source_target_pairs={{0,1},{1,2},{2,3},{3,4},{4,5},{5,6},{6,7},{7,0},{8,9},{9,10},{10,1... | collective-permute-start | bytes 503816 | tf_op jit(solution)/shard_map/ppermute | solution.py:48
  104.3 5.4 %collective-permute-start.25 = (bf16[656,128]{1,0:T(8,128)(2,1)S(1)}, bf16[656,128]{1,0:T(8,128)(2,1)S(1)}, u32[]{:S(2)}, u32[]{:S(2)}) collective-permute-start(bf16[656,128]{1,0:T(8,128)(2,1)S(1)} %get-tuple-element.63), channel_id=1, source_target_pairs={{0,7},{1,0},{2,1},{3,2},{4,3},{5,4},{6,5},{7,6},{8,15},{9,8},{10,9... | collective-permute-start | bytes 503816 | tf_op jit(solution)/shard_map/ppermute | solution.py:48
  111.3 6.7 %collective-permute-start.26 = (bf16[656,128]{1,0:T(8,128)(2,1)S(1)}, bf16[656,128]{1,0:T(8,128)(2,1)S(1)}, u32[]{:S(2)}, u32[]{:S(2)}) collective-permute-start(bf16[656,128]{1,0:T(8,128)(2,1)S(1)} %get-tuple-element.64), channel_id=1, source_target_pairs={{0,1},{1,2},{2,3},{3,4},{4,5},{5,6},{6,7},{7,0},{8,9},{9,10},{10,1... | collective-permute-start | bytes 503816 | tf_op jit(solution)/shard_map/ppermute | solution.py:48
  113.4 5.4 %collective-permute-start.27 = (bf16[656,128]{1,0:T(8,128)(2,1)S(1)}, bf16[656,128]{1,0:T(8,128)(2,1)S(1)}, u32[]{:S(2)}, u32[]{:S(2)}) collective-permute-start(bf16[656,128]{1,0:T(8,128)(2,1)S(1)} %get-tuple-element.65), channel_id=1, source_target_pairs={{0,7},{1,0},{2,1},{3,2},{4,3},{5,4},{6,5},{7,6},{8,15},{9,8},{10,9... | collective-permute-start | bytes 503816 | tf_op jit(solution)/shard_map/ppermute | solution.py:48
  (10 other events, 67.9 us)

commit v8 on v7

--- a/solution.py
+++ b/solution.py
@@ -104,27 +104,23 @@
     return values / norm, norm
 
 
-def image_unit_kernel(scale_ref, raw_ref, text_ref, out_ref, pairs_ref, raw, text, unit, sem):
+def units_kernel(
+    text_ref, image_ref, text_out, image_out, pairs_ref, text_raw, image_raw, text, image, sem, out_sem
+):
     copies = run([
-        pltpu.make_async_copy(raw_ref, raw, sem.at[0]), pltpu.make_async_copy(text_ref, text, sem.at[1])
+        pltpu.make_async_copy(text_ref, text_raw, sem.at[0]), pltpu.make_async_copy(image_ref, image_raw, sem.at[1])
     ])
     copies[0].wait()
-    unit[...] = unit_rows(raw[...])[0].astype(BF16)
-    out = run([pltpu.make_async_copy(unit, out_ref, sem.at[2])])
+    text[...] = unit_rows(text_raw[...])[0].astype(BF16)
+    out = run([
+        pltpu.make_async_copy(text, text_out.at[pl.ds(k * PIECE, PIECE), :], out_sem.at[k]) for k in range(PEERS)
+    ])
     copies[1].wait()
-    other = unit_rows(text[...])[0].astype(BF16)
-    total = jnp.sum(unit[...].astype(F32) * other.astype(F32), keepdims=True)
-    pairs_ref[...] = jnp.broadcast_to(total * (scale_ref[0] * LOG2E), pairs_ref.shape)
+    image[...] = unit_rows(image_raw[...])[0].astype(BF16)
+    out += run([pltpu.make_async_copy(image, image_out, out_sem.at[PEERS])])
+    total = jnp.sum(image[...].astype(F32) * text[...].astype(F32), keepdims=True)
+    pairs_ref[...] = jnp.broadcast_to(total, pairs_ref.shape)
     wait(out)
-
-
-def text_units_kernel(raw_ref, out_ref, raw, unit, sem):
-    wait(run([pltpu.make_async_copy(raw_ref, raw, sem.at[0])]))
-    unit[...] = unit_rows(raw[...])[0].astype(BF16)
-    wait(run([
-        pltpu.make_async_copy(unit, out_ref.at[pl.ds(k * PIECE, PIECE), :], sem.at[k])
-        for k in range(PEERS)
-    ]))
 
 
 def to_lanes(column):
@@ -175,15 +171,17 @@
         part = col_lse[:, k * TILE : (k + 1) * TILE]
         keep_ref[k : k + 1, :] = jnp.where(first, part, row_lse[k])
         give_ref[k : k + 1, :] = jnp.where(first, row_lse[(k + STEPS // 2) % STEPS], part)
-    give_ref[STEPS:, :] = jnp.broadcast_to(pairs_ref[:1, :1], (STEPS, TILE))
+    pairs = jnp.broadcast_to(pairs_ref[:1, :1] * scale, (STEPS, TILE))
+    keep_ref[STEPS:, :] = pairs
+    give_ref[STEPS:, :] = pairs
     wait(out)
 
 
-def spread_kernel(at_ref, keep_ref, recv_ref, pairs_ref, out_ref):
-    keep, recv = keep_ref[...], recv_ref[:STEPS, :]
+def spread_kernel(at_ref, keep_ref, recv_ref, out_ref):
+    keep, recv = keep_ref[:STEPS, :], recv_ref[:STEPS, :]
     top = jnp.maximum(keep, recv)
     both = top + jnp.log2(jnp.exp2(keep - top) + jnp.exp2(recv - top))
-    pairs = recv_ref[STEPS:, :] + pairs_ref[:1, :1]
+    pairs = keep_ref[STEPS:, :] + recv_ref[STEPS:, :]
     first = at_ref[2] == 0
     block = jnp.concatenate([jnp.where(first, keep, both), jnp.where(first, recv, pairs)], axis=0)
     for k in range(PEERS):
@@ -404,22 +402,21 @@
     raw = pltpu.VMEM((PIECE, width), BF16)
     sems = pltpu.SemaphoreType.DMA
 
-    image_unit, pairs = call(
-        image_unit_kernel, [array((PIECE, width), BF16), local((8, 128), F32)],
-        scale, Outside(image_emb), Outside(text_emb), scratch=[raw, raw, raw, sems((3,))],
+    text_units, image_unit, pairs = call(
+        units_kernel, [outside, array((PIECE, width), BF16), local((8, 128), F32)],
+        Outside(text_emb), Outside(image_emb), scratch=[raw] * 4 + [sems((2,)), sems((PEERS + 1,))],
     )
     plan, pieces = gather_image(image_unit)
-    text_units = call(text_units_kernel, outside, Outside(text_emb), scratch=[raw, raw, sems((PEERS,))])
     text = exchange(text_units, XY)
 
 
-    lines = local((STEPS, TILE), F32)
+    lines = local((2 * STEPS, TILE), F32)
     image, logits, keep, give = call(
-        functools.partial(logits_kernel, plan), [outside, local((SIDE, SIDE), F32), lines, local((2 * STEPS, TILE), F32)],
+        functools.partial(logits_kernel, plan), [outside, local((SIDE, SIDE), F32), lines, lines],
         at, scale, pairs, text, *map(Outside, pieces),
         scratch=[pltpu.VMEM((SIDE, width), BF16), sems((len(plan),)), sems((2,))],
     )
-    spread = call(spread_kernel, local((PEERS * LINES, TILE), F32), at, keep, send(give, "c", 1), pairs)
+    spread = call(spread_kernel, local((PEERS * LINES, TILE), F32), at, keep, send(give, "c", 1))
     lines = local((2 * STEPS, TILE), F32)
     keep, give = call(join_kernel, [lines, lines], at, exchange(spread, MIXED))
     recv = send(give, "c", 1)

time: 127 us -> 127 us (level)
  starting transfers between devices: 46.9 us -> 49.7 us
  Pallas kernels: 30.1 us -> 28.4 us
    ppermute x28, starting transfers between devices: 32.7 us -> 35.3 us  [send(): return lax.ppermute(x, 'd', shift(axis, by))]
    pallas_call x13 -> x12, Pallas kernels: 30.1 us -> 28.4 us  [call(): pl.pallas_call(kernel, out_shape=outputs, in_specs=specs, out_specs=jax.t...]
  transfers between devices with their start and end apart: 30 -> 30, of which waited for: 19 -> 19; matrix products, arithmetic and copies ran while one was open for 0% -> 0% of each run, Pallas kernels for 11% -> 9%
where the time goes in v8:
time: 127 us
  starting transfers between devices  49.7 us (39%)
  waiting for transfers between devices  35.3 us (28%)
  Pallas kernels  28.4 us (22%)
  blocking collectives  10.9 us (9%)
  between operations  2.3 us (2%)
    ppermute x28, starting transfers between devices, send(): return lax.ppermute(x, 'd', shift(axis, by))  35.3 us
    ppermute x28, waiting for transfers between devices, send(): return lax.ppermute(x, 'd', shift(axis, by))  32.1 us
    pallas_call x12, Pallas kernels, call(): pl.pallas_call(kernel, out_shape=outputs, in_specs=specs, out_specs=jax.t...  28.4 us
    all_to_all x2, starting transfers between devices, exchange(): return lax.all_to_all(x, 'd', 0, 0, axis_index_groups=groups, tiled=True)  14.3 us
    all_to_all x1, blocking collectives, exchange(): return lax.all_to_all(x, 'd', 0, 0, axis_index_groups=groups, tiled=True)  10.9 us
    all_to_all x2, waiting for transfers between devices, exchange(): return lax.all_to_all(x, 'd', 0, 0, axis_index_groups=groups, tiled=True)  3.14 us
  transfers between devices with their start and end apart: 30, of which 19 were waited for; matrix products, arithmetic and copies ran while one was open for 0% of the time, Pallas kernels for 9%

profile of v8, /device:TPU:28, one launch (start us, length us, event | category | flops | bytes accessed | tf_op | source)
XLA Modules:
  0.0 126.7 jit_solution(14293322303204814162)
XLA Ops:
  0.6 2.7 %shard_map.58 = (bf16[1024,1280]{1,0:T(8,128)(2,1)}, bf16[64,1280]{1,0:T(8,128)(2,1)}, f32[8,128]{1,0:T(8,128)S(1)}) custom-call(bf16[64,1280]{1,0:T(8,128)(2,1)} %raw_ref.3, bf16[64,1280]{1,0:T(8,128)(2,1)} %raw_ref.2), custom_call_target="tpu_custom_call" | custom-call | tf_op jit(solution)/shard_map/pallas_call | solution.py:75
  3.4 7.3 %all-to-all-start = ((bf16[16,64,1280]{2,1,0:T(8,128)(2,1)}), bf16[16,64,1280]{2,1,0:T(8,128)(2,1)S(1)}, u32[]{:S(2)}, u32[]{:S(2)}) async-start(bf16[16,64,1280]{2,1,0:T(8,128)(2,1)} %bitcast.18), calls=%async_computation | async-start | bytes 5242880 | tf_op jit(solution)/shard_map/all_to_all | solution.py:52
  10.7 5.9 %collective-permute-start.1 = (bf16[64,1280]{1,0:T(8,128)(2,1)S(1)}, bf16[64,1280]{1,0:T(8,128)(2,1)S(1)}, u32[]{:S(2)}, u32[]{:S(2)}) collective-permute-start(bf16[64,1280]{1,0:T(8,128)(2,1)S(1)} %copy-done.3), channel_id=1, source_target_pairs={{0,7},{1,0},{2,1},{3,2},{4,3},{5,4},{6,5},{7,6},{8,15},{9,8},{10,9... | collective-permute-start | bytes 491528 | tf_op jit(solution)/shard_map/ppermute | solution.py:48
  16.6 2.9 %collective-permute-done.1.refs_2_ = bf16[64,1280]{1,0:T(8,128)(2,1)S(1)} collective-permute-done((bf16[64,1280]{1,0:T(8,128)(2,1)S(1)}, bf16[64,1280]{1,0:T(8,128)(2,1)S(1)}, u32[]{:S(2)}, u32[]{:S(2)}) %collective-permute-start.1) | collective-permute-done | bytes 163872 | tf_op jit(solution)/shard_map/ppermute | solution.py:48
  19.5 3.7 %collective-permute-start.3 = (bf16[64,1280]{1,0:T(8,128)(2,1)S(1)}, bf16[64,1280]{1,0:T(8,128)(2,1)S(1)}, u32[]{:S(2)}, u32[]{:S(2)}) collective-permute-start(bf16[64,1280]{1,0:T(8,128)(2,1)S(1)} %collective-permute-done.1.refs_2_), channel_id=1, source_target_pairs={{0,7},{1,0},{2,1},{3,2},{4,3},{5,4},{6,5},{7,6},{8,15},{9,8},{10,9... | collective-permute-start | bytes 491528 | tf_op jit(solution)/shard_map/ppermute | solution.py:48
  23.2 2.8 %collective-permute-done.3.refs_4_ = bf16[64,1280]{1,0:T(8,128)(2,1)S(1)} collective-permute-done((bf16[64,1280]{1,0:T(8,128)(2,1)S(1)}, bf16[64,1280]{1,0:T(8,128)(2,1)S(1)}, u32[]{:S(2)}, u32[]{:S(2)}) %collective-permute-start.3) | collective-permute-done | bytes 163872 | tf_op jit(solution)/shard_map/ppermute | solution.py:48
  26.0 3.7 %collective-permute-start.5 = (bf16[64,1280]{1,0:T(8,128)(2,1)S(1)}, bf16[64,1280]{1,0:T(8,128)(2,1)S(1)}, u32[]{:S(2)}, u32[]{:S(2)}) collective-permute-start(bf16[64,1280]{1,0:T(8,128)(2,1)S(1)} %collective-permute-done.3.refs_4_), channel_id=1, source_target_pairs={{0,7},{1,0},{2,1},{3,2},{4,3},{5,4},{6,5},{7,6},{8,15},{9,8},{10,9... | collective-permute-start | bytes 491528 | tf_op jit(solution)/shard_map/ppermute | solution.py:48
  30.4 2.2 %collective-permute-done.5.refs_6_ = bf16[64,1280]{1,0:T(8,128)(2,1)S(1)} collective-permute-done((bf16[64,1280]{1,0:T(8,128)(2,1)S(1)}, bf16[64,1280]{1,0:T(8,128)(2,1)S(1)}, u32[]{:S(2)}, u32[]{:S(2)}) %collective-permute-start.5) | collective-permute-done | bytes 163872 | tf_op jit(solution)/shard_map/ppermute | solution.py:48
  32.6 4.0 %collective-permute-done.4.refs_5_ = bf16[64,1280]{1,0:T(8,128)(2,1)S(1)} collective-permute-done((bf16[64,1280]{1,0:T(8,128)(2,1)}, bf16[64,1280]{1,0:T(8,128)(2,1)S(1)}, u32[]{:S(2)}, u32[]{:S(2)}) %collective-permute-start.4) | collective-permute-done | bytes 163872 | tf_op jit(solution)/shard_map/ppermute | solution.py:48
  37.0 1.7 %collective-permute-start.6 = (bf16[32,1280]{1,0:T(8,128)(2,1)S(1)}, bf16[32,1280]{1,0:T(8,128)(2,1)}, u32[]{:S(2)}, u32[]{:S(2)}) collective-permute-start(bf16[32,1280]{1,0:T(8,128)(2,1)S(1)} %slice.8), channel_id=1, source_target_pairs={{0,1},{1,2},{2,3},{3,4},{4,5},{5,6},{6,7},{7,0},{8,9},{9,10},{10,1... | collective-permute-start | bytes 245768 | tf_op jit(solution)/shard_map/ppermute | solution.py:48
  39.3 2.3 %collective-permute-done.7.refs_8_ = bf16[32,1280]{1,0:T(8,128)(2,1)} collective-permute-done((bf16[32,1280]{1,0:T(8,128)(2,1)S(1)}, bf16[32,1280]{1,0:T(8,128)(2,1)}, u32[]{:S(2)}, u32[]{:S(2)}) %collective-permute-start.7) | collective-permute-done | bytes 81952 | tf_op jit(solution)/shard_map/ppermute | solution.py:48
  45.1 6.3 %shard_map.59 = (bf16[1024,1280]{1,0:T(8,128)(2,1)}, f32[1024,1024]{1,0:T(8,128)S(1)}, f32[8,256]{1,0:T(8,128)S(1)}, f32[8,256]{1,0:T(8,128)S(1)}) custom-call(s32[5]{0:T(128)S(1)} %stack.23.at_ref, f32[1]{0:T(128)S(6)} %exp.3.scale_ref, f32[8,128]{1,0:T(8,128)S(1)} %get-tuple-element.38.pairs_ref, bf16[1024,1280]{1,0:T(8,128)(2,1)S(1)} %bitcast.11, ...), custom_call_target="tpu_custom_call" | custom-call | tf_op jit(solution)/shard_map/pallas_call | solution.py:75
  53.2 10.9 %all_to_all.33 = f32[16,8,256]{2,1,0:T(8,128)S(1)} all-to-all(f32[16,8,256]{2,1,0:T(8,128)S(1)} %bitcast.16), channel_id=1, replica_groups={{0,16,32,48,64,80,96,112,128,144,160,176,192,208,224,240},{1,17,33,49,6..., dimensions={0} | all-to-all | bytes 262144 | tf_op jit(solution)/shard_map/all_to_all | solution.py:52
  64.8 4.9 %collective-permute-start.18 = (f32[8,256]{1,0:T(8,128)S(1)}, f32[8,256]{1,0:T(8,128)S(1)}, u32[]{:S(2)}, u32[]{:S(2)}) collective-permute-start(f32[8,256]{1,0:T(8,128)S(1)} %get-tuple-element.45), channel_id=1, source_target_pairs={{0,8},{1,9},{2,10},{3,11},{4,12},{5,13},{6,14},{7,15},{8,0},{9,1},... | collective-permute-start | bytes 24584 | tf_op jit(solution)/shard_map/ppermute | solution.py:48
  70.6 2.9 %shard_map.62 = (bf16[512,1024]{1,0:T(8,128)(2,1)S(1)}, bf16[1024,1024]{1,0:T(8,128)(2,1)S(1)}, bf16[512,1280]{1,0:T(8,128)(2,1)S(1)}, f32[8,128]{1,0:T(8,128)S(1)}) custom-call(s32[5]{0:T(128)S(1)} %stack.23.at_ref, f32[1]{0:T(128)S(6)} %exp.3.scale_ref, f32[1024,1024]{1,0:T(8,128)S(1)} %get-tuple-element.41.logits_ref, bf16[1024,1280]{1,0:T(8,128)(2,1)S(1)} %bitcast.12, ...), custom_call_target="tpu_custom_call" | custom-call | tf_op jit(solution)/shard_map/pallas_call | solution.py:75
  73.9 4.3 %shard_map.63 = (bf16[10496,128]{1,0:T(8,128)(2,1)}, f32[512,1280]{1,0:T(8,128)S(1)}) custom-call(f32[1]{0:T(128)S(6)} %exp.3.scale_ref, bf16[512,1024]{1,0:T(8,128)(2,1)S(1)} %get-tuple-element.47.weights_ref, bf16[1024,1024]{1,0:T(8,128)(2,1)S(1)} %get-tuple-element.48.turned_ref, bf16[1024,1280]{1,0:T(8,128)(2,1)S(1)} %copy-done, ...), custom_call_target="tpu_custom_call" | custom-call | tf_op jit(solution)/shard_map/pallas_call | solution.py:75
  78.2 1.8 %shard_map.64 = (bf16[10496,128]{1,0:T(8,128)(2,1)}, f32[64,1280]{1,0:T(8,128)}, bf16[336,128]{1,0:T(8,128)(2,1)}, bf16[336,128]{1,0:T(8,128)(2,1)}, bf16[64,128...) custom-call(s32[5]{0:T(128)S(1)} %stack.23.at_ref, ...), custom_call_target="tpu_custom_call", output_to_operand_aliasing={{0}: (4, {})} | custom-call | tf_op jit(solution)/shard_map/pallas_call | solution.py:75
  80.0 7.1 %all-to-all-start.2 = ((bf16[16,656,128]{2,1,0:T(8,128)(2,1)}), bf16[16,656,128]{2,1,0:T(8,128)(2,1)S(1)}, u32[]{:S(2)}, u32[]{:S(2)}) async-start(bf16[16,656,128]{2,1,0:T(8,128)(2,1)} %bitcast.17), calls=%async_computation.2 | async-start | bytes 5373952 | tf_op jit(solution)/shard_map/all_to_all | solution.py:52
  88.5 1.9 %collective-permute-start.21 = (bf16[336,128]{1,0:T(8,128)(2,1)S(1)}, bf16[336,128]{1,0:T(8,128)(2,1)S(1)}, u32[]{:S(2)}, u32[]{:S(2)}) collective-permute-start(bf16[336,128]{1,0:T(8,128)(2,1)S(1)} %copy-done.12), channel_id=1, source_target_pairs={{0,7},{1,0},{2,1},{3,2},{4,3},{5,4},{6,5},{7,6},{8,15},{9,8},{10,9... | collective-permute-start | bytes 258056 | tf_op jit(solution)/shard_map/ppermute | solution.py:48
  90.4 2.5 %collective-permute-done.20.below_ref = bf16[336,128]{1,0:T(8,128)(2,1)S(1)} collective-permute-done((bf16[336,128]{1,0:T(8,128)(2,1)S(1)}, bf16[336,128]{1,0:T(8,128)(2,1)S(1)}, u32[]{:S(2)}, u32[]{:S(2)}) %collective-permute-start.20) | collective-permute-done | bytes 86048 | tf_op jit(solution)/shard_map/ppermute | solution.py:48
  95.4 2.5 %collective-permute-start.23 = (bf16[656,128]{1,0:T(8,128)(2,1)S(1)}, bf16[656,128]{1,0:T(8,128)(2,1)S(1)}, u32[]{:S(2)}, u32[]{:S(2)}) collective-permute-start(bf16[656,128]{1,0:T(8,128)(2,1)S(1)} %get-tuple-element.63), channel_id=1, source_target_pairs={{0,7},{1,0},{2,1},{3,2},{4,3},{5,4},{6,5},{7,6},{8,15},{9,8},{10,9... | collective-permute-start | bytes 503816 | tf_op jit(solution)/shard_map/ppermute | solution.py:48
  97.9 3.3 %collective-permute-done.22.below_ref = bf16[656,128]{1,0:T(8,128)(2,1)S(1)} collective-permute-done((bf16[656,128]{1,0:T(8,128)(2,1)S(1)}, bf16[656,128]{1,0:T(8,128)(2,1)S(1)}, u32[]{:S(2)}, u32[]{:S(2)}) %collective-permute-start.22) | collective-permute-done | bytes 167968 | tf_op jit(solution)/shard_map/ppermute | solution.py:48
  101.3 1.6 %shard_map.66 = (bf16[656,128]{1,0:T(8,128)(2,1)S(1)}, bf16[656,128]{1,0:T(8,128)(2,1)S(1)}) custom-call(s32[5]{0:T(128)S(1)} %stack.23.at_ref, f32[8,128]{1,0:T(8,128)S(1)} %get-tuple-element.46.sums_ref, bf16[64,1280]{1,0:T(8,128)(2,1)} %get-tuple-element.56.up_ref, bf16[64,1280]{1,0:T(8,128)(2,1)} %get-tuple-element.57.down_ref, ...), custom_call_target="tpu_custom_call" | custom-call | tf_op jit(solution)/shard_map/pallas_call | solution.py:75
  102.9 1.7 %collective-permute-start.24 = (bf16[656,128]{1,0:T(8,128)(2,1)S(1)}, bf16[656,128]{1,0:T(8,128)(2,1)S(1)}, u32[]{:S(2)}, u32[]{:S(2)}) collective-permute-start(bf16[656,128]{1,0:T(8,128)(2,1)S(1)} %get-tuple-element.64), channel_id=1, source_target_pairs={{0,1},{1,2},{2,3},{3,4},{4,5},{5,6},{6,7},{7,0},{8,9},{9,10},{10,1... | collective-permute-start | bytes 503816 | tf_op jit(solution)/shard_map/ppermute | solution.py:48
  104.5 1.7 %collective-permute-start.25 = (bf16[656,128]{1,0:T(8,128)(2,1)S(1)}, bf16[656,128]{1,0:T(8,128)(2,1)S(1)}, u32[]{:S(2)}, u32[]{:S(2)}) collective-permute-start(bf16[656,128]{1,0:T(8,128)(2,1)S(1)} %get-tuple-element.65), channel_id=1, source_target_pairs={{0,7},{1,0},{2,1},{3,2},{4,3},{5,4},{6,5},{7,6},{8,15},{9,8},{10,9... | collective-permute-start | bytes 503816 | tf_op jit(solution)/shard_map/ppermute | solution.py:48
  106.3 3.3 %collective-permute-done.24.below_ref = bf16[656,128]{1,0:T(8,128)(2,1)S(1)} collective-permute-done((bf16[656,128]{1,0:T(8,128)(2,1)S(1)}, bf16[656,128]{1,0:T(8,128)(2,1)S(1)}, u32[]{:S(2)}, u32[]{:S(2)}) %collective-permute-start.24) | collective-permute-done | bytes 167968 | tf_op jit(solution)/shard_map/ppermute | solution.py:48
  109.9 1.6 %shard_map.67 = (bf16[656,128]{1,0:T(8,128)(2,1)S(1)}, bf16[656,128]{1,0:T(8,128)(2,1)S(1)}) custom-call(s32[5]{0:T(128)S(1)} %stack.23.at_ref, f32[8,128]{1,0:T(8,128)S(1)} %get-tuple-element.46.sums_ref, bf16[64,1280]{1,0:T(8,128)(2,1)} %get-tuple-element.54.up_ref, bf16[64,1280]{1,0:T(8,128)(2,1)} %get-tuple-element.55.down_ref, ...), custom_call_target="tpu_custom_call" | custom-call | tf_op jit(solution)/shard_map/pallas_call | solution.py:75
  111.5 2.1 %collective-permute-start.26 = (bf16[656,128]{1,0:T(8,128)(2,1)S(1)}, bf16[656,128]{1,0:T(8,128)(2,1)S(1)}, u32[]{:S(2)}, u32[]{:S(2)}) collective-permute-start(bf16[656,128]{1,0:T(8,128)(2,1)S(1)} %get-tuple-element.66), channel_id=1, source_target_pairs={{0,1},{1,2},{2,3},{3,4},{4,5},{5,6},{6,7},{7,0},{8,9},{9,10},{10,1... | collective-permute-start | bytes 503816 | tf_op jit(solution)/shard_map/ppermute | solution.py:48
  114.8 3.3 %collective-permute-done.26.below_ref = bf16[656,128]{1,0:T(8,128)(2,1)S(1)} collective-permute-done((bf16[656,128]{1,0:T(8,128)(2,1)S(1)}, bf16[656,128]{1,0:T(8,128)(2,1)S(1)}, u32[]{:S(2)}, u32[]{:S(2)}) %collective-permute-start.26) | collective-permute-done | bytes 167968 | tf_op jit(solution)/shard_map/ppermute | solution.py:48
  119.0 2.5 %shard_map.68 = (bf16[64,1280]{1,0:T(8,128)(2,1)}, f32[8,128]{1,0:T(8,128)S(1)}) custom-call(s32[5]{0:T(128)S(1)} %stack.23.at_ref, f32[8,128]{1,0:T(8,128)S(1)} %get-tuple-element.46.sums_ref, bf16[64,1280]{1,0:T(8,128)(2,1)} %raw_ref.2, f32[64,1280]{1,0:T(8,128)} %get-tuple-element.53.own_ref, bf16[656,128]{1,0:T(8,128)(2,1)S(1)} %collective-permute-done.26.below_ref, ...), custom_call_target="tpu_custom_call" | custom-call | tf_op jit(solution)/shard_map/pallas_call | solution.py:75
  121.5 2.7 %all-to-all-done.2 = bf16[16,656,128]{2,1,0:T(8,128)(2,1)S(1)} async-done(((bf16[16,656,128]{2,1,0:T(8,128)(2,1)}), bf16[16,656,128]{2,1,0:T(8,128)(2,1)S(1)}, u32[]{:S(2)}, u32[]{:S(2)}) %all-to-all-start.2) | async-done | bytes 2687008 | tf_op jit(solution)/shard_map/all_to_all | solution.py:52
  124.2 1.8 %shard_map.69 = (bf16[64,1280]{1,0:T(8,128)(2,1)}, f32[1]{0:T(128)S(4)}) custom-call(bf16[64,1280]{1,0:T(8,128)(2,1)} %raw_ref.3, f32[8,128]{1,0:T(8,128)S(1)} %get-tuple-element.68.loss_ref, bf16[10496,128]{1,0:T(8,128)(2,1)S(1)} %bitcast.14), custom_call_target="tpu_custom_call" | custom-call | tf_op jit(solution)/shard_map/pallas_call | solution.py:75
  (72 shorter events, 14.5 us)
Async XLA Ops:
  3.4 41.6 %all-to-all-start = ((bf16[16,64,1280]{2,1,0:T(8,128)(2,1)}), bf16[16,64,1280]{2,1,0:T(8,128)(2,1)S(1)}, u32[]{:S(2)}, u32[]{:S(2)}) async-start(bf16[16,64,1280]{2,1,0:T(8,128)(2,1)} %bitcast.18), calls=%async_computation | async-start | bytes 5242880 | tf_op jit(solution)/shard_map/all_to_all | solution.py:52
  10.7 8.8 %collective-permute-start.1 = (bf16[64,1280]{1,0:T(8,128)(2,1)S(1)}, bf16[64,1280]{1,0:T(8,128)(2,1)S(1)}, u32[]{:S(2)}, u32[]{:S(2)}) collective-permute-start(bf16[64,1280]{1,0:T(8,128)(2,1)S(1)} %copy-done.3), channel_id=1, source_target_pairs={{0,7},{1,0},{2,1},{3,2},{4,3},{5,4},{6,5},{7,6},{8,15},{9,8},{10,9... | collective-permute-start | bytes 491528 | tf_op jit(solution)/shard_map/ppermute | solution.py:48
  16.6 6.6 %collective-permute-start = (bf16[64,1280]{1,0:T(8,128)(2,1)S(1)}, bf16[64,1280]{1,0:T(8,128)(2,1)S(1)}, u32[]{:S(2)}, u32[]{:S(2)}) collective-permute-start(bf16[64,1280]{1,0:T(8,128)(2,1)S(1)} %copy-done.3), channel_id=1, source_target_pairs={{0,1},{1,2},{2,3},{3,4},{4,5},{5,6},{6,7},{7,0},{8,9},{9,10},{10,1... | collective-permute-start | bytes 491528 | tf_op jit(solution)/shard_map/ppermute | solution.py:48
  19.5 25.5 %copy-start.4 = (bf16[64,1280]{1,0:T(8,128)(2,1)}, bf16[64,1280]{1,0:T(8,128)(2,1)S(1)}, u32[]{:S(2)}) copy-start(bf16[64,1280]{1,0:T(8,128)(2,1)S(1)} %collective-permute-done.1.refs_2_) | copy-start | bytes 491524
  19.5 6.5 %collective-permute-start.3 = (bf16[64,1280]{1,0:T(8,128)(2,1)S(1)}, bf16[64,1280]{1,0:T(8,128)(2,1)S(1)}, u32[]{:S(2)}, u32[]{:S(2)}) collective-permute-start(bf16[64,1280]{1,0:T(8,128)(2,1)S(1)} %collective-permute-done.1.refs_2_), channel_id=1, source_target_pairs={{0,7},{1,0},{2,1},{3,2},{4,3},{5,4},{6,5},{7,6},{8,15},{9,8},{10,9... | collective-permute-start | bytes 491528 | tf_op jit(solution)/shard_map/ppermute | solution.py:48
  23.2 21.8 %copy-start.5 = (bf16[64,1280]{1,0:T(8,128)(2,1)}, bf16[64,1280]{1,0:T(8,128)(2,1)S(1)}, u32[]{:S(2)}) copy-start(bf16[64,1280]{1,0:T(8,128)(2,1)S(1)} %collective-permute-done.refs_1_) | copy-start | bytes 491524
  23.2 6.6 %collective-permute-start.2 = (bf16[64,1280]{1,0:T(8,128)(2,1)S(1)}, bf16[64,1280]{1,0:T(8,128)(2,1)}, u32[]{:S(2)}, u32[]{:S(2)}) collective-permute-start(bf16[64,1280]{1,0:T(8,128)(2,1)S(1)} %collective-permute-done.refs_1_), channel_id=1, source_target_pairs={{0,1},{1,2},{2,3},{3,4},{4,5},{5,6},{6,7},{7,0},{8,9},{9,10},{10,1... | collective-permute-start | bytes 491528 | tf_op jit(solution)/shard_map/ppermute | solution.py:48
  26.0 6.5 %collective-permute-start.5 = (bf16[64,1280]{1,0:T(8,128)(2,1)S(1)}, bf16[64,1280]{1,0:T(8,128)(2,1)S(1)}, u32[]{:S(2)}, u32[]{:S(2)}) collective-permute-start(bf16[64,1280]{1,0:T(8,128)(2,1)S(1)} %collective-permute-done.3.refs_4_), channel_id=1, source_target_pairs={{0,7},{1,0},{2,1},{3,2},{4,3},{5,4},{6,5},{7,6},{8,15},{9,8},{10,9... | collective-permute-start | bytes 491528 | tf_op jit(solution)/shard_map/ppermute | solution.py:48
  29.8 6.7 %collective-permute-start.4 = (bf16[64,1280]{1,0:T(8,128)(2,1)}, bf16[64,1280]{1,0:T(8,128)(2,1)S(1)}, u32[]{:S(2)}, u32[]{:S(2)}) collective-permute-start(bf16[64,1280]{1,0:T(8,128)(2,1)} %collective-permute-done.2.refs_3_), channel_id=1, source_target_pairs={{0,1},{1,2},{2,3},{3,4},{4,5},{5,6},{6,7},{7,0},{8,9},{9,10},{10,1... | collective-permute-start | bytes 491528 | tf_op jit(solution)/shard_map/ppermute | solution.py:48
  29.8 6.8 %collective-permute-start.8 = (bf16[64,1280]{1,0:T(8,128)(2,1)S(1)}, bf16[64,1280]{1,0:T(8,128)(2,1)S(1)}, u32[]{:S(2)}, u32[]{:S(2)}) collective-permute-start(bf16[64,1280]{1,0:T(8,128)(2,1)S(1)} %copy-done.3), channel_id=1, source_target_pairs={{0,8},{1,9},{2,10},{3,11},{4,12},{5,13},{6,14},{7,15},{8,0},{9,1},... | collective-permute-start | bytes 491528 | tf_op jit(solution)/shard_map/ppermute | solution.py:48
  29.8 7.1 %collective-permute-start.10 = (bf16[64,1280]{1,0:T(8,128)(2,1)S(1)}, bf16[64,1280]{1,0:T(8,128)(2,1)S(1)}, u32[]{:S(2)}, u32[]{:S(2)}) collective-permute-start(bf16[64,1280]{1,0:T(8,128)(2,1)S(1)} %collective-permute-done.1.refs_2_), channel_id=1, source_target_pairs={{0,8},{1,9},{2,10},{3,11},{4,12},{5,13},{6,14},{7,15},{8,0},{9,1},... | collective-permute-start | bytes 491528 | tf_op jit(solution)/shard_map/ppermute | solution.py:48
  30.3 8.4 %collective-permute-start.9 = (bf16[64,1280]{1,0:T(8,128)(2,1)S(1)}, bf16[64,1280]{1,0:T(8,128)(2,1)S(1)}, u32[]{:S(2)}, u32[]{:S(2)}) collective-permute-start(bf16[64,1280]{1,0:T(8,128)(2,1)S(1)} %collective-permute-done.refs_1_), channel_id=1, source_target_pairs={{0,8},{1,9},{2,10},{3,11},{4,12},{5,13},{6,14},{7,15},{8,0},{9,1},... | collective-permute-start | bytes 491528 | tf_op jit(solution)/shard_map/ppermute | solution.py:48
  32.6 6.2 %collective-permute-start.12 = (bf16[64,1280]{1,0:T(8,128)(2,1)S(1)}, bf16[64,1280]{1,0:T(8,128)(2,1)S(1)}, u32[]{:S(2)}, u32[]{:S(2)}) collective-permute-start(bf16[64,1280]{1,0:T(8,128)(2,1)S(1)} %collective-permute-done.3.refs_4_), channel_id=1, source_target_pairs={{0,8},{1,9},{2,10},{3,11},{4,12},{5,13},{6,14},{7,15},{8,0},{9,1},... | collective-permute-start | bytes 491528 | tf_op jit(solution)/shard_map/ppermute | solution.py:48
  36.6 7.2 %collective-permute-start.11 = (bf16[64,1280]{1,0:T(8,128)(2,1)}, bf16[64,1280]{1,0:T(8,128)(2,1)}, u32[]{:S(2)}, u32[]{:S(2)}) collective-permute-start(bf16[64,1280]{1,0:T(8,128)(2,1)} %collective-permute-done.2.refs_3_), channel_id=1, source_target_pairs={{0,8},{1,9},{2,10},{3,11},{4,12},{5,13},{6,14},{7,15},{8,0},{9,1},... | collective-permute-start | bytes 491528 | tf_op jit(solution)/shard_map/ppermute | solution.py:48
  36.6 5.0 %collective-permute-start.7 = (bf16[32,1280]{1,0:T(8,128)(2,1)S(1)}, bf16[32,1280]{1,0:T(8,128)(2,1)}, u32[]{:S(2)}, u32[]{:S(2)}) collective-permute-start(bf16[32,1280]{1,0:T(8,128)(2,1)S(1)} %slice.9), channel_id=1, source_target_pairs={{0,7},{1,0},{2,1},{3,2},{4,3},{5,4},{6,5},{7,6},{8,15},{9,8},{10,9... | collective-permute-start | bytes 245768 | tf_op jit(solution)/shard_map/ppermute | solution.py:48
  37.0 6.0 %collective-permute-start.6 = (bf16[32,1280]{1,0:T(8,128)(2,1)S(1)}, bf16[32,1280]{1,0:T(8,128)(2,1)}, u32[]{:S(2)}, u32[]{:S(2)}) collective-permute-start(bf16[32,1280]{1,0:T(8,128)(2,1)S(1)} %slice.8), channel_id=1, source_target_pairs={{0,1},{1,2},{2,3},{3,4},{4,5},{5,6},{6,7},{7,0},{8,9},{9,10},{10,1... | collective-permute-start | bytes 245768 | tf_op jit(solution)/shard_map/ppermute | solution.py:48
  38.7 5.0 %collective-permute-start.14 = (bf16[64,1280]{1,0:T(8,128)(2,1)S(1)}, bf16[64,1280]{1,0:T(8,128)(2,1)S(1)}, u32[]{:S(2)}, u32[]{:S(2)}) collective-permute-start(bf16[64,1280]{1,0:T(8,128)(2,1)S(1)} %collective-permute-done.5.refs_6_), channel_id=1, source_target_pairs={{0,8},{1,9},{2,10},{3,11},{4,12},{5,13},{6,14},{7,15},{8,0},{9,1},... | collective-permute-start | bytes 491528 | tf_op jit(solution)/shard_map/ppermute | solution.py:48
  38.8 5.8 %collective-permute-start.13 = (bf16[64,1280]{1,0:T(8,128)(2,1)S(1)}, bf16[64,1280]{1,0:T(8,128)(2,1)}, u32[]{:S(2)}, u32[]{:S(2)}) collective-permute-start(bf16[64,1280]{1,0:T(8,128)(2,1)S(1)} %collective-permute-done.4.refs_5_), channel_id=1, source_target_pairs={{0,8},{1,9},{2,10},{3,11},{4,12},{5,13},{6,14},{7,15},{8,0},{9,1},... | collective-permute-start | bytes 491528 | tf_op jit(solution)/shard_map/ppermute | solution.py:48
  41.6 2.1 %collective-permute-start.16 = (bf16[32,1280]{1,0:T(8,128)(2,1)}, bf16[32,1280]{1,0:T(8,128)(2,1)}, u32[]{:S(2)}, u32[]{:S(2)}) collective-permute-start(bf16[32,1280]{1,0:T(8,128)(2,1)} %collective-permute-done.7.refs_8_), channel_id=1, source_target_pairs={{0,8},{1,9},{2,10},{3,11},{4,12},{5,13},{6,14},{7,15},{8,0},{9,1},... | collective-permute-start | bytes 245768 | tf_op jit(solution)/shard_map/ppermute | solution.py:48
  43.0 1.6 %collective-permute-start.15 = (bf16[32,1280]{1,0:T(8,128)(2,1)}, bf16[32,1280]{1,0:T(8,128)(2,1)}, u32[]{:S(2)}, u32[]{:S(2)}) collective-permute-start(bf16[32,1280]{1,0:T(8,128)(2,1)} %collective-permute-done.6.refs_7_), channel_id=1, source_target_pairs={{0,8},{1,9},{2,10},{3,11},{4,12},{5,13},{6,14},{7,15},{8,0},{9,1},... | collective-permute-start | bytes 245768 | tf_op jit(solution)/shard_map/ppermute | solution.py:48
  51.4 1.3 collective-permute-start.17
  64.8 5.7 %collective-permute-start.18 = (f32[8,256]{1,0:T(8,128)S(1)}, f32[8,256]{1,0:T(8,128)S(1)}, u32[]{:S(2)}, u32[]{:S(2)}) collective-permute-start(f32[8,256]{1,0:T(8,128)S(1)} %get-tuple-element.45), channel_id=1, source_target_pairs={{0,8},{1,9},{2,10},{3,11},{4,12},{5,13},{6,14},{7,15},{8,0},{9,1},... | collective-permute-start | bytes 24584 | tf_op jit(solution)/shard_map/ppermute | solution.py:48
  73.4 4.7 %collective-permute-start.19 = (bf16[512,1280]{1,0:T(8,128)(2,1)S(1)}, bf16[512,1280]{1,0:T(8,128)(2,1)S(1)}, u32[]{:S(2)}, u32[]{:S(2)}) collective-permute-start(bf16[512,1280]{1,0:T(8,128)(2,1)S(1)} %get-tuple-element.51), channel_id=1, source_target_pairs={{0,8},{1,9},{2,10},{3,11},{4,12},{5,13},{6,14},{7,15},{8,0},{9,1},... | collective-permute-start | bytes 3932168 | tf_op jit(solution)/shard_map/ppermute | solution.py:48
  80.0 44.2 %all-to-all-start.2 = ((bf16[16,656,128]{2,1,0:T(8,128)(2,1)}), bf16[16,656,128]{2,1,0:T(8,128)(2,1)S(1)}, u32[]{:S(2)}, u32[]{:S(2)}) async-start(bf16[16,656,128]{2,1,0:T(8,128)(2,1)} %bitcast.17), calls=%async_computation.2 | async-start | bytes 5373952 | tf_op jit(solution)/shard_map/all_to_all | solution.py:52
  87.1 5.8 %collective-permute-start.20 = (bf16[336,128]{1,0:T(8,128)(2,1)S(1)}, bf16[336,128]{1,0:T(8,128)(2,1)S(1)}, u32[]{:S(2)}, u32[]{:S(2)}) collective-permute-start(bf16[336,128]{1,0:T(8,128)(2,1)S(1)} %copy-done.13), channel_id=1, source_target_pairs={{0,1},{1,2},{2,3},{3,4},{4,5},{5,6},{6,7},{7,0},{8,9},{9,10},{10,1... | collective-permute-start | bytes 258056 | tf_op jit(solution)/shard_map/ppermute | solution.py:48
  88.5 4.5 %collective-permute-start.21 = (bf16[336,128]{1,0:T(8,128)(2,1)S(1)}, bf16[336,128]{1,0:T(8,128)(2,1)S(1)}, u32[]{:S(2)}, u32[]{:S(2)}) collective-permute-start(bf16[336,128]{1,0:T(8,128)(2,1)S(1)} %copy-done.12), channel_id=1, source_target_pairs={{0,7},{1,0},{2,1},{3,2},{4,3},{5,4},{6,5},{7,6},{8,15},{9,8},{10,9... | collective-permute-start | bytes 258056 | tf_op jit(solution)/shard_map/ppermute | solution.py:48
  94.6 6.7 %collective-permute-start.22 = (bf16[656,128]{1,0:T(8,128)(2,1)S(1)}, bf16[656,128]{1,0:T(8,128)(2,1)S(1)}, u32[]{:S(2)}, u32[]{:S(2)}) collective-permute-start(bf16[656,128]{1,0:T(8,128)(2,1)S(1)} %get-tuple-element.62), channel_id=1, source_target_pairs={{0,1},{1,2},{2,3},{3,4},{4,5},{5,6},{6,7},{7,0},{8,9},{9,10},{10,1... | collective-permute-start | bytes 503816 | tf_op jit(solution)/shard_map/ppermute | solution.py:48
  95.4 5.9 %collective-permute-start.23 = (bf16[656,128]{1,0:T(8,128)(2,1)S(1)}, bf16[656,128]{1,0:T(8,128)(2,1)S(1)}, u32[]{:S(2)}, u32[]{:S(2)}) collective-permute-start(bf16[656,128]{1,0:T(8,128)(2,1)S(1)} %get-tuple-element.63), channel_id=1, source_target_pairs={{0,7},{1,0},{2,1},{3,2},{4,3},{5,4},{6,5},{7,6},{8,15},{9,8},{10,9... | collective-permute-start | bytes 503816 | tf_op jit(solution)/shard_map/ppermute | solution.py:48
  102.9 6.7 %collective-permute-start.24 = (bf16[656,128]{1,0:T(8,128)(2,1)S(1)}, bf16[656,128]{1,0:T(8,128)(2,1)S(1)}, u32[]{:S(2)}, u32[]{:S(2)}) collective-permute-start(bf16[656,128]{1,0:T(8,128)(2,1)S(1)} %get-tuple-element.64), channel_id=1, source_target_pairs={{0,1},{1,2},{2,3},{3,4},{4,5},{5,6},{6,7},{7,0},{8,9},{9,10},{10,1... | collective-permute-start | bytes 503816 | tf_op jit(solution)/shard_map/ppermute | solution.py:48
  104.5 5.4 %collective-permute-start.25 = (bf16[656,128]{1,0:T(8,128)(2,1)S(1)}, bf16[656,128]{1,0:T(8,128)(2,1)S(1)}, u32[]{:S(2)}, u32[]{:S(2)}) collective-permute-start(bf16[656,128]{1,0:T(8,128)(2,1)S(1)} %get-tuple-element.65), channel_id=1, source_target_pairs={{0,7},{1,0},{2,1},{3,2},{4,3},{5,4},{6,5},{7,6},{8,15},{9,8},{10,9... | collective-permute-start | bytes 503816 | tf_op jit(solution)/shard_map/ppermute | solution.py:48
  111.5 6.7 %collective-permute-start.26 = (bf16[656,128]{1,0:T(8,128)(2,1)S(1)}, bf16[656,128]{1,0:T(8,128)(2,1)S(1)}, u32[]{:S(2)}, u32[]{:S(2)}) collective-permute-start(bf16[656,128]{1,0:T(8,128)(2,1)S(1)} %get-tuple-element.66), channel_id=1, source_target_pairs={{0,1},{1,2},{2,3},{3,4},{4,5},{5,6},{6,7},{7,0},{8,9},{9,10},{10,1... | collective-permute-start | bytes 503816 | tf_op jit(solution)/shard_map/ppermute | solution.py:48
  113.6 5.4 %collective-permute-start.27 = (bf16[656,128]{1,0:T(8,128)(2,1)S(1)}, bf16[656,128]{1,0:T(8,128)(2,1)S(1)}, u32[]{:S(2)}, u32[]{:S(2)}) collective-permute-start(bf16[656,128]{1,0:T(8,128)(2,1)S(1)} %get-tuple-element.67), channel_id=1, source_target_pairs={{0,7},{1,0},{2,1},{3,2},{4,3},{5,4},{6,5},{7,6},{8,15},{9,8},{10,9... | collective-permute-start | bytes 503816 | tf_op jit(solution)/shard_map/ppermute | solution.py:48
  (12 other events, 71.5 us)

commit v9 on v8

--- a/solution.py
+++ b/solution.py
@@ -131,32 +131,46 @@
     return jnp.broadcast_to(lanes, (128, lanes.shape[1])).T[:, :1]
 
 
-def logits_kernel(plan, at_ref, scale_ref, pairs_ref, text_ref, *refs):
+def rows_of(at_ref, by, start, rows):
+    first = lax.rem(at_ref[3] + by + DEEP, DEEP) * PIECE + start
+    return pl.ds(pl.multiple_of(first, 32), rows)
+
+
+def near_kernel(plan, at_ref, *refs):
+    pieces, (near_out, first_ref, near, sem, out_sem) = refs[: len(plan)], refs[len(plan) :]
+    wait(run([
+        pltpu.make_async_copy(piece, near.at[rows_of(at_ref, *rest), :], sem.at[k])
+        for k, (piece, rest) in enumerate(zip(pieces, plan))
+    ]))
+    out = run([pltpu.make_async_copy(near, near_out, out_sem.at[0])])
+    first_ref[...] = near[:TILE, :]
+    wait(out)
+
+
+def logits_kernel(plan, at_ref, scale_ref, pairs_ref, text_ref, first_ref, near_ref, *refs):
     pieces = refs[: len(plan)]
-    image_out, logits_ref, keep_ref, give_ref, image_ref, sem, out_sem = refs[len(plan) :]
+    far_out, logits_ref, keep_ref, give_ref, second, far, sem, near_sem, out_sem = refs[len(plan) :]
     core = at_ref[2]
-    copies = []
-    for k, (piece, (flip, by, start, rows)) in enumerate(zip(pieces, plan)):
-        block = lax.rem(at_ref[3] + by + DEEP, DEEP)
-        first = pl.multiple_of(flip * (SIDE // 2) + block * PIECE + start, 32)
-        copies.append(pltpu.make_async_copy(piece, image_ref.at[pl.ds(first, rows), :], sem.at[k]))
-    near = len(plan) // 2
-    halves = [pl.ds(k * (SIDE // 2), SIDE // 2) for k in range(2)]
-    out = [pltpu.make_async_copy(image_ref.at[h, :], image_out.at[h, :], out_sem.at[k]) for k, h in enumerate(halves)]
-    wait(run(copies[:near]))
-    run(copies[near:] + out[:1])
+    near = run([pltpu.make_async_copy(near_ref.at[pl.ds(TILE, TILE), :], second, near_sem.at[0])])
+    copies = run([
+        pltpu.make_async_copy(piece, far.at[rows_of(at_ref, *rest), :], sem.at[k])
+        for k, (piece, rest) in enumerate(zip(pieces, plan))
+    ])
     text = text_ref[...]
     scale = scale_ref[0] * LOG2E
     top = jnp.full((1, SIDE), LOW, F32)
     sums = jnp.zeros((1, SIDE), F32)
     row_lse = []
     for k in range(STEPS):
+        tile = slice(k * TILE, (k + 1) * TILE)
+        if k == 1:
+            wait(near)
         if k == STEPS // 2:
-            wait(copies[near:])
-            run(out[1:])
-        tile = slice(k * TILE, (k + 1) * TILE)
+            wait(copies)
+            out = run([pltpu.make_async_copy(far, far_out, out_sem.at[0])])
+        image = (first_ref, second, far.at[pl.ds(0, TILE), :], far.at[pl.ds(TILE, TILE), :])[k][...]
         logits = scale * lax.dot_general(
-            image_ref[tile, :], text, (((1,), (1,)), ((), ())), preferred_element_type=F32
+            image, text, (((1,), (1,)), ((), ())), preferred_element_type=F32
         )
         logits_ref[tile, :] = logits
         row_top = jnp.max(logits, axis=1, keepdims=True)
@@ -257,16 +271,16 @@
             ).astype(BF16)
 
 
-def text_back_kernel(scale_ref, weights_ref, turned_ref, image_ref, text_ref, sums_ref, out_ref, mine_ref, back, sem):
-    image = image_ref[...]
+def text_back_kernel(scale_ref, weights_ref, turned_ref, near_ref, far_ref, text_ref, sums_ref, out_ref, mine_ref, back, sem):
+    near, far = near_ref[...], far_ref[...]
     mark = tag(sums_ref[:1, :1], MARK)
     half = PEERS // 2
     copies = []
     for h in range(2):
-        term = (
-            scale_ref[0]
-            * jnp.dot(turned_ref[h * half * PIECE : (h + 1) * half * PIECE, :], image, preferred_element_type=F32)
-        ).astype(BF16)
+        turned = turned_ref[h * half * PIECE : (h + 1) * half * PIECE, :]
+        term = jnp.dot(turned[:, : SIDE // 2], near, preferred_element_type=F32)
+        term += jnp.dot(turned[:, SIDE // 2 :], far, preferred_element_type=F32)
+        term = (scale_ref[0] * term).astype(BF16)
         for p in range(half):
             start = (h * half + p) * PART
             for b in range(WIDTH // 128):
@@ -377,15 +391,14 @@
 
 
 def gather_image(unit):
-    plan, arrays = [(0, 0, 0, PIECE)], [unit]
+    plan, arrays = [(0, 0, PIECE)], [unit]
     up, down, half = unit, unit, PIECE // 2
     for by in range(1, DEEP // 2):
         up, down = send(up, "z", 1), send(down, "z", -1)
-        plan += [(0, -by, 0, PIECE), (0, by, 0, PIECE)]
+        plan += [(-by, 0, PIECE), (by, 0, PIECE)]
         arrays += [up, down]
-    plan += [(0, -(DEEP // 2), 0, half), (0, DEEP // 2, half, half)]
+    plan += [(-(DEEP // 2), 0, half), (DEEP // 2, half, half)]
     arrays += [send(up[:half], "z", 1), send(down[half:], "z", -1)]
-    plan += [(1, *rest) for _, *rest in plan]
     arrays += [send(a, "c", 1) for a in arrays]
     return plan, arrays
 
@@ -410,18 +423,23 @@
     text = exchange(text_units, XY)
 
 
+    half = (SIDE // 2, width)
+    side = pltpu.VMEM(half, BF16)
+    near, first = call(
+        functools.partial(near_kernel, plan), [array(half, BF16), local((TILE, width), BF16)],
+        at, *map(Outside, pieces[: len(plan)]), scratch=[side, sems((len(plan),)), sems((1,))],
+    )
     lines = local((2 * STEPS, TILE), F32)
-    image, logits, keep, give = call(
-        functools.partial(logits_kernel, plan), [outside, local((SIDE, SIDE), F32), lines, lines],
-        at, scale, pairs, text, *map(Outside, pieces),
-        scratch=[pltpu.VMEM((SIDE, width), BF16), sems((len(plan),)), sems((2,))],
+    far, logits, keep, give = call(
+        functools.partial(logits_kernel, plan), [array(half, BF16), local((SIDE, SIDE), F32), lines, lines],
+        at, scale, pairs, text, first, Outside(near), *map(Outside, pieces[len(plan) :]),
+        scratch=[pltpu.VMEM((TILE, width), BF16), side, sems((len(plan),)), sems((1,)), sems((1,))],
     )
     spread = call(spread_kernel, local((PEERS * LINES, TILE), F32), at, keep, send(give, "c", 1))
     lines = local((2 * STEPS, TILE), F32)
     keep, give = call(join_kernel, [lines, lines], at, exchange(spread, MIXED))
     recv = send(give, "c", 1)
 
-    half = (SIDE // 2, width)
     weights, turned, other, sums = call(
         weights_kernel,
         [local((SIDE // 2, SIDE), BF16), local((SIDE, SIDE), BF16), local(half, BF16), local((2 * STEPS, 128), F32)],
@@ -430,7 +448,7 @@
     swapped = send(other, "c", 1)
     parts = array((PEERS * PART, 128), BF16)
     text_parts, mine = call(
-        text_back_kernel, [parts, local(half, F32)], scale, weights, turned, image, text, sums,
+        text_back_kernel, [parts, local(half, F32)], scale, weights, turned, near, far, text, sums,
         scratch=[pltpu.VMEM(parts.shape, BF16), sems((2,))],
     )
     end = array((FIRST, 128), BF16)

time: 127 us -> 127 us (level)
  Pallas kernels: 28.4 us -> 31.6 us
  starting transfers between devices: 49.7 us -> 46.8 us
  waiting for transfers between devices: 35.3 us -> 33.5 us
    pallas_call x12 -> x13, Pallas kernels: 28.4 us -> 31.6 us  [call(): pl.pallas_call(kernel, out_shape=outputs, in_specs=specs, out_specs=jax.t...]
    ppermute x28, starting transfers between devices: 35.3 us -> 32.6 us  [send(): return lax.ppermute(x, 'd', shift(axis, by))]
  transfers between devices with their start and end apart: 30 -> 30, of which waited for: 19 -> 17; matrix products, arithmetic and copies ran while one was open for 0% -> 1% of each run, Pallas kernels for 9% -> 12%
where the time goes in v9:
time: 127 us; the launch traced here: 126 us
  starting transfers between devices  46.8 us (37%)
  waiting for transfers between devices  33.5 us (26%)
  Pallas kernels  31.6 us (25%)
  blocking collectives  11.2 us (9%)
  between operations  2.32 us (2%)
    ppermute x28, starting transfers between devices, send(): return lax.ppermute(x, 'd', shift(axis, by))  32.6 us
    pallas_call x13, Pallas kernels, call(): pl.pallas_call(kernel, out_shape=outputs, in_specs=specs, out_specs=jax.t...  31.6 us
    ppermute x28, waiting for transfers between devices, send(): return lax.ppermute(x, 'd', shift(axis, by))  31.1 us
    all_to_all x2, starting transfers between devices, exchange(): return lax.all_to_all(x, 'd', 0, 0, axis_index_groups=groups, tiled=True)  14.2 us
    all_to_all x1, blocking collectives, exchange(): return lax.all_to_all(x, 'd', 0, 0, axis_index_groups=groups, tiled=True)  11.2 us
  transfers between devices with their start and end apart: 30, of which 17 were waited for; matrix products, arithmetic and copies ran while one was open for 1% of the time, Pallas kernels for 12%

profile of v9, /device:TPU:28, one launch (start us, length us, event | category | flops | bytes accessed | tf_op | source)
XLA Modules:
  0.0 126.5 jit_solution(14780720260308097861)
XLA Ops:
  0.6 2.7 %shard_map.58 = (bf16[1024,1280]{1,0:T(8,128)(2,1)}, bf16[64,1280]{1,0:T(8,128)(2,1)}, f32[8,128]{1,0:T(8,128)S(1)}) custom-call(bf16[64,1280]{1,0:T(8,128)(2,1)} %raw_ref.3, bf16[64,1280]{1,0:T(8,128)(2,1)} %raw_ref.2), custom_call_target="tpu_custom_call" | custom-call | tf_op jit(solution)/shard_map/pallas_call | solution.py:75
  3.4 7.1 %all-to-all-start = ((bf16[16,64,1280]{2,1,0:T(8,128)(2,1)}), bf16[16,64,1280]{2,1,0:T(8,128)(2,1)S(1)}, u32[]{:S(2)}, u32[]{:S(2)}) async-start(bf16[16,64,1280]{2,1,0:T(8,128)(2,1)} %bitcast.18), calls=%async_computation | async-start | bytes 5242880 | tf_op jit(solution)/shard_map/all_to_all | solution.py:52
  10.5 5.9 %collective-permute-start.1 = (bf16[64,1280]{1,0:T(8,128)(2,1)}, bf16[64,1280]{1,0:T(8,128)(2,1)S(1)}, u32[]{:S(2)}, u32[]{:S(2)}) collective-permute-start(bf16[64,1280]{1,0:T(8,128)(2,1)} %get-tuple-element.42.refs_0_), channel_id=1, source_target_pairs={{0,7},{1,0},{2,1},{3,2},{4,3},{5,4},{6,5},{7,6},{8,15},{9,8},{10,9... | collective-permute-start | bytes 491528 | tf_op jit(solution)/shard_map/ppermute | solution.py:48
  16.4 3.2 %collective-permute-done.1.refs_2_ = bf16[64,1280]{1,0:T(8,128)(2,1)S(1)} collective-permute-done((bf16[64,1280]{1,0:T(8,128)(2,1)}, bf16[64,1280]{1,0:T(8,128)(2,1)S(1)}, u32[]{:S(2)}, u32[]{:S(2)}) %collective-permute-start.1) | collective-permute-done | bytes 163872 | tf_op jit(solution)/shard_map/ppermute | solution.py:48
  19.6 3.6 %collective-permute-start.3 = (bf16[64,1280]{1,0:T(8,128)(2,1)S(1)}, bf16[64,1280]{1,0:T(8,128)(2,1)S(1)}, u32[]{:S(2)}, u32[]{:S(2)}) collective-permute-start(bf16[64,1280]{1,0:T(8,128)(2,1)S(1)} %collective-permute-done.1.refs_2_), channel_id=1, source_target_pairs={{0,7},{1,0},{2,1},{3,2},{4,3},{5,4},{6,5},{7,6},{8,15},{9,8},{10,9... | collective-permute-start | bytes 491528 | tf_op jit(solution)/shard_map/ppermute | solution.py:48
  23.2 2.8 %collective-permute-done.3.refs_4_ = bf16[64,1280]{1,0:T(8,128)(2,1)S(1)} collective-permute-done((bf16[64,1280]{1,0:T(8,128)(2,1)S(1)}, bf16[64,1280]{1,0:T(8,128)(2,1)S(1)}, u32[]{:S(2)}, u32[]{:S(2)}) %collective-permute-start.3) | collective-permute-done | bytes 163872 | tf_op jit(solution)/shard_map/ppermute | solution.py:48
  26.0 3.7 %collective-permute-start.5 = (bf16[64,1280]{1,0:T(8,128)(2,1)S(1)}, bf16[64,1280]{1,0:T(8,128)(2,1)}, u32[]{:S(2)}, u32[]{:S(2)}) collective-permute-start(bf16[64,1280]{1,0:T(8,128)(2,1)S(1)} %collective-permute-done.3.refs_4_), channel_id=1, source_target_pairs={{0,7},{1,0},{2,1},{3,2},{4,3},{5,4},{6,5},{7,6},{8,15},{9,8},{10,9... | collective-permute-start | bytes 491528 | tf_op jit(solution)/shard_map/ppermute | solution.py:48
  30.4 2.2 %collective-permute-done.5.refs_6_ = bf16[64,1280]{1,0:T(8,128)(2,1)} collective-permute-done((bf16[64,1280]{1,0:T(8,128)(2,1)S(1)}, bf16[64,1280]{1,0:T(8,128)(2,1)}, u32[]{:S(2)}, u32[]{:S(2)}) %collective-permute-start.5) | collective-permute-done | bytes 163872 | tf_op jit(solution)/shard_map/ppermute | solution.py:48
  33.4 3.1 %collective-permute-done.4.refs_5_ = bf16[64,1280]{1,0:T(8,128)(2,1)S(1)} collective-permute-done((bf16[64,1280]{1,0:T(8,128)(2,1)}, bf16[64,1280]{1,0:T(8,128)(2,1)S(1)}, u32[]{:S(2)}, u32[]{:S(2)}) %collective-permute-start.4) | collective-permute-done | bytes 163872 | tf_op jit(solution)/shard_map/ppermute | solution.py:48
  39.3 2.3 %collective-permute-done.7.refs_8_ = bf16[32,1280]{1,0:T(8,128)(2,1)} collective-permute-done((bf16[32,1280]{1,0:T(8,128)(2,1)S(1)}, bf16[32,1280]{1,0:T(8,128)(2,1)}, u32[]{:S(2)}, u32[]{:S(2)}) %collective-permute-start.7) | collective-permute-done | bytes 81952 | tf_op jit(solution)/shard_map/ppermute | solution.py:48
  41.6 2.0 %collective-permute-done.6.refs_7_ = bf16[32,1280]{1,0:T(8,128)(2,1)S(1)} collective-permute-done((bf16[32,1280]{1,0:T(8,128)(2,1)S(1)}, bf16[32,1280]{1,0:T(8,128)(2,1)S(1)}, u32[]{:S(2)}, u32[]{:S(2)}) %collective-permute-start.6) | collective-permute-done | bytes 81952 | tf_op jit(solution)/shard_map/ppermute | solution.py:48
  44.4 3.1 %shard_map.59 = (bf16[512,1280]{1,0:T(8,128)(2,1)}, bf16[256,1280]{1,0:T(8,128)(2,1)S(1)}) custom-call(s32[5]{0:T(128)S(1)} %stack.23.at_ref, bf16[64,1280]{1,0:T(8,128)(2,1)} %get-tuple-element.42.refs_0_, bf16[64,1280]{1,0:T(8,128)(2,1)} %copy-done.8, bf16[64,1280]{1,0:T(8,128)(2,1)} %copy-done.7, bf16[64,1280]{1,0:T(8,128)(2,1)} %collective-permute-done.2.refs_3_, ...), custom_call_target="tpu_custom_call" | custom-call | tf_op jit(solution)/shard_map/pallas_call | solution.py:75
  47.6 6.3 %shard_map.60 = (bf16[512,1280]{1,0:T(8,128)(2,1)}, f32[1024,1024]{1,0:T(8,128)S(1)}, f32[8,256]{1,0:T(8,128)S(1)}, f32[8,256]{1,0:T(8,128)S(1)}) custom-call(s32[5]{0:T(128)S(1)} %stack.23.at_ref, f32[1]{0:T(128)S(6)} %exp.3.scale_ref, f32[8,128]{1,0:T(8,128)S(1)} %get-tuple-element.40.pairs_ref, bf16[1024,1280]{1,0:T(8,128)(2,1)S(1)} %bitcast.11, ...), custom_call_target="tpu_custom_call" | custom-call | tf_op jit(solution)/shard_map/pallas_call | solution.py:75
  55.9 11.2 %all_to_all.33 = f32[16,8,256]{2,1,0:T(8,128)S(1)} all-to-all(f32[16,8,256]{2,1,0:T(8,128)S(1)} %bitcast.16), channel_id=1, replica_groups={{0,16,32,48,64,80,96,112,128,144,160,176,192,208,224,240},{1,17,33,49,6..., dimensions={0} | all-to-all | bytes 262144 | tf_op jit(solution)/shard_map/all_to_all | solution.py:52
  67.9 1.7 %collective-permute-start.18 = (f32[8,256]{1,0:T(8,128)S(1)}, f32[8,256]{1,0:T(8,128)S(1)}, u32[]{:S(2)}, u32[]{:S(2)}) collective-permute-start(f32[8,256]{1,0:T(8,128)S(1)} %get-tuple-element.49), channel_id=1, source_target_pairs={{0,8},{1,9},{2,10},{3,11},{4,12},{5,13},{6,14},{7,15},{8,0},{9,1},... | collective-permute-start | bytes 24584 | tf_op jit(solution)/shard_map/ppermute | solution.py:48
  70.4 2.9 %shard_map.63 = (bf16[512,1024]{1,0:T(8,128)(2,1)S(1)}, bf16[1024,1024]{1,0:T(8,128)(2,1)S(1)}, bf16[512,1280]{1,0:T(8,128)(2,1)S(1)}, f32[8,128]{1,0:T(8,128)S(1)}) custom-call(s32[5]{0:T(128)S(1)} %stack.23.at_ref, f32[1]{0:T(128)S(6)} %exp.3.scale_ref, f32[1024,1024]{1,0:T(8,128)S(1)} %get-tuple-element.45.logits_ref, bf16[1024,1280]{1,0:T(8,128)(2,1)S(1)} %bitcast.12, ...), custom_call_target="tpu_custom_call" | custom-call | tf_op jit(solution)/shard_map/pallas_call | solution.py:75
  73.7 4.3 %shard_map.64 = (bf16[10496,128]{1,0:T(8,128)(2,1)}, f32[512,1280]{1,0:T(8,128)S(1)}) custom-call(f32[1]{0:T(128)S(6)} %exp.3.scale_ref, bf16[512,1024]{1,0:T(8,128)(2,1)S(1)} %get-tuple-element.51.weights_ref, bf16[1024,1024]{1,0:T(8,128)(2,1)S(1)} %get-tuple-element.52.turned_ref, bf16[512,1280]{1,0:T(8,128)(2,1)S(1)} %copy-done, ...), custom_call_target="tpu_custom_call" | custom-call | tf_op jit(solution)/shard_map/pallas_call | solution.py:75
  78.0 1.8 %shard_map.65 = (bf16[10496,128]{1,0:T(8,128)(2,1)}, f32[64,1280]{1,0:T(8,128)}, bf16[336,128]{1,0:T(8,128)(2,1)}, bf16[336,128]{1,0:T(8,128)(2,1)}, bf16[64,128...) custom-call(s32[5]{0:T(128)S(1)} %stack.23.at_ref, ...), custom_call_target="tpu_custom_call", output_to_operand_aliasing={{0}: (4, {})} | custom-call | tf_op jit(solution)/shard_map/pallas_call | solution.py:75
  79.8 7.1 %all-to-all-start.2 = ((bf16[16,656,128]{2,1,0:T(8,128)(2,1)}), bf16[16,656,128]{2,1,0:T(8,128)(2,1)S(1)}, u32[]{:S(2)}, u32[]{:S(2)}) async-start(bf16[16,656,128]{2,1,0:T(8,128)(2,1)} %bitcast.17), calls=%async_computation.2 | async-start | bytes 5373952 | tf_op jit(solution)/shard_map/all_to_all | solution.py:52
  86.9 1.7 %collective-permute-start.20 = (bf16[336,128]{1,0:T(8,128)(2,1)S(1)}, bf16[336,128]{1,0:T(8,128)(2,1)S(1)}, u32[]{:S(2)}, u32[]{:S(2)}) collective-permute-start(bf16[336,128]{1,0:T(8,128)(2,1)S(1)} %copy-done.12), channel_id=1, source_target_pairs={{0,1},{1,2},{2,3},{3,4},{4,5},{5,6},{6,7},{7,0},{8,9},{9,10},{10,1... | collective-permute-start | bytes 258056 | tf_op jit(solution)/shard_map/ppermute | solution.py:48
  88.6 1.9 %collective-permute-start.21 = (bf16[336,128]{1,0:T(8,128)(2,1)S(1)}, bf16[336,128]{1,0:T(8,128)(2,1)S(1)}, u32[]{:S(2)}, u32[]{:S(2)}) collective-permute-start(bf16[336,128]{1,0:T(8,128)(2,1)S(1)} %copy-done.11), channel_id=1, source_target_pairs={{0,7},{1,0},{2,1},{3,2},{4,3},{5,4},{6,5},{7,6},{8,15},{9,8},{10,9... | collective-permute-start | bytes 258056 | tf_op jit(solution)/shard_map/ppermute | solution.py:48
  90.5 2.5 %collective-permute-done.20.below_ref = bf16[336,128]{1,0:T(8,128)(2,1)S(1)} collective-permute-done((bf16[336,128]{1,0:T(8,128)(2,1)S(1)}, bf16[336,128]{1,0:T(8,128)(2,1)S(1)}, u32[]{:S(2)}, u32[]{:S(2)}) %collective-permute-start.20) | collective-permute-done | bytes 86048 | tf_op jit(solution)/shard_map/ppermute | solution.py:48
  95.5 2.5 %collective-permute-start.23 = (bf16[656,128]{1,0:T(8,128)(2,1)S(1)}, bf16[656,128]{1,0:T(8,128)(2,1)S(1)}, u32[]{:S(2)}, u32[]{:S(2)}) collective-permute-start(bf16[656,128]{1,0:T(8,128)(2,1)S(1)} %get-tuple-element.67), channel_id=1, source_target_pairs={{0,7},{1,0},{2,1},{3,2},{4,3},{5,4},{6,5},{7,6},{8,15},{9,8},{10,9... | collective-permute-start | bytes 503816 | tf_op jit(solution)/shard_map/ppermute | solution.py:48
  98.0 3.3 %collective-permute-done.22.below_ref = bf16[656,128]{1,0:T(8,128)(2,1)S(1)} collective-permute-done((bf16[656,128]{1,0:T(8,128)(2,1)S(1)}, bf16[656,128]{1,0:T(8,128)(2,1)S(1)}, u32[]{:S(2)}, u32[]{:S(2)}) %collective-permute-start.22) | collective-permute-done | bytes 167968 | tf_op jit(solution)/shard_map/ppermute | solution.py:48
  102.9 1.7 %collective-permute-start.24 = (bf16[656,128]{1,0:T(8,128)(2,1)S(1)}, bf16[656,128]{1,0:T(8,128)(2,1)S(1)}, u32[]{:S(2)}, u32[]{:S(2)}) collective-permute-start(bf16[656,128]{1,0:T(8,128)(2,1)S(1)} %get-tuple-element.68), channel_id=1, source_target_pairs={{0,1},{1,2},{2,3},{3,4},{4,5},{5,6},{6,7},{7,0},{8,9},{9,10},{10,1... | collective-permute-start | bytes 503816 | tf_op jit(solution)/shard_map/ppermute | solution.py:48
  104.6 1.7 %collective-permute-start.25 = (bf16[656,128]{1,0:T(8,128)(2,1)S(1)}, bf16[656,128]{1,0:T(8,128)(2,1)S(1)}, u32[]{:S(2)}, u32[]{:S(2)}) collective-permute-start(bf16[656,128]{1,0:T(8,128)(2,1)S(1)} %get-tuple-element.69), channel_id=1, source_target_pairs={{0,7},{1,0},{2,1},{3,2},{4,3},{5,4},{6,5},{7,6},{8,15},{9,8},{10,9... | collective-permute-start | bytes 503816 | tf_op jit(solution)/shard_map/ppermute | solution.py:48
  106.3 3.3 %collective-permute-done.24.below_ref = bf16[656,128]{1,0:T(8,128)(2,1)S(1)} collective-permute-done((bf16[656,128]{1,0:T(8,128)(2,1)S(1)}, bf16[656,128]{1,0:T(8,128)(2,1)S(1)}, u32[]{:S(2)}, u32[]{:S(2)}) %collective-permute-start.24) | collective-permute-done | bytes 167968 | tf_op jit(solution)/shard_map/ppermute | solution.py:48
  111.6 2.1 %collective-permute-start.26 = (bf16[656,128]{1,0:T(8,128)(2,1)S(1)}, bf16[656,128]{1,0:T(8,128)(2,1)S(1)}, u32[]{:S(2)}, u32[]{:S(2)}) collective-permute-start(bf16[656,128]{1,0:T(8,128)(2,1)S(1)} %get-tuple-element.70), channel_id=1, source_target_pairs={{0,1},{1,2},{2,3},{3,4},{4,5},{5,6},{6,7},{7,0},{8,9},{9,10},{10,1... | collective-permute-start | bytes 503816 | tf_op jit(solution)/shard_map/ppermute | solution.py:48
  114.9 3.3 %collective-permute-done.26.below_ref = bf16[656,128]{1,0:T(8,128)(2,1)S(1)} collective-permute-done((bf16[656,128]{1,0:T(8,128)(2,1)S(1)}, bf16[656,128]{1,0:T(8,128)(2,1)S(1)}, u32[]{:S(2)}, u32[]{:S(2)}) %collective-permute-start.26) | collective-permute-done | bytes 167968 | tf_op jit(solution)/shard_map/ppermute | solution.py:48
  119.0 2.5 %shard_map.69 = (bf16[64,1280]{1,0:T(8,128)(2,1)}, f32[8,128]{1,0:T(8,128)S(1)}) custom-call(s32[5]{0:T(128)S(1)} %stack.23.at_ref, f32[8,128]{1,0:T(8,128)S(1)} %get-tuple-element.50.sums_ref, bf16[64,1280]{1,0:T(8,128)(2,1)} %raw_ref.2, f32[64,1280]{1,0:T(8,128)} %get-tuple-element.57.own_ref, bf16[656,128]{1,0:T(8,128)(2,1)S(1)} %collective-permute-done.26.below_ref, ...), custom_call_target="tpu_custom_call" | custom-call | tf_op jit(solution)/shard_map/pallas_call | solution.py:75
  121.6 2.4 %all-to-all-done.2 = bf16[16,656,128]{2,1,0:T(8,128)(2,1)S(1)} async-done(((bf16[16,656,128]{2,1,0:T(8,128)(2,1)}), bf16[16,656,128]{2,1,0:T(8,128)(2,1)S(1)}, u32[]{:S(2)}, u32[]{:S(2)}) %all-to-all-start.2) | async-done | bytes 2687008 | tf_op jit(solution)/shard_map/all_to_all | solution.py:52
  123.9 1.8 %shard_map.70 = (bf16[64,1280]{1,0:T(8,128)(2,1)}, f32[1]{0:T(128)S(4)}) custom-call(bf16[64,1280]{1,0:T(8,128)(2,1)} %raw_ref.3, f32[8,128]{1,0:T(8,128)S(1)} %get-tuple-element.72.loss_ref, bf16[10496,128]{1,0:T(8,128)(2,1)S(1)} %bitcast.14), custom_call_target="tpu_custom_call" | custom-call | tf_op jit(solution)/shard_map/pallas_call | solution.py:75
  (71 shorter events, 16.5 us)
Async XLA Ops:
  3.4 44.2 %all-to-all-start = ((bf16[16,64,1280]{2,1,0:T(8,128)(2,1)}), bf16[16,64,1280]{2,1,0:T(8,128)(2,1)S(1)}, u32[]{:S(2)}, u32[]{:S(2)}) async-start(bf16[16,64,1280]{2,1,0:T(8,128)(2,1)} %bitcast.18), calls=%async_computation | async-start | bytes 5242880 | tf_op jit(solution)/shard_map/all_to_all | solution.py:52
  10.5 9.1 %collective-permute-start.1 = (bf16[64,1280]{1,0:T(8,128)(2,1)}, bf16[64,1280]{1,0:T(8,128)(2,1)S(1)}, u32[]{:S(2)}, u32[]{:S(2)}) collective-permute-start(bf16[64,1280]{1,0:T(8,128)(2,1)} %get-tuple-element.42.refs_0_), channel_id=1, source_target_pairs={{0,7},{1,0},{2,1},{3,2},{4,3},{5,4},{6,5},{7,6},{8,15},{9,8},{10,9... | collective-permute-start | bytes 491528 | tf_op jit(solution)/shard_map/ppermute | solution.py:48
  16.4 6.8 %collective-permute-start = (bf16[64,1280]{1,0:T(8,128)(2,1)}, bf16[64,1280]{1,0:T(8,128)(2,1)S(1)}, u32[]{:S(2)}, u32[]{:S(2)}) collective-permute-start(bf16[64,1280]{1,0:T(8,128)(2,1)} %get-tuple-element.42.refs_0_), channel_id=1, source_target_pairs={{0,1},{1,2},{2,3},{3,4},{4,5},{5,6},{6,7},{7,0},{8,9},{9,10},{10,1... | collective-permute-start | bytes 491528 | tf_op jit(solution)/shard_map/ppermute | solution.py:48
  19.6 19.1 %copy-start.7 = (bf16[64,1280]{1,0:T(8,128)(2,1)}, bf16[64,1280]{1,0:T(8,128)(2,1)S(1)}, u32[]{:S(2)}) copy-start(bf16[64,1280]{1,0:T(8,128)(2,1)S(1)} %collective-permute-done.1.refs_2_) | copy-start | bytes 491524
  19.6 6.4 %collective-permute-start.3 = (bf16[64,1280]{1,0:T(8,128)(2,1)S(1)}, bf16[64,1280]{1,0:T(8,128)(2,1)S(1)}, u32[]{:S(2)}, u32[]{:S(2)}) collective-permute-start(bf16[64,1280]{1,0:T(8,128)(2,1)S(1)} %collective-permute-done.1.refs_2_), channel_id=1, source_target_pairs={{0,7},{1,0},{2,1},{3,2},{4,3},{5,4},{6,5},{7,6},{8,15},{9,8},{10,9... | collective-permute-start | bytes 491528 | tf_op jit(solution)/shard_map/ppermute | solution.py:48
  23.2 16.1 %copy-start.8 = (bf16[64,1280]{1,0:T(8,128)(2,1)}, bf16[64,1280]{1,0:T(8,128)(2,1)S(1)}, u32[]{:S(2)}) copy-start(bf16[64,1280]{1,0:T(8,128)(2,1)S(1)} %collective-permute-done.refs_1_) | copy-start | bytes 491524
  23.2 6.6 %collective-permute-start.2 = (bf16[64,1280]{1,0:T(8,128)(2,1)S(1)}, bf16[64,1280]{1,0:T(8,128)(2,1)}, u32[]{:S(2)}, u32[]{:S(2)}) collective-permute-start(bf16[64,1280]{1,0:T(8,128)(2,1)S(1)} %collective-permute-done.refs_1_), channel_id=1, source_target_pairs={{0,1},{1,2},{2,3},{3,4},{4,5},{5,6},{6,7},{7,0},{8,9},{9,10},{10,1... | collective-permute-start | bytes 491528 | tf_op jit(solution)/shard_map/ppermute | solution.py:48
  26.0 6.5 %collective-permute-start.5 = (bf16[64,1280]{1,0:T(8,128)(2,1)S(1)}, bf16[64,1280]{1,0:T(8,128)(2,1)}, u32[]{:S(2)}, u32[]{:S(2)}) collective-permute-start(bf16[64,1280]{1,0:T(8,128)(2,1)S(1)} %collective-permute-done.3.refs_4_), channel_id=1, source_target_pairs={{0,7},{1,0},{2,1},{3,2},{4,3},{5,4},{6,5},{7,6},{8,15},{9,8},{10,9... | collective-permute-start | bytes 491528 | tf_op jit(solution)/shard_map/ppermute | solution.py:48
  29.8 6.7 %collective-permute-start.4 = (bf16[64,1280]{1,0:T(8,128)(2,1)}, bf16[64,1280]{1,0:T(8,128)(2,1)S(1)}, u32[]{:S(2)}, u32[]{:S(2)}) collective-permute-start(bf16[64,1280]{1,0:T(8,128)(2,1)} %collective-permute-done.2.refs_3_), channel_id=1, source_target_pairs={{0,1},{1,2},{2,3},{3,4},{4,5},{5,6},{6,7},{7,0},{8,9},{9,10},{10,1... | collective-permute-start | bytes 491528 | tf_op jit(solution)/shard_map/ppermute | solution.py:48
  29.8 6.8 %collective-permute-start.8 = (bf16[64,1280]{1,0:T(8,128)(2,1)}, bf16[64,1280]{1,0:T(8,128)(2,1)S(1)}, u32[]{:S(2)}, u32[]{:S(2)}) collective-permute-start(bf16[64,1280]{1,0:T(8,128)(2,1)} %get-tuple-element.42.refs_0_), channel_id=1, source_target_pairs={{0,8},{1,9},{2,10},{3,11},{4,12},{5,13},{6,14},{7,15},{8,0},{9,1},... | collective-permute-start | bytes 491528 | tf_op jit(solution)/shard_map/ppermute | solution.py:48
  29.8 8.1 %collective-permute-start.10 = (bf16[64,1280]{1,0:T(8,128)(2,1)S(1)}, bf16[64,1280]{1,0:T(8,128)(2,1)S(1)}, u32[]{:S(2)}, u32[]{:S(2)}) collective-permute-start(bf16[64,1280]{1,0:T(8,128)(2,1)S(1)} %collective-permute-done.1.refs_2_), channel_id=1, source_target_pairs={{0,8},{1,9},{2,10},{3,11},{4,12},{5,13},{6,14},{7,15},{8,0},{9,1},... | collective-permute-start | bytes 491528 | tf_op jit(solution)/shard_map/ppermute | solution.py:48
  30.3 8.4 %collective-permute-start.9 = (bf16[64,1280]{1,0:T(8,128)(2,1)S(1)}, bf16[64,1280]{1,0:T(8,128)(2,1)S(1)}, u32[]{:S(2)}, u32[]{:S(2)}) collective-permute-start(bf16[64,1280]{1,0:T(8,128)(2,1)S(1)} %collective-permute-done.refs_1_), channel_id=1, source_target_pairs={{0,8},{1,9},{2,10},{3,11},{4,12},{5,13},{6,14},{7,15},{8,0},{9,1},... | collective-permute-start | bytes 491528 | tf_op jit(solution)/shard_map/ppermute | solution.py:48
  32.5 6.2 %collective-permute-start.12 = (bf16[64,1280]{1,0:T(8,128)(2,1)S(1)}, bf16[64,1280]{1,0:T(8,128)(2,1)S(1)}, u32[]{:S(2)}, u32[]{:S(2)}) collective-permute-start(bf16[64,1280]{1,0:T(8,128)(2,1)S(1)} %collective-permute-done.3.refs_4_), channel_id=1, source_target_pairs={{0,8},{1,9},{2,10},{3,11},{4,12},{5,13},{6,14},{7,15},{8,0},{9,1},... | collective-permute-start | bytes 491528 | tf_op jit(solution)/shard_map/ppermute | solution.py:48
  36.5 11.0 %collective-permute-start.11 = (bf16[64,1280]{1,0:T(8,128)(2,1)}, bf16[64,1280]{1,0:T(8,128)(2,1)}, u32[]{:S(2)}, u32[]{:S(2)}) collective-permute-start(bf16[64,1280]{1,0:T(8,128)(2,1)} %collective-permute-done.2.refs_3_), channel_id=1, source_target_pairs={{0,8},{1,9},{2,10},{3,11},{4,12},{5,13},{6,14},{7,15},{8,0},{9,1},... | collective-permute-start | bytes 491528 | tf_op jit(solution)/shard_map/ppermute | solution.py:48
  36.6 5.0 %collective-permute-start.7 = (bf16[32,1280]{1,0:T(8,128)(2,1)S(1)}, bf16[32,1280]{1,0:T(8,128)(2,1)}, u32[]{:S(2)}, u32[]{:S(2)}) collective-permute-start(bf16[32,1280]{1,0:T(8,128)(2,1)S(1)} %slice.9), channel_id=1, source_target_pairs={{0,7},{1,0},{2,1},{3,2},{4,3},{5,4},{6,5},{7,6},{8,15},{9,8},{10,9... | collective-permute-start | bytes 245768 | tf_op jit(solution)/shard_map/ppermute | solution.py:48
  37.9 5.7 %collective-permute-start.6 = (bf16[32,1280]{1,0:T(8,128)(2,1)S(1)}, bf16[32,1280]{1,0:T(8,128)(2,1)S(1)}, u32[]{:S(2)}, u32[]{:S(2)}) collective-permute-start(bf16[32,1280]{1,0:T(8,128)(2,1)S(1)} %slice.8), channel_id=1, source_target_pairs={{0,1},{1,2},{2,3},{3,4},{4,5},{5,6},{6,7},{7,0},{8,9},{9,10},{10,1... | collective-permute-start | bytes 245768 | tf_op jit(solution)/shard_map/ppermute | solution.py:48
  38.7 8.9 %collective-permute-start.14 = (bf16[64,1280]{1,0:T(8,128)(2,1)}, bf16[64,1280]{1,0:T(8,128)(2,1)}, u32[]{:S(2)}, u32[]{:S(2)}) collective-permute-start(bf16[64,1280]{1,0:T(8,128)(2,1)} %collective-permute-done.5.refs_6_), channel_id=1, source_target_pairs={{0,8},{1,9},{2,10},{3,11},{4,12},{5,13},{6,14},{7,15},{8,0},{9,1},... | collective-permute-start | bytes 491528 | tf_op jit(solution)/shard_map/ppermute | solution.py:48
  38.7 8.9 %collective-permute-start.13 = (bf16[64,1280]{1,0:T(8,128)(2,1)S(1)}, bf16[64,1280]{1,0:T(8,128)(2,1)}, u32[]{:S(2)}, u32[]{:S(2)}) collective-permute-start(bf16[64,1280]{1,0:T(8,128)(2,1)S(1)} %collective-permute-done.4.refs_5_), channel_id=1, source_target_pairs={{0,8},{1,9},{2,10},{3,11},{4,12},{5,13},{6,14},{7,15},{8,0},{9,1},... | collective-permute-start | bytes 491528 | tf_op jit(solution)/shard_map/ppermute | solution.py:48
  41.6 5.9 %collective-permute-start.16 = (bf16[32,1280]{1,0:T(8,128)(2,1)}, bf16[32,1280]{1,0:T(8,128)(2,1)}, u32[]{:S(2)}, u32[]{:S(2)}) collective-permute-start(bf16[32,1280]{1,0:T(8,128)(2,1)} %collective-permute-done.7.refs_8_), channel_id=1, source_target_pairs={{0,8},{1,9},{2,10},{3,11},{4,12},{5,13},{6,14},{7,15},{8,0},{9,1},... | collective-permute-start | bytes 245768 | tf_op jit(solution)/shard_map/ppermute | solution.py:48
  43.6 4.0 %collective-permute-start.15 = (bf16[32,1280]{1,0:T(8,128)(2,1)S(1)}, bf16[32,1280]{1,0:T(8,128)(2,1)}, u32[]{:S(2)}, u32[]{:S(2)}) collective-permute-start(bf16[32,1280]{1,0:T(8,128)(2,1)S(1)} %collective-permute-done.6.refs_7_), channel_id=1, source_target_pairs={{0,8},{1,9},{2,10},{3,11},{4,12},{5,13},{6,14},{7,15},{8,0},{9,1},... | collective-permute-start | bytes 245768 | tf_op jit(solution)/shard_map/ppermute | solution.py:48
  53.9 1.4 %collective-permute-start.17 = (f32[8,256]{1,0:T(8,128)S(1)}, f32[8,256]{1,0:T(8,128)S(1)}, u32[]{:S(2)}, u32[]{:S(2)}) collective-permute-start(f32[8,256]{1,0:T(8,128)S(1)} %get-tuple-element.47), channel_id=1, source_target_pairs={{0,8},{1,9},{2,10},{3,11},{4,12},{5,13},{6,14},{7,15},{8,0},{9,1},... | collective-permute-start | bytes 24584 | tf_op jit(solution)/shard_map/ppermute | solution.py:48
  67.9 2.5 %collective-permute-start.18 = (f32[8,256]{1,0:T(8,128)S(1)}, f32[8,256]{1,0:T(8,128)S(1)}, u32[]{:S(2)}, u32[]{:S(2)}) collective-permute-start(f32[8,256]{1,0:T(8,128)S(1)} %get-tuple-element.49), channel_id=1, source_target_pairs={{0,8},{1,9},{2,10},{3,11},{4,12},{5,13},{6,14},{7,15},{8,0},{9,1},... | collective-permute-start | bytes 24584 | tf_op jit(solution)/shard_map/ppermute | solution.py:48
  73.3 4.8 %collective-permute-start.19 = (bf16[512,1280]{1,0:T(8,128)(2,1)S(1)}, bf16[512,1280]{1,0:T(8,128)(2,1)S(1)}, u32[]{:S(2)}, u32[]{:S(2)}) collective-permute-start(bf16[512,1280]{1,0:T(8,128)(2,1)S(1)} %get-tuple-element.55), channel_id=1, source_target_pairs={{0,8},{1,9},{2,10},{3,11},{4,12},{5,13},{6,14},{7,15},{8,0},{9,1},... | collective-permute-start | bytes 3932168 | tf_op jit(solution)/shard_map/ppermute | solution.py:48
  79.8 44.1 %all-to-all-start.2 = ((bf16[16,656,128]{2,1,0:T(8,128)(2,1)}), bf16[16,656,128]{2,1,0:T(8,128)(2,1)S(1)}, u32[]{:S(2)}, u32[]{:S(2)}) async-start(bf16[16,656,128]{2,1,0:T(8,128)(2,1)} %bitcast.17), calls=%async_computation.2 | async-start | bytes 5373952 | tf_op jit(solution)/shard_map/all_to_all | solution.py:52
  86.9 6.0 %collective-permute-start.20 = (bf16[336,128]{1,0:T(8,128)(2,1)S(1)}, bf16[336,128]{1,0:T(8,128)(2,1)S(1)}, u32[]{:S(2)}, u32[]{:S(2)}) collective-permute-start(bf16[336,128]{1,0:T(8,128)(2,1)S(1)} %copy-done.12), channel_id=1, source_target_pairs={{0,1},{1,2},{2,3},{3,4},{4,5},{5,6},{6,7},{7,0},{8,9},{9,10},{10,1... | collective-permute-start | bytes 258056 | tf_op jit(solution)/shard_map/ppermute | solution.py:48
  88.6 4.5 %collective-permute-start.21 = (bf16[336,128]{1,0:T(8,128)(2,1)S(1)}, bf16[336,128]{1,0:T(8,128)(2,1)S(1)}, u32[]{:S(2)}, u32[]{:S(2)}) collective-permute-start(bf16[336,128]{1,0:T(8,128)(2,1)S(1)} %copy-done.11), channel_id=1, source_target_pairs={{0,7},{1,0},{2,1},{3,2},{4,3},{5,4},{6,5},{7,6},{8,15},{9,8},{10,9... | collective-permute-start | bytes 258056 | tf_op jit(solution)/shard_map/ppermute | solution.py:48
  94.7 6.7 %collective-permute-start.22 = (bf16[656,128]{1,0:T(8,128)(2,1)S(1)}, bf16[656,128]{1,0:T(8,128)(2,1)S(1)}, u32[]{:S(2)}, u32[]{:S(2)}) collective-permute-start(bf16[656,128]{1,0:T(8,128)(2,1)S(1)} %get-tuple-element.66), channel_id=1, source_target_pairs={{0,1},{1,2},{2,3},{3,4},{4,5},{5,6},{6,7},{7,0},{8,9},{9,10},{10,1... | collective-permute-start | bytes 503816 | tf_op jit(solution)/shard_map/ppermute | solution.py:48
  95.5 5.8 %collective-permute-start.23 = (bf16[656,128]{1,0:T(8,128)(2,1)S(1)}, bf16[656,128]{1,0:T(8,128)(2,1)S(1)}, u32[]{:S(2)}, u32[]{:S(2)}) collective-permute-start(bf16[656,128]{1,0:T(8,128)(2,1)S(1)} %get-tuple-element.67), channel_id=1, source_target_pairs={{0,7},{1,0},{2,1},{3,2},{4,3},{5,4},{6,5},{7,6},{8,15},{9,8},{10,9... | collective-permute-start | bytes 503816 | tf_op jit(solution)/shard_map/ppermute | solution.py:48
  102.9 6.7 %collective-permute-start.24 = (bf16[656,128]{1,0:T(8,128)(2,1)S(1)}, bf16[656,128]{1,0:T(8,128)(2,1)S(1)}, u32[]{:S(2)}, u32[]{:S(2)}) collective-permute-start(bf16[656,128]{1,0:T(8,128)(2,1)S(1)} %get-tuple-element.68), channel_id=1, source_target_pairs={{0,1},{1,2},{2,3},{3,4},{4,5},{5,6},{6,7},{7,0},{8,9},{9,10},{10,1... | collective-permute-start | bytes 503816 | tf_op jit(solution)/shard_map/ppermute | solution.py:48
  104.6 5.4 %collective-permute-start.25 = (bf16[656,128]{1,0:T(8,128)(2,1)S(1)}, bf16[656,128]{1,0:T(8,128)(2,1)S(1)}, u32[]{:S(2)}, u32[]{:S(2)}) collective-permute-start(bf16[656,128]{1,0:T(8,128)(2,1)S(1)} %get-tuple-element.69), channel_id=1, source_target_pairs={{0,7},{1,0},{2,1},{3,2},{4,3},{5,4},{6,5},{7,6},{8,15},{9,8},{10,9... | collective-permute-start | bytes 503816 | tf_op jit(solution)/shard_map/ppermute | solution.py:48
  111.6 6.7 %collective-permute-start.26 = (bf16[656,128]{1,0:T(8,128)(2,1)S(1)}, bf16[656,128]{1,0:T(8,128)(2,1)S(1)}, u32[]{:S(2)}, u32[]{:S(2)}) collective-permute-start(bf16[656,128]{1,0:T(8,128)(2,1)S(1)} %get-tuple-element.70), channel_id=1, source_target_pairs={{0,1},{1,2},{2,3},{3,4},{4,5},{5,6},{6,7},{7,0},{8,9},{9,10},{10,1... | collective-permute-start | bytes 503816 | tf_op jit(solution)/shard_map/ppermute | solution.py:48
  113.7 5.4 %collective-permute-start.27 = (bf16[656,128]{1,0:T(8,128)(2,1)S(1)}, bf16[656,128]{1,0:T(8,128)(2,1)S(1)}, u32[]{:S(2)}, u32[]{:S(2)}) collective-permute-start(bf16[656,128]{1,0:T(8,128)(2,1)S(1)} %get-tuple-element.71), channel_id=1, source_target_pairs={{0,7},{1,0},{2,1},{3,2},{4,3},{5,4},{6,5},{7,6},{8,15},{9,8},{10,9... | collective-permute-start | bytes 503816 | tf_op jit(solution)/shard_map/ppermute | solution.py:48
  (11 other events, 72.2 us)
